TPU v7x, 32 devices: a whole 2x2x4 slice. The times are simulated.
32 devices in a mesh: section: 4 (over y, x), dp: 8 (over z, core).
Axes of the slice: x: 2, y: 2, z: 4, core: 2. Of those that a mesh axis runs over, the one named last changes fastest.
Arguments:
- state_start: float32 [32, 15, 1024], P('dp'), may hold values from -6 to 6
- static_maps: float32 [75, 1024], replicated, may hold values from -6 to 6
- grouping: int32 [8, 4], P('dp'), may hold values from 0 to 3, each once within a row
- cotangent: float32 [4, 32, 15, 1024], P('section', 'dp'), may hold values from -6 to 6
- w_input: float32 [9, 100, 128], replicated, may hold values from -0.1875 to 0.1875
- b_input: float32 [128], replicated, may hold values from -3 to 3
- w_first: float32 [9, 128, 128], replicated, may hold values from -0.1875 to 0.1875
- gain_first: float32 [128], replicated, may hold values from 0.1 to 1.9
- shift_first: float32 [128], replicated, may hold values from -3 to 3
- w_second: float32 [9, 128, 128], replicated, may hold values from -0.1875 to 0.1875
- gain_second: float32 [128], replicated, may hold values from 0.1 to 1.9
- shift_second: float32 [128], replicated, may hold values from -3 to 3
- w_query: float32 [128, 128], replicated, may hold values from -0.5 to 0.5
- w_key: float32 [128, 128], replicated, may hold values from -0.5 to 0.5
- w_value: float32 [128, 128], replicated, may hold values from -0.5 to 0.5
- w_mixer: float32 [128, 128], replicated, may hold values from -1.5 to 1.5
- w_velocity: float32 [9, 128, 10], replicated, may hold values from -0.1875 to 0.1875
- b_velocity: float32 [10], replicated, may hold values from -3 to 3
Outputs:
- trajectory: float32 [4, 32, 15, 1024], P('section', 'dp')
- state_grads: float32 [4, 32, 15, 1024], P('section', 'dp')
- grad_w_input: float32 [9, 100, 128], replicated
- grad_b_input: float32 [128], replicated
- grad_w_first: float32 [9, 128, 128], replicated
- grad_gain_first: float32 [128], replicated
- grad_shift_first: float32 [128], replicated
- grad_w_second: float32 [9, 128, 128], replicated
- grad_gain_second: float32 [128], replicated
- grad_shift_second: float32 [128], replicated
- grad_w_query: float32 [128, 128], replicated
- grad_w_key: float32 [128, 128], replicated
- grad_w_value: float32 [128, 128], replicated
- grad_w_mixer: float32 [128, 128], replicated
- grad_w_velocity: float32 [9, 128, 10], replicated
- grad_b_velocity: float32 [10], replicated
Inputs may be any that keep to these rules, and one draw needn't show every extreme that they name: `grouping`: each row is an ordering of the 4 samples of one dp index.
All inputs are finite; a program needn't handle non-finite values.
Results may differ from a plain program's by a relative error of at most 0.0003.
Values sent between devices are 32-bit elements; how exact they have to be, the bound alone decides.
No kernel may reach another device: no remote copies, remote signals or barrier semaphores. Data moves between devices by JAX's collectives and lax.ppermute only.
A program may use at most 192 MiB of HBM per device.

v0:
```python
import math

import jax
import jax.numpy as jnp
from jax import lax
from jax.sharding import PartitionSpec as P

HEADS = 4
LAT = 16
ATT_ROWS = 8


HIGHEST = lax.Precision.HIGHEST
EPSILON = 1e-05


def passed_along(value, axis, steps):
    count = lax.axis_size(axis)
    first, last = (max(0, -steps), min(count, count - steps))
    return lax.ppermute(value, axis, [(source, source + steps) for source in range(first, last)])


def convolve(inputs, weight, lat_rows):
    count_items, pixels, channels = inputs.shape
    lon_cols = pixels // lat_rows
    planes = inputs.reshape(count_items, lat_rows, lon_cols, channels)
    padded = jnp.pad(planes, ((0, 0), (1, 1), (0, 0), (0, 0)))
    padded = jnp.concatenate([padded[:, :, -1:], padded, padded[:, :, :1]], axis=2)
    patches = jnp.concatenate(
        [
            padded[:, row_off : row_off + lat_rows, col_off : col_off + lon_cols]
            for row_off in range(3)
            for col_off in range(3)
        ],
        axis=3,
    )
    patches = patches.reshape(count_items, pixels, 9 * channels)
    return jnp.dot(patches, weight.reshape(9 * channels, weight.shape[2]), precision=HIGHEST)


def differences(values, lat_rows):
    count_items, quantities, pixels = values.shape
    planes = values.reshape(count_items, quantities, lat_rows, pixels // lat_rows)
    along_lon = 0.5 * (jnp.roll(planes, -1, axis=3) - jnp.roll(planes, 1, axis=3))
    padded = jnp.pad(planes, ((0, 0), (0, 0), (1, 1), (0, 0)))
    along_lat = 0.5 * (padded[:, :, 2:] - padded[:, :, :-2])
    return (along_lon.reshape(values.shape), along_lat.reshape(values.shape))


def inlet_part(state_in, static_maps, w_input, b_input, w_first, lat_rows):
    quantities = state_in.shape[1] // 3
    along_lon, along_lat = differences(state_in[:, :quantities], lat_rows)
    statics = jnp.broadcast_to(static_maps[None], (state_in.shape[0],) + static_maps.shape)
    stacked = jnp.concatenate([state_in, along_lon, along_lat, statics], axis=1)
    inputs = jnp.swapaxes(stacked, 1, 2)
    act_one = jax.nn.silu(convolve(inputs, w_input, lat_rows) + b_input)
    return (act_one, convolve(act_one, w_first, lat_rows))


def middle_part(
    pre_one, total_one, squares_one, gain_first, shift_first, w_second, count, lat_rows
):
    average = total_one / count
    spread = squares_one / count - average * average
    normed = gain_first * (pre_one - average) * lax.rsqrt(spread + EPSILON) + shift_first
    return convolve(jax.nn.silu(normed), w_second, lat_rows)


def attend(act_two, w_query, w_key, w_value, w_mixer, block_size, head_count):
    count_items, pixels, channels = act_two.shape
    blocks = act_two.reshape(count_items * pixels // block_size, block_size, channels)
    head_width = channels // head_count

    def project(weight):
        return jnp.dot(blocks, weight, precision=HIGHEST).reshape(
            blocks.shape[0], block_size, head_count, head_width
        )

    query_rows, key_rows, value_rows = (project(w_query), project(w_key), project(w_value))
    scores = jnp.einsum("bqhd,bkhd->bhqk", query_rows, key_rows, precision=HIGHEST) / math.sqrt(
        head_width
    )
    scores = scores - jnp.max(scores, axis=3, keepdims=True)
    probs = jnp.exp(scores)
    probs = probs / jnp.sum(probs, axis=3, keepdims=True)
    mixed_rows = jnp.einsum("bhqk,bkhd->bqhd", probs, value_rows, precision=HIGHEST).reshape(
        blocks.shape[0], block_size, channels
    )
    return jnp.dot(mixed_rows, w_mixer, precision=HIGHEST).reshape(act_two.shape)


def outlet_part(
    state_in,
    act_one,
    pre_two,
    total_two,
    squares_two,
    gain_second,
    shift_second,
    w_query,
    w_key,
    w_value,
    w_mixer,
    w_velocity,
    b_velocity,
    count,
    lat_rows,
    block_size,
    head_count,
    step_size,
):
    average = total_two / count
    spread = squares_two / count - average * average
    act_two = (
        act_one + gain_second * (pre_two - average) * lax.rsqrt(spread + EPSILON) + shift_second
    )
    act_three = act_two + attend(act_two, w_query, w_key, w_value, w_mixer, block_size, head_count)
    forcing = jnp.swapaxes(convolve(act_three, w_velocity, lat_rows) + b_velocity, 1, 2)
    quantities = state_in.shape[1] // 3
    amount = state_in[:, :quantities]
    flows = state_in[:, quantities:]
    flux_lon, unused_lat = differences(amount * state_in[:, quantities : 2 * quantities], lat_rows)
    unused_lon, flux_lat = differences(amount * state_in[:, 2 * quantities :], lat_rows)
    new_amount = amount - step_size * (flux_lon + flux_lat)
    new_flows = flows + step_size * (forcing - flows)
    return jnp.concatenate([new_amount, new_flows], axis=1)


def make_guard(active):

    def guarded(local_fn, operands):

        def skipped(skip_operands):
            return jax.tree.map(jnp.zeros_like, local_fn(skip_operands))

        return lax.cond(active, local_fn, skipped, operands)

    return guarded


def step_forward(
    state_in, weights_all, static_maps, count, block_size, step_size, first_sum, second_sum, guard
):

    def inlet_local(operands):
        return inlet_part(
            operands, static_maps, weights_all[0], weights_all[1], weights_all[2], LAT
        )

    act_one, pre_one = guard(inlet_local, state_in)
    total_one, squares_one = first_sum(
        (jnp.sum(pre_one, axis=(0, 1)), jnp.sum(pre_one * pre_one, axis=(0, 1)))
    )

    def middle_local(operands):
        return middle_part(
            operands[0],
            operands[1],
            operands[2],
            weights_all[3],
            weights_all[4],
            weights_all[5],
            count,
            LAT,
        )

    pre_two = guard(middle_local, (pre_one, total_one, squares_one))
    total_two, squares_two = second_sum(
        (jnp.sum(pre_two, axis=(0, 1)), jnp.sum(pre_two * pre_two, axis=(0, 1)))
    )

    def outlet_local(operands):
        return outlet_part(
            operands[0],
            operands[1],
            operands[2],
            operands[3],
            operands[4],
            weights_all[6],
            weights_all[7],
            weights_all[8],
            weights_all[9],
            weights_all[10],
            weights_all[11],
            weights_all[12],
            weights_all[13],
            count,
            LAT,
            block_size,
            HEADS,
            step_size,
        )

    outgoing = guard(outlet_local, (state_in, act_one, pre_two, total_two, squares_two))
    return (outgoing, jnp.stack([total_one, squares_one, total_two, squares_two]))


def step_backward(
    state_in,
    seed_now,
    stats_now,
    weights_all,
    static_maps,
    count,
    block_size,
    step_size,
    second_grad_sum,
    first_grad_sum,
    guard,
):

    def inlet_local(state_in, w_input, b_input, w_first):
        return inlet_part(state_in, static_maps, w_input, b_input, w_first, LAT)

    def middle_local(pre_one, total_one, squares_one, gain_first, shift_first, w_second):
        return middle_part(
            pre_one, total_one, squares_one, gain_first, shift_first, w_second, count, LAT
        )

    def outlet_local(
        state_in,
        act_one,
        pre_two,
        total_two,
        squares_two,
        gain_second,
        shift_second,
        w_query,
        w_key,
        w_value,
        w_mixer,
        w_velocity,
        b_velocity,
    ):
        return outlet_part(
            state_in,
            act_one,
            pre_two,
            total_two,
            squares_two,
            gain_second,
            shift_second,
            w_query,
            w_key,
            w_value,
            w_mixer,
            w_velocity,
            b_velocity,
            count,
            LAT,
            block_size,
            HEADS,
            step_size,
        )

    def first_piece(operands):
        state_now, seed_here, stats_here = operands
        act_one, pre_one = inlet_local(state_now, weights_all[0], weights_all[1], weights_all[2])
        pre_two = middle_local(
            pre_one, stats_here[0], stats_here[1], weights_all[3], weights_all[4], weights_all[5]
        )
        unused_out, pull_three = jax.vjp(
            outlet_local,
            state_now,
            act_one,
            pre_two,
            stats_here[2],
            stats_here[3],
            weights_all[6],
            weights_all[7],
            weights_all[8],
            weights_all[9],
            weights_all[10],
            weights_all[11],
            weights_all[12],
            weights_all[13],
        )
        return (pre_one, pre_two, pull_three(seed_here))

    pre_one, pre_two, back_three = guard(first_piece, (state_in, seed_now, stats_now))
    d_total_two, d_squares_two = second_grad_sum((back_three[3], back_three[4]))

    def second_piece(operands):
        pre_one_here, pre_two_here, d_pre_part, d_total, d_squares, stats_here = operands
        d_pre_two = d_pre_part + d_total + 2.0 * pre_two_here * d_squares
        unused_pre, pull_two = jax.vjp(
            middle_local,
            pre_one_here,
            stats_here[0],
            stats_here[1],
            weights_all[3],
            weights_all[4],
            weights_all[5],
        )
        return pull_two(d_pre_two)

    back_two = guard(
        second_piece, (pre_one, pre_two, back_three[2], d_total_two, d_squares_two, stats_now)
    )
    d_total_one, d_squares_one = first_grad_sum((back_two[1], back_two[2]))

    def third_piece(operands):
        state_now, d_act_one, d_pre_part, d_total, d_squares, pre_one_here = operands
        d_pre_one = d_pre_part + d_total + 2.0 * pre_one_here * d_squares
        unused_pair, pull_one = jax.vjp(
            inlet_local, state_now, weights_all[0], weights_all[1], weights_all[2]
        )
        return pull_one((d_act_one, d_pre_one))

    back_one = guard(
        third_piece, (state_in, back_three[1], back_two[0], d_total_one, d_squares_one, pre_one)
    )
    d_state = back_one[0] + back_three[0]
    step_grads = (
        back_one[1],
        back_one[2],
        back_one[3],
        back_two[3],
        back_two[4],
        back_two[5],
        back_three[5],
        back_three[6],
        back_three[7],
        back_three[8],
        back_three[9],
        back_three[10],
        back_three[11],
        back_three[12],
    )
    return (d_state, step_grads)


def on_device(
    state_start,
    static_maps,
    grouping,
    cotangent,
    w_input,
    b_input,
    w_first,
    gain_first,
    shift_first,
    w_second,
    gain_second,
    shift_second,
    w_query,
    w_key,
    w_value,
    w_mixer,
    w_velocity,
    b_velocity,
):
    segments = lax.axis_size("section")
    segment_rank = lax.axis_index("section")
    micro_count = segments // 2
    per_micro = state_start.shape[0] // micro_count
    pixels = state_start.shape[2]
    count = float(per_micro * pixels * lax.axis_size("dp"))
    step_size = 2.0 / segments
    block_size = ATT_ROWS * (pixels // LAT)
    channels = w_first.shape[2]
    local_order = grouping[0]
    weights_all = (
        w_input,
        b_input,
        w_first,
        gain_first,
        shift_first,
        w_second,
        gain_second,
        shift_second,
        w_query,
        w_key,
        w_value,
        w_mixer,
        w_velocity,
        b_velocity,
    )
    zero_grads = tuple((jnp.zeros_like(weight) for weight in weights_all))
    cot_local = cotangent[0]

    def members_of(micro_slot):
        return lax.dynamic_slice_in_dim(local_order, micro_slot * per_micro, per_micro)

    def first_dp(pair):
        return lax.psum(pair, "dp")

    def second_dp(pair):
        return lax.psum(pair, "dp")

    def second_grad_dp(pair):
        return lax.psum(pair, "dp")

    def first_grad_dp(pair):
        return lax.psum(pair, "dp")

    def forward_tick(tick_now, carry):
        sent, path, entered, moments = carry
        received = passed_along(sent, "section", 1)
        slot_raw = tick_now - segment_rank
        active = (slot_raw >= 0) & (slot_raw < micro_count)
        micro_slot = jnp.clip(slot_raw, 0, micro_count - 1)
        members = members_of(micro_slot)
        fresh = jnp.take(state_start, members, axis=0)
        incoming = jnp.where(segment_rank == 0, fresh, received)
        outgoing, stats_now = step_forward(
            incoming,
            weights_all,
            static_maps,
            count,
            block_size,
            step_size,
            first_dp,
            second_dp,
            make_guard(active),
        )
        path = path.at[members].set(jnp.where(active, outgoing, path[members]))
        entered = entered.at[members].set(jnp.where(active, incoming, entered[members]))
        moments = jnp.where(
            active,
            lax.dynamic_update_slice_in_dim(moments, stats_now[None], micro_slot, 0),
            moments,
        )
        return (outgoing, path, entered, moments)

    start_carry = (
        jnp.zeros_like(state_start[:per_micro]),
        jnp.zeros_like(state_start),
        jnp.zeros_like(state_start),
        jnp.zeros((micro_count, 4, channels), jnp.float32),
    )
    unused_sent, path, entered, moments = lax.fori_loop(
        0, micro_count + segments - 1, forward_tick, start_carry
    )

    def backward_tick(tick_now, carry):
        sent, grads_state, totals = carry
        received = passed_along(sent, "section", -1)
        slot_raw = tick_now - (segments - 1 - segment_rank)
        active = (slot_raw >= 0) & (slot_raw < micro_count)
        micro_slot = jnp.clip(slot_raw, 0, micro_count - 1)
        members = members_of(micro_slot)
        seed = received + jnp.take(cot_local, members, axis=0)
        state_now = jnp.take(entered, members, axis=0)
        stats_saved = lax.dynamic_index_in_dim(moments, micro_slot, 0, keepdims=False)
        d_state, step_grads = step_backward(
            state_now,
            seed,
            stats_saved,
            weights_all,
            static_maps,
            count,
            block_size,
            step_size,
            second_grad_dp,
            first_grad_dp,
            make_guard(active),
        )
        grads_state = grads_state.at[members].set(jnp.where(active, d_state, grads_state[members]))
        totals = jax.tree.map(jnp.add, totals, step_grads)
        return (d_state, grads_state, totals)

    back_carry = (jnp.zeros_like(state_start[:per_micro]), jnp.zeros_like(state_start), zero_grads)
    unused_back, grads_state, totals = lax.fori_loop(
        0, micro_count + segments - 1, backward_tick, back_carry
    )
    path_out = path[None]
    grads_out = grads_state[None]
    summed = lax.psum(
        (
            totals[0],
            totals[1],
            totals[2],
            totals[3],
            totals[4],
            totals[5],
            totals[6],
            totals[7],
            totals[8],
            totals[9],
            totals[10],
            totals[11],
            totals[12],
            totals[13],
        ),
        ("section", "dp"),
    )
    return (
        path_out,
        grads_out,
        summed[0],
        summed[1],
        summed[2],
        summed[3],
        summed[4],
        summed[5],
        summed[6],
        summed[7],
        summed[8],
        summed[9],
        summed[10],
        summed[11],
        summed[12],
        summed[13],
    )


def solution(mesh):
    return jax.shard_map(
        on_device,
        mesh=mesh,
        in_specs=(
            P("dp", None, None),
            P(),
            P("dp", None),
            P("section", "dp", None, None),
            P(),
            P(),
            P(),
            P(),
            P(),
            P(),
            P(),
            P(),
            P(),
            P(),
            P(),
            P(),
            P(),
            P(),
        ),
        out_specs=(
            P("section", "dp", None, None),
            P("section", "dp", None, None),
            P(),
            P(),
            P(),
            P(),
            P(),
            P(),
            P(),
            P(),
            P(),
            P(),
            P(),
            P(),
            P(),
            P(),
        ),
        check_vma=False,
    )
```

profile of v0, /device:TPU:0, one launch (start us, length us, event | category | flops | bytes accessed | tf_op | source)
XLA Modules:
  0.0 4210.4 jit_solution(7103644240065115410)
XLA Ops:
  19.2 751.5 %while.66 = (s32[]{:T(128)}, f32[2,15,1024]{2,1,0:T(8,128)}, f32[4,15,1024]{2,1,0:T(8,128)}, f32[4,15,1024]{2,1,0:T(8,128)S(1)}, f32[2,4,128]{2,1,0:T(4,128)}, /...) while((s32[]{:T(128)}, f32[2,15,1024]{2,1,0:T(8,128)}, ...), condition=%wide.region_19.21_spmd, body=%wide.region_0.20_spmd.sunk | while | flops 15243010048 | bytes 279776288 | solution.py:432
  30.0 78.9 %conditional.15 = (f32[2,1024,128]{2,1,0:T(8,128)S(1)}, f32[2,1024,128]{2,1,0:T(8,128)S(1)}) conditional(s32[]{:T(128)} %convert_element_type.49, () %tuple.348, (f32[2,15,1024]{2,1,0:T(8,128)S(1)}, f32[75,1024]{1,0:T(8,128)}, f32[9,100,128]{2,1,0:T(8,128)}, f32[128]{0:T(128)}, f32[9,128,128]{2,1,0:T(8,128)}) %tuple.349), branch_computations={%region_1.2_spmd, %region_2.3_spmd} | conditional | flops 6459822080 | bytes 110220200 | solution.py:136
  54.6 28.0 concatenate.236
  82.6 15.7 divide_multiply_fusion
  109.1 16.9 all-reduce.86
  137.8 14.2 all-reduce.87
  152.0 75.9 %conditional.17 = (f32[2,15,1024]{2,1,0:T(8,128)}) conditional(s32[]{:T(128)} %convert_element_type.49, () %tuple.346, (f32[2,15,1024]{2,1,0:T(8,128)S(1)}, f32[128]{0:T(128)S(1)}, f32[128]{0:T(128)}, f32[2,1024,128]{2,1,0:T(8,128)S(1)}, f32[128]{0:T(128)}, /*index=5*/f32[2,1024,128]{2,1,0:T(8,128)S(1)}, f32[128]{0:T(128)}, f32[128,128]{0,1:T(8,128)}, ...), branch_computations={%region_13.14_spmd, %region_14.17_spmd} | conditional | flops 5151842816 | bytes 116071712 | solution.py:136
  157.8 16.2 multiply_reduce_fusion
  183.7 15.8 fusion.21
  243.1 79.2 %conditional.15 = (f32[2,1024,128]{2,1,0:T(8,128)S(1)}, f32[2,1024,128]{2,1,0:T(8,128)S(1)}) conditional(s32[]{:T(128)} %convert_element_type.49, () %tuple.348, (f32[2,15,1024]{2,1,0:T(8,128)S(1)}, f32[75,1024]{1,0:T(8,128)}, f32[9,100,128]{2,1,0:T(8,128)}, f32[128]{0:T(128)}, f32[9,128,128]{2,1,0:T(8,128)}) %tuple.349), branch_computations={%region_1.2_spmd, %region_2.3_spmd} | conditional | flops 6459822080 | bytes 110220200 | solution.py:136
  267.7 28.0 concatenate.236
  295.8 16.1 divide_multiply_fusion
  322.6 14.1 all-reduce.86
  348.5 14.2 all-reduce.87
  362.7 76.1 %conditional.17 = (f32[2,15,1024]{2,1,0:T(8,128)}) conditional(s32[]{:T(128)} %convert_element_type.49, () %tuple.346, (f32[2,15,1024]{2,1,0:T(8,128)S(1)}, f32[128]{0:T(128)S(1)}, f32[128]{0:T(128)}, f32[2,1024,128]{2,1,0:T(8,128)S(1)}, f32[128]{0:T(128)}, /*index=5*/f32[2,1024,128]{2,1,0:T(8,128)S(1)}, f32[128]{0:T(128)}, f32[128,128]{0,1:T(8,128)}, ...), branch_computations={%region_13.14_spmd, %region_14.17_spmd} | conditional | flops 5151842816 | bytes 116071712 | solution.py:136
  368.3 16.2 multiply_reduce_fusion
  394.2 15.9 fusion.21
  463.7 14.1 all-reduce.86
  478.2 14.2 all-reduce.87
  502.3 159.1 %collective-permute-start = (f32[2,15,1024]{2,1,0:T(8,128)}, f32[2,15,1024]{2,1,0:T(8,128)S(1)}, u32[]{:S(2)}, u32[]{:S(2)}) collective-permute-start(f32[2,15,1024]{2,1,0:T(8,128)} %get-tuple-element.2832), channel_id=1, source_target_pairs={{0,8},{8,16},{16,24},{1,9},{9,17},{17,25},{2,10},{10,18},{18,26},{... | collective-permute-start | bytes 368648 | tf_op jit(solution)/shard_map/while/body/eval_jaxpr/ppermute | solution.py:20
  675.4 14.1 all-reduce.86
  689.9 14.2 all-reduce.87
  731.1 14.1 all-reduce.86
  745.6 14.2 all-reduce.87
  771.5 3288.3 %while.67 = (s32[]{:T(128)}, f32[2,15,1024]{1,2,0:T(8,128)}, f32[4,15,1024]{2,1,0:T(8,128)}, f32[9,100,128]{2,1,0:T(8,128)}, f32[128]{0:T(128)}, /*index=5*/f32[...) while((s32[]{:T(128)}, f32[2,15,1024]{1,2,0:T(8,128)}, ...), condition=%wide.region_47.49_spmd.clone, body=%wide.region_20.48_spmd.clone.sunk | while | flops 48306683904 | bytes 971328256 | solution.py:464
  789.5 155.2 %collective-permute-done.1 = f32[2,15,1024]{2,1,0:T(8,128)S(1)} collective-permute-done((f32[2,15,1024]{2,1,0:T(8,128)S(1)}, f32[2,15,1024]{2,1,0:T(8,128)S(1)}, u32[]{:S(2)}, u32[]{:S(2)}) %collective-permute-start.1) | collective-permute-done | bytes 122912 | tf_op jit(solution)/shard_map/while/body/eval_jaxpr/ppermute | solution.py:20
  944.7 17.9 conditional.18
  962.7 13.6 all-reduce.88
  986.6 13.6 all-reduce.89
  1031.3 17.7 conditional.18
  1117.6 150.6 %collective-permute-done.1 = f32[2,15,1024]{2,1,0:T(8,128)S(1)} collective-permute-done((f32[2,15,1024]{2,1,0:T(8,128)S(1)}, f32[2,15,1024]{2,1,0:T(8,128)S(1)}, u32[]{:S(2)}, u32[]{:S(2)}) %collective-permute-start.1) | collective-permute-done | bytes 122912 | tf_op jit(solution)/shard_map/while/body/eval_jaxpr/ppermute | solution.py:20
  1268.2 17.9 conditional.18
  1286.1 13.7 all-reduce.88
  1354.8 1523.6 %collective-permute-done.1 = f32[2,15,1024]{2,1,0:T(8,128)S(1)} collective-permute-done((f32[2,15,1024]{2,1,0:T(8,128)S(1)}, f32[2,15,1024]{2,1,0:T(8,128)S(1)}, u32[]{:S(2)}, u32[]{:S(2)}) %collective-permute-start.1) | collective-permute-done | bytes 122912 | tf_op jit(solution)/shard_map/while/body/eval_jaxpr/ppermute | solution.py:20
  2878.5 320.8 %conditional.18 = (f32[2,1024,128]{2,1,0:T(8,128)}, f32[2,1024,128]{2,1,0:T(8,128)}, f32[2,1024,128]{2,1,0:T(8,128)}, f32[2,1024,128]{2,1,0:T(8,128)}, f32[128]{...) conditional(s32[]{:T(128)} %convert_element_type.50, () %tuple.360, ...), branch_computations={%region_21.22_spmd, %region_22.33_spmd} | conditional | flops 25290614784 | bytes 598983680 | solution.py:136
  2905.8 28.5 concatenate.311
  2934.3 15.8 divide_multiply_fusion.3
  2977.5 16.5 multiply_reduce_fusion.2
  3003.7 16.0 fusion.47
  3089.6 16.6 fusion.48
  3108.8 24.7 convert_reduce_fusion
  3146.0 20.2 fusion.39
  3168.7 15.0 fusion.38
  3199.2 13.6 all-reduce.88
  3212.9 55.8 %conditional.19 = (f32[2,1024,128]{2,1,0:T(8,128)}, f32[128]{0:T(128)S(1)}, f32[128]{0:T(128)S(1)}, f32[128]{0:T(128)S(1)}, f32[128]{0:T(128)S(1)}, /*index=5*/f32[9,128,128]{2,1,0:T(8,128)}) conditional(s32[]{:T(128)} %convert_element_type.50, () %tuple.359, (f32[128]{0:T(128)}, f32[128]{0:T(128)S(1)}, f32[2,1024,128]{2,1,0:T(8,128)}, ...), branch_computations={%region_35.36_spmd, %region_36.41_spmd} | conditional | flops 7259629568 | bytes 118467184 | solution.py:136
  3282.3 165.6 %conditional.20 = (f32[2,15,1024]{1,2,0:T(8,128)}, f32[9,100,128]{2,1,0:T(8,128)}, f32[128]{0:T(128)}, f32[9,128,128]{2,1,0:T(8,128)}) conditional(s32[]{:T(128)} %convert_element_type.50, () %tuple.358, (f32[128]{0:T(128)S(1)}, f32[2,1024,128]{2,1,0:T(8,128)}, f32[128]{0:T(128)S(1)}, f32[2,1024,128]{2,1,0:T(8,128)}, ...), branch_computations={%region_43.44_spmd, %region_44.46_spmd} | conditional | flops 15755333632 | bytes 234179648 | solution.py:136
  3309.1 28.0 concatenate.369
  3337.1 16.5 fusion.118
  3473.5 320.8 %conditional.18 = (f32[2,1024,128]{2,1,0:T(8,128)}, f32[2,1024,128]{2,1,0:T(8,128)}, f32[2,1024,128]{2,1,0:T(8,128)}, f32[2,1024,128]{2,1,0:T(8,128)}, f32[128]{...) conditional(s32[]{:T(128)} %convert_element_type.50, () %tuple.360, ...), branch_computations={%region_21.22_spmd, %region_22.33_spmd} | conditional | flops 25290614784 | bytes 598983680 | solution.py:136
  3500.9 28.5 concatenate.311
  3529.4 15.8 divide_multiply_fusion.3
  3572.8 16.3 multiply_reduce_fusion.2
  3598.8 16.0 fusion.47
  3684.6 16.9 fusion.48
  3704.0 24.7 convert_reduce_fusion
  3741.0 20.4 fusion.39
  3763.9 14.8 fusion.38
  3794.3 13.6 all-reduce.88
  3808.0 55.7 %conditional.19 = (f32[2,1024,128]{2,1,0:T(8,128)}, f32[128]{0:T(128)S(1)}, f32[128]{0:T(128)S(1)}, f32[128]{0:T(128)S(1)}, f32[128]{0:T(128)S(1)}, /*index=5*/f32[9,128,128]{2,1,0:T(8,128)}) conditional(s32[]{:T(128)} %convert_element_type.50, () %tuple.359, (f32[128]{0:T(128)}, f32[128]{0:T(128)S(1)}, f32[2,1024,128]{2,1,0:T(8,128)}, ...), branch_computations={%region_35.36_spmd, %region_36.41_spmd} | conditional | flops 7259629568 | bytes 118467184 | solution.py:136
  3877.4 165.5 %conditional.20 = (f32[2,15,1024]{1,2,0:T(8,128)}, f32[9,100,128]{2,1,0:T(8,128)}, f32[128]{0:T(128)}, f32[9,128,128]{2,1,0:T(8,128)}) conditional(s32[]{:T(128)} %convert_element_type.50, () %tuple.358, (f32[128]{0:T(128)S(1)}, f32[2,1024,128]{2,1,0:T(8,128)}, f32[128]{0:T(128)S(1)}, f32[2,1024,128]{2,1,0:T(8,128)}, ...), branch_computations={%region_43.44_spmd, %region_44.46_spmd} | conditional | flops 15755333632 | bytes 234179648 | solution.py:136
  3904.1 28.0 concatenate.369
  3932.2 16.6 fusion.118
  4059.8 38.7 all-reduce.80
  4100.6 91.1 %all-reduce.92.cloned.1.call-done = (f32[9,100,128]{2,1,0:T(8,128)}, f32[9,128,128]{2,1,0:T(8,128)}, f32[9,128,128]{2,1,0:T(8,128)}, f32[128,128]{1,0:T(8,128)},...) async-done(((f32[9,100,128]{2,1,0:T(8,128)}, f32[9,128,128]{2,1,0:T(8,128)}, f32[9,128,128]{2,1,0:T(8,128)}, f32[128,128]{1,0:T(8,128)}, ...) | async-done | bytes 1902608 | tf_op jit(solution)/shard_map/psum | solution.py:469
  (1597 shorter events, 1296.9 us)
Async XLA Ops:
  7.2 4184.5 %all-reduce.92.cloned.1.call-start = ((), (), s32[]{:S(2)}) async-start(), calls=%async_computation | async-start | bytes 3842048 | tf_op jit(solution)/shard_map/psum | solution.py:469
  19.8 9.4 collective-permute-start
  30.0 96.0 %copy-start.48 = (f32[128]{0:T(128)S(1)}, f32[128]{0:T(128)}, u32[]{:S(2)}) copy-start(f32[128]{0:T(128)} %get-tuple-element.2872) | copy-start | bytes 1540 | tf_op jit(solution)/shard_map/while
  30.0 96.0 %copy-start.56 = (f32[128]{0:T(128)S(1)}, f32[128]{0:T(128)}, u32[]{:S(2)}) copy-start(f32[128]{0:T(128)} %get-tuple-element.2873) | copy-start | bytes 1540 | tf_op jit(solution)/shard_map/while
  50.4 32.2 copy-start.4
  50.4 32.3 copy-start.63
  126.0 26.0 copy-start.53
  152.0 80.4 %copy-start.61 = (f32[2,4,128]{2,1,0:T(4,128)S(1)}, f32[2,4,128]{2,1,0:T(4,128)}, u32[]{:S(2)}) copy-start(f32[2,4,128]{2,1,0:T(4,128)} %get-tuple-element.2835) | copy-start | bytes 12292 | tf_op jit(solution)/shard_map/while
  152.0 80.4 %copy-start.69 = (f32[128]{0:T(128)S(1)}, f32[128]{0:T(128)}, u32[]{:S(2)}) copy-start(f32[128]{0:T(128)} %get-tuple-element.2666) | copy-start | bytes 1540 | tf_op jit(solution)/shard_map/while
  236.1 6.3 collective-permute-start
  243.1 93.6 %copy-start.48 = (f32[128]{0:T(128)S(1)}, f32[128]{0:T(128)}, u32[]{:S(2)}) copy-start(f32[128]{0:T(128)} %get-tuple-element.2872) | copy-start | bytes 1540 | tf_op jit(solution)/shard_map/while
  243.1 93.6 %copy-start.56 = (f32[128]{0:T(128)S(1)}, f32[128]{0:T(128)}, u32[]{:S(2)}) copy-start(f32[128]{0:T(128)} %get-tuple-element.2873) | copy-start | bytes 1540 | tf_op jit(solution)/shard_map/while
  263.5 32.2 copy-start.4
  263.5 32.3 copy-start.63
  336.7 26.0 copy-start.53
  362.7 80.6 %copy-start.61 = (f32[2,4,128]{2,1,0:T(4,128)S(1)}, f32[2,4,128]{2,1,0:T(4,128)}, u32[]{:S(2)}) copy-start(f32[2,4,128]{2,1,0:T(4,128)} %get-tuple-element.2835) | copy-start | bytes 12292 | tf_op jit(solution)/shard_map/while
  362.7 80.7 %copy-start.69 = (f32[128]{0:T(128)S(1)}, f32[128]{0:T(128)}, u32[]{:S(2)}) copy-start(f32[128]{0:T(128)} %get-tuple-element.2666) | copy-start | bytes 1540 | tf_op jit(solution)/shard_map/while
  446.9 7.7 collective-permute-start
  455.3 22.5 copy-start.48
  455.3 22.5 copy-start.56
  502.3 164.1 %collective-permute-start = (f32[2,15,1024]{2,1,0:T(8,128)}, f32[2,15,1024]{2,1,0:T(8,128)S(1)}, u32[]{:S(2)}, u32[]{:S(2)}) collective-permute-start(f32[2,15,1024]{2,1,0:T(8,128)} %get-tuple-element.2832), channel_id=1, source_target_pairs={{0,8},{8,16},{16,24},{1,9},{9,17},{17,25},{2,10},{10,18},{18,26},{... | collective-permute-start | bytes 368648 | tf_op jit(solution)/shard_map/while/body/eval_jaxpr/ppermute | solution.py:20
  667.1 22.4 copy-start.56
  714.1 8.1 collective-permute-start
  779.5 165.2 %copy-start.21 = (f32[4,15,1024]{2,1,0:T(8,128)}, f32[4,15,1024]{2,1,0:T(8,128)S(1)}, u32[]{:S(2)}) copy-start(f32[4,15,1024]{2,1,0:T(8,128)S(1)} %get-tuple-element.2988) | copy-start | bytes 737284 | tf_op jit(solution)/shard_map/while
  781.2 163.5 %collective-permute-start.1 = (f32[2,15,1024]{2,1,0:T(8,128)S(1)}, f32[2,15,1024]{2,1,0:T(8,128)S(1)}, u32[]{:S(2)}, u32[]{:S(2)}) collective-permute-start(f32[2,15,1024]{2,1,0:T(8,128)S(1)} %broadcast_select_fusion.19), channel_id=1, source_target_pairs={{8,0},{16,8},{24,16},{9,1},{17,9},{25,17},{10,2},{18,10},{26,18},{... | collective-permute-start | bytes 368648 | tf_op jit(solution)/shard_map/while/body/eval_jaxpr/ppermute | solution.py:20
  783.3 161.5 %copy-start.66 = (s32[2]{0:T(128)}, s32[2]{0:T(128)S(1)}, u32[]{:S(2)}) copy-start(s32[2]{0:T(128)S(1)} %get-tuple-element.2710) | copy-start | bytes 28 | tf_op jit(solution)/shard_map/while
  976.4 23.9 copy-start.5
  976.4 23.9 copy-start.8
  976.4 23.9 copy-start.18
  976.4 23.9 copy-start.64
  1022.6 8.6 collective-permute-start.1
  1062.6 23.9 copy-start.5
  1062.6 23.9 copy-start.8
  1062.6 23.9 copy-start.18
  1062.6 23.9 copy-start.64
  1107.6 160.6 %copy-start.21 = (f32[4,15,1024]{2,1,0:T(8,128)}, f32[4,15,1024]{2,1,0:T(8,128)S(1)}, u32[]{:S(2)}) copy-start(f32[4,15,1024]{2,1,0:T(8,128)S(1)} %get-tuple-element.2988) | copy-start | bytes 737284 | tf_op jit(solution)/shard_map/while
  1109.3 158.9 %collective-permute-start.1 = (f32[2,15,1024]{2,1,0:T(8,128)S(1)}, f32[2,15,1024]{2,1,0:T(8,128)S(1)}, u32[]{:S(2)}, u32[]{:S(2)}) collective-permute-start(f32[2,15,1024]{2,1,0:T(8,128)S(1)} %broadcast_select_fusion.19), channel_id=1, source_target_pairs={{8,0},{16,8},{24,16},{9,1},{17,9},{25,17},{10,2},{18,10},{26,18},{... | collective-permute-start | bytes 368648 | tf_op jit(solution)/shard_map/while/body/eval_jaxpr/ppermute | solution.py:20
  1111.4 156.8 %copy-start.66 = (s32[2]{0:T(128)}, s32[2]{0:T(128)S(1)}, u32[]{:S(2)}) copy-start(s32[2]{0:T(128)S(1)} %get-tuple-element.2710) | copy-start | bytes 28 | tf_op jit(solution)/shard_map/while
  1299.7 23.9 copy-start.5
  1299.8 23.9 copy-start.8
  1299.8 23.9 copy-start.18
  1299.8 23.9 copy-start.64
  1344.8 1533.6 %copy-start.21 = (f32[4,15,1024]{2,1,0:T(8,128)}, f32[4,15,1024]{2,1,0:T(8,128)S(1)}, u32[]{:S(2)}) copy-start(f32[4,15,1024]{2,1,0:T(8,128)S(1)} %get-tuple-element.2988) | copy-start | bytes 737284 | tf_op jit(solution)/shard_map/while
  1346.5 1531.9 %collective-permute-start.1 = (f32[2,15,1024]{2,1,0:T(8,128)S(1)}, f32[2,15,1024]{2,1,0:T(8,128)S(1)}, u32[]{:S(2)}, u32[]{:S(2)}) collective-permute-start(f32[2,15,1024]{2,1,0:T(8,128)S(1)} %broadcast_select_fusion.19), channel_id=1, source_target_pairs={{8,0},{16,8},{24,16},{9,1},{17,9},{25,17},{10,2},{18,10},{26,18},{... | collective-permute-start | bytes 368648 | tf_op jit(solution)/shard_map/while/body/eval_jaxpr/ppermute | solution.py:20
  1348.6 1529.9 %copy-start.66 = (s32[2]{0:T(128)}, s32[2]{0:T(128)S(1)}, u32[]{:S(2)}) copy-start(s32[2]{0:T(128)S(1)} %get-tuple-element.2710) | copy-start | bytes 28 | tf_op jit(solution)/shard_map/while
  2902.0 32.3 copy-start.6
  2902.0 32.4 copy-start.65
  3106.3 27.2 copy-start.16
  3212.9 69.4 %copy-start.5 = (f32[9,100,128]{2,1,0:T(8,128)S(1)}, f32[9,100,128]{2,1,0:T(8,128)}, u32[]{:S(2)}) copy-start(f32[9,100,128]{2,1,0:T(8,128)} %get-tuple-element.2992) | copy-start | bytes 1382404 | tf_op jit(solution)/shard_map/while
  3212.9 69.4 %copy-start.8 = (f32[9,128,128]{2,1,0:T(8,128)S(1)}, f32[9,128,128]{2,1,0:T(8,128)}, u32[]{:S(2)}) copy-start(f32[9,128,128]{2,1,0:T(8,128)} %get-tuple-element.2994) | copy-start | bytes 1769476 | tf_op jit(solution)/shard_map/while
  3212.9 69.4 %copy-start.18 = (f32[75,1024]{1,0:T(8,128)S(1)}, f32[75,1024]{1,0:T(8,128)}, u32[]{:S(2)}) copy-start(f32[75,1024]{1,0:T(8,128)} %get-tuple-element.2991) | copy-start | bytes 921604 | tf_op jit(solution)/shard_map/while
  3212.9 69.4 %copy-start.64 = (f32[128]{0:T(128)S(1)}, f32[128]{0:T(128)}, u32[]{:S(2)}) copy-start(f32[128]{0:T(128)} %get-tuple-element.2993) | copy-start | bytes 1540 | tf_op jit(solution)/shard_map/while
  3282.3 168.0 %copy-start.67 = (s32[2]{0:T(128)S(1)}, s32[2]{0:T(128)}, u32[]{:S(2)}) copy-start(s32[2]{0:T(128)} %copy-done.66) | copy-start | bytes 28 | tf_op jit(solution)/shard_map/while
  3282.3 174.1 %copy-start.81 = (f32[128]{0:T(128)S(1)}, f32[128]{0:T(128)}, u32[]{:S(2)}) copy-start(f32[128]{0:T(128)} %get-tuple-element.2932) | copy-start | bytes 1540 | tf_op jit(solution)/shard_map/while
  3464.7 8.8 collective-permute-start.1
  3497.0 32.3 copy-start.6
  3497.0 32.4 copy-start.65
  3701.5 27.2 copy-start.16
  3807.9 69.4 %copy-start.5 = (f32[9,100,128]{2,1,0:T(8,128)S(1)}, f32[9,100,128]{2,1,0:T(8,128)}, u32[]{:S(2)}) copy-start(f32[9,100,128]{2,1,0:T(8,128)} %get-tuple-element.2992) | copy-start | bytes 1382404 | tf_op jit(solution)/shard_map/while
  3807.9 69.4 %copy-start.8 = (f32[9,128,128]{2,1,0:T(8,128)S(1)}, f32[9,128,128]{2,1,0:T(8,128)}, u32[]{:S(2)}) copy-start(f32[9,128,128]{2,1,0:T(8,128)} %get-tuple-element.2994) | copy-start | bytes 1769476 | tf_op jit(solution)/shard_map/while
  3807.9 69.4 %copy-start.18 = (f32[75,1024]{1,0:T(8,128)S(1)}, f32[75,1024]{1,0:T(8,128)}, u32[]{:S(2)}) copy-start(f32[75,1024]{1,0:T(8,128)} %get-tuple-element.2991) | copy-start | bytes 921604 | tf_op jit(solution)/shard_map/while
  3808.0 69.4 %copy-start.64 = (f32[128]{0:T(128)S(1)}, f32[128]{0:T(128)}, u32[]{:S(2)}) copy-start(f32[128]{0:T(128)} %get-tuple-element.2993) | copy-start | bytes 1540 | tf_op jit(solution)/shard_map/while
  3877.3 167.9 %copy-start.67 = (s32[2]{0:T(128)S(1)}, s32[2]{0:T(128)}, u32[]{:S(2)}) copy-start(s32[2]{0:T(128)} %copy-done.66) | copy-start | bytes 28 | tf_op jit(solution)/shard_map/while
  3877.3 174.1 %copy-start.81 = (f32[128]{0:T(128)S(1)}, f32[128]{0:T(128)}, u32[]{:S(2)}) copy-start(f32[128]{0:T(128)} %get-tuple-element.2932) | copy-start | bytes 1540 | tf_op jit(solution)/shard_map/while
  (269 other events, 2502.3 us)
Sparse Core Ops, SparseCore 0:
  4059.9 131.7 all-reduce.91
where the time goes:
time: 4220 us; the launch traced here: 4210 us
  waiting for transfers between devices  1920 us (45%)
  local copies, waits for them, and re-layouts  699 us (17%)
  matrix products  689 us (16%)
  blocking collectives  319 us (8%)
  other arithmetic  271 us (6%)
  starting transfers between devices  177 us (4%)
  loops' own time  119 us (3%)
    ppermute x10, waiting for transfers between devices, passed_along(): lax.ppermute(value, axis, [(source, source + steps) for source in range(f...  1830 us
    dot_general x32, matrix products, convolve(): jnp.dot(patches, weight.reshape(9 * channels, weight.shape[2]), precision...  348 us
    concatenate x70, local copies, waits for them, and re-layouts, convolve(): jnp.concatenate([padded[:, row_off:row_off + lat_rows, col_off:col_off +...  289 us
    ppermute x10, starting transfers between devices, passed_along(): lax.ppermute(value, axis, [(source, source + steps) for source in range(f...  177 us
    dot_general x8, matrix products, attend(): jnp.einsum('bhqk,bkhd->bqhd', probs, value_rows, precision=HIGHEST)  147 us
    dot_general x8, matrix products, attend(): jnp.einsum('bqhd,bkhd->bhqk', query_rows, key_rows, precision=HIGHEST)  136 us
    psum x1, waiting for transfers between devices, on_device(): lax.psum((totals[0], totals[1], totals[2], totals[3], totals[4], totals[5...  91.1 us
    another operation x30, loops' own time, guarded(): return lax.cond(active, local_fn, skipped, operands)  91.1 us
  transfers between devices with their start and end apart: 11, of which 6 were waited for; matrix products, arithmetic and copies ran while one was open for 1% of the time, Pallas kernels for 0%

commit v1 on v0

v1 whole, which is shorter than its diff:
```python
import math

import jax
import jax.numpy as jnp
from jax import lax
from jax.sharding import PartitionSpec as P

HEADS = 4
LAT = 16
ATT_ROWS = 8


HIGHEST = lax.Precision.HIGHEST
EPSILON = 1e-05


def passed_along(value, axis, steps):
    count = lax.axis_size(axis)
    first, last = (max(0, -steps), min(count, count - steps))
    return lax.ppermute(value, axis, [(source, source + steps) for source in range(first, last)])


def convolve(inputs, weight, lat_rows):
    count_items, pixels, channels = inputs.shape
    lon_cols = pixels // lat_rows
    planes = inputs.reshape(count_items, lat_rows, lon_cols, channels)
    padded = jnp.pad(planes, ((0, 0), (1, 1), (0, 0), (0, 0)))
    padded = jnp.concatenate([padded[:, :, -1:], padded, padded[:, :, :1]], axis=2)
    patches = jnp.concatenate(
        [
            padded[:, row_off : row_off + lat_rows, col_off : col_off + lon_cols]
            for row_off in range(3)
            for col_off in range(3)
        ],
        axis=3,
    )
    patches = patches.reshape(count_items, pixels, 9 * channels)
    return jnp.dot(patches, weight.reshape(9 * channels, weight.shape[2]), precision=HIGHEST)


def differences(values, lat_rows):
    count_items, quantities, pixels = values.shape
    planes = values.reshape(count_items, quantities, lat_rows, pixels // lat_rows)
    along_lon = 0.5 * (jnp.roll(planes, -1, axis=3) - jnp.roll(planes, 1, axis=3))
    padded = jnp.pad(planes, ((0, 0), (0, 0), (1, 1), (0, 0)))
    along_lat = 0.5 * (padded[:, :, 2:] - padded[:, :, :-2])
    return (along_lon.reshape(values.shape), along_lat.reshape(values.shape))


def inlet_part(state_in, static_maps, w_input, b_input, w_first, lat_rows):
    quantities = state_in.shape[1] // 3
    along_lon, along_lat = differences(state_in[:, :quantities], lat_rows)
    statics = jnp.broadcast_to(static_maps[None], (state_in.shape[0],) + static_maps.shape)
    stacked = jnp.concatenate([state_in, along_lon, along_lat, statics], axis=1)
    inputs = jnp.swapaxes(stacked, 1, 2)
    act_one = jax.nn.silu(convolve(inputs, w_input, lat_rows) + b_input)
    return (act_one, convolve(act_one, w_first, lat_rows))


def middle_part(
    pre_one, total_one, squares_one, gain_first, shift_first, w_second, count, lat_rows
):
    average = total_one / count
    spread = squares_one / count - average * average
    normed = gain_first * (pre_one - average) * lax.rsqrt(spread + EPSILON) + shift_first
    return convolve(jax.nn.silu(normed), w_second, lat_rows)


def attend(act_two, w_query, w_key, w_value, w_mixer, block_size, head_count):
    count_items, pixels, channels = act_two.shape
    blocks = act_two.reshape(count_items * pixels // block_size, block_size, channels)
    head_width = channels // head_count

    def project(weight):
        return jnp.dot(blocks, weight, precision=HIGHEST).reshape(
            blocks.shape[0], block_size, head_count, head_width
        )

    query_rows, key_rows, value_rows = (project(w_query), project(w_key), project(w_value))
    scores = jnp.einsum("bqhd,bkhd->bhqk", query_rows, key_rows, precision=HIGHEST) / math.sqrt(
        head_width
    )
    scores = scores - jnp.max(scores, axis=3, keepdims=True)
    probs = jnp.exp(scores)
    probs = probs / jnp.sum(probs, axis=3, keepdims=True)
    mixed_rows = jnp.einsum("bhqk,bkhd->bqhd", probs, value_rows, precision=HIGHEST).reshape(
        blocks.shape[0], block_size, channels
    )
    return jnp.dot(mixed_rows, w_mixer, precision=HIGHEST).reshape(act_two.shape)


def outlet_part(
    state_in,
    act_one,
    pre_two,
    total_two,
    squares_two,
    gain_second,
    shift_second,
    w_query,
    w_key,
    w_value,
    w_mixer,
    w_velocity,
    b_velocity,
    count,
    lat_rows,
    block_size,
    head_count,
    step_size,
):
    average = total_two / count
    spread = squares_two / count - average * average
    act_two = (
        act_one + gain_second * (pre_two - average) * lax.rsqrt(spread + EPSILON) + shift_second
    )
    act_three = act_two + attend(act_two, w_query, w_key, w_value, w_mixer, block_size, head_count)
    forcing = jnp.swapaxes(convolve(act_three, w_velocity, lat_rows) + b_velocity, 1, 2)
    quantities = state_in.shape[1] // 3
    amount = state_in[:, :quantities]
    flows = state_in[:, quantities:]
    flux_lon, unused_lat = differences(amount * state_in[:, quantities : 2 * quantities], lat_rows)
    unused_lon, flux_lat = differences(amount * state_in[:, 2 * quantities :], lat_rows)
    new_amount = amount - step_size * (flux_lon + flux_lat)
    new_flows = flows + step_size * (forcing - flows)
    return jnp.concatenate([new_amount, new_flows], axis=1)


def patches_of(inputs, lat_rows):
    count_items, pixels, channels = inputs.shape
    lon_cols = pixels // lat_rows
    planes = inputs.reshape(count_items, lat_rows, lon_cols, channels)
    padded = jnp.pad(planes, ((0, 0), (1, 1), (0, 0), (0, 0)))
    padded = jnp.concatenate([padded[:, :, -1:], padded, padded[:, :, :1]], axis=2)
    patches = jnp.concatenate(
        [
            padded[:, row_off : row_off + lat_rows, col_off : col_off + lon_cols]
            for row_off in range(3)
            for col_off in range(3)
        ],
        axis=3,
    )
    return patches.reshape(count_items, pixels, 9 * channels)


def shift_along(value, axis, steps):
    count = lax.axis_size(axis)
    return lax.ppermute(value, axis, [(own, (own + steps) % count) for own in range(count)])


def butterfly(value):
    pairs = [(own, own ^ 1) for own in range(lax.axis_size("section"))]
    reach = 1
    while reach < lax.axis_size("dp"):
        value = value + lax.ppermute(
            value, "dp", [(own, own ^ reach) for own in range(lax.axis_size("dp"))]
        )
        reach *= 2
    return value + lax.ppermute(value, "section", pairs)


def slotted(value, micro_slot, micro_count):
    wide = jnp.zeros((micro_count,) + value.shape, value.dtype)
    wide = lax.dynamic_update_index_in_dim(wide, value, micro_slot, 0)
    summed = lax.psum(wide, ("section", "dp"))
    return lax.dynamic_index_in_dim(summed, micro_slot, 0, keepdims=False)


def on_device(
    state_start,
    static_maps,
    grouping,
    cotangent,
    *weights_all,
):
    segments = lax.axis_size("section")
    segment_rank = lax.axis_index("section")
    micro_count = segments // 2
    per_micro = state_start.shape[0] // micro_count
    pixels = state_start.shape[2]
    count = float(per_micro * pixels * lax.axis_size("dp"))
    step_size = 2.0 / segments
    block_size = ATT_ROWS * (pixels // LAT)
    local_order = grouping[0]
    micro_slot = segment_rank // per_micro
    cot_local = cotangent[0]
    w_input, b_input, w_first, gain_first, shift_first, w_second = weights_all[:6]
    rest = weights_all[6:]
    quantities = state_start.shape[1] // 3
    moving = 5 * quantities

    def place(offset):
        return lax.rem(segment_rank + offset + segments, segments)

    def pick(array, index):
        return lax.dynamic_index_in_dim(array, index, 0, keepdims=False)

    got = [pick(cot_local, local_order[segment_rank])]
    for offset in range(1, segments):
        mine = pick(cot_local, local_order[place(offset)])
        got.append(shift_along(mine, "section", offset))
    got = jnp.stack(got)

    state = pick(state_start, local_order[segment_rank])[None]
    w_moving = w_input[:, :moving]
    w_static = w_input[:, moving:]
    static_patches = patches_of(jnp.swapaxes(static_maps, 0, 1)[None], LAT)[0]
    static_part = jnp.dot(static_patches, w_static.reshape(-1, w_static.shape[2]), precision=HIGHEST)

    def inlet(state_in, static_in, w_moving, b_input, w_first):
        along_lon, along_lat = differences(state_in[:, :quantities], LAT)
        inputs = jnp.swapaxes(jnp.concatenate([state_in, along_lon, along_lat], axis=1), 1, 2)
        act_one = jax.nn.silu(convolve(inputs, w_moving, LAT) + static_in[None] + b_input)
        return (act_one, convolve(act_one, w_first, LAT))

    def middle(pre_one, sums, gain_first, shift_first, w_second):
        return middle_part(
            pre_one, sums[0], sums[1], gain_first, shift_first, w_second, count, LAT
        )

    def outlet(state_in, act_one, pre_two, sums, *rest):
        return outlet_part(
            state_in, act_one, pre_two, sums[0], sums[1], *rest, count, LAT, block_size, HEADS, step_size
        )

    def sums_of(pre):
        return jnp.stack([jnp.sum(pre, axis=(0, 1)), jnp.sum(pre * pre, axis=(0, 1))])

    def forward(state_in, unused):
        act_one, pre_one = inlet(state_in, static_part, w_moving, b_input, w_first)
        sums_one = slotted(sums_of(pre_one), micro_slot, micro_count)
        pre_two = middle(pre_one, sums_one, gain_first, shift_first, w_second)
        sums_two = slotted(sums_of(pre_two), micro_slot, micro_count)
        state_out = outlet(state_in, act_one, pre_two, sums_two, *rest)
        return state_out, (state_in, state_out[0], act_one, pre_one, pre_two, sums_one, sums_two)

    unused_last, (entered, path, acts_one, pres_one, pres_two, all_sums_one, all_sums_two) = lax.scan(
        forward, state, None, length=segments
    )

    def to_steps(values):
        stacked = values
        back = [pick(stacked, segment_rank)]
        for offset in range(1, segments):
            back.append(shift_along(pick(stacked, place(offset)), "section", offset))
        back = jnp.stack(back)
        senders = local_order[lax.rem(segment_rank - jnp.arange(segments) + segments, segments)]
        return jnp.take(back, jnp.argsort(senders), axis=0)[None]

    path_out = to_steps(path)

    def backward(carry, saved):
        d_state, totals = carry
        cot_now, state_in, act_one, pre_one, pre_two, sums_one, sums_two = saved
        seed = d_state + cot_now
        unused_out, pull_three = jax.vjp(outlet, state_in, act_one, pre_two, sums_two, *rest)
        back_three = pull_three(seed)
        d_sums_two = butterfly(back_three[3])
        d_pre_two = back_three[2] + d_sums_two[0] + 2.0 * pre_two * d_sums_two[1]
        unused_out, pull_two = jax.vjp(middle, pre_one, sums_one, gain_first, shift_first, w_second)
        back_two = pull_two(d_pre_two)
        d_sums_one = butterfly(back_two[1])
        d_pre_one = back_two[0] + d_sums_one[0] + 2.0 * pre_one * d_sums_one[1]
        unused_out, pull_one = jax.vjp(inlet, state_in, static_part, w_moving, b_input, w_first)
        back_one = pull_one((back_three[1], d_pre_one))
        d_state = back_one[0] + back_three[0]
        step_grads = back_one[1:] + back_two[2:] + back_three[4:]
        return (d_state, jax.tree.map(jnp.add, totals, step_grads)), d_state[0]

    zeros = jax.tree.map(
        jnp.zeros_like, (static_part, w_moving, b_input, w_first, gain_first, shift_first, w_second) + rest
    )
    cots = jnp.stack([pick(got, place(-step)) for step in range(segments)])
    (unused_start, totals), grads = lax.scan(
        backward,
        (jnp.zeros_like(state), zeros),
        (cots, entered, acts_one, pres_one, pres_two, all_sums_one, all_sums_two),
        reverse=True,
    )
    grads_out = to_steps(grads)
    d_static = lax.dot_general(
        static_patches, totals[0], (((0,), (0,)), ((), ())), precision=HIGHEST
    ).reshape(w_static.shape)
    d_w_input = jnp.concatenate([totals[1], d_static], axis=1)
    totals = (d_w_input,) + tuple(totals[2:])
    flat = jnp.concatenate([total.reshape(-1) for total in totals])
    summed = lax.psum(flat.reshape(-1, 128), ("section", "dp")).reshape(-1) if flat.size % 128 == 0 else lax.psum(flat, ("section", "dp"))
    outs = []
    start = 0
    for total in totals:
        outs.append(summed[start : start + total.size].reshape(total.shape))
        start += total.size
    return (path_out, grads_out) + tuple(outs)


def solution(mesh):
    return jax.shard_map(
        on_device,
        mesh=mesh,
        in_specs=(
            P("dp", None, None),
            P(),
            P("dp", None),
            P("section", "dp", None, None),
            P(),
            P(),
            P(),
            P(),
            P(),
            P(),
            P(),
            P(),
            P(),
            P(),
            P(),
            P(),
            P(),
            P(),
        ),
        out_specs=(
            P("section", "dp", None, None),
            P("section", "dp", None, None),
            P(),
            P(),
            P(),
            P(),
            P(),
            P(),
            P(),
            P(),
            P(),
            P(),
            P(),
            P(),
            P(),
            P(),
        ),
        check_vma=False,
    )
```

time: 4220 us -> 1800 us (0.43)
  waiting for transfers between devices: 1920 us -> 154 us
  local copies, waits for them, and re-layouts: 699 us -> 427 us
  starting transfers between devices: 177 us -> 47.6 us
  loops' own time: 119 us -> 15.5 us
  other arithmetic: 271 us -> 176 us
  matrix products: 689 us -> 613 us
    ppermute x10 -> x41, waiting for transfers between devices: 1830 us -> 31.2 us  [the longest x24 19.8 us: butterfly(): lax.ppermute(value, 'dp', [(own, own ^ reach) for own in range(lax.axis_s...]
    concatenate x70 -> x96, local copies, waits for them, and re-layouts: 289 us -> 87.6 us  [convolve(): jnp.concatenate([padded[:, row_off:row_off + lat_rows, col_off:col_off +...]
    ppermute x10 -> x41, starting transfers between devices: 177 us -> 47.5 us  [the longest x24 23.7 us: butterfly(): lax.ppermute(value, 'dp', [(own, own ^ reach) for own in range(lax.axis_s...]
    dot_general x32 -> x52, matrix products: 348 us -> 238 us  [convolve(): jnp.dot(patches, weight.reshape(9 * channels, weight.shape[2]), precision...]
    another operation x32 -> x2, loops' own time: 119 us -> 15.5 us  [the longest x1 9.39 us: on_device(): lax.scan(backward, (jnp.zeros_like(state), zeros), (cots, entered, acts_o...]
    cond x330 -> x0, local copies, waits for them, and re-layouts: 81.1 us -> none
    while x450 -> x557, local copies, waits for them, and re-layouts: 22.4 us -> 94.5 us
    dot_general x24 -> x48, matrix products: 41.9 us -> 87.8 us  [project(): jnp.dot(blocks, weight, precision=HIGHEST)]
  transfers between devices with their start and end apart: 11 -> 42, of which waited for: 6 -> 20; matrix products, arithmetic and copies ran while one was open for 1% -> 67% of each run, Pallas kernels for 0% -> 0%
where the time goes in v1:
time: 1800 us; the launch traced here: 1780 us
  matrix products  613 us (34%)
  local copies, waits for them, and re-layouts  427 us (24%)
  blocking collectives  322 us (18%)
  other arithmetic  176 us (10%)
  waiting for transfers between devices  154 us (9%)
  starting transfers between devices  47.6 us (3%)
  between operations  22.7 us (1%)
    psum x8, blocking collectives, slotted(): summed = lax.psum(wide, ('section', 'dp'))  322 us
    dot_general x52, matrix products, convolve(): jnp.dot(patches, weight.reshape(9 * channels, weight.shape[2]), precision...  238 us
    dot_general x16, matrix products, attend(): jnp.einsum('bhqk,bkhd->bqhd', probs, value_rows, precision=HIGHEST)  133 us
    psum x1, waiting for transfers between devices, on_device(): lax.psum(flat, ('section', 'dp'))  122 us
    dot_general x16, matrix products, attend(): jnp.einsum('bqhd,bkhd->bhqk', query_rows, key_rows, precision=HIGHEST)  118 us
    while x552, local copies, waits for them, and re-layouts  92.1 us
    dot_general x48, matrix products, project(): jnp.dot(blocks, weight, precision=HIGHEST)  87.8 us
    concatenate x96, local copies, waits for them, and re-layouts, convolve(): jnp.concatenate([padded[:, row_off:row_off + lat_rows, col_off:col_off +...  87.6 us
  transfers between devices with their start and end apart: 42, of which 20 were waited for; matrix products, arithmetic and copies ran while one was open for 67% of the time, Pallas kernels for 0%

profile of v1, /device:TPU:0, one launch (start us, length us, event | category | flops | bytes accessed | tf_op | source)
XLA Modules:
  0.0 1777.1 jit_solution(2563747633513476320)
XLA Ops:
  49.1 14.3 concatenate.520
  63.3 7.7 fusion.194
  71.0 535.7 %while.75 = (s32[]{:T(128)}, f32[1,15,1024]{2,1,0:T(8,128)S(1)}, f32[4,1,15,1024]{3,2,1,0:T(8,128)}, f32[4,15,1024]{2,1,0:T(8,128)S(1)}, f32[4,1,1024,128]{3,2,1...) while((s32[]{:T(128)}, f32[1,15,1024]{2,1,0:T(8,128)S(1)}, ...), condition=%wide.wide.region_9.10_spmd, body=%wide.wide.region_0.9_spmd.sunk | while | flops 6559225856 | bytes 114806152 | solution.py:237
  85.1 40.0 %psum.32 = f32[2,2,128]{2,1,0:T(2,128)S(1)} all-reduce(f32[2,2,128]{2,1,0:T(2,128)S(1)} %constant_dynamic-update-slice_fusion.223), channel_id=1, replica_groups=mesh['section'=4,'dp'=8] {'section','dp'}, use_global_device_ids=true, to_apply=%region_3.3 | all-reduce | flops 512 | bytes 4096 | tf_op jit(solution)/shard_map/while/body/eval_jaxpr/psum | solution.py:165
  133.4 40.5 %psum.33 = f32[2,2,128]{2,1,0:T(2,128)S(1)} all-reduce(f32[2,2,128]{2,1,0:T(2,128)S(1)} %constant_dynamic-update-slice_fusion.234), channel_id=1, replica_groups=mesh['section'=4,'dp'=8] {'section','dp'}, use_global_device_ids=true, to_apply=%region_6.6 | all-reduce | flops 512 | bytes 4096 | tf_op jit(solution)/shard_map/while/body/eval_jaxpr/psum | solution.py:165
  178.1 7.1 multiply_reduce_fusion.17
  188.0 6.3 fusion.553
  218.3 39.9 %psum.32 = f32[2,2,128]{2,1,0:T(2,128)S(1)} all-reduce(f32[2,2,128]{2,1,0:T(2,128)S(1)} %constant_dynamic-update-slice_fusion.223), channel_id=1, replica_groups=mesh['section'=4,'dp'=8] {'section','dp'}, use_global_device_ids=true, to_apply=%region_3.3 | all-reduce | flops 512 | bytes 4096 | tf_op jit(solution)/shard_map/while/body/eval_jaxpr/psum | solution.py:165
  266.5 40.6 %psum.33 = f32[2,2,128]{2,1,0:T(2,128)S(1)} all-reduce(f32[2,2,128]{2,1,0:T(2,128)S(1)} %constant_dynamic-update-slice_fusion.234), channel_id=1, replica_groups=mesh['section'=4,'dp'=8] {'section','dp'}, use_global_device_ids=true, to_apply=%region_6.6 | all-reduce | flops 512 | bytes 4096 | tf_op jit(solution)/shard_map/while/body/eval_jaxpr/psum | solution.py:165
  311.3 7.1 multiply_reduce_fusion.17
  321.3 6.5 fusion.553
  351.5 39.9 %psum.32 = f32[2,2,128]{2,1,0:T(2,128)S(1)} all-reduce(f32[2,2,128]{2,1,0:T(2,128)S(1)} %constant_dynamic-update-slice_fusion.223), channel_id=1, replica_groups=mesh['section'=4,'dp'=8] {'section','dp'}, use_global_device_ids=true, to_apply=%region_3.3 | all-reduce | flops 512 | bytes 4096 | tf_op jit(solution)/shard_map/while/body/eval_jaxpr/psum | solution.py:165
  399.7 40.9 %psum.33 = f32[2,2,128]{2,1,0:T(2,128)S(1)} all-reduce(f32[2,2,128]{2,1,0:T(2,128)S(1)} %constant_dynamic-update-slice_fusion.234), channel_id=1, replica_groups=mesh['section'=4,'dp'=8] {'section','dp'}, use_global_device_ids=true, to_apply=%region_6.6 | all-reduce | flops 512 | bytes 4096 | tf_op jit(solution)/shard_map/while/body/eval_jaxpr/psum | solution.py:165
  444.9 7.1 multiply_reduce_fusion.17
  454.8 6.3 fusion.553
  484.9 40.0 %psum.32 = f32[2,2,128]{2,1,0:T(2,128)S(1)} all-reduce(f32[2,2,128]{2,1,0:T(2,128)S(1)} %constant_dynamic-update-slice_fusion.223), channel_id=1, replica_groups=mesh['section'=4,'dp'=8] {'section','dp'}, use_global_device_ids=true, to_apply=%region_3.3 | all-reduce | flops 512 | bytes 4096 | tf_op jit(solution)/shard_map/while/body/eval_jaxpr/psum | solution.py:165
  533.2 40.7 %psum.33 = f32[2,2,128]{2,1,0:T(2,128)S(1)} all-reduce(f32[2,2,128]{2,1,0:T(2,128)S(1)} %constant_dynamic-update-slice_fusion.234), channel_id=1, replica_groups=mesh['section'=4,'dp'=8] {'section','dp'}, use_global_device_ids=true, to_apply=%region_6.6 | all-reduce | flops 512 | bytes 4096 | tf_op jit(solution)/shard_map/while/body/eval_jaxpr/psum | solution.py:165
  578.1 7.1 multiply_reduce_fusion.17
  588.0 6.3 fusion.553
  626.6 974.1 %while.76 = (s32[]{:T(128)}, f32[1,15,1024]{2,1,0:T(8,128)S(1)}, f32[1024,128]{1,0:T(8,128)}, f32[9,25,128]{2,1,0:T(8,128)}, f32[128]{0:T(128)}, /*index=5*/f32[...) while((s32[]{:T(128)}, f32[1,15,1024]{2,1,0:T(8,128)S(1)}, ...), condition=%wide.wide.region_27.29_spmd.clone, body=%wide.wide.region_11.28_spmd.clone.sunk | while | flops 15926175744 | bytes 362330752 | solution.py:274
  641.9 7.1 multiply_reduce_fusion.18
  651.9 12.2 convert_reduce_fusion.3
  669.2 6.2 fusion.617
  675.4 9.1 fusion.616
  684.5 8.3 fusion.612
  700.7 6.3 fusion.645
  736.6 6.9 convolution_add_fusion.33
  767.7 7.0 concatenate.630
  795.8 6.3 copy.257
  802.3 7.0 convolution_add_fusion.31
  844.6 6.2 copy.256
  881.3 7.1 multiply_reduce_fusion.18
  891.3 12.2 convert_reduce_fusion.3
  908.4 6.2 fusion.617
  914.6 9.3 fusion.616
  923.9 8.3 fusion.612
  940.2 6.3 fusion.645
  976.9 6.7 convolution_add_fusion.33
  1009.4 7.0 concatenate.630
  1037.4 6.5 copy.257
  1045.6 7.1 convolution_add_fusion.31
  1087.9 6.2 copy.256
  1125.6 7.3 multiply_reduce_fusion.18
  1135.8 12.2 convert_reduce_fusion.3
  1152.8 6.2 fusion.617
  1159.0 9.1 fusion.616
  1168.2 8.3 fusion.612
  1184.4 6.5 fusion.645
  1221.3 6.6 convolution_add_fusion.33
  1252.3 7.0 concatenate.630
  1280.4 6.3 copy.257
  1286.9 7.1 convolution_add_fusion.31
  1329.5 6.2 copy.256
  1367.1 7.1 multiply_reduce_fusion.18
  1377.1 12.2 convert_reduce_fusion.3
  1400.6 9.1 fusion.616
  1409.7 8.3 fusion.612
  1425.9 6.3 fusion.645
  1462.7 6.9 convolution_add_fusion.33
  1495.3 7.0 concatenate.630
  1523.4 6.3 copy.257
  1531.3 7.1 convolution_add_fusion.31
  1573.7 6.2 copy.256
  1637.2 122.3 %all-reduce.79.cloned.1.call-done = f32[487818]{0:T(1024)} async-done(((f32[487818]{0:T(1024)}), f32[487818]{0:T(1024)}) %all-reduce.79.cloned.1.call-update) | async-done | bytes 1951288 | tf_op jit(solution)/shard_map/psum | solution.py:287
  (1669 shorter events, 893.8 us)
Async XLA Ops:
  7.2 24.0 %copy-start = (f32[4,15,1024]{2,0,1:T(4,128)S(1)}, f32[4,15,1024]{2,0,1:T(4,128)}, u32[]{:S(2)}) copy-start(f32[4,15,1024]{2,0,1:T(4,128)} %param.24) | copy-start | bytes 737284
  7.2 1752.3 %all-reduce.79.cloned.1.call-start = ((), (), s32[]{:S(2)}) async-start(), calls=%async_computation | async-start | bytes 3907584 | tf_op jit(solution)/shard_map/psum | solution.py:287
  19.3 600.8 %collective-permute-start.11 = (f32[15,1024]{1,0:T(8,128)}, f32[15,1024]{1,0:T(8,128)}, u32[]{:S(2)}, u32[]{:S(2)}) collective-permute-start(f32[15,1024]{1,0:T(8,128)} %bitcast.675), channel_id=1, source_target_pairs={{0,8},{8,16},{16,24},{24,0},{1,9},{9,17},{17,25},{25,1},{2,10},{10... | collective-permute-start | bytes 184328 | tf_op jit(solution)/shard_map/ppermute | solution.py:148
  22.9 599.7 %collective-permute-start.12 = (f32[15,1024]{1,0:T(8,128)}, f32[15,1024]{1,0:T(8,128)}, u32[]{:S(2)}, u32[]{:S(2)}) collective-permute-start(f32[15,1024]{1,0:T(8,128)} %bitcast.674), channel_id=1, source_target_pairs={{0,16},{8,24},{16,0},{24,8},{1,17},{9,25},{17,1},{25,9},{2,18},{10... | collective-permute-start | bytes 184328 | tf_op jit(solution)/shard_map/ppermute | solution.py:148
  25.1 598.4 %collective-permute-start.13 = (f32[15,1024]{1,0:T(8,128)}, f32[15,1024]{1,0:T(8,128)}, u32[]{:S(2)}, u32[]{:S(2)}) collective-permute-start(f32[15,1024]{1,0:T(8,128)} %bitcast.673), channel_id=1, source_target_pairs={{0,24},{8,0},{16,8},{24,16},{1,25},{9,1},{17,9},{25,17},{2,26},{10... | collective-permute-start | bytes 184328 | tf_op jit(solution)/shard_map/ppermute | solution.py:148
  49.1 22.0 %copy-start.43 = (f32[128]{0:T(128)S(1)}, f32[128]{0:T(128)}, u32[]{:S(2)}) copy-start(f32[128]{0:T(128)} %param.34) | copy-start | bytes 1540
  49.1 22.0 %copy-start.61 = (f32[10]{0:T(128)S(1)}, f32[10]{0:T(128)}, u32[]{:S(2)}) copy-start(f32[10]{0:T(128)} %param.41) | copy-start | bytes 124
  606.7 19.1 %copy-start.26 = (f32[9,128,10]{1,0,2:T(8,128)}, f32[9,128,10]{1,0,2:T(8,128)S(1)}, u32[]{:S(2)}) copy-start(f32[9,128,10]{1,0,2:T(8,128)S(1)} %get-tuple-element.3365) | copy-start | bytes 138244
  607.4 1022.0 %collective-permute-start.8 = (f32[15,1024]{1,0:T(8,128)}, f32[15,1024]{1,0:T(8,128)}, u32[]{:S(2)}, u32[]{:S(2)}) collective-permute-start(f32[15,1024]{1,0:T(8,128)} %get-tuple-element.1834), channel_id=1, source_target_pairs={{0,8},{8,16},{16,24},{24,0},{1,9},{9,17},{17,25},{25,1},{2,10},{10... | collective-permute-start | bytes 184328 | tf_op jit(solution)/shard_map/ppermute | solution.py:148
  618.7 1012.5 %collective-permute-start.9 = (f32[15,1024]{1,0:T(8,128)}, f32[15,1024]{1,0:T(8,128)}, u32[]{:S(2)}, u32[]{:S(2)}) collective-permute-start(f32[15,1024]{1,0:T(8,128)} %get-tuple-element.1833), channel_id=1, source_target_pairs={{0,16},{8,24},{16,0},{24,8},{1,17},{9,25},{17,1},{25,9},{2,18},{10... | collective-permute-start | bytes 184328 | tf_op jit(solution)/shard_map/ppermute | solution.py:148
  621.0 1010.2 %collective-permute-start.10 = (f32[15,1024]{1,0:T(8,128)}, f32[15,1024]{1,0:T(8,128)}, u32[]{:S(2)}, u32[]{:S(2)}) collective-permute-start(f32[15,1024]{1,0:T(8,128)} %get-tuple-element.1832), channel_id=1, source_target_pairs={{0,24},{8,0},{16,8},{24,16},{1,25},{9,1},{17,9},{25,17},{2,26},{10... | collective-permute-start | bytes 184328 | tf_op jit(solution)/shard_map/ppermute | solution.py:148
  626.7 149.2 %copy-start.44 = (f32[128]{0:T(128)}, f32[128]{0:T(128)S(1)}, u32[]{:S(2)}) copy-start(f32[128]{0:T(128)S(1)} %get-tuple-element.3340) | copy-start | bytes 1540 | tf_op jit(solution)/shard_map/while
  675.4 21.2 %copy-start.7 = (f32[2,4,512,32]{2,3,1,0:T(8,128)}, f32[2,4,512,32]{2,3,1,0:T(8,128)S(1)}, u32[]{:S(2)}) copy-start(f32[2,4,512,32]{2,3,1,0:T(8,128)S(1)} %fusion.617) | copy-start | bytes 1572868 | tf_op jit(solution)/shard_map/while
  700.7 47.2 %collective-permute-start = (f32[2,128]{1,0:T(2,128)}, f32[2,128]{1,0:T(2,128)}, u32[]{:S(2)}, u32[]{:S(2)}) collective-permute-start(f32[2,128]{1,0:T(2,128)} %pad_add_fusion.40), channel_id=1, source_target_pairs={{0,1},{1,0},{2,3},{3,2},{4,5},{5,4},{6,7},{7,6},{8,9},{9,8},{10,11... | collective-permute-start | bytes 3080 | tf_op jit(solution)/shard_map/while/body/eval_jaxpr/ppermute | solution.py:155
  748.6 3.6 collective-permute-start.1
  752.8 4.5 collective-permute-start.2
  757.3 18.6 %collective-permute-start.3 = (f32[2,128]{1,0:T(2,128)S(1)}, f32[2,128]{1,0:T(2,128)S(1)}, u32[]{:S(2)}, u32[]{:S(2)}) collective-permute-start(f32[2,128]{1,0:T(2,128)S(1)} %add.1538), channel_id=1, source_target_pairs={{0,8},{8,0},{16,24},{24,16},{1,9},{9,1},{17,25},{25,17},{2,10},{10... | collective-permute-start | bytes 3080 | tf_op jit(solution)/shard_map/while/body/eval_jaxpr/ppermute | solution.py:159
  792.2 10.0 collective-permute-start.4
  802.1 7.2 collective-permute-start.5
  809.3 4.5 collective-permute-start.6
  813.9 3.6 collective-permute-start.7
  866.2 151.3 %copy-start.44 = (f32[128]{0:T(128)}, f32[128]{0:T(128)S(1)}, u32[]{:S(2)}) copy-start(f32[128]{0:T(128)S(1)} %get-tuple-element.3340) | copy-start | bytes 1540 | tf_op jit(solution)/shard_map/while
  914.6 21.4 %copy-start.7 = (f32[2,4,512,32]{2,3,1,0:T(8,128)}, f32[2,4,512,32]{2,3,1,0:T(8,128)S(1)}, u32[]{:S(2)}) copy-start(f32[2,4,512,32]{2,3,1,0:T(8,128)S(1)} %fusion.617) | copy-start | bytes 1572868 | tf_op jit(solution)/shard_map/while
  940.2 47.9 %collective-permute-start = (f32[2,128]{1,0:T(2,128)}, f32[2,128]{1,0:T(2,128)}, u32[]{:S(2)}, u32[]{:S(2)}) collective-permute-start(f32[2,128]{1,0:T(2,128)} %pad_add_fusion.40), channel_id=1, source_target_pairs={{0,1},{1,0},{2,3},{3,2},{4,5},{5,4},{6,7},{7,6},{8,9},{9,8},{10,11... | collective-permute-start | bytes 3080 | tf_op jit(solution)/shard_map/while/body/eval_jaxpr/ppermute | solution.py:155
  988.8 3.6 collective-permute-start.1
  993.0 4.5 collective-permute-start.2
  997.5 20.0 %collective-permute-start.3 = (f32[2,128]{1,0:T(2,128)S(1)}, f32[2,128]{1,0:T(2,128)S(1)}, u32[]{:S(2)}, u32[]{:S(2)}) collective-permute-start(f32[2,128]{1,0:T(2,128)S(1)} %add.1538), channel_id=1, source_target_pairs={{0,8},{8,0},{16,24},{24,16},{1,9},{9,1},{17,25},{25,17},{2,10},{10... | collective-permute-start | bytes 3080 | tf_op jit(solution)/shard_map/while/body/eval_jaxpr/ppermute | solution.py:159
  1033.8 10.2 collective-permute-start.4
  1044.0 8.7 collective-permute-start.5
  1052.7 4.5 collective-permute-start.6
  1057.3 3.6 collective-permute-start.7
  1110.5 150.0 %copy-start.44 = (f32[128]{0:T(128)}, f32[128]{0:T(128)S(1)}, u32[]{:S(2)}) copy-start(f32[128]{0:T(128)S(1)} %get-tuple-element.3340) | copy-start | bytes 1540 | tf_op jit(solution)/shard_map/while
  1159.0 21.2 %copy-start.7 = (f32[2,4,512,32]{2,3,1,0:T(8,128)}, f32[2,4,512,32]{2,3,1,0:T(8,128)S(1)}, u32[]{:S(2)}) copy-start(f32[2,4,512,32]{2,3,1,0:T(8,128)S(1)} %fusion.617) | copy-start | bytes 1572868 | tf_op jit(solution)/shard_map/while
  1184.4 48.0 %collective-permute-start = (f32[2,128]{1,0:T(2,128)}, f32[2,128]{1,0:T(2,128)}, u32[]{:S(2)}, u32[]{:S(2)}) collective-permute-start(f32[2,128]{1,0:T(2,128)} %pad_add_fusion.40), channel_id=1, source_target_pairs={{0,1},{1,0},{2,3},{3,2},{4,5},{5,4},{6,7},{7,6},{8,9},{9,8},{10,11... | collective-permute-start | bytes 3080 | tf_op jit(solution)/shard_map/while/body/eval_jaxpr/ppermute | solution.py:155
  1233.2 3.6 collective-permute-start.1
  1237.4 4.5 collective-permute-start.2
  1241.9 18.5 %collective-permute-start.3 = (f32[2,128]{1,0:T(2,128)S(1)}, f32[2,128]{1,0:T(2,128)S(1)}, u32[]{:S(2)}, u32[]{:S(2)}) collective-permute-start(f32[2,128]{1,0:T(2,128)S(1)} %add.1538), channel_id=1, source_target_pairs={{0,8},{8,0},{16,24},{24,16},{1,9},{9,1},{17,25},{25,17},{2,10},{10... | collective-permute-start | bytes 3080 | tf_op jit(solution)/shard_map/while/body/eval_jaxpr/ppermute | solution.py:159
  1276.7 10.0 collective-permute-start.4
  1286.8 7.3 collective-permute-start.5
  1294.1 4.5 collective-permute-start.6
  1298.6 3.6 collective-permute-start.7
  1352.0 151.5 %copy-start.44 = (f32[128]{0:T(128)}, f32[128]{0:T(128)S(1)}, u32[]{:S(2)}) copy-start(f32[128]{0:T(128)S(1)} %get-tuple-element.3340) | copy-start | bytes 1540 | tf_op jit(solution)/shard_map/while
  1400.6 21.2 %copy-start.7 = (f32[2,4,512,32]{2,3,1,0:T(8,128)}, f32[2,4,512,32]{2,3,1,0:T(8,128)S(1)}, u32[]{:S(2)}) copy-start(f32[2,4,512,32]{2,3,1,0:T(8,128)S(1)} %fusion.617) | copy-start | bytes 1572868 | tf_op jit(solution)/shard_map/while
  1425.9 48.1 %collective-permute-start = (f32[2,128]{1,0:T(2,128)}, f32[2,128]{1,0:T(2,128)}, u32[]{:S(2)}, u32[]{:S(2)}) collective-permute-start(f32[2,128]{1,0:T(2,128)} %pad_add_fusion.40), channel_id=1, source_target_pairs={{0,1},{1,0},{2,3},{3,2},{4,5},{5,4},{6,7},{7,6},{8,9},{9,8},{10,11... | collective-permute-start | bytes 3080 | tf_op jit(solution)/shard_map/while/body/eval_jaxpr/ppermute | solution.py:155
  1454.8 18.4 %copy-start.15 = (f32[2,4,32,512]{3,2,1,0:T(8,128)S(1)}, f32[2,4,32,512]{3,2,1,0:T(8,128)}, u32[]{:S(2)}) copy-start(f32[2,4,32,512]{3,2,1,0:T(8,128)} %copy-done.14) | copy-start | bytes 1572868 | tf_op jit(solution)/shard_map/while
  1474.7 3.6 collective-permute-start.1
  1479.0 4.5 collective-permute-start.2
  1483.5 20.0 %collective-permute-start.3 = (f32[2,128]{1,0:T(2,128)S(1)}, f32[2,128]{1,0:T(2,128)S(1)}, u32[]{:S(2)}, u32[]{:S(2)}) collective-permute-start(f32[2,128]{1,0:T(2,128)S(1)} %add.1538), channel_id=1, source_target_pairs={{0,8},{8,0},{16,24},{24,16},{1,9},{9,1},{17,25},{25,17},{2,10},{10... | collective-permute-start | bytes 3080 | tf_op jit(solution)/shard_map/while/body/eval_jaxpr/ppermute | solution.py:159
  1519.8 10.0 collective-permute-start.4
  1529.7 8.7 collective-permute-start.5
  1538.5 4.5 collective-permute-start.6
  1543.0 3.6 collective-permute-start.7
  1600.8 18.6 %copy-start.34 = (f32[128,128]{1,0:T(8,128)S(1)}, f32[128,128]{1,0:T(8,128)}, u32[]{:S(2)}) copy-start(f32[128,128]{1,0:T(8,128)} %get-tuple-element.1116) | copy-start | bytes 196612
  1600.8 20.1 %copy-start.35 = (f32[128,128]{1,0:T(8,128)S(1)}, f32[128,128]{1,0:T(8,128)}, u32[]{:S(2)}) copy-start(f32[128,128]{1,0:T(8,128)} %get-tuple-element.1117) | copy-start | bytes 196612
  1600.8 21.6 %copy-start.36 = (f32[128,128]{1,0:T(8,128)S(1)}, f32[128,128]{1,0:T(8,128)}, u32[]{:S(2)}) copy-start(f32[128,128]{1,0:T(8,128)} %get-tuple-element.1118) | copy-start | bytes 196612
  1600.8 23.1 %copy-start.39 = (f32[128,128]{1,0:T(8,128)S(1)}, f32[128,128]{1,0:T(8,128)}, u32[]{:S(2)}) copy-start(f32[128,128]{1,0:T(8,128)} %get-tuple-element.1119) | copy-start | bytes 196612
  1600.8 26.0 %copy-start.62 = (f32[10]{0:T(128)S(1)}, f32[10]{0:T(128)}, u32[]{:S(2)}) copy-start(f32[10]{0:T(128)} %get-tuple-element.1121) | copy-start | bytes 124
  1605.3 22.8 %copy-start.72 = (s32[4]{0:T(128)S(1)}, s32[4]{0:T(128)}, u32[]{:S(2)}) copy-start(s32[4]{0:T(128)} %get-tuple-element.1099) | copy-start | bytes 52
  1605.4 22.8 %copy-start.42 = (f32[4,15,1024]{2,1,0:T(8,128)S(1)}, f32[4,15,1024]{2,1,0:T(8,128)}, u32[]{:S(2)}) copy-start(f32[4,15,1024]{2,1,0:T(8,128)} %get-tuple-element.1106) | copy-start | bytes 737284
  1605.4 25.9 %copy-start.48 = (f32[1,15,1024]{2,1,0:T(8,128)S(1)}, f32[1,15,1024]{2,1,0:T(8,128)}, u32[]{:S(2)}) copy-start(f32[1,15,1024]{2,1,0:T(8,128)} %get-tuple-element.1831) | copy-start | bytes 184324
  1628.2 5.3 collective-permute-start.14
  1628.8 5.0 collective-permute-start.15
  1629.4 5.3 collective-permute-start.16
  1632.2 137.9 %copy-start.1 = (f32[4,15,1024]{2,0,1:T(4,128)S(1)}, f32[4,15,1024]{2,0,1:T(4,128)}, u32[]{:S(2)}) copy-start(f32[4,15,1024]{2,0,1:T(4,128)} %param.24) | copy-start | bytes 737284
  (174 other events, 1516.0 us)
Sparse Core Ops, SparseCore 0:
  1628.3 131.1 all-reduce.78

commit v2 on v1

v2 whole, which is shorter than its diff:
```python
import functools
import math

import jax
import jax.numpy as jnp
from jax import lax
from jax.experimental import pallas as pl
from jax.experimental.pallas import tpu as pltpu
from jax.sharding import PartitionSpec as P

HEADS = 4
LAT = 16
ATT_ROWS = 8
EPSILON = 1e-05
F32 = jnp.float32
BF16 = jnp.bfloat16
GROUP = 8


def dot(left, right, left_dim=1, right_dim=0):
    return lax.dot_general(
        left, right, (((left_dim,), (right_dim,)), ((), ())), preferred_element_type=F32
    )


def halves(value):
    high = value.astype(BF16)
    return high, (value - high.astype(F32)).astype(BF16)


def thirds(value):
    high = value.astype(BF16)
    rest = value - high.astype(F32)
    middle = rest.astype(BF16)
    return high, middle, (rest - middle.astype(F32)).astype(BF16)


def stacked(value):
    return jnp.concatenate(halves(value), axis=0)


def beside(value):
    return jnp.concatenate(halves(value), axis=1)


def folded(value, axis):
    size = value.shape[axis] // 2
    if axis == 0:
        return value[:size] + value[size:]
    return value[:, :size] + value[:, size:]


def cells_of(value):
    return lax.broadcasted_iota(jnp.int32, value.shape, value.ndim - 1)


def lon_moved(value, offset, lon):
    cells = value.shape[1]
    column = lax.rem(cells_of(value), lon)
    near = pltpu.roll(value, (-offset) % cells, 1)
    wrapped = pltpu.roll(value, (offset * (lon - 1)) % cells, 1)
    edge = lon - 1 if offset > 0 else 0
    return jnp.where(column == edge, wrapped, near)


def lat_moved(value, offset, lon):
    cells = value.shape[1]
    moved = pltpu.roll(value, (-offset * lon) % cells, 1)
    cell = cells_of(value)
    if offset > 0:
        return jnp.where(cell < cells - lon, moved, 0.0)
    return jnp.where(cell >= lon, moved, 0.0)


def along_lon(value, lon):
    return 0.5 * (lon_moved(value, 1, lon) - lon_moved(value, -1, lon))


def along_lat(value, lon):
    return 0.5 * (lat_moved(value, 1, lon) - lat_moved(value, -1, lon))


def fill_patches(patches_ref, value, lon):
    cells, channels = value.shape
    planes = value.reshape(cells // lon, lon, channels)
    blank = jnp.zeros((lon, patches_ref.shape[1]), BF16)
    patches_ref[:lon] = blank
    patches_ref[lon + cells :] = blank
    for place, offset in enumerate((-1, 0, 1)):
        moved = value
        if offset:
            moved = pltpu.roll(planes, (-offset) % lon, 1).reshape(cells, channels)
        high, low = halves(moved)
        start = place * 2 * channels
        patches_ref[lon : lon + cells, start : start + channels] = high
        patches_ref[lon : lon + cells, start + channels : start + 2 * channels] = low


def conv_patches(patches_ref, weight_ref, lon):
    cells = patches_ref.shape[0] - 2 * lon
    rows = [patches_ref[lon * place : lon * place + cells] for place in range(3)]
    return folded(dot(jnp.concatenate(rows, axis=1), weight_ref[...]), 1)


def sigmoid(value):
    return 1.0 / (1.0 + jnp.exp(-value))


def norm_of(sums, gain, count):
    mean = sums[0:1] / count
    spread = sums[1:2] / count - mean * mean
    scale = lax.rsqrt(spread + EPSILON)
    return mean, scale, gain * scale


def sums_of(value, other):
    total = jnp.sum(value, axis=0, keepdims=True)
    product = jnp.sum(value * other, axis=0, keepdims=True)
    row = lax.broadcasted_iota(jnp.int32, (GROUP, value.shape[1]), 0)
    return jnp.where(row == 0, total, jnp.where(row == 1, product, 0.0))


def inlet_channels(state, lon):
    amount = state[:GROUP]
    groups = jnp.concatenate([state, along_lon(amount, lon), along_lat(amount, lon)], axis=0)
    blank = jnp.zeros((GROUP, state.shape[1]), F32)
    return jnp.concatenate(
        [lon_moved(groups, -1, lon), groups, lon_moved(groups, 1, lon), blank], axis=0
    )


def advected(state, step_size, lon):
    amount, east, north = state[:GROUP], state[GROUP : 2 * GROUP], state[2 * GROUP :]
    return amount - step_size * (along_lon(amount * east, lon) + along_lat(amount * north, lon))


def attention_scores(key_rows, query_rows):
    key_high, key_mid, key_low = thirds(key_rows)
    query_high, query_mid, query_low = thirds(query_rows)
    left = jnp.concatenate([key_high, key_high, key_mid, key_mid, key_high, key_low], axis=0)
    right = jnp.concatenate(
        [query_high, query_mid, query_high, query_mid, query_low, query_high], axis=0
    )
    return dot(left, right, 0, 0)


def by_halves(left_halves, right):
    high, low = halves(right)
    return folded(dot(left_halves, high) + dot(left_halves, low), 0)


def static_kernel(lon, maps_ref, weight_ref, bias_ref, out_ref, patches_ref):
    maps = maps_ref[...]
    fill_patches(patches_ref, maps.T, lon)
    out_ref[...] = conv_patches(patches_ref, weight_ref, lon) + bias_ref[...]


def inlet_kernel(
    lon, state_ref, static_ref, w_input_ref, w_first_ref,
    inner_ref, pre_ref, sums_ref, patches_ref,
):
    cells = state_ref.shape[1]
    moving = inlet_channels(state_ref[...], lon).T
    width = patches_ref.shape[1]
    blank = jnp.zeros((lon, width), BF16)
    patches_ref[:lon] = blank
    patches_ref[lon + cells :] = blank
    patches_ref[lon : lon + cells, :256] = beside(moving)
    rows = [patches_ref[lon * place : lon * place + cells, :256] for place in range(3)]
    inner = folded(dot(jnp.concatenate(rows, axis=1), w_input_ref[...]), 1) + static_ref[...]
    inner_ref[...] = inner
    fill_patches(patches_ref, inner * sigmoid(inner), lon)
    pre = conv_patches(patches_ref, w_first_ref, lon)
    pre_ref[...] = pre
    sums_ref[...] = sums_of(pre, pre)


def middle_kernel(
    lon, count, pre_one_ref, sums_one_ref, gain_ref, shift_ref, w_second_ref,
    pre_ref, sums_ref, patches_ref,
):
    mean, unused_scale, factor = norm_of(sums_one_ref[...], gain_ref[...], count)
    normed = (pre_one_ref[...] - mean) * factor + shift_ref[...]
    fill_patches(patches_ref, normed * sigmoid(normed), lon)
    pre = conv_patches(patches_ref, w_second_ref, lon)
    pre_ref[...] = pre
    sums_ref[...] = sums_of(pre, pre)


def act_two_channels(inner, pre_two, sums, gain, shift, count):
    mean, unused_scale, factor = norm_of(sums, gain, count)
    return (inner * sigmoid(inner) + (pre_two - mean) * factor + shift).T


def project(w_qkv_ref, act_two, head_width, qkv_ref):
    channels = act_two.shape[0]
    rows = folded(dot(w_qkv_ref[...], stacked(act_two)), 0)
    qkv_ref[:channels] = rows[:channels] * (1.0 / math.sqrt(head_width))
    qkv_ref[channels:] = rows[channels:]


def outlet_kernel(
    lon, count, block_size, step_size,
    state_ref, inner_ref, pre_two_ref, sums_two_ref, gain_ref, shift_ref,
    w_qkv_ref, w_mixer_ref, w_velocity_ref, b_velocity_ref,
    out_ref, qkv_ref, mixed_ref,
):
    channels = inner_ref.shape[1]
    cells = inner_ref.shape[0]
    head_width = channels // HEADS
    act_two = act_two_channels(
        inner_ref[...], pre_two_ref[...], sums_two_ref[...], gain_ref[...], shift_ref[...], count
    )
    project(w_qkv_ref, act_two, head_width, qkv_ref)

    def one_head(turn, unused):
        head, block = turn % HEADS, turn // HEADS
        lanes = pl.ds(pl.multiple_of(block * block_size, block_size), block_size)
        start = pl.multiple_of(head * head_width, head_width)
        query = qkv_ref[pl.ds(start, head_width), lanes]
        key = qkv_ref[pl.ds(start + channels, head_width), lanes]
        value = qkv_ref[pl.ds(start + 2 * channels, head_width), lanes]
        scores = attention_scores(key, query)
        top = jnp.max(scores, axis=0, keepdims=True)
        powers = jnp.exp(scores - top)
        total = jnp.sum(powers, axis=0, keepdims=True)
        mixed_ref[pl.ds(start, head_width), lanes] = by_halves(stacked(value), powers) / total
        return unused

    lax.fori_loop(0, HEADS * (cells // block_size), one_head, 0)
    act_three = act_two + folded(dot(w_mixer_ref[...], stacked(mixed_ref[...])), 0)
    parts = folded(dot(w_velocity_ref[...], stacked(act_three)), 0)
    forcing = jnp.zeros((2 * GROUP, cells), F32) + b_velocity_ref[...]
    for column, lon_offset in enumerate((-1, 0, 1)):
        total = None
        for row, lat_offset in enumerate((-1, 0, 1)):
            start = (row * 3 + column) * 2 * GROUP
            part = parts[start : start + 2 * GROUP]
            if lat_offset:
                part = lat_moved(part, lat_offset, lon)
            total = part if total is None else total + part
        forcing = forcing + (lon_moved(total, lon_offset, lon) if lon_offset else total)
    state = state_ref[...]
    flows = state[GROUP:]
    out_ref[:GROUP] = advected(state, step_size, lon)
    out_ref[GROUP:] = flows + step_size * (forcing - flows)


def outlet_back_kernel(
    lon, count, block_size, step_size,
    state_ref, seed_ref, inner_ref, pre_two_ref, sums_two_ref, gain_ref, shift_ref,
    w_qkv_ref, w_mixer_ref, w_qkv_back_ref, w_mixer_back_ref, w_velocity_back_ref,
    acc_qkv_ref, acc_mixer_ref, acc_velocity_ref, acc_small_ref,
    d_state_ref, d_two_ref, sums_ref,
    out_qkv_ref, out_mixer_ref, out_velocity_ref, out_small_ref,
    qkv_ref, mixed_ref, d_mixed_ref, d_qkv_ref,
):
    channels = inner_ref.shape[1]
    cells = inner_ref.shape[0]
    head_width = channels // HEADS
    state, seed = state_ref[...], seed_ref[...]
    amount, east, north = state[:GROUP], state[GROUP : 2 * GROUP], state[2 * GROUP :]
    d_amount = seed[:GROUP]
    d_lon = step_size * along_lon(d_amount, lon)
    d_lat = step_size * along_lat(d_amount, lon)
    d_state_ref[:GROUP] = d_amount + d_lon * east + d_lat * north
    d_state_ref[GROUP : 2 * GROUP] = (1.0 - step_size) * seed[GROUP : 2 * GROUP] + d_lon * amount
    d_state_ref[2 * GROUP :] = (1.0 - step_size) * seed[2 * GROUP :] + d_lat * amount
    d_forcing = step_size * seed[GROUP:]
    pieces = []
    for lat_offset in (-1, 0, 1):
        rows = lat_moved(d_forcing, -lat_offset, lon) if lat_offset else d_forcing
        for lon_offset in (-1, 0, 1):
            pieces.append(lon_moved(rows, -lon_offset, lon) if lon_offset else rows)
    d_parts = stacked(jnp.concatenate(pieces, axis=0))
    d_three = folded(dot(w_velocity_back_ref[...], d_parts), 0)
    d_three_halves = stacked(d_three)
    d_mixed_ref[...] = folded(dot(w_mixer_back_ref[...], d_three_halves), 0)
    act_two = act_two_channels(
        inner_ref[...], pre_two_ref[...], sums_two_ref[...], gain_ref[...], shift_ref[...], count
    )
    act_two_halves = stacked(act_two)
    project(w_qkv_ref, act_two, head_width, qkv_ref)

    def one_head(turn, unused):
        head, block = turn % HEADS, turn // HEADS
        lanes = pl.ds(pl.multiple_of(block * block_size, block_size), block_size)
        start = pl.multiple_of(head * head_width, head_width)
        query = qkv_ref[pl.ds(start, head_width), lanes]
        key = qkv_ref[pl.ds(start + channels, head_width), lanes]
        value = qkv_ref[pl.ds(start + 2 * channels, head_width), lanes]
        scores = attention_scores(key, query)
        top = jnp.max(scores, axis=0, keepdims=True)
        powers = jnp.exp(scores - top)
        weight = 1.0 / jnp.sum(powers, axis=0, keepdims=True)
        power_high, power_low = halves(powers)
        value_halves = stacked(value)
        mixed = folded(dot(value_halves, power_high) + dot(value_halves, power_low), 0) * weight
        mixed_ref[pl.ds(start, head_width), lanes] = mixed
        d_mixed = d_mixed_ref[pl.ds(start, head_width), lanes] * weight
        inner_sum = jnp.sum(d_mixed * mixed, axis=0, keepdims=True)
        d_mixed_cells = beside(d_mixed.T)
        d_value = folded(dot(power_high, d_mixed_cells) + dot(power_low, d_mixed_cells), 1)
        d_powers = attention_scores(value, d_mixed)
        d_high, d_low = halves(powers * (d_powers - inner_sum))
        query_cells = beside(query.T)
        d_key = folded(dot(d_high, query_cells) + dot(d_low, query_cells), 1)
        key_halves = stacked(key)
        d_query = folded(dot(key_halves, d_high) + dot(key_halves, d_low), 0)
        d_qkv_ref[pl.ds(start, head_width), lanes] = d_query * (1.0 / math.sqrt(head_width))
        d_qkv_ref[pl.ds(start + channels, head_width), lanes] = d_key.T
        d_qkv_ref[pl.ds(start + 2 * channels, head_width), lanes] = d_value.T
        return unused

    lax.fori_loop(0, HEADS * (cells // block_size), one_head, 0)
    mixed_halves = stacked(mixed_ref[...])
    act_three = act_two + folded(dot(w_mixer_ref[...], mixed_halves), 0)
    d_qkv_halves = stacked(d_qkv_ref[...])
    d_two = (d_three + folded(dot(w_qkv_back_ref[...], d_qkv_halves), 0)).T
    d_two_ref[...] = d_two
    mean, scale, unused_factor = norm_of(sums_two_ref[...], gain_ref[...], count)
    sums = sums_of(d_two, pre_two_ref[...] - mean)
    sums_ref[...] = sums
    def pairs(left, right):
        return folded(folded(dot(left, right, 1, 1), 0), 1)

    out_velocity_ref[...] = acc_velocity_ref[...] + pairs(d_parts, stacked(act_three))
    out_mixer_ref[...] = acc_mixer_ref[...] + pairs(mixed_halves, d_three_halves)
    out_qkv_ref[...] = acc_qkv_ref[...] + pairs(act_two_halves, d_qkv_halves)
    bias = jnp.sum(d_forcing, axis=1, keepdims=True)
    row = lax.broadcasted_iota(jnp.int32, (GROUP, channels), 0)
    small = jnp.where(row == 0, sums[1:2] * scale, jnp.where(row == 1, sums[0:1], 0.0))
    out_small_ref[:GROUP] = acc_small_ref[:GROUP] + small
    out_small_ref[GROUP:] = acc_small_ref[GROUP:] + bias


def d_pre_of(d_normed, centred, sums, all_grad_sums, gain, count):
    unused_mean, scale, factor = norm_of(sums, gain, count)
    d_spread = -0.5 * gain * scale * scale * scale * all_grad_sums[1:2]
    return factor * (d_normed - all_grad_sums[0:1] / count) + (2.0 * d_spread / count) * centred


def weight_pairs(acc_ref, out_ref, left_halves, patches_ref, lon):
    cells = patches_ref.shape[0] - 2 * lon
    width = patches_ref.shape[1] // 3
    for tap in range(9):
        row, column = divmod(8 - tap, 3)
        right = patches_ref[lon * row : lon * row + cells, column * width : (column + 1) * width]
        out_ref[tap] = acc_ref[tap] + folded(folded(dot(left_halves, right), 0), 1)


def middle_back_kernel(
    lon, count,
    d_two_ref, pre_two_ref, sums_two_ref, all_two_ref, gain_two_ref,
    pre_one_ref, sums_one_ref, gain_ref, shift_ref, w_second_back_ref,
    acc_weight_ref, acc_small_ref,
    d_normed_ref, sums_ref, out_weight_ref, out_small_ref,
    patches_ref,
):
    sums_two = sums_two_ref[...]
    d_pre = d_pre_of(
        d_two_ref[...], pre_two_ref[...] - sums_two[0:1] / count, sums_two, all_two_ref[...],
        gain_two_ref[...], count,
    )
    fill_patches(patches_ref, d_pre, lon)
    d_act = conv_patches(patches_ref, w_second_back_ref, lon)
    mean, scale, factor = norm_of(sums_one_ref[...], gain_ref[...], count)
    centred = pre_one_ref[...] - mean
    normed = centred * factor + shift_ref[...]
    gate = sigmoid(normed)
    d_normed = d_act * gate * (1.0 + normed * (1.0 - gate))
    d_normed_ref[...] = d_normed
    sums = sums_of(d_normed, centred)
    sums_ref[...] = sums
    weight_pairs(acc_weight_ref, out_weight_ref, stacked((normed * gate).T), patches_ref, lon)
    row = lax.broadcasted_iota(jnp.int32, sums.shape, 0)
    small = jnp.where(row == 0, sums[1:2] * scale, jnp.where(row == 1, sums[0:1], 0.0))
    out_small_ref[...] = acc_small_ref[...] + small


def inlet_back_kernel(
    lon, count,
    state_ref, d_normed_ref, pre_one_ref, sums_one_ref, all_one_ref, gain_ref,
    inner_ref, d_two_ref, d_state_in_ref, w_first_back_ref, w_input_back_ref,
    acc_first_ref, acc_input_ref, acc_inner_ref,
    d_state_ref, out_first_ref, out_input_ref, out_inner_ref,
    patches_ref,
):
    cells = inner_ref.shape[0]
    sums_one = sums_one_ref[...]
    d_pre = d_pre_of(
        d_normed_ref[...], pre_one_ref[...] - sums_one[0:1] / count, sums_one, all_one_ref[...],
        gain_ref[...], count,
    )
    fill_patches(patches_ref, d_pre, lon)
    d_act = conv_patches(patches_ref, w_first_back_ref, lon) + d_two_ref[...]
    inner = inner_ref[...]
    gate = sigmoid(inner)
    d_inner = d_act * gate * (1.0 + inner * (1.0 - gate))
    weight_pairs(acc_first_ref, out_first_ref, stacked((inner * gate).T), patches_ref, lon)
    out_inner_ref[...] = acc_inner_ref[...] + d_inner
    patches_ref[lon : lon + cells, :256] = beside(d_inner)
    rows = [patches_ref[lon * place : lon * place + cells, :256] for place in range(3)]
    d_moving = folded(dot(jnp.concatenate(rows, axis=1), w_input_back_ref[...]), 1).T
    state = state_ref[...]
    moving_halves = stacked(inlet_channels(state, lon))
    for place in range(3):
        out_input_ref[place] = acc_input_ref[place] + folded(
            folded(dot(moving_halves, rows[2 - place]), 0), 1
        )
    size = 5 * GROUP
    d_groups = (
        lon_moved(d_moving[:size], 1, lon)
        + d_moving[size : 2 * size]
        + lon_moved(d_moving[2 * size : 3 * size], -1, lon)
    )
    d_state = d_state_in_ref[...] + d_groups[: 3 * GROUP]
    d_state_ref[:GROUP] = (
        d_state[:GROUP]
        - along_lon(d_groups[3 * GROUP : 4 * GROUP], lon)
        - along_lat(d_groups[4 * GROUP :], lon)
    )
    d_state_ref[GROUP:] = d_state[GROUP:]


def static_back_kernel(lon, maps_ref, d_inner_ref, out_ref, bias_ref, patches_ref):
    d_inner = d_inner_ref[...]
    fill_patches(patches_ref, d_inner, lon)
    cells = d_inner.shape[0]
    width = patches_ref.shape[1] // 3
    left = stacked(maps_ref[...])
    for tap in range(9):
        row, column = divmod(8 - tap, 3)
        right = patches_ref[lon * row : lon * row + cells, column * width : (column + 1) * width]
        out_ref[tap] = folded(folded(dot(left, right), 0), 1)
    bias_ref[...] = jnp.zeros(bias_ref.shape, F32) + jnp.sum(d_inner, axis=0, keepdims=True)


def call(kernel, outs, scratch=(), aliases=None, name=None):
    return pl.pallas_call(
        kernel,
        out_shape=tuple(jax.ShapeDtypeStruct(shape, F32) for shape in outs),
        scratch_shapes=scratch,
        input_output_aliases=aliases or {},
        compiler_params=pltpu.CompilerParams(vmem_limit_bytes=VMEM_LIMIT),
        name=name,
        interpret=INTERPRET,
    )


VMEM_LIMIT = 48 * 1024 * 1024
INTERPRET = False


def cut(weight):
    high = lax.reduce_precision(weight, 8, 7)
    return high.astype(BF16), (weight - high).astype(BF16)


def conv_weight(weight):
    wide = jnp.concatenate(cut(weight), axis=2)
    return jnp.stack([wide, wide], axis=1).reshape(-1, wide.shape[2])


def left_weight(weight):
    high, low = cut(weight)
    return jnp.concatenate(
        [jnp.concatenate([high, high], axis=1), jnp.concatenate([low, low], axis=1)], axis=0
    )


def in_groups(array, axis, groups):
    shape = array.shape
    split = shape[:axis] + (groups, shape[axis] // groups) + shape[axis + 1 :]
    array = array.reshape(split)
    pads = [(0, 0)] * array.ndim
    pads[axis + 1] = (0, GROUP - split[axis + 1])
    return jnp.pad(array, pads).reshape(shape[:axis] + (groups * GROUP,) + shape[axis + 1 :])


def from_groups(array, axis, groups, size):
    shape = array.shape
    array = array.reshape(shape[:axis] + (groups, GROUP) + shape[axis + 1 :])
    array = lax.slice_in_dim(array, 0, size, axis=axis + 1)
    return array.reshape(shape[:axis] + (groups * size,) + shape[axis + 1 :])


def shift_along(value, axis, steps):
    count = lax.axis_size(axis)
    return lax.ppermute(value, axis, [(own, (own + steps) % count) for own in range(count)])


def group_of(value):
    dp, sections = lax.axis_size("dp"), lax.axis_size("section")
    groups = [list(range(2 * dp * pair, 2 * dp * (pair + 1))) for pair in range(sections // 2)]
    wide = jnp.broadcast_to(value[None], (2 * dp,) + value.shape)
    return lax.all_to_all(wide, ("section", "dp"), 0, 0, axis_index_groups=groups)


def micro_sum_direct(value):
    return jnp.sum(group_of(value), axis=0)


def micro_sum(value):
    dp, sections = lax.axis_size("dp"), lax.axis_size("section")
    reach = 1
    while 2 * reach < dp:
        offsets = [1, 2, 3] if 4 * reach <= dp else [1]
        value = value + sum(
            lax.ppermute(value, "dp", [(own, own ^ (offset * reach)) for own in range(dp)])
            for offset in offsets
        )
        reach *= 4
    if reach < dp:
        both = [(own, section) for section in range(sections) for own in range(dp)]
        pairs = lambda flip, jump: [
            (section * dp + own, (section ^ flip) * dp + (own ^ jump)) for own, section in both
        ]
        return value + sum(
            lax.ppermute(value, ("section", "dp"), pairs(flip, jump))
            for flip, jump in ((0, reach), (1, 0), (1, reach))
        )
    return value + lax.ppermute(value, "section", [(own, own ^ 1) for own in range(sections)])


def pick(array, index):
    return lax.dynamic_index_in_dim(array, index, 0, keepdims=False)


def on_device(
    state_start,
    static_maps,
    grouping,
    cotangent,
    w_input,
    b_input,
    w_first,
    gain_first,
    shift_first,
    w_second,
    gain_second,
    shift_second,
    w_query,
    w_key,
    w_value,
    w_mixer,
    w_velocity,
    b_velocity,
):
    segments = lax.axis_size("section")
    segment_rank = lax.axis_index("section")
    micro_count = segments // 2
    per_micro = state_start.shape[0] // micro_count
    cells = state_start.shape[2]
    lon = cells // LAT
    count = float(per_micro * cells * lax.axis_size("dp"))
    step_size = 2.0 / segments
    block_size = ATT_ROWS * lon
    channels = w_first.shape[2]
    quantities = state_start.shape[1] // 3
    moving = 5 * quantities
    local_order = grouping[0]
    cot_local = cotangent[0]
    statics = static_maps.shape[0]

    def place(offset):
        return lax.rem(segment_rank + offset + segments, segments)

    got = [pick(cot_local, local_order[segment_rank])]
    for offset in range(1, segments):
        got.append(shift_along(pick(cot_local, local_order[place(offset)]), "section", offset))
    got = jnp.stack(got)
    cots = jnp.stack([pick(got, place(-step)) for step in range(segments)])
    cots = in_groups(cots, 1, 3)
    state = in_groups(pick(state_start, local_order[segment_rank]), 0, 3)

    w_moving = in_groups(w_input[:, :moving], 1, 5).reshape(3, 3 * 5 * GROUP, channels)
    w_moving = jnp.pad(w_moving, ((0, 0), (0, channels - 3 * 5 * GROUP), (0, 0)))
    w_static = jnp.pad(w_input[:, moving:], ((0, 0), (0, channels - statics), (0, 0)))
    maps = jnp.pad(static_maps, ((0, channels - statics), (0, 0)))
    w_qkv = jnp.concatenate([w_query, w_key, w_value], axis=1)
    w_out = in_groups(w_velocity, 2, 2)
    w_out_rows = jnp.swapaxes(w_out, 1, 2).reshape(-1, channels)
    b_out = in_groups(b_velocity[:, None], 0, 2)
    moving_cat = conv_weight(w_moving)
    moving_back_cat = conv_weight(jnp.swapaxes(w_moving[::-1], 1, 2))
    static_cat = conv_weight(w_static)
    first_cat = conv_weight(w_first)
    first_back_cat = conv_weight(jnp.swapaxes(w_first[::-1], 1, 2))
    second_cat = conv_weight(w_second)
    second_back_cat = conv_weight(jnp.swapaxes(w_second[::-1], 1, 2))
    qkv_cat = left_weight(w_qkv.T)
    qkv_back_cat = left_weight(w_qkv)
    mixer_cat = left_weight(w_mixer.T)
    mixer_back_cat = left_weight(w_mixer)
    out_cat = left_weight(w_out_rows)
    out_back_cat = left_weight(w_out_rows.T)
    gain_one, shift_one = gain_first[None], shift_first[None]
    gain_two, shift_two = gain_second[None], shift_second[None]

    plane = (cells, channels)
    small = (GROUP, channels)
    patches = pltpu.VMEM((cells + 2 * lon, 6 * channels), BF16)
    wide = pltpu.VMEM((3 * channels, cells), F32)
    narrow = pltpu.VMEM((channels, cells), F32)
    state_shape = (3 * GROUP, cells)

    (static_part,) = call(
        functools.partial(static_kernel, lon), [plane], [patches], name="static_inlet"
    )(maps, static_cat, b_input[None])

    inlet = call(
        functools.partial(inlet_kernel, lon), [plane, plane, small], [patches], name="inlet"
    )
    middle = call(
        functools.partial(middle_kernel, lon, count), [plane, small], [patches], name="middle"
    )
    outlet = call(
        functools.partial(outlet_kernel, lon, count, block_size, step_size),
        [state_shape], [wide, narrow], name="outlet",
    )
    outlet_back = call(
        functools.partial(outlet_back_kernel, lon, count, block_size, step_size),
        [state_shape, plane, small, (channels, 3 * channels), (channels, channels),
         (18 * GROUP, channels), (3 * GROUP, channels)],
        [wide, narrow, narrow, wide],
        {12: 3, 13: 4, 14: 5, 15: 6}, name="outlet_back",
    )
    middle_back = call(
        functools.partial(middle_back_kernel, lon, count),
        [plane, small, (9, channels, channels), small], [patches],
        {10: 2, 11: 3}, name="middle_back",
    )
    inlet_back = call(
        functools.partial(inlet_back_kernel, lon, count),
        [state_shape, (9, channels, channels), (3, channels, channels), plane], [patches],
        {11: 1, 12: 2, 13: 3}, name="inlet_back",
    )

    def forward(state_in, unused):
        inner, pre_one, sums_one = inlet(state_in, static_part, moving_cat, first_cat)
        sums_one = micro_sum_direct(sums_one)
        pre_two, sums_two = middle(pre_one, sums_one, gain_one, shift_one, second_cat)
        sums_two = micro_sum_direct(sums_two)
        (state_out,) = outlet(
            state_in, inner, pre_two, sums_two, gain_two, shift_two, qkv_cat, mixer_cat, out_cat, b_out
        )
        return state_out, (state_in, state_out, inner, pre_one, pre_two, sums_one, sums_two)

    unused_last, (entered, path, inners, pres_one, pres_two, all_sums_one, all_sums_two) = lax.scan(
        forward, state, None, length=segments, unroll=min(4, segments)
    )

    def to_steps(values):
        values = from_groups(values, 1, 3, quantities)
        back = [pick(values, segment_rank)]
        for offset in range(1, segments):
            back.append(shift_along(pick(values, place(offset)), "section", offset))
        back = jnp.stack(back)
        senders = local_order[lax.rem(segment_rank - jnp.arange(segments) + segments, segments)]
        return jnp.take(back, jnp.argsort(senders), axis=0)[None]

    path_out = to_steps(path)

    def backward(carry, saved):
        d_state, acc = carry
        cot_now, state_in, inner, pre_one, pre_two, sums_one, sums_two = saved
        seed = d_state + cot_now
        d_partial, d_two, grad_two, qkv, mixer, velocity, small_two = outlet_back(
            state_in, seed, inner, pre_two, sums_two, gain_two, shift_two,
            qkv_cat, mixer_cat, qkv_back_cat, mixer_back_cat, out_back_cat,
            acc["qkv"], acc["mixer"], acc["velocity"], acc["small_two"],
        )
        grad_two = micro_sum(grad_two)
        d_normed, grad_one, second, small_one = middle_back(
            d_two, pre_two, sums_two, grad_two, gain_two,
            pre_one, sums_one, gain_one, shift_one, second_back_cat,
            acc["second"], acc["small_one"],
        )
        grad_one = micro_sum(grad_one)
        d_state, first, moved, inner_sum = inlet_back(
            state_in, d_normed, pre_one, sums_one, grad_one, gain_one,
            inner, d_two, d_partial, first_back_cat, moving_back_cat,
            acc["first"], acc["moving"], acc["inner"],
        )
        acc = dict(
            qkv=qkv, mixer=mixer, velocity=velocity, small_two=small_two, second=second,
            small_one=small_one, first=first, moving=moved, inner=inner_sum,
        )
        return (d_state, acc), d_state

    acc = dict(
        qkv=jnp.zeros((channels, 3 * channels), F32),
        mixer=jnp.zeros((channels, channels), F32),
        velocity=jnp.zeros((18 * GROUP, channels), F32),
        small_two=jnp.zeros((3 * GROUP, channels), F32),
        second=jnp.zeros((9, channels, channels), F32),
        small_one=jnp.zeros(small, F32),
        first=jnp.zeros((9, channels, channels), F32),
        moving=jnp.zeros((3, channels, channels), F32),
        inner=jnp.zeros(plane, F32),
    )
    (unused_start, acc), grads = lax.scan(
        backward,
        (jnp.zeros(state_shape, F32), acc),
        (cots, entered, inners, pres_one, pres_two, all_sums_one, all_sums_two),
        reverse=True,
        unroll=min(4, segments),
    )
    grads_out = to_steps(grads)
    d_static, bias = call(
        functools.partial(static_back_kernel, lon), [(9, channels, channels), small], [patches],
        name="static_back",
    )(maps, acc["inner"])

    sizes = [
        ("first", (9, channels, channels)),
        ("second", (9, channels, channels)),
        ("static", (9, channels, channels)),
        ("moving", (3, channels, channels)),
        ("qkv", (channels, 3 * channels)),
        ("mixer", (channels, channels)),
        ("velocity", (18 * GROUP, channels)),
        ("bias", small),
        ("small_one", small),
        ("small_two", (3 * GROUP, channels)),
    ]
    acc["static"], acc["bias"] = d_static, bias
    names = [name for name, unused_shape in sizes]
    summed = dict(zip(names, final_sum([acc[name] for name in names])))
    d_moving = from_groups(
        summed["moving"][:, : 15 * GROUP].reshape(9, 5 * GROUP, channels), 1, 5, quantities
    )
    d_input = jnp.concatenate([d_moving, summed["static"][:, :statics]], axis=1)
    qkv = summed["qkv"]
    d_out = jnp.swapaxes(summed["velocity"].reshape(9, 2 * GROUP, channels), 1, 2)
    d_out = from_groups(d_out, 2, 2, quantities)
    small_one, small_two = summed["small_one"], summed["small_two"]
    return (
        path_out,
        grads_out,
        d_input,
        summed["bias"][0],
        summed["first"],
        small_one[0],
        small_one[1],
        summed["second"],
        small_two[0],
        small_two[1],
        qkv[:, :channels],
        qkv[:, channels : 2 * channels],
        qkv[:, 2 * channels :],
        summed["mixer"],
        d_out,
        from_groups(small_two[GROUP:, :1], 0, 2, quantities)[:, 0],
    )


def final_sum(values):
    flat = jnp.concatenate([value.reshape(-1, 128) for value in values])
    summed = lax.psum(flat, ("section", "dp"))
    outs = []
    start = 0
    for value in values:
        rows = value.size // flat.shape[1]
        outs.append(summed[start : start + rows].reshape(value.shape))
        start += rows
    return outs


def solution(mesh):
    weights = (P(),) * 14
    return jax.shard_map(
        on_device,
        mesh=mesh,
        in_specs=(P("dp", None, None), P(), P("dp", None), P("section", "dp", None, None)) + weights,
        out_specs=(P("section", "dp", None, None), P("section", "dp", None, None)) + weights,
        check_vma=False,
    )
```

time: 1800 us -> 605 us (0.34)
  matrix products: 613 us -> 0 us
  local copies, waits for them, and re-layouts: 427 us -> 95.6 us
  blocking collectives: 322 us -> 0 us
  Pallas kernels: 0 us -> 162 us
  other arithmetic: 176 us -> 37.9 us
  starting transfers between devices: 47.6 us -> 103 us
  waiting for transfers between devices: 154 us -> 173 us
    dot_general x150 -> x0, matrix products: 613 us -> none  [the longest x52 238 us: convolve(): jnp.dot(patches, weight.reshape(9 * channels, weight.shape[2]), precision...]
    psum x8 -> x0, blocking collectives: 322 us -> none  [slotted(): summed = lax.psum(wide, ('section', 'dp'))]
    pallas_call x0 -> x26, Pallas kernels: none -> 162 us  [the longest x4 78.4 us: backward(): outlet_back(state_in, seed, inner, pre_two, sums_two, gain_two, shift_two...]
    concatenate x106 -> x11, local copies, waits for them, and re-layouts: 114 us -> 2.58 us  [the longest x1 1.16 us: left_weight(): jnp.concatenate([jnp.concatenate([high, high], axis=1), jnp.concatenate([...]
    while x557 -> x0, local copies, waits for them, and re-layouts: 94.5 us -> none
    dot_general x17 -> x0, local copies, waits for them, and re-layouts: 83.3 us -> none  [the longest x16 79.6 us: convolve(): jnp.dot(patches, weight.reshape(9 * channels, weight.shape[2]), precision...]
    reduce_sum x28 -> x8, other arithmetic: 50 us -> 5.19 us  [micro_sum_direct(): return jnp.sum(group_of(value), axis=0)]
    add x76 -> x16, other arithmetic: 41.8 us -> 0.77 us  [the longest x8 0.73 us: micro_sum(): value + sum((lax.ppermute(value, 'dp', [(own, own ^ offset * reach) for o...]
  transfers between devices with their start and end apart: 42 -> 66, of which waited for: 20 -> 42; matrix products, arithmetic and copies ran while one was open for 67% -> 11% of each run, Pallas kernels for 0% -> 6%
where the time goes in v2:
time: 605 us; the launch traced here: 596 us
  waiting for transfers between devices  173 us (29%)
  Pallas kernels  162 us (27%)
  starting transfers between devices  103 us (17%)
  local copies, waits for them, and re-layouts  95.6 us (16%)
  other arithmetic  37.9 us (6%)
  between operations  24.6 us (4%)
    psum x1, waiting for transfers between devices, final_sum(): summed = lax.psum(flat, ('section', 'dp'))  109 us
    pallas_call x4, Pallas kernels, backward(): outlet_back(state_in, seed, inner, pre_two, sums_two, gain_two, shift_two...  78.4 us
    unnamed x374, local copies, waits for them, and re-layouts  56.7 us
    all_to_all x8, starting transfers between devices, group_of(): lax.all_to_all(wide, ('section', 'dp'), 0, 0, axis_index_groups=groups)  39.5 us
    ppermute x24, starting transfers between devices, micro_sum(): lax.ppermute(value, ('section', 'dp'), pairs(flip, jump))  35.2 us
    pallas_call x4, Pallas kernels, forward(): outlet(state_in, inner, pre_two, sums_two, gain_two, shift_two, qkv_cat,...  32.4 us
    all_to_all x8, waiting for transfers between devices, group_of(): lax.all_to_all(wide, ('section', 'dp'), 0, 0, axis_index_groups=groups)  27.8 us
    ppermute x24, waiting for transfers between devices, micro_sum(): lax.ppermute(value, ('section', 'dp'), pairs(flip, jump))  19.6 us
  transfers between devices with their start and end apart: 66, of which 42 were waited for; matrix products, arithmetic and copies ran while one was open for 11% of the time, Pallas kernels for 6%

profile of v2, /device:TPU:0, one launch (start us, length us, event | category | flops | bytes accessed | tf_op | source)
XLA Modules:
  0.0 595.9 jit_solution(11368552702455221672)
XLA Ops:
  17.0 3.1 inlet.4
  22.4 7.4 %all-to-all-start = ((f32[16,8,128]{2,1,0:T(8,128)}), f32[16,8,128]{2,1,0:T(8,128)}, u32[]{:S(2)}, u32[]{:S(2)}) async-start(f32[16,8,128]{2,1,0:T(8,128)} %broadcast_in_dim.51), calls=%async_computation | async-start | bytes 131072 | tf_op jit(solution)/shard_map/eval_jaxpr/all_to_all | solution.py:497
  37.2 1.9 collective-permute-start.3
  59.1 2.0 reduce-precision_convert_fusion.1
  66.1 5.4 all-to-all-start.1
  71.5 1.9 maximum_bitcast_fusion.3
  73.4 5.0 all-to-all-done.1
  84.1 8.0 %outlet.4.state_ref = f32[24,1024]{1,0:T(8,128)S(1)} custom-call(f32[24,1024]{1,0:T(8,128)S(1)} %copy-done.93, f32[1024,128]{1,0:T(8,128)S(1)} %copy-done.43, f32[1024,128]{1,0:T(8,128)S(1)} %copy-done.31, f32[8,128]{1,0:T(8,128)S(1)} %reduce_sum.73.sums_two_ref, f32[1,128]{1,0:T(1,128)S(1)} %bitcast.193, f32[1,128]{1,0:T(1,128)S(1)} %bitcast.225, ...), custom_call_target="tpu_custom_call" | custom-call | tf_op jit(solution)/shard_map/eval_jaxpr/outlet/pallas_call | solution.py:645
  92.2 3.1 inlet.5
  97.6 4.2 all-to-all-start.2
  101.8 2.5 pad_maximum_fusion.3
  104.3 4.4 all-to-all-done.2
  113.6 4.2 all-to-all-start.3
  117.8 2.0 reduce-precision_convert_fusion
  119.8 4.9 all-to-all-done.3
  130.4 8.0 %outlet.5.state_ref = f32[24,1024]{1,0:T(8,128)S(1)} custom-call(f32[24,1024]{1,0:T(8,128)S(1)} %copy-done.75, f32[1024,128]{1,0:T(8,128)S(1)} %copy-done.55, f32[1024,128]{1,0:T(8,128)S(1)} %copy-done.37, f32[8,128]{1,0:T(8,128)S(1)} %reduce_sum.75.sums_two_ref, f32[1,128]{1,0:T(1,128)S(1)} %bitcast.194, f32[1,128]{1,0:T(1,128)S(1)} %bitcast.226, ...), custom_call_target="tpu_custom_call" | custom-call | tf_op jit(solution)/shard_map/eval_jaxpr/outlet/pallas_call | solution.py:645
  138.4 3.1 inlet.6
  143.8 4.2 all-to-all-start.4
  148.0 1.9 maximum_bitcast_fusion.4
  150.7 4.1 all-to-all-done.4
  159.8 4.7 all-to-all-start.5
  177.9 8.0 %outlet.6.state_ref = f32[24,1024]{1,0:T(8,128)S(1)} custom-call(f32[24,1024]{1,0:T(8,128)S(1)} %copy-done.79, f32[1024,128]{1,0:T(8,128)S(1)} %copy-done.61, f32[1024,128]{1,0:T(8,128)S(1)} %copy-done.40, f32[8,128]{1,0:T(8,128)S(1)} %reduce_sum.77.sums_two_ref, f32[1,128]{1,0:T(1,128)S(1)} %bitcast.195, f32[1,128]{1,0:T(1,128)S(1)} %bitcast.227, ...), custom_call_target="tpu_custom_call" | custom-call | tf_op jit(solution)/shard_map/eval_jaxpr/outlet/pallas_call | solution.py:645
  186.0 3.1 inlet.7
  191.4 6.1 %all-to-all-start.6 = ((f32[16,8,128]{2,1,0:T(8,128)}), f32[16,8,128]{2,1,0:T(8,128)S(1)}, u32[]{:S(2)}, u32[]{:S(2)}) async-start(f32[16,8,128]{2,1,0:T(8,128)} %broadcast_in_dim.120), calls=%async_computation.6 | async-start | bytes 131072 | tf_op jit(solution)/shard_map/eval_jaxpr/all_to_all | solution.py:497
  199.6 4.8 all-to-all-done.6
  206.7 3.5 all-to-all-start.7
  212.6 4.5 all-to-all-done.7
  217.3 19.4 %outlet_back.4 = (f32[24,1024]{1,0:T(8,128)S(1)}, f32[1024,128]{1,0:T(8,128)S(1)}, f32[8,128]{1,0:T(8,128)S(1)}, f32[128,384]{1,0:T(8,128)S(1)}, f32[128,128]{1,...) custom-call(f32[24,1024]{1,0:T(8,128)S(1)} %copy-done.83, ...), custom_call_target="tpu_custom_call", output_to_operand_aliasing={{3}: (12, {}), {4}: (13, {}), {5}: (14, {}), {6}: (15, {})} | custom-call | tf_op jit(solution)/shard_map/eval_jaxpr/outlet_back/pallas_call | solution.py:669
  242.6 2.4 collective-permute-start.9
  248.6 3.0 middle_back.4
  256.9 2.0 collective-permute-start.15
  259.5 1.8 collective-permute-start.17
  268.5 4.3 inlet_back.4
  273.0 19.8 %outlet_back.5 = (f32[24,1024]{1,0:T(8,128)S(1)}, f32[1024,128]{1,0:T(8,128)S(1)}, f32[8,128]{1,0:T(8,128)S(1)}, f32[128,384]{1,0:T(8,128)S(1)}, f32[128,128]{1,...) custom-call(f32[24,1024]{1,0:T(8,128)S(1)} %copy-done.80, ...), custom_call_target="tpu_custom_call", output_to_operand_aliasing={{3}: (12, {}), {4}: (13, {}), {5}: (14, {}), {6}: (15, {})} | custom-call | tf_op jit(solution)/shard_map/eval_jaxpr/outlet_back/pallas_call | solution.py:669
  294.8 1.8 collective-permute-done.19
  296.7 2.0 collective-permute-start.21
  299.2 1.8 collective-permute-start.23
  302.3 2.3 collective-permute-done.23
  304.6 3.0 middle_back.5
  309.6 1.8 collective-permute-done.25
  314.7 2.0 collective-permute-start.29
  317.5 2.5 collective-permute-done.29
  320.1 4.3 inlet_back.5
  325.0 19.6 %outlet_back.6 = (f32[24,1024]{1,0:T(8,128)S(1)}, f32[1024,128]{1,0:T(8,128)S(1)}, f32[8,128]{1,0:T(8,128)S(1)}, f32[128,384]{1,0:T(8,128)S(1)}, f32[128,128]{1,...) custom-call(f32[24,1024]{1,0:T(8,128)S(1)} %copy-done.76, ...), custom_call_target="tpu_custom_call", output_to_operand_aliasing={{3}: (12, {}), {4}: (13, {}), {5}: (14, {}), {6}: (15, {})} | custom-call | tf_op jit(solution)/shard_map/eval_jaxpr/outlet_back/pallas_call | solution.py:669
  346.6 1.8 collective-permute-done.31
  348.5 2.0 collective-permute-start.33
  351.0 1.8 collective-permute-start.35
  354.1 2.3 collective-permute-done.35
  356.4 3.0 middle_back.6
  361.4 1.8 collective-permute-done.37
  366.4 2.0 collective-permute-start.41
  369.3 2.5 collective-permute-done.41
  371.9 4.3 inlet_back.6
  376.3 19.6 %outlet_back.7 = (f32[24,1024]{1,0:T(8,128)S(1)}, f32[1024,128]{1,0:T(8,128)S(1)}, f32[8,128]{1,0:T(8,128)S(1)}, f32[128,384]{1,0:T(8,128)S(1)}, f32[128,128]{1,...) custom-call(f32[24,1024]{1,0:T(8,128)S(1)} %copy-done.94, ...), custom_call_target="tpu_custom_call", output_to_operand_aliasing={{3}: (12, {}), {4}: (13, {}), {5}: (14, {}), {6}: (15, {})} | custom-call | tf_op jit(solution)/shard_map/eval_jaxpr/outlet_back/pallas_call | solution.py:669
  399.8 2.0 collective-permute-start.45
  402.4 1.8 collective-permute-start.47
  405.5 2.3 collective-permute-done.47
  407.8 3.6 middle_back.7
  420.8 2.0 collective-permute-start.53
  433.8 4.3 inlet_back.7
  448.5 8.3 %outlet.7 = f32[24,1024]{1,0:T(8,128)S(1)} custom-call(f32[24,1024]{1,0:T(8,128)S(1)} %copy-done.85, f32[1024,128]{1,0:T(8,128)S(1)} %copy-done.53, f32[1024,128]{1,0:T(8,128)S(1)} %copy-done.35, f32[8,128]{1,0:T(8,128)S(1)} %copy-done.127, f32[1,128]{1,0:T(1,128)S(1)} %bitcast.204, f32[1,128]{1,0:T(1,128)S(1)} %bitcast.232, ...), custom_call_target="tpu_custom_call" | custom-call | tf_op jit(solution)/shard_map/eval_jaxpr/outlet/pallas_call | solution.py:645
  464.7 2.2 collective-permute-start.56
  471.4 108.8 %all-reduce.10.cloned.1.call-done = f32[4536,128]{1,0:T(8,128)} async-done(((f32[4536,128]{1,0:T(8,128)}), f32[4536,128]{1,0:T(8,128)}) %all-reduce.10.cloned.1.call-update) | async-done | bytes 2322448 | tf_op jit(solution)/shard_map/psum | solution.py:761
  580.2 2.7 fusion.16
  (621 shorter events, 181.9 us)
Async XLA Ops:
  22.4 38.7 %all-to-all-start = ((f32[16,8,128]{2,1,0:T(8,128)}), f32[16,8,128]{2,1,0:T(8,128)}, u32[]{:S(2)}, u32[]{:S(2)}) async-start(f32[16,8,128]{2,1,0:T(8,128)} %broadcast_in_dim.51), calls=%async_computation | async-start | bytes 131072 | tf_op jit(solution)/shard_map/eval_jaxpr/all_to_all | solution.py:497
  37.2 130.5 %collective-permute-start.3 = (f32[15,1024]{1,0:T(8,128)}, f32[15,1024]{1,0:T(8,128)}, u32[]{:S(2)}, u32[]{:S(2)}) collective-permute-start(f32[15,1024]{1,0:T(8,128)} %bitcast.145), channel_id=1, source_target_pairs={{0,8},{8,16},{16,24},{24,0},{1,9},{9,17},{17,25},{25,1},{2,10},{10... | collective-permute-start | bytes 184328 | tf_op jit(solution)/shard_map/ppermute | solution.py:490
  39.7 129.5 %collective-permute-start.4 = (f32[15,1024]{1,0:T(8,128)}, f32[15,1024]{1,0:T(8,128)}, u32[]{:S(2)}, u32[]{:S(2)}) collective-permute-start(f32[15,1024]{1,0:T(8,128)} %bitcast.144), channel_id=1, source_target_pairs={{0,16},{8,24},{16,0},{24,8},{1,17},{9,25},{17,1},{25,9},{2,18},{10... | collective-permute-start | bytes 184328 | tf_op jit(solution)/shard_map/ppermute | solution.py:490
  41.9 128.9 %collective-permute-start.5 = (f32[15,1024]{1,0:T(8,128)}, f32[15,1024]{1,0:T(8,128)}, u32[]{:S(2)}, u32[]{:S(2)}) collective-permute-start(f32[15,1024]{1,0:T(8,128)} %bitcast.143), channel_id=1, source_target_pairs={{0,24},{8,0},{16,8},{24,16},{1,25},{9,1},{17,9},{25,17},{2,26},{10... | collective-permute-start | bytes 184328 | tf_op jit(solution)/shard_map/ppermute | solution.py:490
  66.1 12.3 %all-to-all-start.1 = ((f32[16,8,128]{2,1,0:T(8,128)}), f32[16,8,128]{2,1,0:T(8,128)}, u32[]{:S(2)}, u32[]{:S(2)}) async-start(f32[16,8,128]{2,1,0:T(8,128)} %broadcast_in_dim.57), calls=%async_computation.1 | async-start | bytes 131072 | tf_op jit(solution)/shard_map/eval_jaxpr/all_to_all | solution.py:497
  97.6 11.1 %all-to-all-start.2 = ((f32[16,8,128]{2,1,0:T(8,128)}), f32[16,8,128]{2,1,0:T(8,128)}, u32[]{:S(2)}, u32[]{:S(2)}) async-start(f32[16,8,128]{2,1,0:T(8,128)} %broadcast_in_dim.60), calls=%async_computation.2 | async-start | bytes 131072 | tf_op jit(solution)/shard_map/eval_jaxpr/all_to_all | solution.py:497
  113.6 11.1 %all-to-all-start.3 = ((f32[16,8,128]{2,1,0:T(8,128)}), f32[16,8,128]{2,1,0:T(8,128)}, u32[]{:S(2)}, u32[]{:S(2)}) async-start(f32[16,8,128]{2,1,0:T(8,128)} %broadcast_in_dim.61), calls=%async_computation.3 | async-start | bytes 131072 | tf_op jit(solution)/shard_map/eval_jaxpr/all_to_all | solution.py:497
  143.8 11.1 %all-to-all-start.4 = ((f32[16,8,128]{2,1,0:T(8,128)}), f32[16,8,128]{2,1,0:T(8,128)}, u32[]{:S(2)}, u32[]{:S(2)}) async-start(f32[16,8,128]{2,1,0:T(8,128)} %broadcast_in_dim.118), calls=%async_computation.4 | async-start | bytes 131072 | tf_op jit(solution)/shard_map/eval_jaxpr/all_to_all | solution.py:497
  159.8 12.4 %all-to-all-start.5 = ((f32[16,8,128]{2,1,0:T(8,128)}), f32[16,8,128]{2,1,0:T(8,128)}, u32[]{:S(2)}, u32[]{:S(2)}) async-start(f32[16,8,128]{2,1,0:T(8,128)} %broadcast_in_dim.119), calls=%async_computation.5 | async-start | bytes 131072 | tf_op jit(solution)/shard_map/eval_jaxpr/all_to_all | solution.py:497
  191.4 13.0 %all-to-all-start.6 = ((f32[16,8,128]{2,1,0:T(8,128)}), f32[16,8,128]{2,1,0:T(8,128)S(1)}, u32[]{:S(2)}, u32[]{:S(2)}) async-start(f32[16,8,128]{2,1,0:T(8,128)} %broadcast_in_dim.120), calls=%async_computation.6 | async-start | bytes 131072 | tf_op jit(solution)/shard_map/eval_jaxpr/all_to_all | solution.py:497
  206.7 10.4 %all-to-all-start.7 = ((f32[16,8,128]{2,1,0:T(8,128)}), f32[16,8,128]{2,1,0:T(8,128)S(1)}, u32[]{:S(2)}, u32[]{:S(2)}) async-start(f32[16,8,128]{2,1,0:T(8,128)} %broadcast_in_dim.121), calls=%async_computation.7 | async-start | bytes 131072 | tf_op jit(solution)/shard_map/eval_jaxpr/all_to_all | solution.py:497
  210.2 369.9 %all-reduce.10.cloned.1.call-start = ((), (), s32[]{:S(2)}) async-start(), calls=%async_computation.8 | async-start | bytes 4644864 | tf_op jit(solution)/shard_map/psum | solution.py:761
  236.8 3.1 collective-permute-start.6
  236.9 3.7 collective-permute-start.7
  237.1 3.5 collective-permute-start.8
  240.6 6.9 %collective-permute-start.10 = (f32[8,128]{1,0:T(8,128)S(1)}, f32[8,128]{1,0:T(8,128)S(1)}, u32[]{:S(2)}, u32[]{:S(2)}) collective-permute-start(f32[8,128]{1,0:T(8,128)S(1)} %add_add_fusion.15), channel_id=1, source_target_pairs={{0,8},{1,9},{2,10},{3,11},{4,12},{5,13},{6,14},{7,15},{8,0},{9,1},... | collective-permute-start | bytes 12296 | tf_op jit(solution)/shard_map/eval_jaxpr/ppermute | solution.py:520
  241.1 6.3 %collective-permute-start.11 = (f32[8,128]{1,0:T(8,128)S(1)}, f32[8,128]{1,0:T(8,128)S(1)}, u32[]{:S(2)}, u32[]{:S(2)}) collective-permute-start(f32[8,128]{1,0:T(8,128)S(1)} %add_add_fusion.15), channel_id=1, source_target_pairs={{0,12},{1,13},{2,14},{3,15},{4,8},{5,9},{6,10},{7,11},{8,4},{9,5},... | collective-permute-start | bytes 12296 | tf_op jit(solution)/shard_map/eval_jaxpr/ppermute | solution.py:520
  242.6 4.8 collective-permute-start.9
  252.5 3.6 collective-permute-start.13
  253.9 3.0 collective-permute-start.14
  256.9 7.2 %collective-permute-start.15 = (f32[8,128]{1,0:T(8,128)S(1)}, f32[8,128]{1,0:T(8,128)S(1)}, u32[]{:S(2)}, u32[]{:S(2)}) collective-permute-start(f32[8,128]{1,0:T(8,128)S(1)} %add_add_fusion.13), channel_id=1, source_target_pairs={{0,4},{1,5},{2,6},{3,7},{4,0},{5,1},{6,2},{7,3},{8,12},{9,13},{10,... | collective-permute-start | bytes 12296 | tf_op jit(solution)/shard_map/eval_jaxpr/ppermute | solution.py:520
  258.9 5.2 collective-permute-start.16
  259.5 5.4 collective-permute-start.17
  292.8 1.9 collective-permute-start.18
  292.9 3.7 collective-permute-start.19
  293.6 3.0 collective-permute-start.20
  296.7 4.5 collective-permute-start.21
  298.7 3.6 collective-permute-start.22
  299.2 5.4 collective-permute-start.23
  307.7 1.9 collective-permute-start.24
  307.8 3.7 collective-permute-start.25
  309.2 3.0 collective-permute-start.26
  312.3 4.5 collective-permute-start.27
  313.9 3.6 collective-permute-start.28
  314.7 5.4 collective-permute-start.29
  344.7 3.7 collective-permute-start.31
  345.4 3.0 collective-permute-start.32
  348.5 4.5 collective-permute-start.33
  350.5 3.6 collective-permute-start.34
  351.0 5.4 collective-permute-start.35
  359.5 1.9 collective-permute-start.36
  359.5 3.7 collective-permute-start.37
  361.0 3.0 collective-permute-start.38
  364.0 4.5 collective-permute-start.39
  365.7 3.6 collective-permute-start.40
  366.4 5.4 collective-permute-start.41
  396.0 1.9 collective-permute-start.42
  396.1 3.7 collective-permute-start.43
  396.8 3.0 collective-permute-start.44
  399.8 4.5 collective-permute-start.45
  401.8 3.6 collective-permute-start.46
  402.4 5.4 collective-permute-start.47
  413.1 3.9 collective-permute-start.48
  413.1 3.9 collective-permute-start.49
  414.4 3.2 collective-permute-start.50
  418.4 6.5 %collective-permute-start.51 = (f32[8,128]{1,0:T(8,128)S(1)}, f32[8,128]{1,0:T(8,128)S(1)}, u32[]{:S(2)}, u32[]{:S(2)}) collective-permute-start(f32[8,128]{1,0:T(8,128)S(1)} %add_add_fusion.1), channel_id=1, source_target_pairs={{0,4},{1,5},{2,6},{3,7},{4,0},{5,1},{6,2},{7,3},{8,12},{9,13},{10,... | collective-permute-start | bytes 12296 | tf_op jit(solution)/shard_map/eval_jaxpr/ppermute | solution.py:520
  420.0 4.9 collective-permute-start.52
  420.8 5.4 collective-permute-start.53
  458.6 6.1 %collective-permute-start = (f32[15,1024]{1,0:T(8,128)S(1)}, f32[15,1024]{1,0:T(8,128)S(1)}, u32[]{:S(2)}, u32[]{:S(2)}) collective-permute-start(f32[15,1024]{1,0:T(8,128)S(1)} %bitcast.248), channel_id=1, source_target_pairs={{0,8},{8,16},{16,24},{24,0},{1,9},{9,17},{17,25},{25,1},{2,10},{10... | collective-permute-start | bytes 184328 | tf_op jit(solution)/shard_map/ppermute | solution.py:490
  459.9 7.0 %collective-permute-start.1 = (f32[15,1024]{1,0:T(8,128)S(1)}, f32[15,1024]{1,0:T(8,128)S(1)}, u32[]{:S(2)}, u32[]{:S(2)}) collective-permute-start(f32[15,1024]{1,0:T(8,128)S(1)} %bitcast.246), channel_id=1, source_target_pairs={{0,16},{8,24},{16,0},{24,8},{1,17},{9,25},{17,1},{25,9},{2,18},{10... | collective-permute-start | bytes 184328 | tf_op jit(solution)/shard_map/ppermute | solution.py:490
  460.5 6.4 %collective-permute-start.2 = (f32[15,1024]{1,0:T(8,128)S(1)}, f32[15,1024]{1,0:T(8,128)S(1)}, u32[]{:S(2)}, u32[]{:S(2)}) collective-permute-start(f32[15,1024]{1,0:T(8,128)S(1)} %bitcast.249), channel_id=1, source_target_pairs={{0,24},{8,0},{16,8},{24,16},{1,25},{9,1},{17,9},{25,17},{2,26},{10... | collective-permute-start | bytes 184328 | tf_op jit(solution)/shard_map/ppermute | solution.py:490
  462.3 5.8 collective-permute-start.54
  462.7 5.5 collective-permute-start.55
  464.7 4.3 collective-permute-start.56
  (178 other events, 1248.0 us)
Sparse Core Ops, SparseCore 0:
  447.3 132.8 all-reduce.9

commit v3 on v2

--- a/solution.py
+++ b/solution.py
@@ -147,12 +147,6 @@
 def by_halves(left_halves, right):
     high, low = halves(right)
     return folded(dot(left_halves, high) + dot(left_halves, low), 0)
-
-
-def static_kernel(lon, maps_ref, weight_ref, bias_ref, out_ref, patches_ref):
-    maps = maps_ref[...]
-    fill_patches(patches_ref, maps.T, lon)
-    out_ref[...] = conv_patches(patches_ref, weight_ref, lon) + bias_ref[...]
 
 
 def inlet_kernel(
@@ -247,8 +241,9 @@
 
 
 def outlet_back_kernel(
-    lon, count, block_size, step_size,
-    state_ref, seed_ref, inner_ref, pre_two_ref, sums_two_ref, gain_ref, shift_ref,
+    lon, count, block_size, step_size, sections,
+    ids_ref, step_ref,
+    state_ref, d_next_ref, cots_ref, inner_ref, pre_two_ref, sums_two_ref, gain_ref, shift_ref,
     w_qkv_ref, w_mixer_ref, w_qkv_back_ref, w_mixer_back_ref, w_velocity_back_ref,
     acc_qkv_ref, acc_mixer_ref, acc_velocity_ref, acc_small_ref,
     d_state_ref, d_two_ref, sums_ref,
@@ -258,7 +253,8 @@
     channels = inner_ref.shape[1]
     cells = inner_ref.shape[0]
     head_width = channels // HEADS
-    state, seed = state_ref[...], seed_ref[...]
+    state = state_ref[...]
+    seed = d_next_ref[...] + cots_ref[lax.rem(ids_ref[0] - step_ref[0] + sections, sections)]
     amount, east, north = state[:GROUP], state[GROUP : 2 * GROUP], state[2 * GROUP :]
     d_amount = seed[:GROUP]
     d_lon = step_size * along_lon(d_amount, lon)
@@ -423,50 +419,253 @@
     d_state_ref[GROUP:] = d_state[GROUP:]
 
 
-def static_back_kernel(lon, maps_ref, d_inner_ref, out_ref, bias_ref, patches_ref):
-    d_inner = d_inner_ref[...]
+def spread(groups, array, size):
+    pad = jnp.zeros((GROUP - size, array.shape[1]), F32)
+    pieces = []
+    for group in range(groups):
+        pieces += [array[group * size : (group + 1) * size], pad]
+    return jnp.concatenate(pieces, axis=0)
+
+
+def enter_kernel(plan, ids_ref, order_ref, state_ref, cot_ref, *out_refs):
+    section, dp = ids_ref[0], ids_ref[1]
+    size = state_ref.shape[1] // 3
+    out_refs[0][...] = spread(3, state_ref[order_ref[0, plan.slot(section, dp)]], size)
+    for steps, out_ref in enumerate(out_refs[1:]):
+        target = lax.rem(section + steps, plan.sections)
+        out_ref[...] = spread(3, cot_ref[0, order_ref[0, plan.slot(target, dp)]], size)
+
+
+def leave_kernel(plan, ids_ref, values_ref, *out_refs):
+    for steps, out_ref in enumerate(out_refs):
+        out_ref[...] = values_ref[lax.rem(ids_ref[0] + steps, plan.sections)]
+
+
+def arrive_kernel(plan, ids_ref, order_ref, *refs):
+    section, dp = ids_ref[0], ids_ref[1]
+    out_ref = refs[-1]
+    size = out_ref.shape[2] // 3
+    for steps, ref in enumerate(refs[:-1]):
+        source = lax.rem(section - steps + plan.sections, plan.sections)
+        place = order_ref[0, plan.slot(source, dp)]
+        for group in range(3):
+            out_ref[0, place, group * size : (group + 1) * size] = ref[group * GROUP : group * GROUP + size]
+
+
+def put_conv_weight(out_ref, taps):
+    for tap, weight in enumerate(taps):
+        wide = beside(weight)
+        rows = weight.shape[0]
+        out_ref[2 * tap * rows : (2 * tap + 1) * rows] = wide
+        out_ref[(2 * tap + 1) * rows : (2 * tap + 2) * rows] = wide
+
+
+def put_left_weight(out_ref, weight):
+    rows = weight.shape[0]
+    for place, half in enumerate(halves(weight)):
+        out_ref[place * rows : (place + 1) * rows] = jnp.concatenate([half, half], axis=1)
+
+
+def first_weights_kernel(
+    lon, quantities, w_input_ref, w_first_ref, b_input_ref, maps_ref,
+    static_part_ref, moving_cat_ref, moving_back_ref, first_cat_ref,
+    patches_ref, weight_ref, taps_ref,
+):
+    channels = w_input_ref.shape[2]
+    moving = 5 * quantities
+    statics = maps_ref.shape[0]
+    taps_ref[...] = jnp.zeros(taps_ref.shape, F32)
+    for tap in range(9):
+        row, column = divmod(tap, 3)
+        for group in range(5):
+            start = (column * 5 + group) * GROUP
+            taps_ref[9 + row, start : start + quantities] = w_input_ref[
+                tap, group * quantities : (group + 1) * quantities
+            ]
+        taps_ref[tap, :statics] = w_input_ref[tap, moving:]
+    put_conv_weight(moving_cat_ref, [taps_ref[9 + row] for row in range(3)])
+    put_conv_weight(moving_back_ref, [taps_ref[11 - row].T for row in range(3)])
+    put_conv_weight(weight_ref, [taps_ref[tap] for tap in range(9)])
+    maps = jnp.concatenate(
+        [maps_ref[...], jnp.zeros((channels - statics, maps_ref.shape[1]), F32)], axis=0
+    )
+    fill_patches(patches_ref, maps.T, lon)
+    static_part_ref[...] = conv_patches(patches_ref, weight_ref, lon) + b_input_ref[...]
+    put_conv_weight(first_cat_ref, [w_first_ref[tap] for tap in range(9)])
+
+
+def second_weights_kernel(w_second_ref, out_ref):
+    put_conv_weight(out_ref, [w_second_ref[tap] for tap in range(9)])
+
+
+def outlet_weights_kernel(
+    quantities, w_query_ref, w_key_ref, w_value_ref, w_mixer_ref, w_velocity_ref,
+    qkv_ref, qkv_back_ref, mixer_ref, mixer_back_ref, velocity_ref, velocity_back_ref,
+    rows_ref,
+):
+    parts = [ref[...] for ref in (w_query_ref, w_key_ref, w_value_ref)]
+    put_left_weight(qkv_ref, jnp.concatenate([part.T for part in parts], axis=0))
+    put_left_weight(qkv_back_ref, jnp.concatenate(parts, axis=1))
+    put_left_weight(mixer_ref, w_mixer_ref[...].T)
+    put_left_weight(mixer_back_ref, w_mixer_ref[...])
+    channels = w_mixer_ref.shape[0]
+    rows_ref[...] = jnp.zeros(rows_ref.shape, F32)
+    for tap in range(9):
+        for group in range(2):
+            start = (tap * 2 + group) * GROUP
+            rows_ref[start : start + quantities] = w_velocity_ref[
+                tap, group * quantities : (group + 1) * quantities
+            ]
+    size = 18 * GROUP
+    put_left_weight(velocity_ref, rows_ref[:size])
+    put_left_weight(velocity_back_ref, rows_ref[...].T[:, :size])
+
+
+def back_weights_kernel(w_first_ref, w_second_ref, first_ref, second_ref):
+    put_conv_weight(first_ref, [w_first_ref[8 - tap].T for tap in range(9)])
+    put_conv_weight(second_ref, [w_second_ref[8 - tap].T for tap in range(9)])
+
+
+def index_of(ids_ref, plan, bits):
+    own = ids_ref[0] * plan.dp + ids_ref[1]
+    return sum(lax.rem(own // bit, 2) << place for place, bit in enumerate(bits))
+
+
+def deal(total_ref, own, out_refs):
+    rows = out_refs[0].shape[0]
+    for turn, out_ref in enumerate(out_refs):
+        out_ref[...] = total_ref[pl.ds(pl.multiple_of((own ^ turn) * rows, GROUP), rows)]
+
+
+def pack_kernel(
+    plan, bits, lon, statics, ids_ref, maps_ref, inner_ref, first_ref, second_ref, moving_ref,
+    qkv_ref, mixer_ref, velocity_ref, small_one_ref, small_two_ref, *refs,
+):
+    out_refs, total_ref, patches_ref = refs[:-2], refs[-2], refs[-1]
+    cells, channels = inner_ref.shape
+    d_inner = inner_ref[...]
     fill_patches(patches_ref, d_inner, lon)
-    cells = d_inner.shape[0]
     width = patches_ref.shape[1] // 3
-    left = stacked(maps_ref[...])
+    maps = maps_ref[...]
+    blank = jnp.zeros((-statics % GROUP, cells), F32)
+    maps = jnp.concatenate([maps, blank], axis=0)
+    rows = maps.shape[0]
+    left = jnp.concatenate(halves(maps), axis=0)
+    start = 0
+
+    def put(value):
+        nonlocal start
+        total_ref[start : start + value.shape[0]] = value
+        start += value.shape[0]
+
+    for tap in range(9):
+        put(first_ref[tap])
+    for tap in range(9):
+        put(second_ref[tap])
     for tap in range(9):
         row, column = divmod(8 - tap, 3)
         right = patches_ref[lon * row : lon * row + cells, column * width : (column + 1) * width]
-        out_ref[tap] = folded(folded(dot(left, right), 0), 1)
-    bias_ref[...] = jnp.zeros(bias_ref.shape, F32) + jnp.sum(d_inner, axis=0, keepdims=True)
-
-
-def call(kernel, outs, scratch=(), aliases=None, name=None):
-    return pl.pallas_call(
-        kernel,
-        out_shape=tuple(jax.ShapeDtypeStruct(shape, F32) for shape in outs),
-        scratch_shapes=scratch,
-        input_output_aliases=aliases or {},
-        compiler_params=pltpu.CompilerParams(vmem_limit_bytes=VMEM_LIMIT),
-        name=name,
-        interpret=INTERPRET,
-    )
-
-
-VMEM_LIMIT = 48 * 1024 * 1024
-INTERPRET = False
-
-
-def cut(weight):
-    high = lax.reduce_precision(weight, 8, 7)
-    return high.astype(BF16), (weight - high).astype(BF16)
-
-
-def conv_weight(weight):
-    wide = jnp.concatenate(cut(weight), axis=2)
-    return jnp.stack([wide, wide], axis=1).reshape(-1, wide.shape[2])
-
-
-def left_weight(weight):
-    high, low = cut(weight)
-    return jnp.concatenate(
-        [jnp.concatenate([high, high], axis=1), jnp.concatenate([low, low], axis=1)], axis=0
-    )
+        put(folded(folded(dot(left, right), 0), 1))
+    for place in range(3):
+        put(moving_ref[place, : 15 * GROUP])
+    for part in range(3):
+        put(qkv_ref[:, part * channels : (part + 1) * channels])
+    put(mixer_ref[...])
+    put(velocity_ref[...])
+    put(small_one_ref[...])
+    put(small_two_ref[...])
+    put(jnp.zeros((GROUP, channels), F32) + jnp.sum(d_inner, axis=0, keepdims=True))
+    total_ref[start:] = jnp.zeros((total_ref.shape[0] - start, channels), F32)
+    deal(total_ref, index_of(ids_ref, plan, bits), out_refs)
+
+
+def reduce_kernel(plan, bits, count, ids_ref, *refs):
+    total_ref = refs[-1]
+    total = refs[0][...]
+    for ref in refs[1:count]:
+        total = total + ref[...]
+    if not bits:
+        refs[count][...] = total
+        return
+    total_ref[...] = total
+    deal(total_ref, index_of(ids_ref, plan, bits), refs[count:-1])
+
+
+def gather_rows(plan, bits, ids_ref, part_refs, out_ref):
+    own = index_of(ids_ref, plan, bits)
+    rows = part_refs[0].shape[0]
+    for turn, ref in enumerate(part_refs):
+        out_ref[pl.ds(pl.multiple_of((own ^ turn) * rows, GROUP), rows)] = ref[...]
+
+
+def gather_kernel(plan, bits, ids_ref, *refs):
+    gather_rows(plan, bits, ids_ref, refs[:-1], refs[-1])
+
+
+def unpack_kernel(
+    plan, bits, quantities, statics, ids_ref, *refs,
+):
+    count = 1 << len(bits)
+    (
+        input_ref, bias_ref, first_ref, gain_one_ref, shift_one_ref, second_ref, gain_two_ref, shift_two_ref,
+        query_ref, key_ref, value_ref, mixer_ref, velocity_ref, velocity_bias_ref, total_ref,
+    ) = refs[count:]
+    gather_rows(plan, bits, ids_ref, refs[:count], total_ref)
+    channels = mixer_ref.shape[0]
+    moving = 5 * quantities
+    start = 0
+
+    def take(rows):
+        nonlocal start
+        start += rows
+        return total_ref[start - rows : start]
+
+    for tap in range(9):
+        first_ref[tap] = take(channels)
+    for tap in range(9):
+        second_ref[tap] = take(channels)
+    for tap in range(9):
+        input_ref[tap, moving:] = take(statics + -statics % GROUP)[:statics]
+    for row in range(3):
+        for column in range(3):
+            for group in range(5):
+                rows = take(GROUP)
+                input_ref[row * 3 + column, group * quantities : (group + 1) * quantities] = rows[:quantities]
+    query_ref[...] = take(channels)
+    key_ref[...] = take(channels)
+    value_ref[...] = take(channels)
+    mixer_ref[...] = take(channels)
+    for tap in range(9):
+        for group in range(2):
+            velocity_ref[tap, group * quantities : (group + 1) * quantities] = take(GROUP)[:quantities]
+    small = take(GROUP)
+    gain_one_ref[...], shift_one_ref[...] = small[0:1], small[1:2]
+    small = take(GROUP)
+    gain_two_ref[...], shift_two_ref[...] = small[0:1], small[1:2]
+    velocity_bias_ref[...] = take(2 * GROUP)
+    bias_ref[...] = take(GROUP)[0:1]
+
+
+def call(kernel, outs, scratch=(), aliases=None, name=None, scalars=0, kinds=None):
+    kinds = kinds or [F32] * len(outs)
+
+    def run(*operands):
+        places = [pltpu.SMEM] * scalars + [pltpu.VMEM] * (len(operands) - scalars)
+        return pl.pallas_call(
+            kernel,
+            out_shape=tuple(jax.ShapeDtypeStruct(shape, kind) for shape, kind in zip(outs, kinds)),
+            in_specs=[pl.BlockSpec(memory_space=place) for place in places],
+            out_specs=tuple(pl.BlockSpec(memory_space=pltpu.VMEM) for unused in outs),
+            scratch_shapes=scratch,
+            input_output_aliases=aliases or {},
+            compiler_params=pltpu.CompilerParams(vmem_limit_bytes=VMEM_LIMIT),
+            name=name,
+        )(*operands)
+
+    return run
+
+
+VMEM_LIMIT = 24 * 1024 * 1024
 
 
 def in_groups(array, axis, groups):
@@ -485,46 +684,75 @@
     return array.reshape(shape[:axis] + (groups * size,) + shape[axis + 1 :])
 
 
-def shift_along(value, axis, steps):
-    count = lax.axis_size(axis)
-    return lax.ppermute(value, axis, [(own, (own + steps) % count) for own in range(count)])
-
-
-def group_of(value):
-    dp, sections = lax.axis_size("dp"), lax.axis_size("section")
-    groups = [list(range(2 * dp * pair, 2 * dp * (pair + 1))) for pair in range(sections // 2)]
-    wide = jnp.broadcast_to(value[None], (2 * dp,) + value.shape)
-    return lax.all_to_all(wide, ("section", "dp"), 0, 0, axis_index_groups=groups)
-
-
-def micro_sum_direct(value):
-    return jnp.sum(group_of(value), axis=0)
-
-
-def micro_sum(value):
-    dp, sections = lax.axis_size("dp"), lax.axis_size("section")
-    reach = 1
-    while 2 * reach < dp:
-        offsets = [1, 2, 3] if 4 * reach <= dp else [1]
-        value = value + sum(
-            lax.ppermute(value, "dp", [(own, own ^ (offset * reach)) for own in range(dp)])
-            for offset in offsets
-        )
-        reach *= 4
-    if reach < dp:
-        both = [(own, section) for section in range(sections) for own in range(dp)]
-        pairs = lambda flip, jump: [
-            (section * dp + own, (section ^ flip) * dp + (own ^ jump)) for own, section in both
+class Plan:
+    def __init__(self, sections, dp):
+        self.sections, self.dp = sections, dp
+        self.halved = sections == 4 and dp >= 4
+        self.half = dp // 2
+        bits = [1 << place for place in range((sections * dp).bit_length() - 1)]
+        dp_bits = [bit for bit in bits if bit < dp]
+        section_bits = [bit for bit in bits if bit >= dp]
+        if self.halved:
+            self.sum_rounds = in_pairs(dp_bits[:-1]) + in_pairs(section_bits)
+        else:
+            self.sum_rounds = in_pairs(dp_bits) + [section_bits[:1]]
+        self.all_rounds = [dp_bits[:1]] + in_pairs(section_bits) + in_pairs(dp_bits[1:])
+
+    def slot(self, section, home):
+        if not self.halved:
+            return section
+        return lax.rem(home // self.half + section // 2, 2) * 2 + lax.rem(section, 2)
+
+    def other(self, section, dp):
+        return dp ^ self.half if self.halved and section >= 2 else dp
+
+    def to_workers(self, steps):
+        return [
+            (section * self.dp + home, self.joint((section + steps) % self.sections, home))
+            for section in range(self.sections)
+            for home in range(self.dp)
         ]
-        return value + sum(
-            lax.ppermute(value, ("section", "dp"), pairs(flip, jump))
-            for flip, jump in ((0, reach), (1, 0), (1, reach))
-        )
-    return value + lax.ppermute(value, "section", [(own, own ^ 1) for own in range(sections)])
-
-
-def pick(array, index):
-    return lax.dynamic_index_in_dim(array, index, 0, keepdims=False)
+
+    def to_homes(self, steps):
+        return [
+            (section * self.dp + own, (section + steps) % self.sections * self.dp + self.other(section, own))
+            for section in range(self.sections)
+            for own in range(self.dp)
+        ]
+
+    def joint(self, section, home):
+        return section * self.dp + self.other(section, home)
+
+
+def in_pairs(bits):
+    return [bits[start : start + 2] for start in range(0, len(bits), 2)]
+
+
+def masks_of(bits):
+    return [sum(bit for place, bit in enumerate(bits) if turn >> place & 1) for turn in range(1, 1 << len(bits))]
+
+
+def exchanged(value, mask):
+    size = lax.axis_size("section") * lax.axis_size("dp")
+    return lax.ppermute(value, ("section", "dp"), [(own, own ^ mask) for own in range(size)])
+
+
+def moved(value, pairs):
+    going = [(source, target) for source, target in pairs if source != target]
+    if not going:
+        return value
+    arrived = lax.ppermute(value, ("section", "dp"), going)
+    if len(going) == len(pairs):
+        return arrived
+    stays = jnp.array([source == target for source, target in sorted(pairs)])
+    own = lax.axis_index("section") * lax.axis_size("dp") + lax.axis_index("dp")
+    return jnp.where(stays[own], value, arrived)
+
+
+def micro_sum(plan, value):
+    for bits in plan.sum_rounds:
+        value = value + sum(exchanged(value, mask) for mask in masks_of(bits))
+    return value
 
 
 def on_device(
@@ -548,66 +776,52 @@
     b_velocity,
 ):
     segments = lax.axis_size("section")
-    segment_rank = lax.axis_index("section")
+    plan = Plan(segments, lax.axis_size("dp"))
     micro_count = segments // 2
     per_micro = state_start.shape[0] // micro_count
     cells = state_start.shape[2]
     lon = cells // LAT
-    count = float(per_micro * cells * lax.axis_size("dp"))
+    count = float(per_micro * cells * plan.dp)
     step_size = 2.0 / segments
     block_size = ATT_ROWS * lon
     channels = w_first.shape[2]
     quantities = state_start.shape[1] // 3
-    moving = 5 * quantities
-    local_order = grouping[0]
-    cot_local = cotangent[0]
     statics = static_maps.shape[0]
-
-    def place(offset):
-        return lax.rem(segment_rank + offset + segments, segments)
-
-    got = [pick(cot_local, local_order[segment_rank])]
-    for offset in range(1, segments):
-        got.append(shift_along(pick(cot_local, local_order[place(offset)]), "section", offset))
-    got = jnp.stack(got)
-    cots = jnp.stack([pick(got, place(-step)) for step in range(segments)])
-    cots = in_groups(cots, 1, 3)
-    state = in_groups(pick(state_start, local_order[segment_rank]), 0, 3)
-
-    w_moving = in_groups(w_input[:, :moving], 1, 5).reshape(3, 3 * 5 * GROUP, channels)
-    w_moving = jnp.pad(w_moving, ((0, 0), (0, channels - 3 * 5 * GROUP), (0, 0)))
-    w_static = jnp.pad(w_input[:, moving:], ((0, 0), (0, channels - statics), (0, 0)))
-    maps = jnp.pad(static_maps, ((0, channels - statics), (0, 0)))
-    w_qkv = jnp.concatenate([w_query, w_key, w_value], axis=1)
-    w_out = in_groups(w_velocity, 2, 2)
-    w_out_rows = jnp.swapaxes(w_out, 1, 2).reshape(-1, channels)
-    b_out = in_groups(b_velocity[:, None], 0, 2)
-    moving_cat = conv_weight(w_moving)
-    moving_back_cat = conv_weight(jnp.swapaxes(w_moving[::-1], 1, 2))
-    static_cat = conv_weight(w_static)
-    first_cat = conv_weight(w_first)
-    first_back_cat = conv_weight(jnp.swapaxes(w_first[::-1], 1, 2))
-    second_cat = conv_weight(w_second)
-    second_back_cat = conv_weight(jnp.swapaxes(w_second[::-1], 1, 2))
-    qkv_cat = left_weight(w_qkv.T)
-    qkv_back_cat = left_weight(w_qkv)
-    mixer_cat = left_weight(w_mixer.T)
-    mixer_back_cat = left_weight(w_mixer)
-    out_cat = left_weight(w_out_rows)
-    out_back_cat = left_weight(w_out_rows.T)
-    gain_one, shift_one = gain_first[None], shift_first[None]
-    gain_two, shift_two = gain_second[None], shift_second[None]
+    ids = jnp.stack([lax.axis_index("section"), lax.axis_index("dp")]).astype(jnp.int32)
 
     plane = (cells, channels)
     small = (GROUP, channels)
+    conv = (9 * 2 * channels, 2 * channels)
     patches = pltpu.VMEM((cells + 2 * lon, 6 * channels), BF16)
     wide = pltpu.VMEM((3 * channels, cells), F32)
     narrow = pltpu.VMEM((channels, cells), F32)
     state_shape = (3 * GROUP, cells)
 
-    (static_part,) = call(
-        functools.partial(static_kernel, lon), [plane], [patches], name="static_inlet"
-    )(maps, static_cat, b_input[None])
+    state, *cots = call(
+        functools.partial(enter_kernel, plan), [state_shape] * (segments + 1), name="enter", scalars=2
+    )(ids, grouping, state_start, cotangent)
+    state = moved(state, plan.to_workers(0))
+    cots = jnp.stack([moved(cot, plan.to_workers(steps)) for steps, cot in enumerate(cots)])
+
+    static_part, moving_cat, moving_back_cat, first_cat = call(
+        functools.partial(first_weights_kernel, lon, quantities),
+        [plane, (6 * channels, 2 * channels), (6 * channels, 2 * channels), conv],
+        [patches, pltpu.VMEM(conv, BF16), pltpu.VMEM((12, channels, channels), F32)],
+        name="first_weights", kinds=[F32, BF16, BF16, BF16],
+    )(w_input, w_first, b_input[None], static_maps)
+    (second_cat,) = call(second_weights_kernel, [conv], name="second_weights", kinds=[BF16])(w_second)
+    qkv_cat, qkv_back_cat, mixer_cat, mixer_back_cat, out_cat, out_back_cat = call(
+        functools.partial(outlet_weights_kernel, quantities),
+        [(6 * channels, 2 * channels), (2 * channels, 6 * channels), (2 * channels, 2 * channels),
+         (2 * channels, 2 * channels), (36 * GROUP, 2 * channels), (2 * channels, 36 * GROUP)],
+        [pltpu.VMEM((2 * channels, channels), F32)], name="outlet_weights", kinds=[BF16] * 6,
+    )(w_query, w_key, w_value, w_mixer, jnp.swapaxes(w_velocity, 1, 2))
+    first_back_cat, second_back_cat = call(
+        back_weights_kernel, [conv, conv], name="back_weights", kinds=[BF16, BF16]
+    )(w_first, w_second)
+    b_out = in_groups(b_velocity[:, None], 0, 2)
+    gain_one, shift_one = gain_first[None], shift_first[None]
+    gain_two, shift_two = gain_second[None], shift_second[None]
 
     inlet = call(
         functools.partial(inlet_kernel, lon), [plane, plane, small], [patches], name="inlet"
@@ -620,11 +834,11 @@
         [state_shape], [wide, narrow], name="outlet",
     )
     outlet_back = call(
-        functools.partial(outlet_back_kernel, lon, count, block_size, step_size),
+        functools.partial(outlet_back_kernel, lon, count, block_size, step_size, segments),
         [state_shape, plane, small, (channels, 3 * channels), (channels, channels),
          (18 * GROUP, channels), (3 * GROUP, channels)],
         [wide, narrow, narrow, wide],
-        {12: 3, 13: 4, 14: 5, 15: 6}, name="outlet_back",
+        {15: 3, 16: 4, 17: 5, 18: 6}, name="outlet_back", scalars=2,
     )
     middle_back = call(
         functools.partial(middle_back_kernel, lon, count),
@@ -639,9 +853,9 @@
 
     def forward(state_in, unused):
         inner, pre_one, sums_one = inlet(state_in, static_part, moving_cat, first_cat)
-        sums_one = micro_sum_direct(sums_one)
+        sums_one = micro_sum(plan, sums_one)
         pre_two, sums_two = middle(pre_one, sums_one, gain_one, shift_one, second_cat)
-        sums_two = micro_sum_direct(sums_two)
+        sums_two = micro_sum(plan, sums_two)
         (state_out,) = outlet(
             state_in, inner, pre_two, sums_two, gain_two, shift_two, qkv_cat, mixer_cat, out_cat, b_out
         )
@@ -652,40 +866,40 @@
     )
 
     def to_steps(values):
-        values = from_groups(values, 1, 3, quantities)
-        back = [pick(values, segment_rank)]
-        for offset in range(1, segments):
-            back.append(shift_along(pick(values, place(offset)), "section", offset))
-        back = jnp.stack(back)
-        senders = local_order[lax.rem(segment_rank - jnp.arange(segments) + segments, segments)]
-        return jnp.take(back, jnp.argsort(senders), axis=0)[None]
+        parts = call(
+            functools.partial(leave_kernel, plan), [state_shape] * segments, name="leave", scalars=1
+        )(ids, values)
+        parts = [moved(part, plan.to_homes(steps)) for steps, part in enumerate(parts)]
+        (out,) = call(
+            functools.partial(arrive_kernel, plan), [(1,) + state_start.shape], name="arrive", scalars=2
+        )(ids, grouping, *parts)
+        return out
 
     path_out = to_steps(path)
 
     def backward(carry, saved):
         d_state, acc = carry
-        cot_now, state_in, inner, pre_one, pre_two, sums_one, sums_two = saved
-        seed = d_state + cot_now
+        step, state_in, inner, pre_one, pre_two, sums_one, sums_two = saved
         d_partial, d_two, grad_two, qkv, mixer, velocity, small_two = outlet_back(
-            state_in, seed, inner, pre_two, sums_two, gain_two, shift_two,
+            ids, step, state_in, d_state, cots, inner, pre_two, sums_two, gain_two, shift_two,
             qkv_cat, mixer_cat, qkv_back_cat, mixer_back_cat, out_back_cat,
             acc["qkv"], acc["mixer"], acc["velocity"], acc["small_two"],
         )
-        grad_two = micro_sum(grad_two)
+        grad_two = micro_sum(plan, grad_two)
         d_normed, grad_one, second, small_one = middle_back(
             d_two, pre_two, sums_two, grad_two, gain_two,
             pre_one, sums_one, gain_one, shift_one, second_back_cat,
             acc["second"], acc["small_one"],
         )
-        grad_one = micro_sum(grad_one)
-        d_state, first, moved, inner_sum = inlet_back(
+        grad_one = micro_sum(plan, grad_one)
+        d_state, first, moving, inner_sum = inlet_back(
             state_in, d_normed, pre_one, sums_one, grad_one, gain_one,
             inner, d_two, d_partial, first_back_cat, moving_back_cat,
             acc["first"], acc["moving"], acc["inner"],
         )
         acc = dict(
             qkv=qkv, mixer=mixer, velocity=velocity, small_two=small_two, second=second,
-            small_one=small_one, first=first, moving=moved, inner=inner_sum,
+            small_one=small_one, first=first, moving=moving, inner=inner_sum,
         )
         return (d_state, acc), d_state
 
@@ -700,72 +914,61 @@
         moving=jnp.zeros((3, channels, channels), F32),
         inner=jnp.zeros(plane, F32),
     )
+    steps = jnp.arange(segments, dtype=jnp.int32)[:, None]
     (unused_start, acc), grads = lax.scan(
         backward,
         (jnp.zeros(state_shape, F32), acc),
-        (cots, entered, inners, pres_one, pres_two, all_sums_one, all_sums_two),
+        (steps, entered, inners, pres_one, pres_two, all_sums_one, all_sums_two),
         reverse=True,
         unroll=min(4, segments),
     )
     grads_out = to_steps(grads)
-    d_static, bias = call(
-        functools.partial(static_back_kernel, lon), [(9, channels, channels), small], [patches],
-        name="static_back",
-    )(maps, acc["inner"])
-
-    sizes = [
-        ("first", (9, channels, channels)),
-        ("second", (9, channels, channels)),
-        ("static", (9, channels, channels)),
-        ("moving", (3, channels, channels)),
-        ("qkv", (channels, 3 * channels)),
-        ("mixer", (channels, channels)),
-        ("velocity", (18 * GROUP, channels)),
-        ("bias", small),
-        ("small_one", small),
-        ("small_two", (3 * GROUP, channels)),
-    ]
-    acc["static"], acc["bias"] = d_static, bias
-    names = [name for name, unused_shape in sizes]
-    summed = dict(zip(names, final_sum([acc[name] for name in names])))
-    d_moving = from_groups(
-        summed["moving"][:, : 15 * GROUP].reshape(9, 5 * GROUP, channels), 1, 5, quantities
-    )
-    d_input = jnp.concatenate([d_moving, summed["static"][:, :statics]], axis=1)
-    qkv = summed["qkv"]
-    d_out = jnp.swapaxes(summed["velocity"].reshape(9, 2 * GROUP, channels), 1, 2)
-    d_out = from_groups(d_out, 2, 2, quantities)
-    small_one, small_two = summed["small_one"], summed["small_two"]
-    return (
-        path_out,
-        grads_out,
-        d_input,
-        summed["bias"][0],
-        summed["first"],
-        small_one[0],
-        small_one[1],
-        summed["second"],
-        small_two[0],
-        small_two[1],
-        qkv[:, :channels],
-        qkv[:, channels : 2 * channels],
-        qkv[:, 2 * channels :],
-        summed["mixer"],
-        d_out,
-        from_groups(small_two[GROUP:, :1], 0, 2, quantities)[:, 0],
-    )
-
-
-def final_sum(values):
-    flat = jnp.concatenate([value.reshape(-1, 128) for value in values])
-    summed = lax.psum(flat, ("section", "dp"))
-    outs = []
-    start = 0
-    for value in values:
-        rows = value.size // flat.shape[1]
-        outs.append(summed[start : start + rows].reshape(value.shape))
-        start += rows
-    return outs
+
+    rounds = plan.all_rounds
+    rows = 2 * 9 * channels + 9 * (statics + -statics % GROUP) + 45 * GROUP + 4 * channels + 23 * GROUP
+    unit = GROUP * segments * plan.dp
+    rows = -(-rows // unit) * unit
+
+    def shares(rows, bits):
+        return [(rows >> len(bits), channels)] * (1 << len(bits))
+
+    def swap(parts, bits):
+        return [parts[0]] + [exchanged(part, mask) for part, mask in zip(parts[1:], masks_of(bits))]
+
+    parts = call(
+        functools.partial(pack_kernel, plan, rounds[0], lon, statics), shares(rows, rounds[0]),
+        [pltpu.VMEM((rows, channels), F32), patches], name="pack", scalars=1,
+    )(
+        ids, static_maps, acc["inner"], acc["first"], acc["second"], acc["moving"], acc["qkv"], acc["mixer"],
+        acc["velocity"], acc["small_one"], acc["small_two"],
+    )
+    for bits, later in zip(rounds, rounds[1:] + [[]]):
+        parts = swap(parts, bits)
+        rows >>= len(bits)
+        parts = call(
+            functools.partial(reduce_kernel, plan, later, len(parts)), shares(rows, later),
+            [pltpu.VMEM((rows, channels), F32)], name="reduce_part", scalars=1,
+        )(ids, *parts)
+    for bits in rounds[::-1]:
+        parts = swap([parts[0]] * (1 << len(bits)), bits)
+        rows <<= len(bits)
+        if bits is rounds[0]:
+            break
+        parts = call(
+            functools.partial(gather_kernel, plan, bits), [(rows, channels)], name="gather_part", scalars=1
+        )(ids, *parts)
+    row = (1, channels)
+    square = (channels, channels)
+    grads_all = call(
+        functools.partial(unpack_kernel, plan, rounds[0], quantities, statics),
+        [w_input.shape, row, w_first.shape, row, row, w_second.shape, row, row, square, square, square, square,
+         (9, 2 * quantities, channels), (2 * GROUP, channels)],
+        [pltpu.VMEM((rows, channels), F32)], name="unpack", scalars=1,
+    )(ids, *parts)
+    grads_all = [grad[0] if grad.shape == row else grad for grad in grads_all]
+    grads_all[-2] = jnp.swapaxes(grads_all[-2], 1, 2)
+    grads_all[-1] = from_groups(grads_all[-1][:, :1], 0, 2, quantities)[:, 0]
+    return (path_out, grads_out) + tuple(grads_all)
 
 
 def solution(mesh):

time: 605 us -> 471 us (0.78)
  local copies, waits for them, and re-layouts: 95.6 us -> 17.3 us
  waiting for transfers between devices: 173 us -> 131 us
  other arithmetic: 37.9 us -> 3.01 us
  starting transfers between devices: 103 us -> 134 us
  between operations: 24.6 us -> 1.9 us
  Pallas kernels: 162 us -> 177 us
    psum x1 -> x0, waiting for transfers between devices: 109 us -> none  [final_sum(): summed = lax.psum(flat, ('section', 'dp'))]
    ppermute x57 -> x123, waiting for transfers between devices: 36.1 us -> 131 us  [the longest x110 107 us: exchanged(): lax.ppermute(value, ('section', 'dp'), [(own, own ^ mask) for own in rang...]
    ppermute x57 -> x123, starting transfers between devices: 62.8 us -> 134 us  [the longest x110 116 us: exchanged(): lax.ppermute(value, ('section', 'dp'), [(own, own ^ mask) for own in rang...]
    unnamed x374 -> x78, local copies, waits for them, and re-layouts: 56.7 us -> 13.5 us
    all_to_all x8 -> x0, starting transfers between devices: 39.5 us -> none  [group_of(): lax.all_to_all(wide, ('section', 'dp'), 0, 0, axis_index_groups=groups)]
    all_to_all x8 -> x0, waiting for transfers between devices: 27.8 us -> none  [group_of(): lax.all_to_all(wide, ('section', 'dp'), 0, 0, axis_index_groups=groups)]
    pallas_call x26 -> x40, Pallas kernels: 162 us -> 177 us  [run(): pl.pallas_call(kernel, out_shape=tuple((jax.ShapeDtypeStruct(shape, kind)...]
    convert_element_type x12 -> x0, other arithmetic: 10.2 us -> none  [cut(): return (high.astype(BF16), (weight - high).astype(BF16))]
  transfers between devices with their start and end apart: 66 -> 123, of which waited for: 42 -> 86; matrix products, arithmetic and copies ran while one was open for 11% -> 1% of each run, Pallas kernels for 6% -> 3%
where the time goes in v3:
time: 471 us; the launch traced here: 464 us
  Pallas kernels  177 us (38%)
  starting transfers between devices  134 us (28%)
  waiting for transfers between devices  131 us (28%)
  local copies, waits for them, and re-layouts  17.3 us (4%)
    pallas_call x40, Pallas kernels, run(): pl.pallas_call(kernel, out_shape=tuple((jax.ShapeDtypeStruct(shape, kind)...  177 us
    ppermute x110, starting transfers between devices, exchanged(): lax.ppermute(value, ('section', 'dp'), [(own, own ^ mask) for own in rang...  116 us
    ppermute x110, waiting for transfers between devices, exchanged(): lax.ppermute(value, ('section', 'dp'), [(own, own ^ mask) for own in rang...  107 us
    ppermute x13, waiting for transfers between devices, moved(): arrived = lax.ppermute(value, ('section', 'dp'), going)  24.2 us
    ppermute x13, starting transfers between devices, moved(): arrived = lax.ppermute(value, ('section', 'dp'), going)  18.2 us
    unnamed x78, local copies, waits for them, and re-layouts  13.5 us
  transfers between devices with their start and end apart: 123, of which 86 were waited for; matrix products, arithmetic and copies ran while one was open for 1% of the time, Pallas kernels for 3%

profile of v3, /device:TPU:0, one launch (start us, length us, event | category | flops | bytes accessed | tf_op | source)
XLA Modules:
  0.0 464.3 jit_solution(15305196545817437197)
XLA Ops:
  10.2 3.1 inlet.4
  13.4 2.5 collective-permute-start.3
  17.4 2.8 collective-permute-done.2
  20.2 7.3 %collective-permute-start.6 = (f32[8,128]{1,0:T(8,128)S(1)}, f32[8,128]{1,0:T(8,128)S(1)}, u32[]{:S(2)}, u32[]{:S(2)}) collective-permute-start(f32[8,128]{1,0:T(8,128)S(1)} %add_add_fusion.31), channel_id=1, source_target_pairs={{0,24},{1,25},{2,26},{3,27},{4,28},{5,29},{6,30},{7,31},{8,16},{9,... | collective-permute-start | bytes 12296 | tf_op jit(solution)/shard_map/eval_jaxpr/ppermute | solution.py:737
  29.1 2.0 collective-permute-done.4
  37.2 2.1 collective-permute-done.8
  49.6 8.2 %outlet.4.state_ref = f32[24,1024]{1,0:T(8,128)S(1)} custom-call(f32[24,1024]{1,0:T(8,128)S(1)} %broadcast_select_fusion.1.state_ref, f32[1024,128]{1,0:T(8,128)S(1)} %copy-done.6, f32[1024,128]{1,0:T(8,128)S(1)} %copy-done.3, f32[8,128]{1,0:T(8,128)S(1)} %add_add_fusion.28.sums_two_ref, f32[1,128]{1,0:T(1,128)S(1)} %bitcast.46, f32[1,128]{1,0:T(1,128)S(1)} %bitcast.78, ...), custom_call_target="tpu_custom_call" | custom-call | tf_op jit(solution)/shard_map/eval_jaxpr/outlet/pallas_call | solution.py:654
  57.9 3.1 inlet.5
  75.3 2.1 collective-permute-done.20
  77.4 2.9 collective-permute-start.24
  84.4 8.0 %outlet.5.state_ref = f32[24,1024]{1,0:T(8,128)S(1)} custom-call(f32[24,1024]{1,0:T(8,128)S(1)} %outlet.4.state_ref, f32[1024,128]{1,0:T(8,128)S(1)} %get-tuple-element.157.inner_ref, f32[1024,128]{1,0:T(8,128)S(1)} %get-tuple-element.160.pre_two_ref, f32[8,128]{1,0:T(8,128)S(1)} %add_add_fusion.24.sums_two_ref, f32[1,128]{1,0:T(1,128)S(1)} %bitcast.47, ...), custom_call_target="tpu_custom_call" | custom-call | tf_op jit(solution)/shard_map/eval_jaxpr/outlet/pallas_call | solution.py:654
  92.5 3.1 inlet.6
  109.9 2.1 collective-permute-done.32
  112.0 2.8 collective-permute-start.36
  119.0 8.3 %outlet.6.state_ref = f32[24,1024]{1,0:T(8,128)S(1)} custom-call(f32[24,1024]{1,0:T(8,128)S(1)} %outlet.5.state_ref, f32[1024,128]{1,0:T(8,128)S(1)} %get-tuple-element.162.inner_ref, f32[1024,128]{1,0:T(8,128)S(1)} %get-tuple-element.165.pre_two_ref, f32[8,128]{1,0:T(8,128)S(1)} %add_add_fusion.20.sums_two_ref, f32[1,128]{1,0:T(1,128)S(1)} %bitcast.48, ...), custom_call_target="tpu_custom_call" | custom-call | tf_op jit(solution)/shard_map/eval_jaxpr/outlet/pallas_call | solution.py:654
  127.3 3.1 inlet.7
  138.3 3.9 collective-permute-start.56
  142.1 2.0 collective-permute-start.55
  147.2 2.0 collective-permute-start.44
  150.8 4.5 collective-permute-start.48
  155.3 2.5 collective-permute-start.46
  159.4 2.0 collective-permute-done.47
  161.5 21.1 %outlet_back.4 = (f32[24,1024]{1,0:T(8,128)S(1)}, f32[1024,128]{1,0:T(8,128)S(1)}, f32[8,128]{1,0:T(8,128)S(1)}, f32[128,384]{1,0:T(8,128)S(1)}, f32[128,128]{1,...) custom-call(s32[2]{0:T(128)S(1)} %pad_add_fusion.ids_ref, ...), custom_call_target="tpu_custom_call", output_to_operand_aliasing={{3}: (15, {}), {4}: (16, {}), {5}: (17, {}), {6}: (18, {})} | custom-call | tf_op jit(solution)/shard_map/eval_jaxpr/outlet_back/pallas_call | solution.py:654
  182.8 2.0 collective-permute-start.58
  193.0 3.0 middle_back.4
  201.9 2.0 collective-permute-start.66
  205.5 2.0 collective-permute-done.67
  207.6 4.3 inlet_back.4
  211.9 20.8 %outlet_back.5 = (f32[24,1024]{1,0:T(8,128)S(1)}, f32[1024,128]{1,0:T(8,128)S(1)}, f32[8,128]{1,0:T(8,128)S(1)}, f32[128,384]{1,0:T(8,128)S(1)}, f32[128,128]{1,...) custom-call(s32[2]{0:T(128)S(1)} %pad_add_fusion.ids_ref, ...), custom_call_target="tpu_custom_call", output_to_operand_aliasing={{3}: (15, {}), {4}: (16, {}), {5}: (17, {}), {6}: (18, {})} | custom-call | tf_op jit(solution)/shard_map/eval_jaxpr/outlet_back/pallas_call | solution.py:654
  232.9 2.0 collective-permute-start.70
  243.0 3.0 middle_back.5
  251.9 2.0 collective-permute-start.78
  255.5 2.0 collective-permute-done.79
  257.5 4.3 inlet_back.5
  261.8 21.0 %outlet_back.6 = (f32[24,1024]{1,0:T(8,128)S(1)}, f32[1024,128]{1,0:T(8,128)S(1)}, f32[8,128]{1,0:T(8,128)S(1)}, f32[128,384]{1,0:T(8,128)S(1)}, f32[128,128]{1,...) custom-call(s32[2]{0:T(128)S(1)} %pad_add_fusion.ids_ref, ...), custom_call_target="tpu_custom_call", output_to_operand_aliasing={{3}: (15, {}), {4}: (16, {}), {5}: (17, {}), {6}: (18, {})} | custom-call | tf_op jit(solution)/shard_map/eval_jaxpr/outlet_back/pallas_call | solution.py:654
  283.1 2.0 collective-permute-start.82
  293.2 3.0 middle_back.6
  302.0 2.0 collective-permute-start.90
  305.7 2.0 collective-permute-done.91
  307.7 4.3 inlet_back.6
  312.0 20.8 %outlet_back.7 = (f32[24,1024]{1,0:T(8,128)S(1)}, f32[1024,128]{1,0:T(8,128)S(1)}, f32[8,128]{1,0:T(8,128)S(1)}, f32[128,384]{1,0:T(8,128)S(1)}, f32[128,128]{1,...) custom-call(s32[2]{0:T(128)S(1)} %pad_add_fusion.ids_ref, ...), custom_call_target="tpu_custom_call", output_to_operand_aliasing={{3}: (15, {}), {4}: (16, {}), {5}: (17, {}), {6}: (18, {})} | custom-call | tf_op jit(solution)/shard_map/eval_jaxpr/outlet_back/pallas_call | solution.py:654
  333.1 2.0 collective-permute-start.94
  343.2 3.0 middle_back.7
  352.0 2.0 collective-permute-start.102
  355.7 2.0 collective-permute-done.103
  357.7 4.3 inlet_back.7
  362.0 2.0 pack.1
  364.0 2.6 collective-permute-done.109.refs_1_
  368.5 2.5 collective-permute-start.112
  371.0 5.7 %collective-permute-done.110.refs_1_ = f32[512,128]{1,0:T(8,128)S(1)} collective-permute-done((f32[512,128]{1,0:T(8,128)S(1)}, f32[512,128]{1,0:T(8,128)S(1)}, u32[]{:S(2)}, u32[]{:S(2)}) %collective-permute-start.110) | collective-permute-done | bytes 262176 | tf_op jit(solution)/shard_map/ppermute | solution.py:737
  376.7 4.9 %collective-permute-done.111.refs_2_ = f32[512,128]{1,0:T(8,128)S(1)} collective-permute-done((f32[512,128]{1,0:T(8,128)S(1)}, f32[512,128]{1,0:T(8,128)S(1)}, u32[]{:S(2)}, u32[]{:S(2)}) %collective-permute-start.111) | collective-permute-done | bytes 262176 | tf_op jit(solution)/shard_map/ppermute | solution.py:737
  383.1 2.2 collective-permute-start.114
  386.6 3.2 collective-permute-done.114.refs_2_
  391.9 2.1 collective-permute-start.117
  394.0 2.3 collective-permute-start.118
  397.6 2.5 collective-permute-done.118.refs_3_
  404.2 4.0 collective-permute-done.119.refs_1_
  408.2 4.2 collective-permute-done.120.refs_2_
  413.1 8.1 %outlet.7 = f32[24,1024]{1,0:T(8,128)S(1)} custom-call(f32[24,1024]{1,0:T(8,128)S(1)} %outlet.6.state_ref, f32[1024,128]{1,0:T(8,128)S(1)} %get-tuple-element.167.inner_ref, f32[1024,128]{1,0:T(8,128)S(1)} %get-tuple-element.170.pre_two_ref, f32[8,128]{1,0:T(8,128)S(1)} %add_add_fusion.16.sums_two_ref, f32[1,128]{1,0:T(1,128)S(1)} %bitcast.57, ...), custom_call_target="tpu_custom_call" | custom-call | tf_op jit(solution)/shard_map/eval_jaxpr/outlet/pallas_call | solution.py:654
  422.9 5.1 %collective-permute-start.51 = (f32[24,1024]{1,0:T(8,128)S(1)}, f32[24,1024]{1,0:T(8,128)S(1)}, u32[]{:S(2)}, u32[]{:S(2)}) collective-permute-start(f32[24,1024]{1,0:T(8,128)S(1)} %get-tuple-element.174), channel_id=1, source_target_pairs={{0,16},{1,17},{2,18},{3,19},{4,20},{5,21},{6,22},{7,23},{8,24},{9,... | collective-permute-start | bytes 294920 | tf_op jit(solution)/shard_map/ppermute | solution.py:744
  431.3 10.9 %collective-permute-done.50.refs_1_ = f32[24,1024]{1,0:T(8,128)S(1)} collective-permute-done((f32[24,1024]{1,0:T(8,128)S(1)}, f32[24,1024]{1,0:T(8,128)S(1)}, u32[]{:S(2)}, u32[]{:S(2)}) %collective-permute-start.50) | collective-permute-done | bytes 98336 | tf_op jit(solution)/shard_map/ppermute | solution.py:744
  442.2 2.0 collective-permute-done.51.refs_2_
  448.5 10.4 %collective-permute-done.106.refs_1_ = f32[24,1024]{1,0:T(8,128)S(1)} collective-permute-done((f32[24,1024]{1,0:T(8,128)S(1)}, f32[24,1024]{1,0:T(8,128)S(1)}, u32[]{:S(2)}, u32[]{:S(2)}) %collective-permute-start.106) | collective-permute-done | bytes 98336 | tf_op jit(solution)/shard_map/ppermute | solution.py:744
  461.3 2.0 unpack.1
  (365 shorter events, 168.5 us)
Async XLA Ops:
  5.0 4.5 collective-permute-start
  13.4 3.9 collective-permute-start.3
  20.2 8.9 %collective-permute-start.6 = (f32[8,128]{1,0:T(8,128)S(1)}, f32[8,128]{1,0:T(8,128)S(1)}, u32[]{:S(2)}, u32[]{:S(2)}) collective-permute-start(f32[8,128]{1,0:T(8,128)S(1)} %add_add_fusion.31), channel_id=1, source_target_pairs={{0,24},{1,25},{2,26},{3,27},{4,28},{5,29},{6,30},{7,31},{8,16},{9,... | collective-permute-start | bytes 12296 | tf_op jit(solution)/shard_map/eval_jaxpr/ppermute | solution.py:737
  27.5 3.6 collective-permute-start.4
  35.7 3.6 collective-permute-start.8
  39.3 8.2 %collective-permute-start.12 = (f32[8,128]{1,0:T(8,128)S(1)}, f32[8,128]{1,0:T(8,128)S(1)}, u32[]{:S(2)}, u32[]{:S(2)}) collective-permute-start(f32[8,128]{1,0:T(8,128)S(1)} %add_add_fusion.29), channel_id=1, source_target_pairs={{0,24},{1,25},{2,26},{3,27},{4,28},{5,29},{6,30},{7,31},{8,16},{9,... | collective-permute-start | bytes 12296 | tf_op jit(solution)/shard_map/eval_jaxpr/ppermute | solution.py:737
  40.2 7.3 %collective-permute-start.10 = (f32[8,128]{1,0:T(8,128)S(1)}, f32[8,128]{1,0:T(8,128)S(1)}, u32[]{:S(2)}, u32[]{:S(2)}) collective-permute-start(f32[8,128]{1,0:T(8,128)S(1)} %add_add_fusion.29), channel_id=1, source_target_pairs={{0,8},{1,9},{2,10},{3,11},{4,12},{5,13},{6,14},{7,15},{8,0},{9,1},... | collective-permute-start | bytes 12296 | tf_op jit(solution)/shard_map/eval_jaxpr/ppermute | solution.py:737
  40.9 6.7 %collective-permute-start.11 = (f32[8,128]{1,0:T(8,128)S(1)}, f32[8,128]{1,0:T(8,128)S(1)}, u32[]{:S(2)}, u32[]{:S(2)}) collective-permute-start(f32[8,128]{1,0:T(8,128)S(1)} %add_add_fusion.29), channel_id=1, source_target_pairs={{0,16},{1,17},{2,18},{3,19},{4,20},{5,21},{6,22},{7,23},{8,24},{9,... | collective-permute-start | bytes 12296 | tf_op jit(solution)/shard_map/eval_jaxpr/ppermute | solution.py:737
  65.4 4.5 collective-permute-start.18
  66.3 3.6 collective-permute-start.16
  77.4 4.5 collective-permute-start.24
  80.2 3.6 collective-permute-start.22
  80.8 3.6 collective-permute-start.23
  99.9 4.5 collective-permute-start.30
  100.9 3.6 collective-permute-start.28
  112.0 4.5 collective-permute-start.36
  114.8 3.6 collective-permute-start.34
  131.2 3.6 collective-permute-start.38
  134.8 9.9 %collective-permute-start.42 = (f32[8,128]{1,0:T(8,128)S(1)}, f32[8,128]{1,0:T(8,128)S(1)}, u32[]{:S(2)}, u32[]{:S(2)}) collective-permute-start(f32[8,128]{1,0:T(8,128)S(1)} %add_add_fusion.19), channel_id=1, source_target_pairs={{0,24},{1,25},{2,26},{3,27},{4,28},{5,29},{6,30},{7,31},{8,16},{9,... | collective-permute-start | bytes 12296 | tf_op jit(solution)/shard_map/eval_jaxpr/ppermute | solution.py:737
  135.7 9.6 %collective-permute-start.40 = (f32[8,128]{1,0:T(8,128)S(1)}, f32[8,128]{1,0:T(8,128)S(1)}, u32[]{:S(2)}, u32[]{:S(2)}) collective-permute-start(f32[8,128]{1,0:T(8,128)S(1)} %add_add_fusion.19), channel_id=1, source_target_pairs={{0,8},{1,9},{2,10},{3,11},{4,12},{5,13},{6,14},{7,15},{8,0},{9,1},... | collective-permute-start | bytes 12296 | tf_op jit(solution)/shard_map/eval_jaxpr/ppermute | solution.py:737
  136.4 9.0 %collective-permute-start.41 = (f32[8,128]{1,0:T(8,128)S(1)}, f32[8,128]{1,0:T(8,128)S(1)}, u32[]{:S(2)}, u32[]{:S(2)}) collective-permute-start(f32[8,128]{1,0:T(8,128)S(1)} %add_add_fusion.19), channel_id=1, source_target_pairs={{0,16},{1,17},{2,18},{3,19},{4,20},{5,21},{6,22},{7,23},{8,24},{9,... | collective-permute-start | bytes 12296 | tf_op jit(solution)/shard_map/eval_jaxpr/ppermute | solution.py:737
  138.3 19.5 %collective-permute-start.56 = (f32[24,1024]{1,0:T(8,128)S(1)}, f32[24,1024]{1,0:T(8,128)S(1)}, u32[]{:S(2)}, u32[]{:S(2)}) collective-permute-start(f32[24,1024]{1,0:T(8,128)S(1)} %copy-done.34), channel_id=1, source_target_pairs={{0,28},{1,29},{2,30},{3,31},{4,24},{5,25},{6,26},{7,27},{8,0},{9,1... | collective-permute-start | bytes 294920 | tf_op jit(solution)/shard_map/ppermute | solution.py:744
  142.1 15.6 %collective-permute-start.55 = (f32[24,1024]{1,0:T(8,128)S(1)}, f32[24,1024]{1,0:T(8,128)S(1)}, u32[]{:S(2)}, u32[]{:S(2)}) collective-permute-start(f32[24,1024]{1,0:T(8,128)S(1)} %copy-done.32), channel_id=1, source_target_pairs={{0,20},{1,21},{2,22},{3,23},{4,16},{5,17},{6,18},{7,19},{8,28},{9,... | collective-permute-start | bytes 294920 | tf_op jit(solution)/shard_map/ppermute | solution.py:744
  147.2 3.6 collective-permute-start.44
  150.1 7.7 %collective-permute-start.54 = (f32[24,1024]{1,0:T(8,128)S(1)}, f32[24,1024]{1,0:T(8,128)S(1)}, u32[]{:S(2)}, u32[]{:S(2)}) collective-permute-start(f32[24,1024]{1,0:T(8,128)S(1)} %copy-done.30), channel_id=1, source_target_pairs={{0,8},{1,9},{2,10},{3,11},{4,12},{5,13},{6,14},{7,15},{8,20},{9,21... | collective-permute-start | bytes 294920 | tf_op jit(solution)/shard_map/ppermute | solution.py:744
  150.8 7.0 %collective-permute-start.48 = (f32[8,128]{1,0:T(8,128)S(1)}, f32[8,128]{1,0:T(8,128)S(1)}, u32[]{:S(2)}, u32[]{:S(2)}) collective-permute-start(f32[8,128]{1,0:T(8,128)S(1)} %add_add_fusion.17), channel_id=1, source_target_pairs={{0,24},{1,25},{2,26},{3,27},{4,28},{5,29},{6,30},{7,31},{8,16},{9,... | collective-permute-start | bytes 12296 | tf_op jit(solution)/shard_map/eval_jaxpr/ppermute | solution.py:737
  155.3 4.1 collective-permute-start.46
  157.8 3.6 collective-permute-start.47
  182.8 3.6 collective-permute-start.58
  186.4 4.5 collective-permute-start.62
  189.3 3.6 collective-permute-start.61
  200.4 4.5 collective-permute-start.68
  201.9 3.6 collective-permute-start.66
  203.9 3.6 collective-permute-start.67
  236.5 4.5 collective-permute-start.74
  250.4 4.5 collective-permute-start.80
  251.9 3.6 collective-permute-start.78
  286.7 4.5 collective-permute-start.86
  300.6 4.5 collective-permute-start.92
  302.0 3.6 collective-permute-start.90
  336.7 4.5 collective-permute-start.98
  350.6 4.5 collective-permute-start.104
  352.0 3.6 collective-permute-start.102
  367.4 9.2 %collective-permute-start.110 = (f32[512,128]{1,0:T(8,128)S(1)}, f32[512,128]{1,0:T(8,128)S(1)}, u32[]{:S(2)}, u32[]{:S(2)}) collective-permute-start(f32[512,128]{1,0:T(8,128)S(1)} %get-tuple-element.253), channel_id=1, source_target_pairs={{0,8},{1,9},{2,10},{3,11},{4,12},{5,13},{6,14},{7,15},{8,0},{9,1},... | collective-permute-start | bytes 786440 | tf_op jit(solution)/shard_map/ppermute | solution.py:737
  367.5 14.0 %collective-permute-start.111 = (f32[512,128]{1,0:T(8,128)S(1)}, f32[512,128]{1,0:T(8,128)S(1)}, u32[]{:S(2)}, u32[]{:S(2)}) collective-permute-start(f32[512,128]{1,0:T(8,128)S(1)} %get-tuple-element.254), channel_id=1, source_target_pairs={{0,16},{1,17},{2,18},{3,19},{4,20},{5,21},{6,22},{7,23},{8,24},{9,... | collective-permute-start | bytes 786440 | tf_op jit(solution)/shard_map/ppermute | solution.py:737
  368.5 13.1 %collective-permute-start.112 = (f32[512,128]{1,0:T(8,128)S(1)}, f32[512,128]{1,0:T(8,128)S(1)}, u32[]{:S(2)}, u32[]{:S(2)}) collective-permute-start(f32[512,128]{1,0:T(8,128)S(1)} %get-tuple-element.255), channel_id=1, source_target_pairs={{0,24},{1,25},{2,26},{3,27},{4,28},{5,29},{6,30},{7,31},{8,16},{9,... | collective-permute-start | bytes 786440 | tf_op jit(solution)/shard_map/ppermute | solution.py:737
  382.2 4.5 collective-permute-start.113
  383.1 6.7 %collective-permute-start.114 = (f32[128,128]{1,0:T(8,128)S(1)}, f32[128,128]{1,0:T(8,128)S(1)}, u32[]{:S(2)}, u32[]{:S(2)}) collective-permute-start(f32[128,128]{1,0:T(8,128)S(1)} %get-tuple-element.258), channel_id=1, source_target_pairs={{0,4},{1,5},{2,6},{3,7},{4,0},{5,1},{6,2},{7,3},{8,12},{9,13},{10,... | collective-permute-start | bytes 196616 | tf_op jit(solution)/shard_map/ppermute | solution.py:737
  385.2 6.1 %collective-permute-start.115 = (f32[128,128]{1,0:T(8,128)S(1)}, f32[128,128]{1,0:T(8,128)S(1)}, u32[]{:S(2)}, u32[]{:S(2)}) collective-permute-start(f32[128,128]{1,0:T(8,128)S(1)} %get-tuple-element.259), channel_id=1, source_target_pairs={{0,6},{1,7},{2,4},{3,5},{4,2},{5,3},{6,0},{7,1},{8,14},{9,15},{10,... | collective-permute-start | bytes 196616 | tf_op jit(solution)/shard_map/ppermute | solution.py:737
  391.9 5.7 %collective-permute-start.116 = (f32[128,128]{1,0:T(8,128)S(1)}, f32[128,128]{1,0:T(8,128)S(1)}, u32[]{:S(2)}, u32[]{:S(2)}) collective-permute-start(f32[128,128]{1,0:T(8,128)S(1)} %reduce_part.5.refs_0_), channel_id=1, source_target_pairs={{0,2},{1,3},{2,0},{3,1},{4,6},{5,7},{6,4},{7,5},{8,10},{9,11},{10,... | collective-permute-start | bytes 196616 | tf_op jit(solution)/shard_map/ppermute | solution.py:737
  391.9 5.7 %collective-permute-start.117 = (f32[128,128]{1,0:T(8,128)S(1)}, f32[128,128]{1,0:T(8,128)S(1)}, u32[]{:S(2)}, u32[]{:S(2)}) collective-permute-start(f32[128,128]{1,0:T(8,128)S(1)} %reduce_part.5.refs_0_), channel_id=1, source_target_pairs={{0,4},{1,5},{2,6},{3,7},{4,0},{5,1},{6,2},{7,3},{8,12},{9,13},{10,... | collective-permute-start | bytes 196616 | tf_op jit(solution)/shard_map/ppermute | solution.py:737
  394.0 6.1 %collective-permute-start.118 = (f32[128,128]{1,0:T(8,128)S(1)}, f32[128,128]{1,0:T(8,128)S(1)}, u32[]{:S(2)}, u32[]{:S(2)}) collective-permute-start(f32[128,128]{1,0:T(8,128)S(1)} %reduce_part.5.refs_0_), channel_id=1, source_target_pairs={{0,6},{1,7},{2,4},{3,5},{4,2},{5,3},{6,0},{7,1},{8,14},{9,15},{10,... | collective-permute-start | bytes 196616 | tf_op jit(solution)/shard_map/ppermute | solution.py:737
  400.6 7.5 %collective-permute-start.119 = (f32[512,128]{1,0:T(8,128)S(1)}, f32[512,128]{1,0:T(8,128)S(1)}, u32[]{:S(2)}, u32[]{:S(2)}) collective-permute-start(f32[512,128]{1,0:T(8,128)S(1)} %gather_part.2.refs_0_), channel_id=1, source_target_pairs={{0,8},{1,9},{2,10},{3,11},{4,12},{5,13},{6,14},{7,15},{8,0},{9,1},... | collective-permute-start | bytes 786440 | tf_op jit(solution)/shard_map/ppermute | solution.py:737
  402.4 10.0 %collective-permute-start.120 = (f32[512,128]{1,0:T(8,128)S(1)}, f32[512,128]{1,0:T(8,128)S(1)}, u32[]{:S(2)}, u32[]{:S(2)}) collective-permute-start(f32[512,128]{1,0:T(8,128)S(1)} %gather_part.2.refs_0_), channel_id=1, source_target_pairs={{0,16},{1,17},{2,18},{3,19},{4,20},{5,21},{6,22},{7,23},{8,24},{9,... | collective-permute-start | bytes 786440 | tf_op jit(solution)/shard_map/ppermute | solution.py:737
  402.7 9.8 %collective-permute-start.121 = (f32[512,128]{1,0:T(8,128)S(1)}, f32[512,128]{1,0:T(8,128)S(1)}, u32[]{:S(2)}, u32[]{:S(2)}) collective-permute-start(f32[512,128]{1,0:T(8,128)S(1)} %gather_part.2.refs_0_), channel_id=1, source_target_pairs={{0,24},{1,25},{2,26},{3,27},{4,28},{5,29},{6,30},{7,31},{8,16},{9,... | collective-permute-start | bytes 786440 | tf_op jit(solution)/shard_map/ppermute | solution.py:737
  413.1 48.2 %collective-permute-start.122 = (f32[2048,128]{1,0:T(8,128)S(1)}, f32[2048,128]{1,0:T(8,128)S(1)}, u32[]{:S(2)}, u32[]{:S(2)}) collective-permute-start(f32[2048,128]{1,0:T(8,128)S(1)} %gather_part.3.refs_0_), channel_id=1, source_target_pairs={{0,1},{1,0},{2,3},{3,2},{4,5},{5,4},{6,7},{7,6},{8,9},{9,8},{10,11... | collective-permute-start | bytes 3145736 | tf_op jit(solution)/shard_map/ppermute | solution.py:737
  421.8 8.2 %collective-permute-start.49 = (f32[24,1024]{1,0:T(8,128)S(1)}, f32[24,1024]{1,0:T(8,128)S(1)}, u32[]{:S(2)}, u32[]{:S(2)}) collective-permute-start(f32[24,1024]{1,0:T(8,128)S(1)} %get-tuple-element.172), channel_id=1, source_target_pairs={{16,20},{17,21},{18,22},{19,23},{20,16},{21,17},{22,18},{23,19},{2... | collective-permute-start | bytes 294920 | tf_op jit(solution)/shard_map/ppermute | solution.py:744
  422.5 19.7 %collective-permute-start.50 = (f32[24,1024]{1,0:T(8,128)S(1)}, f32[24,1024]{1,0:T(8,128)S(1)}, u32[]{:S(2)}, u32[]{:S(2)}) collective-permute-start(f32[24,1024]{1,0:T(8,128)S(1)} %get-tuple-element.173), channel_id=1, source_target_pairs={{0,8},{1,9},{2,10},{3,11},{4,12},{5,13},{6,14},{7,15},{8,16},{9,17... | collective-permute-start | bytes 294920 | tf_op jit(solution)/shard_map/ppermute | solution.py:744
  422.9 21.3 %collective-permute-start.51 = (f32[24,1024]{1,0:T(8,128)S(1)}, f32[24,1024]{1,0:T(8,128)S(1)}, u32[]{:S(2)}, u32[]{:S(2)}) collective-permute-start(f32[24,1024]{1,0:T(8,128)S(1)} %get-tuple-element.174), channel_id=1, source_target_pairs={{0,16},{1,17},{2,18},{3,19},{4,20},{5,21},{6,22},{7,23},{8,24},{9,... | collective-permute-start | bytes 294920 | tf_op jit(solution)/shard_map/ppermute | solution.py:744
  428.0 17.1 %collective-permute-start.52 = (f32[24,1024]{1,0:T(8,128)S(1)}, f32[24,1024]{1,0:T(8,128)S(1)}, u32[]{:S(2)}, u32[]{:S(2)}) collective-permute-start(f32[24,1024]{1,0:T(8,128)S(1)} %get-tuple-element.175), channel_id=1, source_target_pairs={{0,24},{1,25},{2,26},{3,27},{4,28},{5,29},{6,30},{7,31},{8,0},{9,1... | collective-permute-start | bytes 294920 | tf_op jit(solution)/shard_map/ppermute | solution.py:744
  430.0 17.8 %collective-permute-start.105 = (f32[24,1024]{1,0:T(8,128)S(1)}, f32[24,1024]{1,0:T(8,128)S(1)}, u32[]{:S(2)}, u32[]{:S(2)}) collective-permute-start(f32[24,1024]{1,0:T(8,128)S(1)} %get-tuple-element.237), channel_id=1, source_target_pairs={{16,20},{17,21},{18,22},{19,23},{20,16},{21,17},{22,18},{23,19},{2... | collective-permute-start | bytes 294920 | tf_op jit(solution)/shard_map/ppermute | solution.py:744
  442.2 16.7 %collective-permute-start.106 = (f32[24,1024]{1,0:T(8,128)S(1)}, f32[24,1024]{1,0:T(8,128)S(1)}, u32[]{:S(2)}, u32[]{:S(2)}) collective-permute-start(f32[24,1024]{1,0:T(8,128)S(1)} %get-tuple-element.238), channel_id=1, source_target_pairs={{0,8},{1,9},{2,10},{3,11},{4,12},{5,13},{6,14},{7,15},{8,16},{9,17... | collective-permute-start | bytes 294920 | tf_op jit(solution)/shard_map/ppermute | solution.py:744
  444.2 15.7 %collective-permute-start.107 = (f32[24,1024]{1,0:T(8,128)S(1)}, f32[24,1024]{1,0:T(8,128)S(1)}, u32[]{:S(2)}, u32[]{:S(2)}) collective-permute-start(f32[24,1024]{1,0:T(8,128)S(1)} %get-tuple-element.239), channel_id=1, source_target_pairs={{0,16},{1,17},{2,18},{3,19},{4,20},{5,21},{6,22},{7,23},{8,24},{9,... | collective-permute-start | bytes 294920 | tf_op jit(solution)/shard_map/ppermute | solution.py:744
  445.1 14.7 %collective-permute-start.108 = (f32[24,1024]{1,0:T(8,128)S(1)}, f32[24,1024]{1,0:T(8,128)S(1)}, u32[]{:S(2)}, u32[]{:S(2)}) collective-permute-start(f32[24,1024]{1,0:T(8,128)S(1)} %get-tuple-element.240), channel_id=1, source_target_pairs={{0,24},{1,25},{2,26},{3,27},{4,28},{5,29},{6,30},{7,31},{8,0},{9,1... | collective-permute-start | bytes 294920 | tf_op jit(solution)/shard_map/ppermute | solution.py:744
  (96 other events, 572.0 us)

commit v4 on v3

--- a/solution.py
+++ b/solution.py
@@ -12,6 +12,7 @@
 LAT = 16
 ATT_ROWS = 8
 EPSILON = 1e-05
+LOG2_E = 1.0 / math.log(2.0)
 F32 = jnp.float32
 BF16 = jnp.bfloat16
 GROUP = 8
@@ -134,6 +135,14 @@
     return amount - step_size * (along_lon(amount * east, lon) + along_lat(amount * north, lon))
 
 
+def row_products(left_rows, right_rows):
+    left_high, left_low = halves(left_rows)
+    right_high, right_low = halves(right_rows)
+    left = jnp.concatenate([left_high, left_high, left_low, left_low], axis=0)
+    right = jnp.concatenate([right_high, right_low, right_high, right_low], axis=0)
+    return dot(left, right, 0, 0)
+
+
 def attention_scores(key_rows, query_rows):
     key_high, key_mid, key_low = thirds(key_rows)
     query_high, query_mid, query_low = thirds(query_rows)
@@ -144,9 +153,23 @@
     return dot(left, right, 0, 0)
 
 
-def by_halves(left_halves, right):
-    high, low = halves(right)
-    return folded(dot(left_halves, high) + dot(left_halves, low), 0)
+def heads_of(channels, cells, block_size):
+    width = channels // HEADS
+    return [
+        (slice(head * width, (head + 1) * width), slice(start, start + block_size))
+        for start in range(0, cells, block_size)
+        for head in range(HEADS)
+    ]
+
+
+def below(rows, offset):
+    return slice(rows.start + offset, rows.stop + offset)
+
+
+def entered_inlet_kernel(lon, ids_ref, own_ref, arrived_ref, *refs):
+    state_ref = refs[3]
+    state_ref[...] = jnp.where(ids_ref[0] < 2, own_ref[...], arrived_ref[...])
+    inlet_kernel(lon, state_ref, *refs[:3], *refs[4:])
 
 
 def inlet_kernel(
@@ -189,7 +212,7 @@
 def project(w_qkv_ref, act_two, head_width, qkv_ref):
     channels = act_two.shape[0]
     rows = folded(dot(w_qkv_ref[...], stacked(act_two)), 0)
-    qkv_ref[:channels] = rows[:channels] * (1.0 / math.sqrt(head_width))
+    qkv_ref[:channels] = rows[:channels] * (LOG2_E / math.sqrt(head_width))
     qkv_ref[channels:] = rows[channels:]
 
 
@@ -197,31 +220,43 @@
     lon, count, block_size, step_size,
     state_ref, inner_ref, pre_two_ref, sums_two_ref, gain_ref, shift_ref,
     w_qkv_ref, w_mixer_ref, w_velocity_ref, b_velocity_ref,
-    out_ref, qkv_ref, mixed_ref,
+    out_ref, qkv_ref, mixed_ref, weight_ref, powers_ref,
+    slots_ref, done_ref,
 ):
     channels = inner_ref.shape[1]
     cells = inner_ref.shape[0]
-    head_width = channels // HEADS
     act_two = act_two_channels(
         inner_ref[...], pre_two_ref[...], sums_two_ref[...], gain_ref[...], shift_ref[...], count
     )
-    project(w_qkv_ref, act_two, head_width, qkv_ref)
-
-    def one_head(turn, unused):
-        head, block = turn % HEADS, turn // HEADS
-        lanes = pl.ds(pl.multiple_of(block * block_size, block_size), block_size)
-        start = pl.multiple_of(head * head_width, head_width)
-        query = qkv_ref[pl.ds(start, head_width), lanes]
-        key = qkv_ref[pl.ds(start + channels, head_width), lanes]
-        value = qkv_ref[pl.ds(start + 2 * channels, head_width), lanes]
-        scores = attention_scores(key, query)
+    project(w_qkv_ref, act_two, channels // HEADS, qkv_ref)
+    heads = heads_of(channels, cells, block_size)
+
+    def scores_of(turn):
+        rows, lanes = heads[turn]
+        return attention_scores(qkv_ref[below(rows, channels), lanes], qkv_ref[rows, lanes])
+
+    def keep(turn):
+        return pltpu.make_async_copy(
+            slots_ref.at[turn % 2], powers_ref.at[turn], done_ref.at[turn % 2]
+        )
+
+    following = scores_of(0)
+    for turn, (rows, lanes) in enumerate(heads):
+        scores = following
+        if turn + 1 < len(heads):
+            following = scores_of(turn + 1)
         top = jnp.max(scores, axis=0, keepdims=True)
-        powers = jnp.exp(scores - top)
-        total = jnp.sum(powers, axis=0, keepdims=True)
-        mixed_ref[pl.ds(start, head_width), lanes] = by_halves(stacked(value), powers) / total
-        return unused
-
-    lax.fori_loop(0, HEADS * (cells // block_size), one_head, 0)
+        powers = jnp.exp2(scores - top)
+        weight = 1.0 / jnp.sum(powers, axis=0, keepdims=True)
+        weight_ref[turn : turn + 1] = weight
+        high, low = halves(powers)
+        if turn >= 2:
+            keep(turn - 2).wait()
+        slots_ref[turn % 2, 0] = high
+        slots_ref[turn % 2, 1] = low
+        keep(turn).start()
+        value = stacked(qkv_ref[below(rows, 2 * channels), lanes])
+        mixed_ref[rows, lanes] = folded(dot(value, high) + dot(value, low), 0) * weight
     act_three = act_two + folded(dot(w_mixer_ref[...], stacked(mixed_ref[...])), 0)
     parts = folded(dot(w_velocity_ref[...], stacked(act_three)), 0)
     forcing = jnp.zeros((2 * GROUP, cells), F32) + b_velocity_ref[...]
@@ -238,23 +273,34 @@
     flows = state[GROUP:]
     out_ref[:GROUP] = advected(state, step_size, lon)
     out_ref[GROUP:] = flows + step_size * (forcing - flows)
+    for turn in range(max(0, len(heads) - 2), len(heads)):
+        keep(turn).wait()
 
 
 def outlet_back_kernel(
-    lon, count, block_size, step_size, sections,
-    ids_ref, step_ref,
+    lon, count, block_size, step_size, sections, step,
+    ids_ref,
     state_ref, d_next_ref, cots_ref, inner_ref, pre_two_ref, sums_two_ref, gain_ref, shift_ref,
-    w_qkv_ref, w_mixer_ref, w_qkv_back_ref, w_mixer_back_ref, w_velocity_back_ref,
+    qkv_ref, mixed_ref, weight_ref, powers_ref,
+    w_mixer_ref, w_qkv_back_ref, w_mixer_back_ref, w_velocity_back_ref,
     acc_qkv_ref, acc_mixer_ref, acc_velocity_ref, acc_small_ref,
     d_state_ref, d_two_ref, sums_ref,
     out_qkv_ref, out_mixer_ref, out_velocity_ref, out_small_ref,
-    qkv_ref, mixed_ref, d_mixed_ref, d_qkv_ref,
+    d_mixed_ref, d_qkv_ref, slots_ref, done_ref,
 ):
     channels = inner_ref.shape[1]
     cells = inner_ref.shape[0]
-    head_width = channels // HEADS
+    heads = heads_of(channels, cells, block_size)
+
+    def fetch(turn):
+        return pltpu.make_async_copy(
+            powers_ref.at[turn], slots_ref.at[turn % 2], done_ref.at[turn % 2]
+        )
+
+    for turn in range(min(2, len(heads))):
+        fetch(turn).start()
     state = state_ref[...]
-    seed = d_next_ref[...] + cots_ref[lax.rem(ids_ref[0] - step_ref[0] + sections, sections)]
+    seed = d_next_ref[...] + cots_ref[lax.rem(ids_ref[0] - step + sections, sections)]
     amount, east, north = state[:GROUP], state[GROUP : 2 * GROUP], state[2 * GROUP :]
     d_amount = seed[:GROUP]
     d_lon = step_size * along_lon(d_amount, lon)
@@ -265,64 +311,58 @@
     d_forcing = step_size * seed[GROUP:]
     pieces = []
     for lat_offset in (-1, 0, 1):
-        rows = lat_moved(d_forcing, -lat_offset, lon) if lat_offset else d_forcing
+        moved_rows = lat_moved(d_forcing, -lat_offset, lon) if lat_offset else d_forcing
         for lon_offset in (-1, 0, 1):
-            pieces.append(lon_moved(rows, -lon_offset, lon) if lon_offset else rows)
+            pieces.append(lon_moved(moved_rows, -lon_offset, lon) if lon_offset else moved_rows)
     d_parts = stacked(jnp.concatenate(pieces, axis=0))
     d_three = folded(dot(w_velocity_back_ref[...], d_parts), 0)
     d_three_halves = stacked(d_three)
     d_mixed_ref[...] = folded(dot(w_mixer_back_ref[...], d_three_halves), 0)
-    act_two = act_two_channels(
-        inner_ref[...], pre_two_ref[...], sums_two_ref[...], gain_ref[...], shift_ref[...], count
-    )
-    act_two_halves = stacked(act_two)
-    project(w_qkv_ref, act_two, head_width, qkv_ref)
-
-    def one_head(turn, unused):
-        head, block = turn % HEADS, turn // HEADS
-        lanes = pl.ds(pl.multiple_of(block * block_size, block_size), block_size)
-        start = pl.multiple_of(head * head_width, head_width)
-        query = qkv_ref[pl.ds(start, head_width), lanes]
-        key = qkv_ref[pl.ds(start + channels, head_width), lanes]
-        value = qkv_ref[pl.ds(start + 2 * channels, head_width), lanes]
-        scores = attention_scores(key, query)
-        top = jnp.max(scores, axis=0, keepdims=True)
-        powers = jnp.exp(scores - top)
-        weight = 1.0 / jnp.sum(powers, axis=0, keepdims=True)
-        power_high, power_low = halves(powers)
-        value_halves = stacked(value)
-        mixed = folded(dot(value_halves, power_high) + dot(value_halves, power_low), 0) * weight
-        mixed_ref[pl.ds(start, head_width), lanes] = mixed
-        d_mixed = d_mixed_ref[pl.ds(start, head_width), lanes] * weight
-        inner_sum = jnp.sum(d_mixed * mixed, axis=0, keepdims=True)
+
+    def d_powers_of(turn):
+        rows, lanes = heads[turn]
+        d_mixed = d_mixed_ref[rows, lanes] * weight_ref[turn : turn + 1]
+        return d_mixed, row_products(qkv_ref[below(rows, 2 * channels), lanes], d_mixed)
+
+    following = d_powers_of(0)
+    for turn, (rows, lanes) in enumerate(heads):
+        d_mixed, d_powers = following
+        if turn + 1 < len(heads):
+            following = d_powers_of(turn + 1)
+        inner_sum = jnp.sum(d_mixed * mixed_ref[rows, lanes], axis=0, keepdims=True)
+        fetch(turn).wait()
+        power_high, power_low = slots_ref[turn % 2, 0], slots_ref[turn % 2, 1]
+        powers = power_high.astype(F32) + power_low.astype(F32)
+        d_high, d_low = halves(powers * (d_powers - inner_sum))
         d_mixed_cells = beside(d_mixed.T)
         d_value = folded(dot(power_high, d_mixed_cells) + dot(power_low, d_mixed_cells), 1)
-        d_powers = attention_scores(value, d_mixed)
-        d_high, d_low = halves(powers * (d_powers - inner_sum))
-        query_cells = beside(query.T)
+        query_cells = beside(qkv_ref[rows, lanes].T)
         d_key = folded(dot(d_high, query_cells) + dot(d_low, query_cells), 1)
-        key_halves = stacked(key)
+        key_halves = stacked(qkv_ref[below(rows, channels), lanes])
         d_query = folded(dot(key_halves, d_high) + dot(key_halves, d_low), 0)
-        d_qkv_ref[pl.ds(start, head_width), lanes] = d_query * (1.0 / math.sqrt(head_width))
-        d_qkv_ref[pl.ds(start + channels, head_width), lanes] = d_key.T
-        d_qkv_ref[pl.ds(start + 2 * channels, head_width), lanes] = d_value.T
-        return unused
-
-    lax.fori_loop(0, HEADS * (cells // block_size), one_head, 0)
-    mixed_halves = stacked(mixed_ref[...])
-    act_three = act_two + folded(dot(w_mixer_ref[...], mixed_halves), 0)
+        if turn + 2 < len(heads):
+            fetch(turn + 2).start()
+        d_qkv_ref[rows, lanes] = d_query * (1.0 / math.sqrt(channels // HEADS))
+        d_qkv_ref[below(rows, channels), lanes] = d_key.T * (1.0 / LOG2_E)
+        d_qkv_ref[below(rows, 2 * channels), lanes] = d_value.T
     d_qkv_halves = stacked(d_qkv_ref[...])
     d_two = (d_three + folded(dot(w_qkv_back_ref[...], d_qkv_halves), 0)).T
     d_two_ref[...] = d_two
     mean, scale, unused_factor = norm_of(sums_two_ref[...], gain_ref[...], count)
     sums = sums_of(d_two, pre_two_ref[...] - mean)
     sums_ref[...] = sums
+
     def pairs(left, right):
         return folded(folded(dot(left, right, 1, 1), 0), 1)
 
+    act_two = act_two_channels(
+        inner_ref[...], pre_two_ref[...], sums_two_ref[...], gain_ref[...], shift_ref[...], count
+    )
+    mixed_halves = stacked(mixed_ref[...])
+    act_three = act_two + folded(dot(w_mixer_ref[...], mixed_halves), 0)
     out_velocity_ref[...] = acc_velocity_ref[...] + pairs(d_parts, stacked(act_three))
     out_mixer_ref[...] = acc_mixer_ref[...] + pairs(mixed_halves, d_three_halves)
-    out_qkv_ref[...] = acc_qkv_ref[...] + pairs(act_two_halves, d_qkv_halves)
+    out_qkv_ref[...] = acc_qkv_ref[...] + pairs(stacked(act_two), d_qkv_halves)
     bias = jnp.sum(d_forcing, axis=1, keepdims=True)
     row = lax.broadcasted_iota(jnp.int32, (GROUP, channels), 0)
     small = jnp.where(row == 0, sums[1:2] * scale, jnp.where(row == 1, sums[0:1], 0.0))
@@ -419,37 +459,45 @@
     d_state_ref[GROUP:] = d_state[GROUP:]
 
 
-def spread(groups, array, size):
-    pad = jnp.zeros((GROUP - size, array.shape[1]), F32)
-    pieces = []
-    for group in range(groups):
-        pieces += [array[group * size : (group + 1) * size], pad]
-    return jnp.concatenate(pieces, axis=0)
-
-
-def enter_kernel(plan, ids_ref, order_ref, state_ref, cot_ref, *out_refs):
-    section, dp = ids_ref[0], ids_ref[1]
-    size = state_ref.shape[1] // 3
-    out_refs[0][...] = spread(3, state_ref[order_ref[0, plan.slot(section, dp)]], size)
-    for steps, out_ref in enumerate(out_refs[1:]):
-        target = lax.rem(section + steps, plan.sections)
-        out_ref[...] = spread(3, cot_ref[0, order_ref[0, plan.slot(target, dp)]], size)
-
-
-def leave_kernel(plan, ids_ref, values_ref, *out_refs):
+def put_sample(out_ref, from_ref, place):
+    size = from_ref.shape[0] // 3
+    out_ref[...] = jnp.zeros(out_ref.shape, F32)
+    for row in range(from_ref.shape[0]):
+        target = row // size * GROUP + row % size
+        out_ref[target : target + 1] = from_ref[row, pl.ds(place, 1)]
+
+
+def enter_kernel(plan, ids_ref, order_ref, state_ref, out_ref):
+    put_sample(out_ref, state_ref, order_ref[0, plan.slot(ids_ref[0], ids_ref[1])])
+
+
+def seeds_kernel(plan, ids_ref, order_ref, cot_ref, *out_refs):
     for steps, out_ref in enumerate(out_refs):
+        target = lax.rem(ids_ref[0] + steps, plan.sections)
+        put_sample(out_ref, cot_ref, order_ref[0, plan.slot(target, ids_ref[1])])
+
+
+def leave_kernel(plan, ids_ref, *refs):
+    values_ref = refs[-1]
+    for step in range(plan.sections):
+        values_ref[step] = refs[step][...]
+    for steps, out_ref in enumerate(refs[plan.sections : -1]):
         out_ref[...] = values_ref[lax.rem(ids_ref[0] + steps, plan.sections)]
 
 
-def arrive_kernel(plan, ids_ref, order_ref, *refs):
+def arrive_kernel(plan, ids_ref, order_ref, kept_ref, *refs):
     section, dp = ids_ref[0], ids_ref[1]
     out_ref = refs[-1]
-    size = out_ref.shape[2] // 3
+    size = out_ref.shape[0] // 3
     for steps, ref in enumerate(refs[:-1]):
         source = lax.rem(section - steps + plan.sections, plan.sections)
         place = order_ref[0, plan.slot(source, dp)]
-        for group in range(3):
-            out_ref[0, place, group * size : (group + 1) * size] = ref[group * GROUP : group * GROUP + size]
+        value = ref[...]
+        if plan.halved and not steps:
+            value = jnp.where(section < 2, kept_ref[...], value)
+        for row in range(out_ref.shape[0]):
+            start = row // size * GROUP + row % size
+            out_ref[row, pl.ds(place, 1)] = value[start : start + 1]
 
 
 def put_conv_weight(out_ref, taps):
@@ -646,16 +694,19 @@
     bias_ref[...] = take(GROUP)[0:1]
 
 
-def call(kernel, outs, scratch=(), aliases=None, name=None, scalars=0, kinds=None):
+def call(kernel, outs, scratch=(), aliases=None, name=None, scalars=0, kinds=None, far_in=(), far_out=()):
     kinds = kinds or [F32] * len(outs)
 
     def run(*operands):
         places = [pltpu.SMEM] * scalars + [pltpu.VMEM] * (len(operands) - scalars)
+        for place in far_in:
+            places[place] = pl.ANY
+        out_places = [pl.ANY if place in far_out else pltpu.VMEM for place in range(len(outs))]
         return pl.pallas_call(
             kernel,
             out_shape=tuple(jax.ShapeDtypeStruct(shape, kind) for shape, kind in zip(outs, kinds)),
             in_specs=[pl.BlockSpec(memory_space=place) for place in places],
-            out_specs=tuple(pl.BlockSpec(memory_space=pltpu.VMEM) for unused in outs),
+            out_specs=tuple(pl.BlockSpec(memory_space=place) for place in out_places),
             scratch_shapes=scratch,
             input_output_aliases=aliases or {},
             compiler_params=pltpu.CompilerParams(vmem_limit_bytes=VMEM_LIMIT),
@@ -665,6 +716,7 @@
     return run
 
 
+KEPT_STEPS = 4
 VMEM_LIMIT = 24 * 1024 * 1024
 
 
@@ -741,12 +793,7 @@
     going = [(source, target) for source, target in pairs if source != target]
     if not going:
         return value
-    arrived = lax.ppermute(value, ("section", "dp"), going)
-    if len(going) == len(pairs):
-        return arrived
-    stays = jnp.array([source == target for source, target in sorted(pairs)])
-    own = lax.axis_index("section") * lax.axis_size("dp") + lax.axis_index("dp")
-    return jnp.where(stays[own], value, arrived)
+    return lax.ppermute(value, ("section", "dp"), going)
 
 
 def micro_sum(plan, value):
@@ -797,11 +844,10 @@
     narrow = pltpu.VMEM((channels, cells), F32)
     state_shape = (3 * GROUP, cells)
 
-    state, *cots = call(
-        functools.partial(enter_kernel, plan), [state_shape] * (segments + 1), name="enter", scalars=2
-    )(ids, grouping, state_start, cotangent)
-    state = moved(state, plan.to_workers(0))
-    cots = jnp.stack([moved(cot, plan.to_workers(steps)) for steps, cot in enumerate(cots)])
+    (own_state,) = call(functools.partial(enter_kernel, plan), [state_shape], name="enter", scalars=2)(
+        ids, grouping, jnp.swapaxes(state_start, 0, 1)
+    )
+    arrived_state = moved(own_state, plan.to_workers(0))
 
     static_part, moving_cat, moving_back_cat, first_cat = call(
         functools.partial(first_weights_kernel, lon, quantities),
@@ -829,17 +875,24 @@
     middle = call(
         functools.partial(middle_kernel, lon, count), [plane, small], [patches], name="middle"
     )
+    heads = HEADS * (cells // block_size)
+    powers = (heads, 2, block_size, block_size)
+    slots = [pltpu.VMEM((2,) + powers[1:], BF16), pltpu.SemaphoreType.DMA((2,))]
     outlet = call(
         functools.partial(outlet_kernel, lon, count, block_size, step_size),
-        [state_shape], [wide, narrow], name="outlet",
-    )
-    outlet_back = call(
-        functools.partial(outlet_back_kernel, lon, count, block_size, step_size, segments),
-        [state_shape, plane, small, (channels, 3 * channels), (channels, channels),
-         (18 * GROUP, channels), (3 * GROUP, channels)],
-        [wide, narrow, narrow, wide],
-        {15: 3, 16: 4, 17: 5, 18: 6}, name="outlet_back", scalars=2,
-    )
+        [state_shape, (3 * channels, cells), (channels, cells), (heads, block_size), powers],
+        slots, name="outlet", kinds=[F32] * 4 + [BF16], far_out=[4],
+    )
+
+    def outlet_back(step):
+        return call(
+            functools.partial(outlet_back_kernel, lon, count, block_size, step_size, segments, step),
+            [state_shape, plane, small, (channels, 3 * channels), (channels, channels),
+             (18 * GROUP, channels), (3 * GROUP, channels)],
+            [narrow, wide] + slots,
+            {17: 3, 18: 4, 19: 5, 20: 6}, name="outlet_back", scalars=1, far_in=[12],
+        )
+
     middle_back = call(
         functools.partial(middle_back_kernel, lon, count),
         [plane, small, (9, channels, channels), small], [patches],
@@ -851,57 +904,52 @@
         {11: 1, 12: 2, 13: 3}, name="inlet_back",
     )
 
-    def forward(state_in, unused):
-        inner, pre_one, sums_one = inlet(state_in, static_part, moving_cat, first_cat)
+    state = own_state
+    path, saved = [], []
+    cots = None
+    for step in range(segments):
+        if plan.halved and not step:
+            state, inner, pre_one, sums_one = call(
+                functools.partial(entered_inlet_kernel, lon), [state_shape, plane, plane, small], [patches],
+                name="inlet", scalars=1,
+            )(ids, own_state, arrived_state, static_part, moving_cat, first_cat)
+        else:
+            inner, pre_one, sums_one = inlet(state, static_part, moving_cat, first_cat)
         sums_one = micro_sum(plan, sums_one)
         pre_two, sums_two = middle(pre_one, sums_one, gain_one, shift_one, second_cat)
         sums_two = micro_sum(plan, sums_two)
-        (state_out,) = outlet(
-            state_in, inner, pre_two, sums_two, gain_two, shift_two, qkv_cat, mixer_cat, out_cat, b_out
+        state_out, qkv, mixed, weight, powers_kept = outlet(
+            state, inner, pre_two, sums_two, gain_two, shift_two, qkv_cat, mixer_cat, out_cat, b_out
         )
-        return state_out, (state_in, state_out, inner, pre_one, pre_two, sums_one, sums_two)
-
-    unused_last, (entered, path, inners, pres_one, pres_two, all_sums_one, all_sums_two) = lax.scan(
-        forward, state, None, length=segments, unroll=min(4, segments)
-    )
-
-    def to_steps(values):
+        kept = (qkv, mixed, weight, powers_kept) if step >= segments - KEPT_STEPS else None
+        saved.append((state, inner, pre_one, pre_two, sums_one, sums_two, kept))
+        path.append(state_out)
+        state = state_out
+        if not step:
+            state, cot_local = lax.optimization_barrier((state, cotangent))
+            sent = call(
+                functools.partial(seeds_kernel, plan), [state_shape] * segments, name="seeds", scalars=2
+            )(ids, grouping, jnp.swapaxes(cot_local[0], 0, 1))
+            cots = [moved(cot, plan.to_workers(steps)) for steps, cot in enumerate(sent)]
+            if plan.halved:
+                cots[0] = jnp.where(lax.axis_index("section") < 2, sent[0], cots[0])
+    cots = jnp.stack(cots)
+
+    def sent_home(values):
         parts = call(
-            functools.partial(leave_kernel, plan), [state_shape] * segments, name="leave", scalars=1
-        )(ids, values)
-        parts = [moved(part, plan.to_homes(steps)) for steps, part in enumerate(parts)]
+            functools.partial(leave_kernel, plan), [state_shape] * segments,
+            [pltpu.VMEM((segments,) + state_shape, F32)], name="leave", scalars=1,
+        )(ids, *values)
+        return [parts[0]] + [moved(part, plan.to_homes(steps)) for steps, part in enumerate(parts)]
+
+    def put_home(parts):
+        rows, samples = state_start.shape[1], state_start.shape[0]
         (out,) = call(
-            functools.partial(arrive_kernel, plan), [(1,) + state_start.shape], name="arrive", scalars=2
+            functools.partial(arrive_kernel, plan), [(rows, samples, cells)], name="arrive", scalars=2
         )(ids, grouping, *parts)
-        return out
-
-    path_out = to_steps(path)
-
-    def backward(carry, saved):
-        d_state, acc = carry
-        step, state_in, inner, pre_one, pre_two, sums_one, sums_two = saved
-        d_partial, d_two, grad_two, qkv, mixer, velocity, small_two = outlet_back(
-            ids, step, state_in, d_state, cots, inner, pre_two, sums_two, gain_two, shift_two,
-            qkv_cat, mixer_cat, qkv_back_cat, mixer_back_cat, out_back_cat,
-            acc["qkv"], acc["mixer"], acc["velocity"], acc["small_two"],
-        )
-        grad_two = micro_sum(plan, grad_two)
-        d_normed, grad_one, second, small_one = middle_back(
-            d_two, pre_two, sums_two, grad_two, gain_two,
-            pre_one, sums_one, gain_one, shift_one, second_back_cat,
-            acc["second"], acc["small_one"],
-        )
-        grad_one = micro_sum(plan, grad_one)
-        d_state, first, moving, inner_sum = inlet_back(
-            state_in, d_normed, pre_one, sums_one, grad_one, gain_one,
-            inner, d_two, d_partial, first_back_cat, moving_back_cat,
-            acc["first"], acc["moving"], acc["inner"],
-        )
-        acc = dict(
-            qkv=qkv, mixer=mixer, velocity=velocity, small_two=small_two, second=second,
-            small_one=small_one, first=first, moving=moving, inner=inner_sum,
-        )
-        return (d_state, acc), d_state
+        return jnp.swapaxes(out, 0, 1)[None]
+
+    path_parts = sent_home(path)
 
     acc = dict(
         qkv=jnp.zeros((channels, 3 * channels), F32),
@@ -914,15 +962,41 @@
         moving=jnp.zeros((3, channels, channels), F32),
         inner=jnp.zeros(plane, F32),
     )
-    steps = jnp.arange(segments, dtype=jnp.int32)[:, None]
-    (unused_start, acc), grads = lax.scan(
-        backward,
-        (jnp.zeros(state_shape, F32), acc),
-        (steps, entered, inners, pres_one, pres_two, all_sums_one, all_sums_two),
-        reverse=True,
-        unroll=min(4, segments),
-    )
-    grads_out = to_steps(grads)
+    d_state = jnp.zeros(state_shape, F32)
+    grads = [None] * segments
+    path_out = None
+    for step in reversed(range(segments)):
+        state, inner, pre_one, pre_two, sums_one, sums_two, kept = saved[step]
+        if kept is None:
+            state, d_state = lax.optimization_barrier((state, d_state))
+            kept = outlet(
+                state, inner, pre_two, sums_two, gain_two, shift_two, qkv_cat, mixer_cat, out_cat, b_out
+            )[1:]
+        qkv, mixed, weight, powers_kept = kept
+        d_partial, d_two, grad_two, acc["qkv"], acc["mixer"], acc["velocity"], acc["small_two"] = outlet_back(step)(
+            ids, state, d_state, cots, inner, pre_two, sums_two, gain_two, shift_two,
+            qkv, mixed, weight, powers_kept,
+            mixer_cat, qkv_back_cat, mixer_back_cat, out_back_cat,
+            acc["qkv"], acc["mixer"], acc["velocity"], acc["small_two"],
+        )
+        grad_two = micro_sum(plan, grad_two)
+        d_normed, grad_one, acc["second"], acc["small_one"] = middle_back(
+            d_two, pre_two, sums_two, grad_two, gain_two,
+            pre_one, sums_one, gain_one, shift_one, second_back_cat,
+            acc["second"], acc["small_one"],
+        )
+        grad_one = micro_sum(plan, grad_one)
+        d_state, acc["first"], acc["moving"], acc["inner"] = inlet_back(
+            state, d_normed, pre_one, sums_one, grad_one, gain_one,
+            inner, d_two, d_partial, first_back_cat, moving_back_cat,
+            acc["first"], acc["moving"], acc["inner"],
+        )
+        grads[step] = d_state
+        if path_out is None:
+            d_state, *path_parts = lax.optimization_barrier((d_state, *path_parts))
+            path_out = put_home(path_parts)
+            d_state, path_out = lax.optimization_barrier((d_state, path_out))
+    grad_parts = sent_home(grads)
 
     rounds = plan.all_rounds
     rows = 2 * 9 * channels + 9 * (statics + -statics % GROUP) + 45 * GROUP + 4 * channels + 23 * GROUP
@@ -942,8 +1016,12 @@
         ids, static_maps, acc["inner"], acc["first"], acc["second"], acc["moving"], acc["qkv"], acc["mixer"],
         acc["velocity"], acc["small_one"], acc["small_two"],
     )
+    grads_out = None
     for bits, later in zip(rounds, rounds[1:] + [[]]):
         parts = swap(parts, bits)
+        if grads_out is None:
+            parts, grad_parts = lax.optimization_barrier((parts, grad_parts))
+            grads_out = put_home(grad_parts)
         rows >>= len(bits)
         parts = call(
             functools.partial(reduce_kernel, plan, later, len(parts)), shares(rows, later),

time: 471 us -> 462 us (0.981)
  Pallas kernels: 177 us -> 158 us
  local copies, waits for them, and re-layouts: 17.3 us -> 32.7 us
  waiting for transfers between devices: 131 us -> 125 us
    pallas_call x40 -> x41, Pallas kernels: 177 us -> 158 us  [run(): pl.pallas_call(kernel, out_shape=tuple((jax.ShapeDtypeStruct(shape, kind)...]
    unnamed x78 -> x190, local copies, waits for them, and re-layouts: 13.5 us -> 31.6 us
    ppermute x13, starting transfers between devices: 18.2 us -> 23.1 us  [moved(): return lax.ppermute(value, ('section', 'dp'), going)]
  transfers between devices with their start and end apart: 123 -> 123, of which waited for: 86 -> 78; matrix products, arithmetic and copies ran while one was open for 1% -> 0% of each run, Pallas kernels for 3% -> 4%
where the time goes in v4:
time: 462 us; the launch traced here: 456 us
  Pallas kernels  158 us (34%)
  starting transfers between devices  138 us (30%)
  waiting for transfers between devices  125 us (27%)
  local copies, waits for them, and re-layouts  32.7 us (7%)
    pallas_call x41, Pallas kernels, run(): pl.pallas_call(kernel, out_shape=tuple((jax.ShapeDtypeStruct(shape, kind)...  158 us
    ppermute x110, starting transfers between devices, exchanged(): lax.ppermute(value, ('section', 'dp'), [(own, own ^ mask) for own in rang...  115 us
    ppermute x110, waiting for transfers between devices, exchanged(): lax.ppermute(value, ('section', 'dp'), [(own, own ^ mask) for own in rang...  104 us
    unnamed x190, local copies, waits for them, and re-layouts  31.6 us
    ppermute x13, starting transfers between devices, moved(): return lax.ppermute(value, ('section', 'dp'), going)  23.1 us
    ppermute x13, waiting for transfers between devices, moved(): return lax.ppermute(value, ('section', 'dp'), going)  20.7 us
  transfers between devices with their start and end apart: 123, of which 78 were waited for; matrix products, arithmetic and copies ran while one was open for 0% of the time, Pallas kernels for 4%

profile of v4, /device:TPU:0, one launch (start us, length us, event | category | flops | bytes accessed | tf_op | source)
XLA Modules:
  0.0 455.6 jit_solution(4455784273194539131)
XLA Ops:
  8.9 3.7 inlet.4
  12.7 2.5 collective-permute-start.3
  16.7 2.8 collective-permute-done.2
  19.5 6.3 %collective-permute-start.6 = (f32[8,128]{1,0:T(8,128)S(1)}, f32[8,128]{1,0:T(8,128)S(1)}, u32[]{:S(2)}, u32[]{:S(2)}) collective-permute-start(f32[8,128]{1,0:T(8,128)S(1)} %add_add_fusion.31), channel_id=1, source_target_pairs={{0,24},{1,25},{2,26},{3,27},{4,28},{5,29},{6,30},{7,31},{8,16},{9,... | collective-permute-start | bytes 12296 | tf_op jit(solution)/shard_map/ppermute | solution.py:789
  27.4 2.0 collective-permute-done.4
  47.8 8.3 %outlet.4 = (f32[24,1024]{1,0:T(8,128)S(1)}, f32[384,1024]{1,0:T(8,128)S(1)}, f32[128,1024]{1,0:T(8,128)S(1)}, f32[8,512]{1,0:T(8,128)S(1)}, bf16[8,2,512,512]{3,2,1,0:T(8,128)(2,1)S(1)}) custom-call(f32[24,1024]{1,0:T(8,128)S(1)} %copy-done.56, f32[1024,128]{1,0:T(8,128)S(1)} %copy-done.17, f32[1024,128]{1,0:T(8,128)S(1)} %copy-done.10, ...), custom_call_target="tpu_custom_call" | custom-call | tf_op jit(solution)/shard_map/outlet/pallas_call | solution.py:705
  56.2 3.3 copy-done
  61.8 3.1 inlet.5
  68.1 2.3 collective-permute-done.14
  81.4 2.8 collective-permute-start.24
  88.4 8.5 %outlet.5 = (f32[24,1024]{1,0:T(8,128)S(1)}, f32[384,1024]{1,0:T(8,128)S(1)}, f32[128,1024]{1,0:T(8,128)S(1)}, f32[8,512]{1,0:T(8,128)S(1)}, bf16[8,2,512,512]{3,2,1,0:T(8,128)(2,1)S(1)}) custom-call(f32[24,1024]{1,0:T(8,128)S(1)} %get-tuple-element.195.state_ref.refs_0_, f32[1024,128]{1,0:T(8,128)S(1)} %get-tuple-element.196.inner_ref, ...), custom_call_target="tpu_custom_call" | custom-call | tf_op jit(solution)/shard_map/outlet/pallas_call | solution.py:705
  97.0 3.2 copy-done.1
  101.3 3.1 inlet.6
  107.5 2.3 collective-permute-done.26
  120.9 2.8 collective-permute-start.36
  127.9 8.3 %outlet.6 = (f32[24,1024]{1,0:T(8,128)S(1)}, f32[384,1024]{1,0:T(8,128)S(1)}, f32[128,1024]{1,0:T(8,128)S(1)}, f32[8,512]{1,0:T(8,128)S(1)}, bf16[8,2,512,512]{3,2,1,0:T(8,128)(2,1)S(1)}) custom-call(f32[24,1024]{1,0:T(8,128)S(1)} %get-tuple-element.201.state_ref.refs_1_, f32[1024,128]{1,0:T(8,128)S(1)} %get-tuple-element.202.inner_ref, ...), custom_call_target="tpu_custom_call" | custom-call | tf_op jit(solution)/shard_map/outlet/pallas_call | solution.py:705
  136.2 3.3 copy-done.2
  140.6 3.1 inlet.7
  147.7 2.3 collective-permute-done.42
  161.1 2.8 collective-permute-start.52
  166.1 4.0 collective-permute-start.40
  174.5 8.3 %outlet.7 = (f32[24,1024]{1,0:T(8,128)S(1)}, f32[384,1024]{1,0:T(8,128)S(1)}, f32[128,1024]{1,0:T(8,128)S(1)}, f32[8,512]{1,0:T(8,128)S(1)}, bf16[8,2,512,512]{3,2,1,0:T(8,128)(2,1)S(1)}) custom-call(f32[24,1024]{1,0:T(8,128)S(1)} %copy-done.38, f32[1024,128]{1,0:T(8,128)S(1)} %copy-done.24, f32[1024,128]{1,0:T(8,128)S(1)} %get-tuple-element.216.pre_two_ref, ...), custom_call_target="tpu_custom_call" | custom-call | tf_op jit(solution)/shard_map/outlet/pallas_call | solution.py:705
  183.0 15.2 %outlet_back.4 = (f32[24,1024]{1,0:T(8,128)S(1)}, f32[1024,128]{1,0:T(8,128)S(1)}, f32[8,128]{1,0:T(8,128)S(1)}, f32[128,384]{1,0:T(8,128)S(1)}, f32[128,128]{1,...) custom-call(s32[2]{0:T(128)S(1)} %pad_add_fusion.ids_ref, ...), custom_call_target="tpu_custom_call", output_to_operand_aliasing={{3}: (17, {}), {4}: (18, {}), {5}: (19, {}), {6}: (20, {})} | custom-call | tf_op jit(solution)/shard_map/outlet_back/pallas_call | solution.py:705
  201.3 2.3 collective-permute-done.54
  203.6 3.6 collective-permute-start.58
  208.8 2.0 collective-permute-done.56
  212.1 3.0 middle_back.4
  220.5 2.0 collective-permute-start.63
  225.1 3.8 collective-permute-start.67
  230.7 4.3 inlet_back.4
  235.0 5.7 %collective-permute-done.66.refs_1_ = f32[24,1024]{1,0:T(8,128)S(1)} collective-permute-done((f32[24,1024]{1,0:T(8,128)S(1)}, f32[24,1024]{1,0:T(8,128)S(1)}, u32[]{:S(2)}, u32[]{:S(2)}) %collective-permute-start.66) | collective-permute-done | bytes 98336 | tf_op jit(solution)/shard_map/ppermute | solution.py:796
  244.0 15.0 %outlet_back.5 = (f32[24,1024]{1,0:T(8,128)S(1)}, f32[1024,128]{1,0:T(8,128)S(1)}, f32[8,128]{1,0:T(8,128)S(1)}, f32[128,384]{1,0:T(8,128)S(1)}, f32[128,128]{1,...) custom-call(s32[2]{0:T(128)S(1)} %pad_add_fusion.ids_ref, ...), custom_call_target="tpu_custom_call", output_to_operand_aliasing={{3}: (17, {}), {4}: (18, {}), {5}: (19, {}), {6}: (20, {})} | custom-call | tf_op jit(solution)/shard_map/outlet_back/pallas_call | solution.py:705
  259.2 2.0 collective-permute-start.70
  269.8 3.0 middle_back.5
  273.0 2.1 collective-permute-start.75
  276.0 2.7 collective-permute-done.76
  278.7 2.1 collective-permute-start.80
  284.4 4.3 inlet_back.5
  288.8 15.4 %outlet_back.6 = (f32[24,1024]{1,0:T(8,128)S(1)}, f32[1024,128]{1,0:T(8,128)S(1)}, f32[8,128]{1,0:T(8,128)S(1)}, f32[128,384]{1,0:T(8,128)S(1)}, f32[128,128]{1,...) custom-call(s32[2]{0:T(128)S(1)} %pad_add_fusion.ids_ref, ...), custom_call_target="tpu_custom_call", output_to_operand_aliasing={{3}: (17, {}), {4}: (18, {}), {5}: (19, {}), {6}: (20, {})} | custom-call | tf_op jit(solution)/shard_map/outlet_back/pallas_call | solution.py:705
  314.5 3.0 middle_back.6
  317.7 2.1 collective-permute-start.87
  320.7 2.7 collective-permute-done.88
  323.4 2.1 collective-permute-start.92
  329.2 4.3 inlet_back.6
  333.6 15.3 %outlet_back.7 = (f32[24,1024]{1,0:T(8,128)S(1)}, f32[1024,128]{1,0:T(8,128)S(1)}, f32[8,128]{1,0:T(8,128)S(1)}, f32[128,384]{1,0:T(8,128)S(1)}, f32[128,128]{1,...) custom-call(s32[2]{0:T(128)S(1)} %pad_add_fusion.ids_ref, ...), custom_call_target="tpu_custom_call", output_to_operand_aliasing={{3}: (17, {}), {4}: (18, {}), {5}: (19, {}), {6}: (20, {})} | custom-call | tf_op jit(solution)/shard_map/outlet_back/pallas_call | solution.py:705
  359.1 3.0 middle_back.7
  362.3 2.1 collective-permute-start.99
  365.3 2.7 collective-permute-done.100
  367.9 2.1 collective-permute-start.104
  373.7 4.3 inlet_back.7
  381.4 2.1 collective-permute-start.107
  383.5 3.6 collective-permute-start.108
  387.1 2.3 collective-permute-start.109
  389.3 11.2 %collective-permute-done.107.refs_1_ = f32[24,1024]{1,0:T(8,128)S(1)} collective-permute-done((f32[24,1024]{1,0:T(8,128)S(1)}, f32[24,1024]{1,0:T(8,128)S(1)}, u32[]{:S(2)}, u32[]{:S(2)}) %collective-permute-start.107) | collective-permute-done | bytes 98336 | tf_op jit(solution)/shard_map/ppermute | solution.py:796
  403.2 3.3 collective-permute-start.110
  408.1 5.6 %collective-permute-done.110.refs_1_ = f32[512,128]{1,0:T(8,128)S(1)} collective-permute-done((f32[512,128]{1,0:T(8,128)S(1)}, f32[512,128]{1,0:T(8,128)S(1)}, u32[]{:S(2)}, u32[]{:S(2)}) %collective-permute-start.110) | collective-permute-done | bytes 262176 | tf_op jit(solution)/shard_map/ppermute | solution.py:789
  413.7 6.1 %collective-permute-done.111.refs_2_ = f32[512,128]{1,0:T(8,128)S(1)} collective-permute-done((f32[512,128]{1,0:T(8,128)S(1)}, f32[512,128]{1,0:T(8,128)S(1)}, u32[]{:S(2)}, u32[]{:S(2)}) %collective-permute-start.111) | collective-permute-done | bytes 262176 | tf_op jit(solution)/shard_map/ppermute | solution.py:789
  420.5 3.3 collective-permute-start.114
  424.9 2.5 collective-permute-done.114.refs_2_
  427.4 2.9 collective-permute-done.115.refs_3_
  432.2 3.2 collective-permute-start.118
  436.2 2.1 collective-permute-done.118.refs_3_
  442.4 3.3 collective-permute-done.119.refs_1_
  445.7 3.3 collective-permute-done.120.refs_2_
  (467 shorter events, 176.6 us)
Async XLA Ops:
  2.9 6.0 %collective-permute-start = (f32[24,1024]{1,0:T(8,128)S(1)}, f32[24,1024]{1,0:T(8,128)S(1)}, u32[]{:S(2)}, u32[]{:S(2)}) collective-permute-start(f32[24,1024]{1,0:T(8,128)S(1)} %enter.1.own_ref), channel_id=1, source_target_pairs={{16,20},{17,21},{18,22},{19,23},{20,16},{21,17},{22,18},{23,19},{2... | collective-permute-start | bytes 294920 | tf_op jit(solution)/shard_map/ppermute | solution.py:796
  12.7 3.8 collective-permute-start.3
  15.9 3.6 collective-permute-start.2
  19.5 7.9 %collective-permute-start.6 = (f32[8,128]{1,0:T(8,128)S(1)}, f32[8,128]{1,0:T(8,128)S(1)}, u32[]{:S(2)}, u32[]{:S(2)}) collective-permute-start(f32[8,128]{1,0:T(8,128)S(1)} %add_add_fusion.31), channel_id=1, source_target_pairs={{0,24},{1,25},{2,26},{3,27},{4,28},{5,29},{6,30},{7,31},{8,16},{9,... | collective-permute-start | bytes 12296 | tf_op jit(solution)/shard_map/ppermute | solution.py:789
  36.6 8.0 %collective-permute-start.12 = (f32[8,128]{1,0:T(8,128)S(1)}, f32[8,128]{1,0:T(8,128)S(1)}, u32[]{:S(2)}, u32[]{:S(2)}) collective-permute-start(f32[8,128]{1,0:T(8,128)S(1)} %add_add_fusion.29), channel_id=1, source_target_pairs={{0,24},{1,25},{2,26},{3,27},{4,28},{5,29},{6,30},{7,31},{8,16},{9,... | collective-permute-start | bytes 12296 | tf_op jit(solution)/shard_map/ppermute | solution.py:789
  37.5 7.1 %collective-permute-start.10 = (f32[8,128]{1,0:T(8,128)S(1)}, f32[8,128]{1,0:T(8,128)S(1)}, u32[]{:S(2)}, u32[]{:S(2)}) collective-permute-start(f32[8,128]{1,0:T(8,128)S(1)} %add_add_fusion.29), channel_id=1, source_target_pairs={{0,8},{1,9},{2,10},{3,11},{4,12},{5,13},{6,14},{7,15},{8,0},{9,1},... | collective-permute-start | bytes 12296 | tf_op jit(solution)/shard_map/ppermute | solution.py:789
  38.2 6.4 %collective-permute-start.11 = (f32[8,128]{1,0:T(8,128)S(1)}, f32[8,128]{1,0:T(8,128)S(1)}, u32[]{:S(2)}, u32[]{:S(2)}) collective-permute-start(f32[8,128]{1,0:T(8,128)S(1)} %add_add_fusion.29), channel_id=1, source_target_pairs={{0,16},{1,17},{2,18},{3,19},{4,20},{5,21},{6,22},{7,23},{8,24},{9,... | collective-permute-start | bytes 12296 | tf_op jit(solution)/shard_map/ppermute | solution.py:789
  66.7 3.6 collective-permute-start.14
  70.4 4.5 collective-permute-start.18
  77.8 3.6 collective-permute-start.20
  81.4 4.5 collective-permute-start.24
  84.8 3.6 collective-permute-start.23
  106.2 3.6 collective-permute-start.26
  109.8 4.5 collective-permute-start.30
  111.4 3.6 collective-permute-start.29
  117.3 3.6 collective-permute-start.32
  120.9 4.5 collective-permute-start.36
  123.7 3.6 collective-permute-start.34
  124.3 3.6 collective-permute-start.35
  150.0 4.5 collective-permute-start.46
  151.6 3.6 collective-permute-start.45
  161.1 9.1 %collective-permute-start.52 = (f32[8,128]{1,0:T(8,128)S(1)}, f32[8,128]{1,0:T(8,128)S(1)}, u32[]{:S(2)}, u32[]{:S(2)}) collective-permute-start(f32[8,128]{1,0:T(8,128)S(1)} %add_add_fusion.17), channel_id=1, source_target_pairs={{0,24},{1,25},{2,26},{3,27},{4,28},{5,29},{6,30},{7,31},{8,16},{9,... | collective-permute-start | bytes 12296 | tf_op jit(solution)/shard_map/ppermute | solution.py:789
  163.9 8.0 %collective-permute-start.50 = (f32[8,128]{1,0:T(8,128)S(1)}, f32[8,128]{1,0:T(8,128)S(1)}, u32[]{:S(2)}, u32[]{:S(2)}) collective-permute-start(f32[8,128]{1,0:T(8,128)S(1)} %add_add_fusion.17), channel_id=1, source_target_pairs={{0,8},{1,9},{2,10},{3,11},{4,12},{5,13},{6,14},{7,15},{8,0},{9,1},... | collective-permute-start | bytes 12296 | tf_op jit(solution)/shard_map/ppermute | solution.py:789
  164.4 8.2 %collective-permute-start.51 = (f32[8,128]{1,0:T(8,128)S(1)}, f32[8,128]{1,0:T(8,128)S(1)}, u32[]{:S(2)}, u32[]{:S(2)}) collective-permute-start(f32[8,128]{1,0:T(8,128)S(1)} %add_add_fusion.17), channel_id=1, source_target_pairs={{0,16},{1,17},{2,18},{3,19},{4,20},{5,21},{6,22},{7,23},{8,24},{9,... | collective-permute-start | bytes 12296 | tf_op jit(solution)/shard_map/ppermute | solution.py:789
  166.1 16.7 %collective-permute-start.40 = (f32[24,1024]{1,0:T(8,128)S(1)}, f32[24,1024]{1,0:T(8,128)S(1)}, u32[]{:S(2)}, u32[]{:S(2)}) collective-permute-start(f32[24,1024]{1,0:T(8,128)S(1)} %get-tuple-element.212), channel_id=1, source_target_pairs={{0,28},{1,29},{2,30},{3,31},{4,24},{5,25},{6,26},{7,27},{8,0},{9,1... | collective-permute-start | bytes 294920 | tf_op jit(solution)/shard_map/ppermute | solution.py:796
  170.1 12.7 %collective-permute-start.39 = (f32[24,1024]{1,0:T(8,128)S(1)}, f32[24,1024]{1,0:T(8,128)S(1)}, u32[]{:S(2)}, u32[]{:S(2)}) collective-permute-start(f32[24,1024]{1,0:T(8,128)S(1)} %get-tuple-element.211), channel_id=1, source_target_pairs={{0,20},{1,21},{2,22},{3,23},{4,16},{5,17},{6,18},{7,19},{8,28},{9,... | collective-permute-start | bytes 294920 | tf_op jit(solution)/shard_map/ppermute | solution.py:796
  170.1 12.7 %collective-permute-start.38 = (f32[24,1024]{1,0:T(8,128)S(1)}, f32[24,1024]{1,0:T(8,128)S(1)}, u32[]{:S(2)}, u32[]{:S(2)}) collective-permute-start(f32[24,1024]{1,0:T(8,128)S(1)} %get-tuple-element.210), channel_id=1, source_target_pairs={{0,8},{1,9},{2,10},{3,11},{4,12},{5,13},{6,14},{7,15},{8,20},{9,21... | collective-permute-start | bytes 294920 | tf_op jit(solution)/shard_map/ppermute | solution.py:796
  171.9 10.8 %collective-permute-start.37 = (f32[24,1024]{1,0:T(8,128)S(1)}, f32[24,1024]{1,0:T(8,128)S(1)}, u32[]{:S(2)}, u32[]{:S(2)}) collective-permute-start(f32[24,1024]{1,0:T(8,128)S(1)} %get-tuple-element.209), channel_id=1, source_target_pairs={{16,20},{17,21},{18,22},{19,23},{20,16},{21,17},{22,18},{23,19},{2... | collective-permute-start | bytes 294920 | tf_op jit(solution)/shard_map/ppermute | solution.py:796
  203.6 5.2 %collective-permute-start.58 = (f32[8,128]{1,0:T(8,128)S(1)}, f32[8,128]{1,0:T(8,128)S(1)}, u32[]{:S(2)}, u32[]{:S(2)}) collective-permute-start(f32[8,128]{1,0:T(8,128)S(1)} %add_add_fusion.15), channel_id=1, source_target_pairs={{0,24},{1,25},{2,26},{3,27},{4,28},{5,29},{6,30},{7,31},{8,16},{9,... | collective-permute-start | bytes 12296 | tf_op jit(solution)/shard_map/ppermute | solution.py:789
  208.4 3.6 collective-permute-start.57
  219.0 6.1 %collective-permute-start.64 = (f32[8,128]{1,0:T(8,128)S(1)}, f32[8,128]{1,0:T(8,128)S(1)}, u32[]{:S(2)}, u32[]{:S(2)}) collective-permute-start(f32[8,128]{1,0:T(8,128)S(1)} %add_add_fusion.13), channel_id=1, source_target_pairs={{0,24},{1,25},{2,26},{3,27},{4,28},{5,29},{6,30},{7,31},{8,16},{9,... | collective-permute-start | bytes 12296 | tf_op jit(solution)/shard_map/ppermute | solution.py:789
  220.0 9.0 %collective-permute-start.62 = (f32[8,128]{1,0:T(8,128)S(1)}, f32[8,128]{1,0:T(8,128)S(1)}, u32[]{:S(2)}, u32[]{:S(2)}) collective-permute-start(f32[8,128]{1,0:T(8,128)S(1)} %add_add_fusion.13), channel_id=1, source_target_pairs={{0,8},{1,9},{2,10},{3,11},{4,12},{5,13},{6,14},{7,15},{8,0},{9,1},... | collective-permute-start | bytes 12296 | tf_op jit(solution)/shard_map/ppermute | solution.py:789
  220.5 10.0 %collective-permute-start.63 = (f32[8,128]{1,0:T(8,128)S(1)}, f32[8,128]{1,0:T(8,128)S(1)}, u32[]{:S(2)}, u32[]{:S(2)}) collective-permute-start(f32[8,128]{1,0:T(8,128)S(1)} %add_add_fusion.13), channel_id=1, source_target_pairs={{0,16},{1,17},{2,18},{3,19},{4,20},{5,21},{6,22},{7,23},{8,24},{9,... | collective-permute-start | bytes 12296 | tf_op jit(solution)/shard_map/ppermute | solution.py:789
  223.1 11.9 %collective-permute-start.65 = (f32[24,1024]{1,0:T(8,128)S(1)}, f32[24,1024]{1,0:T(8,128)S(1)}, u32[]{:S(2)}, u32[]{:S(2)}) collective-permute-start(f32[24,1024]{1,0:T(8,128)S(1)} %get-tuple-element.240.kept_ref), channel_id=1, source_target_pairs={{16,20},{17,21},{18,22},{19,23},{20,16},{21,17},{22,18},{23,19},{2... | collective-permute-start | bytes 294920 | tf_op jit(solution)/shard_map/ppermute | solution.py:796
  223.8 17.0 %collective-permute-start.66 = (f32[24,1024]{1,0:T(8,128)S(1)}, f32[24,1024]{1,0:T(8,128)S(1)}, u32[]{:S(2)}, u32[]{:S(2)}) collective-permute-start(f32[24,1024]{1,0:T(8,128)S(1)} %get-tuple-element.236), channel_id=1, source_target_pairs={{0,8},{1,9},{2,10},{3,11},{4,12},{5,13},{6,14},{7,15},{8,16},{9,17... | collective-permute-start | bytes 294920 | tf_op jit(solution)/shard_map/ppermute | solution.py:796
  225.1 17.4 %collective-permute-start.67 = (f32[24,1024]{1,0:T(8,128)S(1)}, f32[24,1024]{1,0:T(8,128)S(1)}, u32[]{:S(2)}, u32[]{:S(2)}) collective-permute-start(f32[24,1024]{1,0:T(8,128)S(1)} %get-tuple-element.237), channel_id=1, source_target_pairs={{0,16},{1,17},{2,18},{3,19},{4,20},{5,21},{6,22},{7,23},{8,24},{9,... | collective-permute-start | bytes 294920 | tf_op jit(solution)/shard_map/ppermute | solution.py:796
  229.0 13.6 %collective-permute-start.68 = (f32[24,1024]{1,0:T(8,128)S(1)}, f32[24,1024]{1,0:T(8,128)S(1)}, u32[]{:S(2)}, u32[]{:S(2)}) collective-permute-start(f32[24,1024]{1,0:T(8,128)S(1)} %get-tuple-element.238), channel_id=1, source_target_pairs={{0,24},{1,25},{2,26},{3,27},{4,28},{5,29},{6,30},{7,31},{8,0},{9,1... | collective-permute-start | bytes 294920 | tf_op jit(solution)/shard_map/ppermute | solution.py:796
  259.2 3.7 collective-permute-start.70
  262.8 4.5 collective-permute-start.74
  278.7 4.5 collective-permute-start.80
  308.1 4.5 collective-permute-start.86
  319.7 3.6 collective-permute-start.88
  323.4 4.5 collective-permute-start.92
  325.5 3.6 collective-permute-start.91
  352.7 4.5 collective-permute-start.98
  367.9 4.5 collective-permute-start.104
  370.1 3.6 collective-permute-start.103
  380.0 22.5 %collective-permute-start.105 = (f32[2048,128]{1,0:T(8,128)S(1)}, f32[2048,128]{1,0:T(8,128)S(1)}, u32[]{:S(2)}, u32[]{:S(2)}) collective-permute-start(f32[2048,128]{1,0:T(8,128)S(1)} %get-tuple-element.313), channel_id=1, source_target_pairs={{0,1},{1,0},{2,3},{3,2},{4,5},{5,4},{6,7},{7,6},{8,9},{9,8},{10,11... | collective-permute-start | bytes 3145736 | tf_op jit(solution)/shard_map/ppermute | solution.py:789
  380.7 8.6 %collective-permute-start.106 = (f32[24,1024]{1,0:T(8,128)S(1)}, f32[24,1024]{1,0:T(8,128)S(1)}, u32[]{:S(2)}, u32[]{:S(2)}) collective-permute-start(f32[24,1024]{1,0:T(8,128)S(1)} %get-tuple-element.319.kept_ref), channel_id=1, source_target_pairs={{16,20},{17,21},{18,22},{19,23},{20,16},{21,17},{22,18},{23,19},{2... | collective-permute-start | bytes 294920 | tf_op jit(solution)/shard_map/ppermute | solution.py:796
  381.4 19.1 %collective-permute-start.107 = (f32[24,1024]{1,0:T(8,128)S(1)}, f32[24,1024]{1,0:T(8,128)S(1)}, u32[]{:S(2)}, u32[]{:S(2)}) collective-permute-start(f32[24,1024]{1,0:T(8,128)S(1)} %get-tuple-element.316), channel_id=1, source_target_pairs={{0,8},{1,9},{2,10},{3,11},{4,12},{5,13},{6,14},{7,15},{8,16},{9,17... | collective-permute-start | bytes 294920 | tf_op jit(solution)/shard_map/ppermute | solution.py:796
  383.5 19.0 %collective-permute-start.108 = (f32[24,1024]{1,0:T(8,128)S(1)}, f32[24,1024]{1,0:T(8,128)S(1)}, u32[]{:S(2)}, u32[]{:S(2)}) collective-permute-start(f32[24,1024]{1,0:T(8,128)S(1)} %get-tuple-element.317), channel_id=1, source_target_pairs={{0,16},{1,17},{2,18},{3,19},{4,20},{5,21},{6,22},{7,23},{8,24},{9,... | collective-permute-start | bytes 294920 | tf_op jit(solution)/shard_map/ppermute | solution.py:796
  387.1 15.4 %collective-permute-start.109 = (f32[24,1024]{1,0:T(8,128)S(1)}, f32[24,1024]{1,0:T(8,128)S(1)}, u32[]{:S(2)}, u32[]{:S(2)}) collective-permute-start(f32[24,1024]{1,0:T(8,128)S(1)} %get-tuple-element.318), channel_id=1, source_target_pairs={{0,24},{1,25},{2,26},{3,27},{4,28},{5,29},{6,30},{7,31},{8,0},{9,1... | collective-permute-start | bytes 294920 | tf_op jit(solution)/shard_map/ppermute | solution.py:796
  403.2 10.5 %collective-permute-start.110 = (f32[512,128]{1,0:T(8,128)S(1)}, f32[512,128]{1,0:T(8,128)S(1)}, u32[]{:S(2)}, u32[]{:S(2)}) collective-permute-start(f32[512,128]{1,0:T(8,128)S(1)} %get-tuple-element.327), channel_id=1, source_target_pairs={{0,8},{1,9},{2,10},{3,11},{4,12},{5,13},{6,14},{7,15},{8,0},{9,1},... | collective-permute-start | bytes 786440 | tf_op jit(solution)/shard_map/ppermute | solution.py:789
  406.5 13.3 %collective-permute-start.111 = (f32[512,128]{1,0:T(8,128)S(1)}, f32[512,128]{1,0:T(8,128)S(1)}, u32[]{:S(2)}, u32[]{:S(2)}) collective-permute-start(f32[512,128]{1,0:T(8,128)S(1)} %get-tuple-element.328), channel_id=1, source_target_pairs={{0,16},{1,17},{2,18},{3,19},{4,20},{5,21},{6,22},{7,23},{8,24},{9,... | collective-permute-start | bytes 786440 | tf_op jit(solution)/shard_map/ppermute | solution.py:789
  406.5 13.3 %collective-permute-start.112 = (f32[512,128]{1,0:T(8,128)S(1)}, f32[512,128]{1,0:T(8,128)S(1)}, u32[]{:S(2)}, u32[]{:S(2)}) collective-permute-start(f32[512,128]{1,0:T(8,128)S(1)} %get-tuple-element.329), channel_id=1, source_target_pairs={{0,24},{1,25},{2,26},{3,27},{4,28},{5,29},{6,30},{7,31},{8,16},{9,... | collective-permute-start | bytes 786440 | tf_op jit(solution)/shard_map/ppermute | solution.py:789
  420.5 4.5 collective-permute-start.113
  420.5 6.9 %collective-permute-start.114 = (f32[128,128]{1,0:T(8,128)S(1)}, f32[128,128]{1,0:T(8,128)S(1)}, u32[]{:S(2)}, u32[]{:S(2)}) collective-permute-start(f32[128,128]{1,0:T(8,128)S(1)} %get-tuple-element.332), channel_id=1, source_target_pairs={{0,4},{1,5},{2,6},{3,7},{4,0},{5,1},{6,2},{7,3},{8,12},{9,13},{10,... | collective-permute-start | bytes 196616 | tf_op jit(solution)/shard_map/ppermute | solution.py:789
  423.8 6.5 %collective-permute-start.115 = (f32[128,128]{1,0:T(8,128)S(1)}, f32[128,128]{1,0:T(8,128)S(1)}, u32[]{:S(2)}, u32[]{:S(2)}) collective-permute-start(f32[128,128]{1,0:T(8,128)S(1)} %get-tuple-element.333), channel_id=1, source_target_pairs={{0,6},{1,7},{2,4},{3,5},{4,2},{5,3},{6,0},{7,1},{8,14},{9,15},{10,... | collective-permute-start | bytes 196616 | tf_op jit(solution)/shard_map/ppermute | solution.py:789
  430.9 4.5 collective-permute-start.116
  431.0 5.2 %collective-permute-start.117 = (f32[128,128]{1,0:T(8,128)S(1)}, f32[128,128]{1,0:T(8,128)S(1)}, u32[]{:S(2)}, u32[]{:S(2)}) collective-permute-start(f32[128,128]{1,0:T(8,128)S(1)} %reduce_part.5.refs_0_), channel_id=1, source_target_pairs={{0,4},{1,5},{2,6},{3,7},{4,0},{5,1},{6,2},{7,3},{8,12},{9,13},{10,... | collective-permute-start | bytes 196616 | tf_op jit(solution)/shard_map/ppermute | solution.py:789
  432.2 6.1 %collective-permute-start.118 = (f32[128,128]{1,0:T(8,128)S(1)}, f32[128,128]{1,0:T(8,128)S(1)}, u32[]{:S(2)}, u32[]{:S(2)}) collective-permute-start(f32[128,128]{1,0:T(8,128)S(1)} %reduce_part.5.refs_0_), channel_id=1, source_target_pairs={{0,6},{1,7},{2,4},{3,5},{4,2},{5,3},{6,0},{7,1},{8,14},{9,15},{10,... | collective-permute-start | bytes 196616 | tf_op jit(solution)/shard_map/ppermute | solution.py:789
  438.9 6.8 %collective-permute-start.119 = (f32[512,128]{1,0:T(8,128)S(1)}, f32[512,128]{1,0:T(8,128)S(1)}, u32[]{:S(2)}, u32[]{:S(2)}) collective-permute-start(f32[512,128]{1,0:T(8,128)S(1)} %gather_part.2.refs_0_), channel_id=1, source_target_pairs={{0,8},{1,9},{2,10},{3,11},{4,12},{5,13},{6,14},{7,15},{8,0},{9,1},... | collective-permute-start | bytes 786440 | tf_op jit(solution)/shard_map/ppermute | solution.py:789
  439.3 9.7 %collective-permute-start.120 = (f32[512,128]{1,0:T(8,128)S(1)}, f32[512,128]{1,0:T(8,128)S(1)}, u32[]{:S(2)}, u32[]{:S(2)}) collective-permute-start(f32[512,128]{1,0:T(8,128)S(1)} %gather_part.2.refs_0_), channel_id=1, source_target_pairs={{0,16},{1,17},{2,18},{3,19},{4,20},{5,21},{6,22},{7,23},{8,24},{9,... | collective-permute-start | bytes 786440 | tf_op jit(solution)/shard_map/ppermute | solution.py:789
  440.7 8.3 %collective-permute-start.121 = (f32[512,128]{1,0:T(8,128)S(1)}, f32[512,128]{1,0:T(8,128)S(1)}, u32[]{:S(2)}, u32[]{:S(2)}) collective-permute-start(f32[512,128]{1,0:T(8,128)S(1)} %gather_part.2.refs_0_), channel_id=1, source_target_pairs={{0,24},{1,25},{2,26},{3,27},{4,28},{5,29},{6,30},{7,31},{8,16},{9,... | collective-permute-start | bytes 786440 | tf_op jit(solution)/shard_map/ppermute | solution.py:789
  (154 other events, 1760.3 us)

commit v5 on v4

--- a/solution.py
+++ b/solution.py
@@ -160,6 +160,11 @@
         for start in range(0, cells, block_size)
         for head in range(HEADS)
     ]
+
+
+def of_head(value, rows):
+    channel = lax.broadcasted_iota(jnp.int32, value.shape, 1)
+    return jnp.where((channel >= rows.start) & (channel < rows.stop), value, 0.0)
 
 
 def below(rows, offset):
@@ -217,10 +222,10 @@
 
 
 def outlet_kernel(
-    lon, count, block_size, step_size,
+    lon, count, block_size, step_size, quantities,
     state_ref, inner_ref, pre_two_ref, sums_two_ref, gain_ref, shift_ref,
     w_qkv_ref, w_mixer_ref, w_velocity_ref, b_velocity_ref,
-    out_ref, qkv_ref, mixed_ref, weight_ref, powers_ref,
+    out_ref, packed_ref, qkv_ref, mixed_ref, weight_ref, powers_ref,
     slots_ref, done_ref,
 ):
     channels = inner_ref.shape[1]
@@ -241,6 +246,7 @@
         )
 
     following = scores_of(0)
+    value_cells = qkv_ref[2 * channels :].T
     for turn, (rows, lanes) in enumerate(heads):
         scores = following
         if turn + 1 < len(heads):
@@ -255,8 +261,17 @@
         slots_ref[turn % 2, 0] = high
         slots_ref[turn % 2, 1] = low
         keep(turn).start()
-        value = stacked(qkv_ref[below(rows, 2 * channels), lanes])
-        mixed_ref[rows, lanes] = folded(dot(value, high) + dot(value, low), 0) * weight
+        value = beside(of_head(value_cells[lanes], rows))
+        part = dot(high, value, 0, 0) + dot(low, value, 0, 0)
+        mixed = part if rows.start == 0 else mixed + part
+        if rows.stop == channels:
+            mixed_ref[:, lanes] = folded(mixed, 1).T
+            first = turn + 1 - HEADS
+            for head in range(HEADS):
+                own_rows = heads[head][0]
+                mixed_ref[own_rows, lanes] = (
+                    mixed_ref[own_rows, lanes] * weight_ref[first + head : first + head + 1]
+                )
     act_three = act_two + folded(dot(w_mixer_ref[...], stacked(mixed_ref[...])), 0)
     parts = folded(dot(w_velocity_ref[...], stacked(act_three)), 0)
     forcing = jnp.zeros((2 * GROUP, cells), F32) + b_velocity_ref[...]
@@ -273,12 +288,13 @@
     flows = state[GROUP:]
     out_ref[:GROUP] = advected(state, step_size, lon)
     out_ref[GROUP:] = flows + step_size * (forcing - flows)
+    put_packed(packed_ref, out_ref[...], quantities)
     for turn in range(max(0, len(heads) - 2), len(heads)):
         keep(turn).wait()
 
 
 def outlet_back_kernel(
-    lon, count, block_size, step_size, sections, step,
+    lon, count, block_size, step_size, quantities, sections, step,
     ids_ref,
     state_ref, d_next_ref, cots_ref, inner_ref, pre_two_ref, sums_two_ref, gain_ref, shift_ref,
     qkv_ref, mixed_ref, weight_ref, powers_ref,
@@ -286,7 +302,7 @@
     acc_qkv_ref, acc_mixer_ref, acc_velocity_ref, acc_small_ref,
     d_state_ref, d_two_ref, sums_ref,
     out_qkv_ref, out_mixer_ref, out_velocity_ref, out_small_ref,
-    d_mixed_ref, d_qkv_ref, slots_ref, done_ref,
+    d_mixed_ref, d_qkv_ref, seed_ref, slots_ref, done_ref,
 ):
     channels = inner_ref.shape[1]
     cells = inner_ref.shape[0]
@@ -300,7 +316,9 @@
     for turn in range(min(2, len(heads))):
         fetch(turn).start()
     state = state_ref[...]
-    seed = d_next_ref[...] + cots_ref[lax.rem(ids_ref[0] - step + sections, sections)]
+    packed = cots_ref[lax.rem(ids_ref[0] - step + sections, sections)]
+    put_groups(seed_ref, packed[: 3 * quantities])
+    seed = seed_ref[...] + d_next_ref[...]
     amount, east, north = state[:GROUP], state[GROUP : 2 * GROUP], state[2 * GROUP :]
     d_amount = seed[:GROUP]
     d_lon = step_size * along_lon(d_amount, lon)
@@ -318,10 +336,14 @@
     d_three = folded(dot(w_velocity_back_ref[...], d_parts), 0)
     d_three_halves = stacked(d_three)
     d_mixed_ref[...] = folded(dot(w_mixer_back_ref[...], d_three_halves), 0)
+    for turn, (rows, lanes) in enumerate(heads):
+        d_mixed_ref[rows, lanes] = d_mixed_ref[rows, lanes] * weight_ref[turn : turn + 1]
+    d_mixed_cells = d_mixed_ref[...].T
+    query_cells = qkv_ref[:channels].T
 
     def d_powers_of(turn):
         rows, lanes = heads[turn]
-        d_mixed = d_mixed_ref[rows, lanes] * weight_ref[turn : turn + 1]
+        d_mixed = d_mixed_ref[rows, lanes]
         return d_mixed, row_products(qkv_ref[below(rows, 2 * channels), lanes], d_mixed)
 
     following = d_powers_of(0)
@@ -334,17 +356,18 @@
         power_high, power_low = slots_ref[turn % 2, 0], slots_ref[turn % 2, 1]
         powers = power_high.astype(F32) + power_low.astype(F32)
         d_high, d_low = halves(powers * (d_powers - inner_sum))
-        d_mixed_cells = beside(d_mixed.T)
-        d_value = folded(dot(power_high, d_mixed_cells) + dot(power_low, d_mixed_cells), 1)
-        query_cells = beside(qkv_ref[rows, lanes].T)
-        d_key = folded(dot(d_high, query_cells) + dot(d_low, query_cells), 1)
+        right = beside(of_head(d_mixed_cells[lanes], rows))
+        d_value = dot(power_high, right) + dot(power_low, right) + (d_value if rows.start else 0.0)
+        right = beside(of_head(query_cells[lanes], rows))
+        d_key = dot(d_high, right) + dot(d_low, right) + (d_key if rows.start else 0.0)
         key_halves = stacked(qkv_ref[below(rows, channels), lanes])
         d_query = folded(dot(key_halves, d_high) + dot(key_halves, d_low), 0)
         if turn + 2 < len(heads):
             fetch(turn + 2).start()
         d_qkv_ref[rows, lanes] = d_query * (1.0 / math.sqrt(channels // HEADS))
-        d_qkv_ref[below(rows, channels), lanes] = d_key.T * (1.0 / LOG2_E)
-        d_qkv_ref[below(rows, 2 * channels), lanes] = d_value.T
+        if rows.stop == channels:
+            d_qkv_ref[channels : 2 * channels, lanes] = folded(d_key, 1).T * (1.0 / LOG2_E)
+            d_qkv_ref[2 * channels :, lanes] = folded(d_value, 1).T
     d_qkv_halves = stacked(d_qkv_ref[...])
     d_two = (d_three + folded(dot(w_qkv_back_ref[...], d_qkv_halves), 0)).T
     d_two_ref[...] = d_two
@@ -415,11 +438,11 @@
 
 
 def inlet_back_kernel(
-    lon, count,
+    lon, count, quantities,
     state_ref, d_normed_ref, pre_one_ref, sums_one_ref, all_one_ref, gain_ref,
     inner_ref, d_two_ref, d_state_in_ref, w_first_back_ref, w_input_back_ref,
     acc_first_ref, acc_input_ref, acc_inner_ref,
-    d_state_ref, out_first_ref, out_input_ref, out_inner_ref,
+    d_state_ref, packed_ref, out_first_ref, out_input_ref, out_inner_ref,
     patches_ref,
 ):
     cells = inner_ref.shape[0]
@@ -457,47 +480,81 @@
         - along_lat(d_groups[4 * GROUP :], lon)
     )
     d_state_ref[GROUP:] = d_state[GROUP:]
-
-
-def put_sample(out_ref, from_ref, place):
-    size = from_ref.shape[0] // 3
+    put_packed(packed_ref, d_state_ref[...], quantities)
+
+
+def put_groups(out_ref, rows):
+    size = rows.shape[0] // 3
     out_ref[...] = jnp.zeros(out_ref.shape, F32)
-    for row in range(from_ref.shape[0]):
-        target = row // size * GROUP + row % size
-        out_ref[target : target + 1] = from_ref[row, pl.ds(place, 1)]
-
-
-def enter_kernel(plan, ids_ref, order_ref, state_ref, out_ref):
-    put_sample(out_ref, state_ref, order_ref[0, plan.slot(ids_ref[0], ids_ref[1])])
-
-
-def seeds_kernel(plan, ids_ref, order_ref, cot_ref, *out_refs):
+    for group in range(3):
+        out_ref[group * GROUP : group * GROUP + size] = rows[group * size : (group + 1) * size]
+
+
+def put_packed(out_ref, grouped, size):
+    out_ref[...] = jnp.zeros(out_ref.shape, F32)
+    for group in range(3):
+        out_ref[group * size : (group + 1) * size] = grouped[group * GROUP : group * GROUP + size]
+
+
+def fetched(far_refs, near_refs, done_ref):
+    copies = [
+        pltpu.make_async_copy(far_ref, near_ref, done_ref.at[place])
+        for place, (far_ref, near_ref) in enumerate(zip(far_refs, near_refs))
+    ]
+    for copy in copies:
+        copy.start()
+    return copies
+
+
+def enter_kernel(plan, ids_ref, order_ref, state_ref, out_ref, near_ref, rows_ref, done_ref):
+    (copy,) = fetched([state_ref], [near_ref], done_ref)
+    copy.wait()
+    place = order_ref[0, plan.slot(ids_ref[0], ids_ref[1])]
+    for row in range(rows_ref.shape[0]):
+        rows_ref[row : row + 1] = near_ref[row, pl.ds(place, 1)]
+    put_groups(out_ref, rows_ref[...])
+
+
+def seeds_kernel(plan, ids_ref, order_ref, cot_ref, *refs):
+    out_refs, near_ref, done_ref = refs[:-2], refs[-2], refs[-1]
+    (copy,) = fetched([cot_ref], [near_ref], done_ref)
+    copy.wait()
     for steps, out_ref in enumerate(out_refs):
         target = lax.rem(ids_ref[0] + steps, plan.sections)
-        put_sample(out_ref, cot_ref, order_ref[0, plan.slot(target, ids_ref[1])])
+        place = order_ref[0, plan.slot(target, ids_ref[1])]
+        out_ref[...] = jnp.zeros(out_ref.shape, F32)
+        for row in range(near_ref.shape[0]):
+            out_ref[row : row + 1] = near_ref[row, pl.ds(place, 1)]
 
 
 def leave_kernel(plan, ids_ref, *refs):
     values_ref = refs[-1]
+    size = refs[0].shape[0]
     for step in range(plan.sections):
-        values_ref[step] = refs[step][...]
-    for steps, out_ref in enumerate(refs[plan.sections : -1]):
+        values_ref[step, :size] = refs[step][...]
+        if step:
+            values_ref[step, size:] = refs[plan.sections + step - 1][...]
+        else:
+            values_ref[step, size:] = jnp.zeros(refs[0].shape, F32)
+    for steps, out_ref in enumerate(refs[2 * plan.sections - 1 : -1]):
         out_ref[...] = values_ref[lax.rem(ids_ref[0] + steps, plan.sections)]
 
 
-def arrive_kernel(plan, ids_ref, order_ref, kept_ref, *refs):
+def arrive_kernel(plan, start, ids_ref, order_ref, kept_ref, *refs):
     section, dp = ids_ref[0], ids_ref[1]
     out_ref = refs[-1]
-    size = out_ref.shape[0] // 3
-    for steps, ref in enumerate(refs[:-1]):
+    size = kept_ref.shape[0] // 2
+    early, late = refs[: plan.sections], refs[plan.sections : -1]
+    for steps, ref in enumerate(early):
         source = lax.rem(section - steps + plan.sections, plan.sections)
         place = order_ref[0, plan.slot(source, dp)]
-        value = ref[...]
+        value = ref[start : start + size]
         if plan.halved and not steps:
-            value = jnp.where(section < 2, kept_ref[...], value)
+            value = jnp.where(section < 2, kept_ref[start : start + size], value)
+        if late:
+            value = jnp.where(section == 0, late[steps][...], value)
         for row in range(out_ref.shape[0]):
-            start = row // size * GROUP + row % size
-            out_ref[row, pl.ds(place, 1)] = value[start : start + 1]
+            out_ref[row, pl.ds(place, 1)] = value[row : row + 1]
 
 
 def put_conv_weight(out_ref, taps):
@@ -517,8 +574,12 @@
 def first_weights_kernel(
     lon, quantities, w_input_ref, w_first_ref, b_input_ref, maps_ref,
     static_part_ref, moving_cat_ref, moving_back_ref, first_cat_ref,
-    patches_ref, weight_ref, taps_ref,
+    patches_ref, weight_ref, taps_ref, *near_refs,
 ):
+    near_refs, done_ref = near_refs[:-1], near_refs[-1]
+    copies = fetched([w_input_ref, maps_ref, b_input_ref, w_first_ref], near_refs, done_ref)
+    w_input_ref, maps_ref, b_input_ref, w_first_ref = near_refs
+    copies[0].wait()
     channels = w_input_ref.shape[2]
     moving = 5 * quantities
     statics = maps_ref.shape[0]
@@ -534,23 +595,32 @@
     put_conv_weight(moving_cat_ref, [taps_ref[9 + row] for row in range(3)])
     put_conv_weight(moving_back_ref, [taps_ref[11 - row].T for row in range(3)])
     put_conv_weight(weight_ref, [taps_ref[tap] for tap in range(9)])
+    copies[1].wait()
+    copies[2].wait()
     maps = jnp.concatenate(
         [maps_ref[...], jnp.zeros((channels - statics, maps_ref.shape[1]), F32)], axis=0
     )
     fill_patches(patches_ref, maps.T, lon)
     static_part_ref[...] = conv_patches(patches_ref, weight_ref, lon) + b_input_ref[...]
+    copies[3].wait()
     put_conv_weight(first_cat_ref, [w_first_ref[tap] for tap in range(9)])
 
 
-def second_weights_kernel(w_second_ref, out_ref):
+def second_weights_kernel(far_ref, out_ref, w_second_ref, done_ref):
+    fetched([far_ref], [w_second_ref], done_ref)[0].wait()
     put_conv_weight(out_ref, [w_second_ref[tap] for tap in range(9)])
 
 
 def outlet_weights_kernel(
     quantities, w_query_ref, w_key_ref, w_value_ref, w_mixer_ref, w_velocity_ref,
     qkv_ref, qkv_back_ref, mixer_ref, mixer_back_ref, velocity_ref, velocity_back_ref,
-    rows_ref,
+    rows_ref, *near_refs,
 ):
+    near_refs, done_ref = near_refs[:-1], near_refs[-1]
+    copies = fetched([w_query_ref, w_key_ref, w_value_ref, w_mixer_ref, w_velocity_ref], near_refs, done_ref)
+    w_query_ref, w_key_ref, w_value_ref, w_mixer_ref, w_velocity_ref = near_refs
+    for copy in copies:
+        copy.wait()
     parts = [ref[...] for ref in (w_query_ref, w_key_ref, w_value_ref)]
     put_left_weight(qkv_ref, jnp.concatenate([part.T for part in parts], axis=0))
     put_left_weight(qkv_back_ref, jnp.concatenate(parts, axis=1))
@@ -569,7 +639,9 @@
     put_left_weight(velocity_back_ref, rows_ref[...].T[:, :size])
 
 
-def back_weights_kernel(w_first_ref, w_second_ref, first_ref, second_ref):
+def back_weights_kernel(far_first_ref, far_second_ref, first_ref, second_ref, w_first_ref, w_second_ref, done_ref):
+    for copy in fetched([far_first_ref, far_second_ref], [w_first_ref, w_second_ref], done_ref):
+        copy.wait()
     put_conv_weight(first_ref, [w_first_ref[8 - tap].T for tap in range(9)])
     put_conv_weight(second_ref, [w_second_ref[8 - tap].T for tap in range(9)])
 
@@ -700,8 +772,8 @@
     def run(*operands):
         places = [pltpu.SMEM] * scalars + [pltpu.VMEM] * (len(operands) - scalars)
         for place in far_in:
-            places[place] = pl.ANY
-        out_places = [pl.ANY if place in far_out else pltpu.VMEM for place in range(len(outs))]
+            places[place] = pltpu.HBM
+        out_places = [pltpu.HBM if place in far_out else pltpu.VMEM for place in range(len(outs))]
         return pl.pallas_call(
             kernel,
             out_shape=tuple(jax.ShapeDtypeStruct(shape, kind) for shape, kind in zip(outs, kinds)),
@@ -772,6 +844,9 @@
             for own in range(self.dp)
         ]
 
+    def to_first_home(self, steps):
+        return [(source, target) for source, target in self.to_homes(steps) if target < self.dp]
+
     def joint(self, section, home):
         return section * self.dp + self.other(section, home)
 
@@ -796,8 +871,8 @@
     return lax.ppermute(value, ("section", "dp"), going)
 
 
-def micro_sum(plan, value):
-    for bits in plan.sum_rounds:
+def micro_sum(plan, value, paired=False):
+    for bits in [[bit] for bits in plan.sum_rounds for bit in bits] if paired else plan.sum_rounds:
         value = value + sum(exchanged(value, mask) for mask in masks_of(bits))
     return value
 
@@ -844,26 +919,41 @@
     narrow = pltpu.VMEM((channels, cells), F32)
     state_shape = (3 * GROUP, cells)
 
-    (own_state,) = call(functools.partial(enter_kernel, plan), [state_shape], name="enter", scalars=2)(
-        ids, grouping, jnp.swapaxes(state_start, 0, 1)
-    )
+    packed = (2 * GROUP, cells)
+
+    def near(*arrays):
+        return [pltpu.VMEM(array.shape, F32) for array in arrays] + [pltpu.SemaphoreType.DMA((len(arrays),))]
+
+    state_rows = jnp.swapaxes(state_start, 0, 1)
+    (own_state,) = call(
+        functools.partial(enter_kernel, plan), [state_shape],
+        [pltpu.VMEM(state_rows.shape, F32), pltpu.VMEM((3 * quantities, cells), F32), pltpu.SemaphoreType.DMA((1,))],
+        name="enter", scalars=2, far_in=[2],
+    )(ids, grouping, state_rows)
     arrived_state = moved(own_state, plan.to_workers(0))
 
     static_part, moving_cat, moving_back_cat, first_cat = call(
         functools.partial(first_weights_kernel, lon, quantities),
         [plane, (6 * channels, 2 * channels), (6 * channels, 2 * channels), conv],
-        [patches, pltpu.VMEM(conv, BF16), pltpu.VMEM((12, channels, channels), F32)],
-        name="first_weights", kinds=[F32, BF16, BF16, BF16],
+        [patches, pltpu.VMEM(conv, BF16), pltpu.VMEM((12, channels, channels), F32)]
+        + near(w_input, static_maps, b_input[None], w_first),
+        name="first_weights", kinds=[F32, BF16, BF16, BF16], far_in=range(4),
     )(w_input, w_first, b_input[None], static_maps)
-    (second_cat,) = call(second_weights_kernel, [conv], name="second_weights", kinds=[BF16])(w_second)
+    (second_cat,) = call(
+        second_weights_kernel, [conv], near(w_second), name="second_weights", kinds=[BF16], far_in=[0]
+    )(w_second)
+    w_velocity_rows = jnp.swapaxes(w_velocity, 1, 2)
     qkv_cat, qkv_back_cat, mixer_cat, mixer_back_cat, out_cat, out_back_cat = call(
         functools.partial(outlet_weights_kernel, quantities),
         [(6 * channels, 2 * channels), (2 * channels, 6 * channels), (2 * channels, 2 * channels),
          (2 * channels, 2 * channels), (36 * GROUP, 2 * channels), (2 * channels, 36 * GROUP)],
-        [pltpu.VMEM((2 * channels, channels), F32)], name="outlet_weights", kinds=[BF16] * 6,
-    )(w_query, w_key, w_value, w_mixer, jnp.swapaxes(w_velocity, 1, 2))
+        [pltpu.VMEM((2 * channels, channels), F32)]
+        + near(w_query, w_key, w_value, w_mixer, w_velocity_rows),
+        name="outlet_weights", kinds=[BF16] * 6, far_in=range(5),
+    )(w_query, w_key, w_value, w_mixer, w_velocity_rows)
     first_back_cat, second_back_cat = call(
-        back_weights_kernel, [conv, conv], name="back_weights", kinds=[BF16, BF16]
+        back_weights_kernel, [conv, conv], near(w_first, w_second), name="back_weights", kinds=[BF16, BF16],
+        far_in=range(2),
     )(w_first, w_second)
     b_out = in_groups(b_velocity[:, None], 0, 2)
     gain_one, shift_one = gain_first[None], shift_first[None]
@@ -879,17 +969,17 @@
     powers = (heads, 2, block_size, block_size)
     slots = [pltpu.VMEM((2,) + powers[1:], BF16), pltpu.SemaphoreType.DMA((2,))]
     outlet = call(
-        functools.partial(outlet_kernel, lon, count, block_size, step_size),
-        [state_shape, (3 * channels, cells), (channels, cells), (heads, block_size), powers],
-        slots, name="outlet", kinds=[F32] * 4 + [BF16], far_out=[4],
+        functools.partial(outlet_kernel, lon, count, block_size, step_size, quantities),
+        [state_shape, packed, (3 * channels, cells), (channels, cells), (heads, block_size), powers],
+        slots, name="outlet", kinds=[F32] * 5 + [BF16], far_out=[5],
     )
 
     def outlet_back(step):
         return call(
-            functools.partial(outlet_back_kernel, lon, count, block_size, step_size, segments, step),
+            functools.partial(outlet_back_kernel, lon, count, block_size, step_size, quantities, segments, step),
             [state_shape, plane, small, (channels, 3 * channels), (channels, channels),
              (18 * GROUP, channels), (3 * GROUP, channels)],
-            [narrow, wide] + slots,
+            [narrow, wide, pltpu.VMEM(state_shape, F32)] + slots,
             {17: 3, 18: 4, 19: 5, 20: 6}, name="outlet_back", scalars=1, far_in=[12],
         )
 
@@ -899,9 +989,9 @@
         {10: 2, 11: 3}, name="middle_back",
     )
     inlet_back = call(
-        functools.partial(inlet_back_kernel, lon, count),
-        [state_shape, (9, channels, channels), (3, channels, channels), plane], [patches],
-        {11: 1, 12: 2, 13: 3}, name="inlet_back",
+        functools.partial(inlet_back_kernel, lon, count, quantities),
+        [state_shape, packed, (9, channels, channels), (3, channels, channels), plane], [patches],
+        {11: 2, 12: 3, 13: 4}, name="inlet_back",
     )
 
     state = own_state
@@ -915,41 +1005,33 @@
             )(ids, own_state, arrived_state, static_part, moving_cat, first_cat)
         else:
             inner, pre_one, sums_one = inlet(state, static_part, moving_cat, first_cat)
-        sums_one = micro_sum(plan, sums_one)
+        sums_one = micro_sum(plan, sums_one, True)
         pre_two, sums_two = middle(pre_one, sums_one, gain_one, shift_one, second_cat)
-        sums_two = micro_sum(plan, sums_two)
-        state_out, qkv, mixed, weight, powers_kept = outlet(
+        sums_two = micro_sum(plan, sums_two, True)
+        state_out, state_packed, qkv, mixed, weight, powers_kept = outlet(
             state, inner, pre_two, sums_two, gain_two, shift_two, qkv_cat, mixer_cat, out_cat, b_out
         )
         kept = (qkv, mixed, weight, powers_kept) if step >= segments - KEPT_STEPS else None
         saved.append((state, inner, pre_one, pre_two, sums_one, sums_two, kept))
-        path.append(state_out)
+        path.append(state_packed)
         state = state_out
         if not step:
             state, cot_local = lax.optimization_barrier((state, cotangent))
             sent = call(
-                functools.partial(seeds_kernel, plan), [state_shape] * segments, name="seeds", scalars=2
+                functools.partial(seeds_kernel, plan), [packed] * segments,
+                [pltpu.VMEM(state_rows.shape, F32), pltpu.SemaphoreType.DMA((1,))],
+                name="seeds", scalars=2, far_in=[2],
             )(ids, grouping, jnp.swapaxes(cot_local[0], 0, 1))
             cots = [moved(cot, plan.to_workers(steps)) for steps, cot in enumerate(sent)]
             if plan.halved:
                 cots[0] = jnp.where(lax.axis_index("section") < 2, sent[0], cots[0])
     cots = jnp.stack(cots)
 
-    def sent_home(values):
-        parts = call(
-            functools.partial(leave_kernel, plan), [state_shape] * segments,
-            [pltpu.VMEM((segments,) + state_shape, F32)], name="leave", scalars=1,
-        )(ids, *values)
-        return [parts[0]] + [moved(part, plan.to_homes(steps)) for steps, part in enumerate(parts)]
-
-    def put_home(parts):
-        rows, samples = state_start.shape[1], state_start.shape[0]
+    def put_home(start, parts):
         (out,) = call(
-            functools.partial(arrive_kernel, plan), [(rows, samples, cells)], name="arrive", scalars=2
+            functools.partial(arrive_kernel, plan, start), [state_rows.shape], name="arrive", scalars=2
         )(ids, grouping, *parts)
         return jnp.swapaxes(out, 0, 1)[None]
-
-    path_parts = sent_home(path)
 
     acc = dict(
         qkv=jnp.zeros((channels, 3 * channels), F32),
@@ -966,12 +1048,18 @@
     grads = [None] * segments
     path_out = None
     for step in reversed(range(segments)):
+        if not step:
+            sent = call(
+                functools.partial(leave_kernel, plan), [(4 * GROUP, cells)] * segments,
+                [pltpu.VMEM((segments, 4 * GROUP, cells), F32)], name="leave", scalars=1,
+            )(ids, *path, *grads[1:])
+            early = [sent[0]] + [moved(part, plan.to_homes(steps)) for steps, part in enumerate(sent)]
         state, inner, pre_one, pre_two, sums_one, sums_two, kept = saved[step]
         if kept is None:
             state, d_state = lax.optimization_barrier((state, d_state))
             kept = outlet(
                 state, inner, pre_two, sums_two, gain_two, shift_two, qkv_cat, mixer_cat, out_cat, b_out
-            )[1:]
+            )[2:]
         qkv, mixed, weight, powers_kept = kept
         d_partial, d_two, grad_two, acc["qkv"], acc["mixer"], acc["velocity"], acc["small_two"] = outlet_back(step)(
             ids, state, d_state, cots, inner, pre_two, sums_two, gain_two, shift_two,
@@ -979,6 +1067,9 @@
             mixer_cat, qkv_back_cat, mixer_back_cat, out_back_cat,
             acc["qkv"], acc["mixer"], acc["velocity"], acc["small_two"],
         )
+        if not step:
+            d_two, grad_two, early = lax.optimization_barrier((d_two, grad_two, early))
+            path_out = put_home(0, early)
         grad_two = micro_sum(plan, grad_two)
         d_normed, grad_one, acc["second"], acc["small_one"] = middle_back(
             d_two, pre_two, sums_two, grad_two, gain_two,
@@ -986,17 +1077,14 @@
             acc["second"], acc["small_one"],
         )
         grad_one = micro_sum(plan, grad_one)
-        d_state, acc["first"], acc["moving"], acc["inner"] = inlet_back(
+        d_state, grads[step], acc["first"], acc["moving"], acc["inner"] = inlet_back(
             state, d_normed, pre_one, sums_one, grad_one, gain_one,
             inner, d_two, d_partial, first_back_cat, moving_back_cat,
             acc["first"], acc["moving"], acc["inner"],
         )
-        grads[step] = d_state
-        if path_out is None:
-            d_state, *path_parts = lax.optimization_barrier((d_state, *path_parts))
-            path_out = put_home(path_parts)
-            d_state, path_out = lax.optimization_barrier((d_state, path_out))
-    grad_parts = sent_home(grads)
+    late = [grads[0]] + [
+        lax.ppermute(grads[0], ("section", "dp"), plan.to_first_home(steps)) for steps in range(1, segments)
+    ]
 
     rounds = plan.all_rounds
     rows = 2 * 9 * channels + 9 * (statics + -statics % GROUP) + 45 * GROUP + 4 * channels + 23 * GROUP
@@ -1020,8 +1108,8 @@
     for bits, later in zip(rounds, rounds[1:] + [[]]):
         parts = swap(parts, bits)
         if grads_out is None:
-            parts, grad_parts = lax.optimization_barrier((parts, grad_parts))
-            grads_out = put_home(grad_parts)
+            parts, late = lax.optimization_barrier((parts, late))
+            grads_out = put_home(2 * GROUP, early + late)
         rows >>= len(bits)
         parts = call(
             functools.partial(reduce_kernel, plan, later, len(parts)), shares(rows, later),

time: 462 us -> 476 us (1.030)
  starting transfers between devices: 138 us -> 120 us
  Pallas kernels: 158 us -> 174 us
  waiting for transfers between devices: 125 us -> 132 us
    ppermute x13 -> x9, waiting for transfers between devices: 20.7 us -> 2.01 us  [moved(): return lax.ppermute(value, ('section', 'dp'), going)]
    ppermute x110 -> x94, waiting for transfers between devices: 104 us -> 122 us  [exchanged(): lax.ppermute(value, ('section', 'dp'), [(own, own ^ mask) for own in rang...]
    pallas_call x41 -> x40, Pallas kernels: 158 us -> 174 us  [run(): pl.pallas_call(kernel, out_shape=tuple((jax.ShapeDtypeStruct(shape, kind)...]
    ppermute x110 -> x94, starting transfers between devices: 115 us -> 100 us  [exchanged(): lax.ppermute(value, ('section', 'dp'), [(own, own ^ mask) for own in rang...]
    ppermute x0 -> x3, waiting for transfers between devices: none -> 7.79 us  [on_device(): lax.ppermute(grads[0], ('section', 'dp'), plan.to_first_home(steps))]
    ppermute x13 -> x9, starting transfers between devices: 23.1 us -> 15.9 us  [moved(): return lax.ppermute(value, ('section', 'dp'), going)]
    unnamed x190 -> x262, local copies, waits for them, and re-layouts: 31.6 us -> 33.9 us
  transfers between devices with their start and end apart: 123 -> 106, of which waited for: 78 -> 76; matrix products, arithmetic and copies ran while one was open for 0% -> 0% of each run, Pallas kernels for 4% -> 11%
where the time goes in v5:
time: 476 us; the launch traced here: 467 us
  Pallas kernels  174 us (37%)
  waiting for transfers between devices  132 us (28%)
  starting transfers between devices  120 us (25%)
  local copies, waits for them, and re-layouts  35.7 us (8%)
    pallas_call x40, Pallas kernels, run(): pl.pallas_call(kernel, out_shape=tuple((jax.ShapeDtypeStruct(shape, kind)...  174 us
    ppermute x94, waiting for transfers between devices, exchanged(): lax.ppermute(value, ('section', 'dp'), [(own, own ^ mask) for own in rang...  122 us
    ppermute x94, starting transfers between devices, exchanged(): lax.ppermute(value, ('section', 'dp'), [(own, own ^ mask) for own in rang...  100 us
    unnamed x262, local copies, waits for them, and re-layouts  33.9 us
    ppermute x9, starting transfers between devices, moved(): return lax.ppermute(value, ('section', 'dp'), going)  15.9 us
  transfers between devices with their start and end apart: 106, of which 76 were waited for; matrix products, arithmetic and copies ran while one was open for 0% of the time, Pallas kernels for 11%

profile of v5, /device:TPU:0, one launch (start us, length us, event | category | flops | bytes accessed | tf_op | source)
XLA Modules:
  0.0 467.1 jit_solution(7585946426996271106)
XLA Ops:
  7.7 2.1 first_weights.1
  9.8 3.7 inlet.4
  14.9 2.9 collective-permute-start.2
  23.0 5.8 %collective-permute-start.4 = (f32[8,128]{1,0:T(8,128)S(1)}, f32[8,128]{1,0:T(8,128)S(1)}, u32[]{:S(2)}, u32[]{:S(2)}) collective-permute-start(f32[8,128]{1,0:T(8,128)S(1)} %add.244), channel_id=1, source_target_pairs={{0,16},{1,17},{2,18},{3,19},{4,20},{5,21},{6,22},{7,23},{8,24},{9,... | collective-permute-start | bytes 12296 | tf_op jit(solution)/shard_map/ppermute | solution.py:864
  35.6 2.0 collective-permute-done.6
  39.1 2.1 collective-permute-done.7
  41.8 2.0 collective-permute-start.8
  56.5 21.7 %outlet.4 = (f32[24,1024]{1,0:T(8,128)S(1)}, f32[16,1024]{1,0:T(8,128)S(1)}, f32[384,1024]{1,0:T(8,128)S(1)}, f32[128,1024]{1,0:T(8,128)S(1)}, f32[8,512]{1,0:T(...) custom-call(f32[24,1024]{1,0:T(8,128)S(1)} %copy-done.58, f32[1024,128]{1,0:T(8,128)S(1)} %copy-done.18, ...), custom_call_target="tpu_custom_call" | custom-call | tf_op jit(solution)/shard_map/outlet/pallas_call | solution.py:777
  78.2 3.3 copy-done
  84.0 3.1 inlet.5
  90.0 2.0 collective-permute-done.10
  93.5 2.1 collective-permute-done.11
  95.6 3.6 collective-permute-done.12
  103.7 2.0 collective-permute-done.14
  114.4 10.6 %outlet.5 = (f32[24,1024]{1,0:T(8,128)S(1)}, f32[16,1024]{1,0:T(8,128)S(1)}, f32[384,1024]{1,0:T(8,128)S(1)}, f32[128,1024]{1,0:T(8,128)S(1)}, f32[8,512]{1,0:T(...) custom-call(f32[24,1024]{1,0:T(8,128)S(1)} %get-tuple-element.195.state_ref, f32[1024,128]{1,0:T(8,128)S(1)} %get-tuple-element.196.inner_ref, ...), custom_call_target="tpu_custom_call" | custom-call | tf_op jit(solution)/shard_map/outlet/pallas_call | solution.py:777
  125.0 3.2 copy-done.1
  129.4 3.1 inlet.6
  138.0 3.1 collective-permute-done.19
  151.7 3.1 collective-permute-done.23
  158.4 10.8 %outlet.6 = (f32[24,1024]{1,0:T(8,128)S(1)}, f32[16,1024]{1,0:T(8,128)S(1)}, f32[384,1024]{1,0:T(8,128)S(1)}, f32[128,1024]{1,0:T(8,128)S(1)}, f32[8,512]{1,0:T(...) custom-call(f32[24,1024]{1,0:T(8,128)S(1)} %get-tuple-element.201.state_ref, f32[1024,128]{1,0:T(8,128)S(1)} %get-tuple-element.202.inner_ref, ...), custom_call_target="tpu_custom_call" | custom-call | tf_op jit(solution)/shard_map/outlet/pallas_call | solution.py:777
  169.2 3.3 copy-done.2
  173.7 3.1 inlet.7
  183.1 3.1 collective-permute-done.31
  195.1 3.8 collective-permute-start.27
  198.9 2.4 collective-permute-start.28
  202.2 2.7 collective-permute-done.35
  205.0 3.5 collective-permute-done.36
  209.5 11.2 %outlet.7 = (f32[24,1024]{1,0:T(8,128)}, f32[16,1024]{1,0:T(8,128)S(1)}, f32[384,1024]{1,0:T(8,128)S(1)}, f32[128,1024]{1,0:T(8,128)S(1)}, f32[8,512]{1,0:T(8,128)S(1)}, /*index=5*/bf16[8,2,512,512]{3,2,1,0:T(8,128)(2,1)S(1)}) custom-call(f32[24,1024]{1,0:T(8,128)S(1)} %copy-done.47, f32[1024,128]{1,0:T(8,128)S(1)} %copy-done.25, ...), custom_call_target="tpu_custom_call" | custom-call | tf_op jit(solution)/shard_map/outlet/pallas_call | solution.py:777
  220.8 13.5 %outlet_back.4 = (f32[24,1024]{1,0:T(8,128)S(1)}, f32[1024,128]{1,0:T(8,128)S(1)}, f32[8,128]{1,0:T(8,128)S(1)}, f32[128,384]{1,0:T(8,128)S(1)}, f32[128,128]{1,...) custom-call(s32[2]{0:T(128)S(1)} %copy-done.74, ...), custom_call_target="tpu_custom_call", output_to_operand_aliasing={{3}: (17, {}), {4}: (18, {}), {5}: (19, {}), {6}: (20, {})} | custom-call | tf_op jit(solution)/shard_map/outlet_back/pallas_call | solution.py:777
  238.9 2.7 collective-permute-start.42
  243.6 3.0 middle_back.4
  252.4 2.0 collective-permute-start.47
  256.1 2.9 collective-permute-done.48
  259.2 4.3 inlet_back.4
  263.6 13.3 %outlet_back.5 = (f32[24,1024]{1,0:T(8,128)S(1)}, f32[1024,128]{1,0:T(8,128)S(1)}, f32[8,128]{1,0:T(8,128)S(1)}, f32[128,384]{1,0:T(8,128)S(1)}, f32[128,128]{1,...) custom-call(s32[2]{0:T(128)S(1)} %copy-done.74, ...), custom_call_target="tpu_custom_call", output_to_operand_aliasing={{3}: (17, {}), {4}: (18, {}), {5}: (19, {}), {6}: (20, {})} | custom-call | tf_op jit(solution)/shard_map/outlet_back/pallas_call | solution.py:777
  281.5 2.7 collective-permute-start.54
  286.1 3.0 middle_back.5
  294.9 2.0 collective-permute-start.59
  298.5 2.9 collective-permute-done.60
  301.5 4.3 inlet_back.5
  306.0 13.3 %outlet_back.6 = (f32[24,1024]{1,0:T(8,128)S(1)}, f32[1024,128]{1,0:T(8,128)S(1)}, f32[8,128]{1,0:T(8,128)S(1)}, f32[128,384]{1,0:T(8,128)S(1)}, f32[128,128]{1,...) custom-call(s32[2]{0:T(128)S(1)} %copy-done.74, ...), custom_call_target="tpu_custom_call", output_to_operand_aliasing={{3}: (17, {}), {4}: (18, {}), {5}: (19, {}), {6}: (20, {})} | custom-call | tf_op jit(solution)/shard_map/outlet_back/pallas_call | solution.py:777
  323.9 2.7 collective-permute-start.66
  328.4 3.1 middle_back.6
  337.3 2.0 collective-permute-start.71
  340.9 2.9 collective-permute-done.72
  343.9 4.3 inlet_back.6
  349.7 4.3 collective-permute-start.75
  354.0 2.2 collective-permute-start.76
  356.3 14.0 %outlet_back.7 = (f32[24,1024]{1,0:T(8,128)S(1)}, f32[1024,128]{1,0:T(8,128)S(1)}, f32[8,128]{1,0:T(8,128)S(1)}, f32[128,384]{1,0:T(8,128)S(1)}, f32[128,128]{1,...) custom-call(s32[2]{0:T(128)S(1)} %copy-done.74, ...), custom_call_target="tpu_custom_call", output_to_operand_aliasing={{3}: (17, {}), {4}: (18, {}), {5}: (19, {}), {6}: (20, {})} | custom-call | tf_op jit(solution)/shard_map/outlet_back/pallas_call | solution.py:777
  375.9 4.2 collective-permute-start.80
  381.7 2.0 collective-permute-done.81
  384.6 3.1 middle_back.7
  398.9 5.0 %inlet_back.7 = (f32[24,1024]{1,0:T(8,128)}, f32[16,1024]{1,0:T(8,128)S(1)}, f32[9,128,128]{2,1,0:T(8,128)S(1)}, f32[3,128,128]{2,1,0:T(8,128)S(1)}, f32[1024,128]{1,0:T(8,128)S(1)}) custom-call(f32[24,1024]{1,0:T(8,128)S(1)} %copy-done.59, ...), custom_call_target="tpu_custom_call", output_to_operand_aliasing={{2}: (11, {}), {3}: (12, {}), {4}: (13, {})} | custom-call | tf_op jit(solution)/shard_map/inlet_back/pallas_call | solution.py:777
  409.8 7.4 %collective-permute-done.90.refs_5_ = f32[16,1024]{1,0:T(8,128)S(1)} collective-permute-done((f32[16,1024]{1,0:T(8,128)S(1)}, f32[16,1024]{1,0:T(8,128)S(1)}, u32[]{:S(2)}, u32[]{:S(2)}) %collective-permute-start.90) | collective-permute-done | bytes 65568 | tf_op jit(solution)/shard_map/ppermute | solution.py:1086
  418.5 3.4 collective-permute-start.95
  421.9 5.7 %collective-permute-done.93.refs_1_ = f32[512,128]{1,0:T(8,128)S(1)} collective-permute-done((f32[512,128]{1,0:T(8,128)S(1)}, f32[512,128]{1,0:T(8,128)S(1)}, u32[]{:S(2)}, u32[]{:S(2)}) %collective-permute-start.93) | collective-permute-done | bytes 262176 | tf_op jit(solution)/shard_map/ppermute | solution.py:864
  427.6 4.3 collective-permute-done.94.refs_2_
  434.7 2.4 collective-permute-start.98
  438.6 2.1 collective-permute-done.98.refs_3_
  441.5 2.3 collective-permute-start.101
  444.9 2.1 collective-permute-done.100.refs_2_
  448.9 2.2 collective-permute-start.102
  452.6 3.9 collective-permute-done.102.refs_1_
  456.5 4.2 collective-permute-done.103.refs_2_
  (520 shorter events, 179.0 us)
Async XLA Ops:
  3.3 6.5 %collective-permute-start = (f32[24,1024]{1,0:T(8,128)S(1)}, f32[24,1024]{1,0:T(8,128)S(1)}, u32[]{:S(2)}, u32[]{:S(2)}) collective-permute-start(f32[24,1024]{1,0:T(8,128)S(1)} %enter.1.own_ref), channel_id=1, source_target_pairs={{16,20},{17,21},{18,22},{19,23},{20,16},{21,17},{22,18},{23,19},{2... | collective-permute-start | bytes 294920 | tf_op jit(solution)/shard_map/ppermute | solution.py:871
  14.9 4.5 collective-permute-start.2
  19.4 3.6 collective-permute-start.3
  23.0 7.4 %collective-permute-start.4 = (f32[8,128]{1,0:T(8,128)S(1)}, f32[8,128]{1,0:T(8,128)S(1)}, u32[]{:S(2)}, u32[]{:S(2)}) collective-permute-start(f32[8,128]{1,0:T(8,128)S(1)} %add.244), channel_id=1, source_target_pairs={{0,16},{1,17},{2,18},{3,19},{4,20},{5,21},{6,22},{7,23},{8,24},{9,... | collective-permute-start | bytes 12296 | tf_op jit(solution)/shard_map/ppermute | solution.py:864
  34.0 3.6 collective-permute-start.6
  37.6 3.6 collective-permute-start.7
  41.8 9.0 %collective-permute-start.8 = (f32[8,128]{1,0:T(8,128)}, f32[8,128]{1,0:T(8,128)}, u32[]{:S(2)}, u32[]{:S(2)}) collective-permute-start(f32[8,128]{1,0:T(8,128)} %add.248), channel_id=1, source_target_pairs={{0,16},{1,17},{2,18},{3,19},{4,20},{5,21},{6,22},{7,23},{8,24},{9,... | collective-permute-start | bytes 12296 | tf_op jit(solution)/shard_map/ppermute | solution.py:864
  88.4 3.6 collective-permute-start.10
  92.0 3.6 collective-permute-start.11
  95.6 3.6 collective-permute-start.12
  102.1 3.6 collective-permute-start.14
  105.7 5.0 %collective-permute-start.15 = (f32[8,128]{1,0:T(8,128)S(1)}, f32[8,128]{1,0:T(8,128)S(1)}, u32[]{:S(2)}, u32[]{:S(2)}) collective-permute-start(f32[8,128]{1,0:T(8,128)S(1)} %add.255), channel_id=1, source_target_pairs={{0,8},{1,9},{2,10},{3,11},{4,12},{5,13},{6,14},{7,15},{8,0},{9,1},... | collective-permute-start | bytes 12296 | tf_op jit(solution)/shard_map/ppermute | solution.py:864
  109.4 91.9 %collective-permute-start.25 = (f32[16,1024]{1,0:T(8,128)}, f32[16,1024]{1,0:T(8,128)}, u32[]{:S(2)}, u32[]{:S(2)}) collective-permute-start(f32[16,1024]{1,0:T(8,128)} %get-tuple-element.209), channel_id=1, source_target_pairs={{16,20},{17,21},{18,22},{19,23},{20,16},{21,17},{22,18},{23,19},{2... | collective-permute-start | bytes 196616 | tf_op jit(solution)/shard_map/ppermute | solution.py:871
  110.7 3.6 collective-permute-start.16
  133.8 3.6 collective-permute-start.18
  192.7 8.6 %collective-permute-start.34 = (f32[8,128]{1,0:T(8,128)S(1)}, f32[8,128]{1,0:T(8,128)S(1)}, u32[]{:S(2)}, u32[]{:S(2)}) collective-permute-start(f32[8,128]{1,0:T(8,128)S(1)} %add.270), channel_id=1, source_target_pairs={{0,2},{1,3},{2,0},{3,1},{4,6},{5,7},{6,4},{7,5},{8,10},{9,11},{10,... | collective-permute-start | bytes 12296 | tf_op jit(solution)/shard_map/ppermute | solution.py:864
  194.6 10.4 %collective-permute-start.26 = (f32[16,1024]{1,0:T(8,128)}, f32[16,1024]{1,0:T(8,128)S(1)}, u32[]{:S(2)}, u32[]{:S(2)}) collective-permute-start(f32[16,1024]{1,0:T(8,128)} %copy-done.123), channel_id=1, source_target_pairs={{0,8},{1,9},{2,10},{3,11},{4,12},{5,13},{6,14},{7,15},{8,20},{9,21... | collective-permute-start | bytes 196616 | tf_op jit(solution)/shard_map/ppermute | solution.py:871
  195.1 9.9 %collective-permute-start.27 = (f32[16,1024]{1,0:T(8,128)}, f32[16,1024]{1,0:T(8,128)S(1)}, u32[]{:S(2)}, u32[]{:S(2)}) collective-permute-start(f32[16,1024]{1,0:T(8,128)} %copy-done.122), channel_id=1, source_target_pairs={{0,20},{1,21},{2,22},{3,23},{4,16},{5,17},{6,18},{7,19},{8,28},{9,... | collective-permute-start | bytes 196616 | tf_op jit(solution)/shard_map/ppermute | solution.py:871
  198.9 6.0 %collective-permute-start.28 = (f32[16,1024]{1,0:T(8,128)S(1)}, f32[16,1024]{1,0:T(8,128)S(1)}, u32[]{:S(2)}, u32[]{:S(2)}) collective-permute-start(f32[16,1024]{1,0:T(8,128)S(1)} %copy-done.121), channel_id=1, source_target_pairs={{0,28},{1,29},{2,30},{3,31},{4,24},{5,25},{6,26},{7,27},{8,0},{9,1... | collective-permute-start | bytes 196616 | tf_op jit(solution)/shard_map/ppermute | solution.py:871
  201.3 3.6 collective-permute-start.35
  234.4 3.7 collective-permute-start.38
  238.1 4.2 collective-permute-start.40
  238.2 4.1 collective-permute-start.41
  238.9 4.5 collective-permute-start.42
  246.7 3.7 collective-permute-start.44
  254.5 4.5 collective-permute-start.48
  277.0 3.7 collective-permute-start.50
  280.7 3.6 collective-permute-start.52
  280.8 3.6 collective-permute-start.53
  281.5 4.5 collective-permute-start.54
  289.2 3.7 collective-permute-start.56
  293.7 3.6 collective-permute-start.58
  294.9 3.6 collective-permute-start.59
  297.0 4.5 collective-permute-start.60
  319.4 3.7 collective-permute-start.62
  323.9 4.5 collective-permute-start.66
  331.6 3.7 collective-permute-start.68
  337.3 3.6 collective-permute-start.71
  339.3 4.5 collective-permute-start.72
  348.9 21.4 %collective-permute-start.73 = (f32[32,1024]{1,0:T(8,128)S(1)}, f32[32,1024]{1,0:T(8,128)S(1)}, u32[]{:S(2)}, u32[]{:S(2)}) collective-permute-start(f32[32,1024]{1,0:T(8,128)S(1)} %get-tuple-element.293.kept_ref), channel_id=1, source_target_pairs={{16,20},{17,21},{18,22},{19,23},{20,16},{21,17},{22,18},{23,19},{2... | collective-permute-start | bytes 393224 | tf_op jit(solution)/shard_map/ppermute | solution.py:871
  349.6 20.7 %collective-permute-start.74 = (f32[32,1024]{1,0:T(8,128)S(1)}, f32[32,1024]{1,0:T(8,128)S(1)}, u32[]{:S(2)}, u32[]{:S(2)}) collective-permute-start(f32[32,1024]{1,0:T(8,128)S(1)} %get-tuple-element.290), channel_id=1, source_target_pairs={{0,8},{1,9},{2,10},{3,11},{4,12},{5,13},{6,14},{7,15},{8,16},{9,17... | collective-permute-start | bytes 393224 | tf_op jit(solution)/shard_map/ppermute | solution.py:871
  349.7 22.6 %collective-permute-start.75 = (f32[32,1024]{1,0:T(8,128)S(1)}, f32[32,1024]{1,0:T(8,128)S(1)}, u32[]{:S(2)}, u32[]{:S(2)}) collective-permute-start(f32[32,1024]{1,0:T(8,128)S(1)} %get-tuple-element.291), channel_id=1, source_target_pairs={{0,16},{1,17},{2,18},{3,19},{4,20},{5,21},{6,22},{7,23},{8,24},{9,... | collective-permute-start | bytes 393224 | tf_op jit(solution)/shard_map/ppermute | solution.py:871
  354.0 18.3 %collective-permute-start.76 = (f32[32,1024]{1,0:T(8,128)S(1)}, f32[32,1024]{1,0:T(8,128)S(1)}, u32[]{:S(2)}, u32[]{:S(2)}) collective-permute-start(f32[32,1024]{1,0:T(8,128)S(1)} %get-tuple-element.292), channel_id=1, source_target_pairs={{0,24},{1,25},{2,26},{3,27},{4,28},{5,29},{6,30},{7,31},{8,0},{9,1... | collective-permute-start | bytes 393224 | tf_op jit(solution)/shard_map/ppermute | solution.py:871
  372.3 3.6 collective-permute-start.78
  375.9 5.7 %collective-permute-start.80 = (f32[8,128]{1,0:T(8,128)S(1)}, f32[8,128]{1,0:T(8,128)S(1)}, u32[]{:S(2)}, u32[]{:S(2)}) collective-permute-start(f32[8,128]{1,0:T(8,128)S(1)} %add_add_fusion.3), channel_id=1, source_target_pairs={{0,8},{1,9},{2,10},{3,11},{4,12},{5,13},{6,14},{7,15},{8,0},{9,1},... | collective-permute-start | bytes 12296 | tf_op jit(solution)/shard_map/ppermute | solution.py:864
  380.1 4.5 collective-permute-start.82
  387.8 3.7 collective-permute-start.84
  394.3 4.5 collective-permute-start.88
  405.8 11.8 %collective-permute-start.89 = (f32[2048,128]{1,0:T(8,128)S(1)}, f32[2048,128]{1,0:T(8,128)S(1)}, u32[]{:S(2)}, u32[]{:S(2)}) collective-permute-start(f32[2048,128]{1,0:T(8,128)S(1)} %get-tuple-element.318), channel_id=1, source_target_pairs={{0,1},{1,0},{2,3},{3,2},{4,5},{5,4},{6,7},{7,6},{8,9},{9,8},{10,11... | collective-permute-start | bytes 3145736 | tf_op jit(solution)/shard_map/ppermute | solution.py:864
  405.9 11.3 %collective-permute-start.90 = (f32[16,1024]{1,0:T(8,128)S(1)}, f32[16,1024]{1,0:T(8,128)S(1)}, u32[]{:S(2)}, u32[]{:S(2)}) collective-permute-start(f32[16,1024]{1,0:T(8,128)S(1)} %get-tuple-element.320.refs_4_), channel_id=1, source_target_pairs={{24,4},{25,5},{26,6},{27,7},{28,0},{29,1},{30,2},{31,3}} | collective-permute-start | bytes 196616 | tf_op jit(solution)/shard_map/ppermute | solution.py:1086
  407.2 10.4 %collective-permute-start.91 = (f32[16,1024]{1,0:T(8,128)S(1)}, f32[16,1024]{1,0:T(8,128)S(1)}, u32[]{:S(2)}, u32[]{:S(2)}) collective-permute-start(f32[16,1024]{1,0:T(8,128)S(1)} %get-tuple-element.320.refs_4_), channel_id=1, source_target_pairs={{16,4},{17,5},{18,6},{19,7},{20,0},{21,1},{22,2},{23,3}} | collective-permute-start | bytes 196616 | tf_op jit(solution)/shard_map/ppermute | solution.py:1086
  408.5 9.1 %collective-permute-start.92 = (f32[16,1024]{1,0:T(8,128)S(1)}, f32[16,1024]{1,0:T(8,128)S(1)}, u32[]{:S(2)}, u32[]{:S(2)}) collective-permute-start(f32[16,1024]{1,0:T(8,128)S(1)} %get-tuple-element.320.refs_4_), channel_id=1, source_target_pairs={{8,0},{9,1},{10,2},{11,3},{12,4},{13,5},{14,6},{15,7}} | collective-permute-start | bytes 196616 | tf_op jit(solution)/shard_map/ppermute | solution.py:1086
  418.3 9.3 %collective-permute-start.93 = (f32[512,128]{1,0:T(8,128)S(1)}, f32[512,128]{1,0:T(8,128)S(1)}, u32[]{:S(2)}, u32[]{:S(2)}) collective-permute-start(f32[512,128]{1,0:T(8,128)S(1)} %get-tuple-element.327), channel_id=1, source_target_pairs={{0,8},{1,9},{2,10},{3,11},{4,12},{5,13},{6,14},{7,15},{8,0},{9,1},... | collective-permute-start | bytes 786440 | tf_op jit(solution)/shard_map/ppermute | solution.py:864
  418.4 13.5 %collective-permute-start.94 = (f32[512,128]{1,0:T(8,128)S(1)}, f32[512,128]{1,0:T(8,128)S(1)}, u32[]{:S(2)}, u32[]{:S(2)}) collective-permute-start(f32[512,128]{1,0:T(8,128)S(1)} %get-tuple-element.328), channel_id=1, source_target_pairs={{0,16},{1,17},{2,18},{3,19},{4,20},{5,21},{6,22},{7,23},{8,24},{9,... | collective-permute-start | bytes 786440 | tf_op jit(solution)/shard_map/ppermute | solution.py:864
  418.5 13.4 %collective-permute-start.95 = (f32[512,128]{1,0:T(8,128)S(1)}, f32[512,128]{1,0:T(8,128)S(1)}, u32[]{:S(2)}, u32[]{:S(2)}) collective-permute-start(f32[512,128]{1,0:T(8,128)S(1)} %get-tuple-element.329), channel_id=1, source_target_pairs={{0,24},{1,25},{2,26},{3,27},{4,28},{5,29},{6,30},{7,31},{8,16},{9,... | collective-permute-start | bytes 786440 | tf_op jit(solution)/shard_map/ppermute | solution.py:864
  432.6 4.5 collective-permute-start.96
  432.7 5.9 %collective-permute-start.97 = (f32[128,128]{1,0:T(8,128)S(1)}, f32[128,128]{1,0:T(8,128)S(1)}, u32[]{:S(2)}, u32[]{:S(2)}) collective-permute-start(f32[128,128]{1,0:T(8,128)S(1)} %get-tuple-element.332), channel_id=1, source_target_pairs={{0,4},{1,5},{2,6},{3,7},{4,0},{5,1},{6,2},{7,3},{8,12},{9,13},{10,... | collective-permute-start | bytes 196616 | tf_op jit(solution)/shard_map/ppermute | solution.py:864
  434.7 6.1 %collective-permute-start.98 = (f32[128,128]{1,0:T(8,128)S(1)}, f32[128,128]{1,0:T(8,128)S(1)}, u32[]{:S(2)}, u32[]{:S(2)}) collective-permute-start(f32[128,128]{1,0:T(8,128)S(1)} %get-tuple-element.333), channel_id=1, source_target_pairs={{0,6},{1,7},{2,4},{3,5},{4,2},{5,3},{6,0},{7,1},{8,14},{9,15},{10,... | collective-permute-start | bytes 196616 | tf_op jit(solution)/shard_map/ppermute | solution.py:864
  441.3 5.6 %collective-permute-start.100 = (f32[128,128]{1,0:T(8,128)S(1)}, f32[128,128]{1,0:T(8,128)S(1)}, u32[]{:S(2)}, u32[]{:S(2)}) collective-permute-start(f32[128,128]{1,0:T(8,128)S(1)} %reduce_part.5.refs_0_), channel_id=1, source_target_pairs={{0,4},{1,5},{2,6},{3,7},{4,0},{5,1},{6,2},{7,3},{8,12},{9,13},{10,... | collective-permute-start | bytes 196616 | tf_op jit(solution)/shard_map/ppermute | solution.py:864
  441.5 6.1 %collective-permute-start.101 = (f32[128,128]{1,0:T(8,128)S(1)}, f32[128,128]{1,0:T(8,128)S(1)}, u32[]{:S(2)}, u32[]{:S(2)}) collective-permute-start(f32[128,128]{1,0:T(8,128)S(1)} %reduce_part.5.refs_0_), channel_id=1, source_target_pairs={{0,6},{1,7},{2,4},{3,5},{4,2},{5,3},{6,0},{7,1},{8,14},{9,15},{10,... | collective-permute-start | bytes 196616 | tf_op jit(solution)/shard_map/ppermute | solution.py:864
  443.8 4.5 collective-permute-start.99
  448.9 7.6 %collective-permute-start.102 = (f32[512,128]{1,0:T(8,128)S(1)}, f32[512,128]{1,0:T(8,128)S(1)}, u32[]{:S(2)}, u32[]{:S(2)}) collective-permute-start(f32[512,128]{1,0:T(8,128)S(1)} %gather_part.2.refs_0_), channel_id=1, source_target_pairs={{0,8},{1,9},{2,10},{3,11},{4,12},{5,13},{6,14},{7,15},{8,0},{9,1},... | collective-permute-start | bytes 786440 | tf_op jit(solution)/shard_map/ppermute | solution.py:864
  451.1 9.6 %collective-permute-start.103 = (f32[512,128]{1,0:T(8,128)S(1)}, f32[512,128]{1,0:T(8,128)S(1)}, u32[]{:S(2)}, u32[]{:S(2)}) collective-permute-start(f32[512,128]{1,0:T(8,128)S(1)} %gather_part.2.refs_0_), channel_id=1, source_target_pairs={{0,16},{1,17},{2,18},{3,19},{4,20},{5,21},{6,22},{7,23},{8,24},{9,... | collective-permute-start | bytes 786440 | tf_op jit(solution)/shard_map/ppermute | solution.py:864
  451.1 9.6 %collective-permute-start.104 = (f32[512,128]{1,0:T(8,128)S(1)}, f32[512,128]{1,0:T(8,128)S(1)}, u32[]{:S(2)}, u32[]{:S(2)}) collective-permute-start(f32[512,128]{1,0:T(8,128)S(1)} %gather_part.2.refs_0_), channel_id=1, source_target_pairs={{0,24},{1,25},{2,26},{3,27},{4,28},{5,29},{6,30},{7,31},{8,16},{9,... | collective-permute-start | bytes 786440 | tf_op jit(solution)/shard_map/ppermute | solution.py:864
  (173 other events, 2311.8 us)

commit v6 on v5

--- a/solution.py
+++ b/solution.py
@@ -27,13 +27,6 @@
 def halves(value):
     high = value.astype(BF16)
     return high, (value - high.astype(F32)).astype(BF16)
-
-
-def thirds(value):
-    high = value.astype(BF16)
-    rest = value - high.astype(F32)
-    middle = rest.astype(BF16)
-    return high, middle, (rest - middle.astype(F32)).astype(BF16)
 
 
 def stacked(value):
@@ -143,16 +136,6 @@
     return dot(left, right, 0, 0)
 
 
-def attention_scores(key_rows, query_rows):
-    key_high, key_mid, key_low = thirds(key_rows)
-    query_high, query_mid, query_low = thirds(query_rows)
-    left = jnp.concatenate([key_high, key_high, key_mid, key_mid, key_high, key_low], axis=0)
-    right = jnp.concatenate(
-        [query_high, query_mid, query_high, query_mid, query_low, query_high], axis=0
-    )
-    return dot(left, right, 0, 0)
-
-
 def heads_of(channels, cells, block_size):
     width = channels // HEADS
     return [
@@ -162,9 +145,9 @@
     ]
 
 
-def of_head(value, rows):
+def of_head(value, rows, other=0.0):
     channel = lax.broadcasted_iota(jnp.int32, value.shape, 1)
-    return jnp.where((channel >= rows.start) & (channel < rows.stop), value, 0.0)
+    return jnp.where((channel >= rows.start) & (channel < rows.stop), value, other)
 
 
 def below(rows, offset):
@@ -172,9 +155,11 @@
 
 
 def entered_inlet_kernel(lon, ids_ref, own_ref, arrived_ref, *refs):
-    state_ref = refs[3]
-    state_ref[...] = jnp.where(ids_ref[0] < 2, own_ref[...], arrived_ref[...])
-    inlet_kernel(lon, state_ref, *refs[:3], *refs[4:])
+    state_ref, cot_ref = refs[3], refs[4]
+    size = state_ref.shape[0]
+    state_ref[...] = jnp.where(ids_ref[0] < 2, own_ref[:size], arrived_ref[:size])
+    cot_ref[...] = jnp.where(ids_ref[0] < 2, own_ref[size:], arrived_ref[size:])
+    inlet_kernel(lon, state_ref, *refs[:3], *refs[5:])
 
 
 def inlet_kernel(
@@ -209,14 +194,14 @@
     sums_ref[...] = sums_of(pre, pre)
 
 
-def act_two_channels(inner, pre_two, sums, gain, shift, count):
+def act_two_of(inner, pre_two, sums, gain, shift, count):
     mean, unused_scale, factor = norm_of(sums, gain, count)
-    return (inner * sigmoid(inner) + (pre_two - mean) * factor + shift).T
-
-
-def project(w_qkv_ref, act_two, head_width, qkv_ref):
-    channels = act_two.shape[0]
-    rows = folded(dot(w_qkv_ref[...], stacked(act_two)), 0)
+    return inner * sigmoid(inner) + (pre_two - mean) * factor + shift
+
+
+def project(w_qkv_ref, act_two_halves, head_width, qkv_ref):
+    channels = act_two_halves.shape[0] // 2
+    rows = folded(dot(w_qkv_ref[...], act_two_halves), 0)
     qkv_ref[:channels] = rows[:channels] * (LOG2_E / math.sqrt(head_width))
     qkv_ref[channels:] = rows[channels:]
 
@@ -224,56 +209,50 @@
 def outlet_kernel(
     lon, count, block_size, step_size, quantities,
     state_ref, inner_ref, pre_two_ref, sums_two_ref, gain_ref, shift_ref,
-    w_qkv_ref, w_mixer_ref, w_velocity_ref, b_velocity_ref,
-    out_ref, packed_ref, qkv_ref, mixed_ref, weight_ref, powers_ref,
-    slots_ref, done_ref,
+    w_heads_ref, w_mixer_ref, w_velocity_ref, b_velocity_ref,
+    out_ref, packed_ref, mixed_ref, top_ref, weight_ref,
+    query_ref,
 ):
-    channels = inner_ref.shape[1]
-    cells = inner_ref.shape[0]
-    act_two = act_two_channels(
+    cells, channels = inner_ref.shape
+    act_two = act_two_of(
         inner_ref[...], pre_two_ref[...], sums_two_ref[...], gain_ref[...], shift_ref[...], count
     )
-    project(w_qkv_ref, act_two, channels // HEADS, qkv_ref)
+    projected = folded(dot(beside(act_two), w_heads_ref[...]), 1)
+    query = projected[:, : HEADS * channels]
+    query_high = query.astype(BF16).astype(F32)
+    channel = lax.rem(lax.broadcasted_iota(jnp.int32, query.shape, 1), channels)
+    query_ref[...] = jnp.where(channel < channels // 2, query_high, query - query_high).astype(BF16)
+    key = projected[:, HEADS * channels : (HEADS + 1) * channels]
+    key_high, key_low = halves((key * (LOG2_E / math.sqrt(channels // HEADS))).T)
+    value = projected[:, (HEADS + 1) * channels :]
     heads = heads_of(channels, cells, block_size)
 
     def scores_of(turn):
         rows, lanes = heads[turn]
-        return attention_scores(qkv_ref[below(rows, channels), lanes], qkv_ref[rows, lanes])
-
-    def keep(turn):
-        return pltpu.make_async_copy(
-            slots_ref.at[turn % 2], powers_ref.at[turn], done_ref.at[turn % 2]
-        )
+        right = [half[rows, lanes] for half in (key_high, key_low, key_high, key_low)]
+        start = turn % HEADS * channels
+        return dot(query_ref[lanes, start : start + channels], jnp.concatenate(right, axis=0))
 
     following = scores_of(0)
-    value_cells = qkv_ref[2 * channels :].T
     for turn, (rows, lanes) in enumerate(heads):
         scores = following
         if turn + 1 < len(heads):
             following = scores_of(turn + 1)
-        top = jnp.max(scores, axis=0, keepdims=True)
+        top = jnp.max(scores, axis=1, keepdims=True)
         powers = jnp.exp2(scores - top)
-        weight = 1.0 / jnp.sum(powers, axis=0, keepdims=True)
-        weight_ref[turn : turn + 1] = weight
+        weight = 1.0 / jnp.sum(powers, axis=1, keepdims=True)
         high, low = halves(powers)
-        if turn >= 2:
-            keep(turn - 2).wait()
-        slots_ref[turn % 2, 0] = high
-        slots_ref[turn % 2, 1] = low
-        keep(turn).start()
-        value = beside(of_head(value_cells[lanes], rows))
-        part = dot(high, value, 0, 0) + dot(low, value, 0, 0)
-        mixed = part if rows.start == 0 else mixed + part
+        right = beside(of_head(value[lanes], rows))
+        own = folded(dot(high, right) + dot(low, right), 1) * weight
+        all_top, all_weight = [jnp.broadcast_to(part, own.shape) for part in (top, weight)]
+        if rows.start:
+            own = own + mixed
+            all_top, all_weight = of_head(all_top, rows, tops), of_head(all_weight, rows, weights)
+        mixed, tops, weights = own, all_top, all_weight
         if rows.stop == channels:
-            mixed_ref[:, lanes] = folded(mixed, 1).T
-            first = turn + 1 - HEADS
-            for head in range(HEADS):
-                own_rows = heads[head][0]
-                mixed_ref[own_rows, lanes] = (
-                    mixed_ref[own_rows, lanes] * weight_ref[first + head : first + head + 1]
-                )
-    act_three = act_two + folded(dot(w_mixer_ref[...], stacked(mixed_ref[...])), 0)
-    parts = folded(dot(w_velocity_ref[...], stacked(act_three)), 0)
+            mixed_ref[lanes], top_ref[lanes], weight_ref[lanes] = mixed, tops, weights
+    act_three = act_two + folded(dot(beside(mixed_ref[...]), w_mixer_ref[...]), 1)
+    parts = folded(dot(w_velocity_ref[...], stacked(act_three.T)), 0)
     forcing = jnp.zeros((2 * GROUP, cells), F32) + b_velocity_ref[...]
     for column, lon_offset in enumerate((-1, 0, 1)):
         total = None
@@ -289,32 +268,23 @@
     out_ref[:GROUP] = advected(state, step_size, lon)
     out_ref[GROUP:] = flows + step_size * (forcing - flows)
     put_packed(packed_ref, out_ref[...], quantities)
-    for turn in range(max(0, len(heads) - 2), len(heads)):
-        keep(turn).wait()
 
 
 def outlet_back_kernel(
     lon, count, block_size, step_size, quantities, sections, step,
     ids_ref,
     state_ref, d_next_ref, cots_ref, inner_ref, pre_two_ref, sums_two_ref, gain_ref, shift_ref,
-    qkv_ref, mixed_ref, weight_ref, powers_ref,
-    w_mixer_ref, w_qkv_back_ref, w_mixer_back_ref, w_velocity_back_ref,
+    mixed_ref, top_ref, weight_ref,
+    w_qkv_ref, w_mixer_ref, w_qkv_back_ref, w_mixer_back_ref, w_velocity_back_ref,
     acc_qkv_ref, acc_mixer_ref, acc_velocity_ref, acc_small_ref,
     d_state_ref, d_two_ref, sums_ref,
     out_qkv_ref, out_mixer_ref, out_velocity_ref, out_small_ref,
-    d_mixed_ref, d_qkv_ref, seed_ref, slots_ref, done_ref,
+    d_mixed_ref, d_qkv_ref, seed_ref, qkv_ref, mixed_rows_ref, top_rows_ref,
 ):
     channels = inner_ref.shape[1]
     cells = inner_ref.shape[0]
     heads = heads_of(channels, cells, block_size)
 
-    def fetch(turn):
-        return pltpu.make_async_copy(
-            powers_ref.at[turn], slots_ref.at[turn % 2], done_ref.at[turn % 2]
-        )
-
-    for turn in range(min(2, len(heads))):
-        fetch(turn).start()
     state = state_ref[...]
     packed = cots_ref[lax.rem(ids_ref[0] - step + sections, sections)]
     put_groups(seed_ref, packed[: 3 * quantities])
@@ -335,26 +305,30 @@
     d_parts = stacked(jnp.concatenate(pieces, axis=0))
     d_three = folded(dot(w_velocity_back_ref[...], d_parts), 0)
     d_three_halves = stacked(d_three)
-    d_mixed_ref[...] = folded(dot(w_mixer_back_ref[...], d_three_halves), 0)
-    for turn, (rows, lanes) in enumerate(heads):
-        d_mixed_ref[rows, lanes] = d_mixed_ref[rows, lanes] * weight_ref[turn : turn + 1]
+    d_mixed_ref[...] = folded(dot(w_mixer_back_ref[...], d_three_halves), 0) * weight_ref[...].T
+    mixed_rows_ref[...] = mixed_ref[...].T
+    top_rows_ref[...] = top_ref[...].T
+    act_two = act_two_of(
+        inner_ref[...], pre_two_ref[...], sums_two_ref[...], gain_ref[...], shift_ref[...], count
+    ).T
+    act_two_halves = stacked(act_two)
+    project(w_qkv_ref, act_two_halves, channels // HEADS, qkv_ref)
     d_mixed_cells = d_mixed_ref[...].T
     query_cells = qkv_ref[:channels].T
 
-    def d_powers_of(turn):
+    def products_of(turn):
         rows, lanes = heads[turn]
-        d_mixed = d_mixed_ref[rows, lanes]
-        return d_mixed, row_products(qkv_ref[below(rows, 2 * channels), lanes], d_mixed)
-
-    following = d_powers_of(0)
+        scores = row_products(qkv_ref[below(rows, channels), lanes], qkv_ref[rows, lanes])
+        return scores, row_products(qkv_ref[below(rows, 2 * channels), lanes], d_mixed_ref[rows, lanes])
+
+    following = products_of(0)
     for turn, (rows, lanes) in enumerate(heads):
-        d_mixed, d_powers = following
+        scores, d_powers = following
         if turn + 1 < len(heads):
-            following = d_powers_of(turn + 1)
-        inner_sum = jnp.sum(d_mixed * mixed_ref[rows, lanes], axis=0, keepdims=True)
-        fetch(turn).wait()
-        power_high, power_low = slots_ref[turn % 2, 0], slots_ref[turn % 2, 1]
-        powers = power_high.astype(F32) + power_low.astype(F32)
+            following = products_of(turn + 1)
+        inner_sum = jnp.sum(d_mixed_ref[rows, lanes] * mixed_rows_ref[rows, lanes], axis=0, keepdims=True)
+        powers = jnp.exp2(scores - top_rows_ref[rows.start : rows.start + 1, lanes])
+        power_high, power_low = halves(powers)
         d_high, d_low = halves(powers * (d_powers - inner_sum))
         right = beside(of_head(d_mixed_cells[lanes], rows))
         d_value = dot(power_high, right) + dot(power_low, right) + (d_value if rows.start else 0.0)
@@ -362,8 +336,6 @@
         d_key = dot(d_high, right) + dot(d_low, right) + (d_key if rows.start else 0.0)
         key_halves = stacked(qkv_ref[below(rows, channels), lanes])
         d_query = folded(dot(key_halves, d_high) + dot(key_halves, d_low), 0)
-        if turn + 2 < len(heads):
-            fetch(turn + 2).start()
         d_qkv_ref[rows, lanes] = d_query * (1.0 / math.sqrt(channels // HEADS))
         if rows.stop == channels:
             d_qkv_ref[channels : 2 * channels, lanes] = folded(d_key, 1).T * (1.0 / LOG2_E)
@@ -378,14 +350,11 @@
     def pairs(left, right):
         return folded(folded(dot(left, right, 1, 1), 0), 1)
 
-    act_two = act_two_channels(
-        inner_ref[...], pre_two_ref[...], sums_two_ref[...], gain_ref[...], shift_ref[...], count
-    )
-    mixed_halves = stacked(mixed_ref[...])
+    mixed_halves = stacked(mixed_rows_ref[...])
     act_three = act_two + folded(dot(w_mixer_ref[...], mixed_halves), 0)
     out_velocity_ref[...] = acc_velocity_ref[...] + pairs(d_parts, stacked(act_three))
     out_mixer_ref[...] = acc_mixer_ref[...] + pairs(mixed_halves, d_three_halves)
-    out_qkv_ref[...] = acc_qkv_ref[...] + pairs(stacked(act_two), d_qkv_halves)
+    out_qkv_ref[...] = acc_qkv_ref[...] + pairs(act_two_halves, d_qkv_halves)
     bias = jnp.sum(d_forcing, axis=1, keepdims=True)
     row = lax.broadcasted_iota(jnp.int32, (GROUP, channels), 0)
     small = jnp.where(row == 0, sums[1:2] * scale, jnp.where(row == 1, sums[0:1], 0.0))
@@ -506,25 +475,23 @@
     return copies
 
 
-def enter_kernel(plan, ids_ref, order_ref, state_ref, out_ref, near_ref, rows_ref, done_ref):
-    (copy,) = fetched([state_ref], [near_ref], done_ref)
-    copy.wait()
+def enter_kernel(plan, ids_ref, order_ref, state_ref, cot_ref, *refs):
+    out_refs, (near_ref, near_cot_ref, rows_ref, done_ref) = refs[:-4], refs[-4:]
+    copies = fetched([state_ref, cot_ref], [near_ref, near_cot_ref], done_ref)
+    size = rows_ref.shape[0]
+    copies[0].wait()
     place = order_ref[0, plan.slot(ids_ref[0], ids_ref[1])]
-    for row in range(rows_ref.shape[0]):
+    for row in range(size):
         rows_ref[row : row + 1] = near_ref[row, pl.ds(place, 1)]
-    put_groups(out_ref, rows_ref[...])
-
-
-def seeds_kernel(plan, ids_ref, order_ref, cot_ref, *refs):
-    out_refs, near_ref, done_ref = refs[:-2], refs[-2], refs[-1]
-    (copy,) = fetched([cot_ref], [near_ref], done_ref)
-    copy.wait()
+    put_groups(out_refs[0].at[: 3 * GROUP], rows_ref[...])
+    copies[1].wait()
     for steps, out_ref in enumerate(out_refs):
+        start = 0 if steps else 3 * GROUP
         target = lax.rem(ids_ref[0] + steps, plan.sections)
         place = order_ref[0, plan.slot(target, ids_ref[1])]
-        out_ref[...] = jnp.zeros(out_ref.shape, F32)
-        for row in range(near_ref.shape[0]):
-            out_ref[row : row + 1] = near_ref[row, pl.ds(place, 1)]
+        out_ref[start:] = jnp.zeros((2 * GROUP, out_ref.shape[1]), F32)
+        for row in range(size):
+            out_ref[start + row : start + row + 1] = near_cot_ref[row, pl.ds(place, 1)]
 
 
 def leave_kernel(plan, ids_ref, *refs):
@@ -571,19 +538,31 @@
         out_ref[place * rows : (place + 1) * rows] = jnp.concatenate([half, half], axis=1)
 
 
-def first_weights_kernel(
-    lon, quantities, w_input_ref, w_first_ref, b_input_ref, maps_ref,
-    static_part_ref, moving_cat_ref, moving_back_ref, first_cat_ref,
-    patches_ref, weight_ref, taps_ref, *near_refs,
+def weights_kernel(
+    lon, quantities,
+    w_input_ref, maps_ref, b_input_ref, w_first_ref, w_second_ref,
+    w_query_ref, w_key_ref, w_value_ref, w_mixer_ref, w_velocity_ref,
+    static_part_ref, moving_cat_ref, moving_back_ref, first_cat_ref, second_cat_ref,
+    heads_ref, mixer_cells_ref, qkv_ref, qkv_back_ref, mixer_ref, mixer_back_ref, velocity_ref, velocity_back_ref,
+    first_back_ref, second_back_ref,
+    patches_ref, weight_ref, taps_ref, rows_ref, *near_refs,
 ):
     near_refs, done_ref = near_refs[:-1], near_refs[-1]
-    copies = fetched([w_input_ref, maps_ref, b_input_ref, w_first_ref], near_refs, done_ref)
-    w_input_ref, maps_ref, b_input_ref, w_first_ref = near_refs
-    copies[0].wait()
+    copies = fetched(
+        [w_input_ref, maps_ref, b_input_ref, w_first_ref, w_second_ref,
+         w_query_ref, w_key_ref, w_value_ref, w_mixer_ref, w_velocity_ref],
+        near_refs, done_ref,
+    )
+    (
+        w_input_ref, maps_ref, b_input_ref, w_first_ref, w_second_ref,
+        w_query_ref, w_key_ref, w_value_ref, w_mixer_ref, w_velocity_ref,
+    ) = near_refs
     channels = w_input_ref.shape[2]
     moving = 5 * quantities
     statics = maps_ref.shape[0]
     taps_ref[...] = jnp.zeros(taps_ref.shape, F32)
+    rows_ref[...] = jnp.zeros(rows_ref.shape, F32)
+    copies[0].wait()
     for tap in range(9):
         row, column = divmod(tap, 3)
         for group in range(5):
@@ -602,32 +581,22 @@
     )
     fill_patches(patches_ref, maps.T, lon)
     static_part_ref[...] = conv_patches(patches_ref, weight_ref, lon) + b_input_ref[...]
-    copies[3].wait()
+    for copy in copies[3:]:
+        copy.wait()
     put_conv_weight(first_cat_ref, [w_first_ref[tap] for tap in range(9)])
-
-
-def second_weights_kernel(far_ref, out_ref, w_second_ref, done_ref):
-    fetched([far_ref], [w_second_ref], done_ref)[0].wait()
-    put_conv_weight(out_ref, [w_second_ref[tap] for tap in range(9)])
-
-
-def outlet_weights_kernel(
-    quantities, w_query_ref, w_key_ref, w_value_ref, w_mixer_ref, w_velocity_ref,
-    qkv_ref, qkv_back_ref, mixer_ref, mixer_back_ref, velocity_ref, velocity_back_ref,
-    rows_ref, *near_refs,
-):
-    near_refs, done_ref = near_refs[:-1], near_refs[-1]
-    copies = fetched([w_query_ref, w_key_ref, w_value_ref, w_mixer_ref, w_velocity_ref], near_refs, done_ref)
-    w_query_ref, w_key_ref, w_value_ref, w_mixer_ref, w_velocity_ref = near_refs
-    for copy in copies:
-        copy.wait()
+    put_conv_weight(second_cat_ref, [w_second_ref[tap] for tap in range(9)])
+    put_conv_weight(first_back_ref, [w_first_ref[8 - tap].T for tap in range(9)])
+    put_conv_weight(second_back_ref, [w_second_ref[8 - tap].T for tap in range(9)])
     parts = [ref[...] for ref in (w_query_ref, w_key_ref, w_value_ref)]
-    put_left_weight(qkv_ref, jnp.concatenate([part.T for part in parts], axis=0))
+    turned = [part.T for part in parts]
+    width = channels // HEADS
+    repeated = [turned[0][head * width : (head + 1) * width] for head in range(HEADS) for unused in range(HEADS)]
+    put_conv_weight(heads_ref, [jnp.concatenate([jnp.concatenate(repeated, axis=0).T, parts[1], parts[2]], axis=1)])
+    put_conv_weight(mixer_cells_ref, [w_mixer_ref[...]])
+    put_left_weight(qkv_ref, jnp.concatenate(turned, axis=0))
     put_left_weight(qkv_back_ref, jnp.concatenate(parts, axis=1))
     put_left_weight(mixer_ref, w_mixer_ref[...].T)
     put_left_weight(mixer_back_ref, w_mixer_ref[...])
-    channels = w_mixer_ref.shape[0]
-    rows_ref[...] = jnp.zeros(rows_ref.shape, F32)
     for tap in range(9):
         for group in range(2):
             start = (tap * 2 + group) * GROUP
@@ -637,13 +606,6 @@
     size = 18 * GROUP
     put_left_weight(velocity_ref, rows_ref[:size])
     put_left_weight(velocity_back_ref, rows_ref[...].T[:, :size])
-
-
-def back_weights_kernel(far_first_ref, far_second_ref, first_ref, second_ref, w_first_ref, w_second_ref, done_ref):
-    for copy in fetched([far_first_ref, far_second_ref], [w_first_ref, w_second_ref], done_ref):
-        copy.wait()
-    put_conv_weight(first_ref, [w_first_ref[8 - tap].T for tap in range(9)])
-    put_conv_weight(second_ref, [w_second_ref[8 - tap].T for tap in range(9)])
 
 
 def index_of(ids_ref, plan, bits):
@@ -766,30 +728,29 @@
     bias_ref[...] = take(GROUP)[0:1]
 
 
-def call(kernel, outs, scratch=(), aliases=None, name=None, scalars=0, kinds=None, far_in=(), far_out=()):
+def call(kernel, outs, scratch=(), aliases=None, name=None, scalars=0, kinds=None, far_in=(), limit=None):
     kinds = kinds or [F32] * len(outs)
 
     def run(*operands):
         places = [pltpu.SMEM] * scalars + [pltpu.VMEM] * (len(operands) - scalars)
         for place in far_in:
             places[place] = pltpu.HBM
-        out_places = [pltpu.HBM if place in far_out else pltpu.VMEM for place in range(len(outs))]
         return pl.pallas_call(
             kernel,
             out_shape=tuple(jax.ShapeDtypeStruct(shape, kind) for shape, kind in zip(outs, kinds)),
             in_specs=[pl.BlockSpec(memory_space=place) for place in places],
-            out_specs=tuple(pl.BlockSpec(memory_space=place) for place in out_places),
+            out_specs=tuple(pl.BlockSpec(memory_space=pltpu.VMEM) for unused in outs),
             scratch_shapes=scratch,
             input_output_aliases=aliases or {},
-            compiler_params=pltpu.CompilerParams(vmem_limit_bytes=VMEM_LIMIT),
+            compiler_params=pltpu.CompilerParams(vmem_limit_bytes=limit or VMEM_LIMIT),
             name=name,
         )(*operands)
 
     return run
 
 
-KEPT_STEPS = 4
 VMEM_LIMIT = 24 * 1024 * 1024
+ALONE_LIMIT = 56 * 1024 * 1024
 
 
 def in_groups(array, axis, groups):
@@ -871,10 +832,22 @@
     return lax.ppermute(value, ("section", "dp"), going)
 
 
-def micro_sum(plan, value, paired=False):
-    for bits in [[bit] for bits in plan.sum_rounds for bit in bits] if paired else plan.sum_rounds:
-        value = value + sum(exchanged(value, mask) for mask in masks_of(bits))
-    return value
+def micro_sum(plan, value, first_core):
+    if not plan.halved or plan.half != 4:
+        for bits in plan.sum_rounds:
+            value = value + sum(exchanged(value, mask) for mask in masks_of(bits))
+        return value
+    value = value + exchanged(value, 1)
+    plane = masks_of([plan.dp, 2 * plan.dp])
+    other = [mask ^ 2 for mask in plane + [0]]
+    own = range(plan.sections * plan.dp)
+    total = value * first_core
+    for turn in range(4):
+        pairs = [(device, device ^ other[turn]) for device in own if device & 1]
+        if turn < 3:
+            pairs += [(device, device ^ plane[turn]) for device in own if not device & 1]
+        total = total + lax.ppermute(value, ("section", "dp"), pairs)
+    return total + exchanged(total, 1)
 
 
 def on_device(
@@ -924,37 +897,33 @@
     def near(*arrays):
         return [pltpu.VMEM(array.shape, F32) for array in arrays] + [pltpu.SemaphoreType.DMA((len(arrays),))]
 
-    state_rows = jnp.swapaxes(state_start, 0, 1)
-    (own_state,) = call(
-        functools.partial(enter_kernel, plan), [state_shape],
-        [pltpu.VMEM(state_rows.shape, F32), pltpu.VMEM((3 * quantities, cells), F32), pltpu.SemaphoreType.DMA((1,))],
-        name="enter", scalars=2, far_in=[2],
-    )(ids, grouping, state_rows)
-    arrived_state = moved(own_state, plan.to_workers(0))
-
-    static_part, moving_cat, moving_back_cat, first_cat = call(
-        functools.partial(first_weights_kernel, lon, quantities),
-        [plane, (6 * channels, 2 * channels), (6 * channels, 2 * channels), conv],
-        [patches, pltpu.VMEM(conv, BF16), pltpu.VMEM((12, channels, channels), F32)]
-        + near(w_input, static_maps, b_input[None], w_first),
-        name="first_weights", kinds=[F32, BF16, BF16, BF16], far_in=range(4),
-    )(w_input, w_first, b_input[None], static_maps)
-    (second_cat,) = call(
-        second_weights_kernel, [conv], near(w_second), name="second_weights", kinds=[BF16], far_in=[0]
-    )(w_second)
+    state_rows, cot_rows = jnp.swapaxes(state_start, 0, 1), jnp.swapaxes(cotangent[0], 0, 1)
+    entry, *sent_cots = call(
+        functools.partial(enter_kernel, plan), [(5 * GROUP, cells)] + [packed] * (segments - 1),
+        [pltpu.VMEM(state_rows.shape, F32)] * 2
+        + [pltpu.VMEM((3 * quantities, cells), F32), pltpu.SemaphoreType.DMA((2,))],
+        name="enter", scalars=2, far_in=[2, 3], limit=ALONE_LIMIT,
+    )(ids, grouping, state_rows, cot_rows)
+    arrived = moved(entry, plan.to_workers(0))
+    first_core = (1.0 - lax.rem(ids[1], 2).astype(F32)) * jnp.ones(small, F32)
     w_velocity_rows = jnp.swapaxes(w_velocity, 1, 2)
-    qkv_cat, qkv_back_cat, mixer_cat, mixer_back_cat, out_cat, out_back_cat = call(
-        functools.partial(outlet_weights_kernel, quantities),
-        [(6 * channels, 2 * channels), (2 * channels, 6 * channels), (2 * channels, 2 * channels),
-         (2 * channels, 2 * channels), (36 * GROUP, 2 * channels), (2 * channels, 36 * GROUP)],
-        [pltpu.VMEM((2 * channels, channels), F32)]
-        + near(w_query, w_key, w_value, w_mixer, w_velocity_rows),
-        name="outlet_weights", kinds=[BF16] * 6, far_in=range(5),
-    )(w_query, w_key, w_value, w_mixer, w_velocity_rows)
-    first_back_cat, second_back_cat = call(
-        back_weights_kernel, [conv, conv], near(w_first, w_second), name="back_weights", kinds=[BF16, BF16],
-        far_in=range(2),
-    )(w_first, w_second)
+    weights = (
+        w_input, static_maps, b_input[None], w_first, w_second, w_query, w_key, w_value, w_mixer, w_velocity_rows
+    )
+    moving_conv, square_conv = (6 * channels, 2 * channels), (2 * channels, 2 * channels)
+    (
+        static_part, moving_cat, moving_back_cat, first_cat, second_cat,
+        heads_cat, mixer_cells, qkv_cat, qkv_back_cat, mixer_cat, mixer_back_cat, out_cat, out_back_cat,
+        first_back_cat, second_back_cat,
+    ) = call(
+        functools.partial(weights_kernel, lon, quantities),
+        [plane, moving_conv, moving_conv, conv, conv,
+         (2 * channels, 2 * (HEADS + 2) * channels), square_conv, moving_conv, moving_conv[::-1],
+         square_conv, square_conv, (36 * GROUP, 2 * channels), (2 * channels, 36 * GROUP), conv, conv],
+        [patches, pltpu.VMEM(conv, BF16), pltpu.VMEM((12, channels, channels), F32),
+         pltpu.VMEM((2 * channels, channels), F32)] + near(*weights),
+        name="weights", kinds=[F32] + [BF16] * 14, far_in=range(10), limit=ALONE_LIMIT,
+    )(*weights)
     b_out = in_groups(b_velocity[:, None], 0, 2)
     gain_one, shift_one = gain_first[None], shift_first[None]
     gain_two, shift_two = gain_second[None], shift_second[None]
@@ -965,13 +934,10 @@
     middle = call(
         functools.partial(middle_kernel, lon, count), [plane, small], [patches], name="middle"
     )
-    heads = HEADS * (cells // block_size)
-    powers = (heads, 2, block_size, block_size)
-    slots = [pltpu.VMEM((2,) + powers[1:], BF16), pltpu.SemaphoreType.DMA((2,))]
     outlet = call(
         functools.partial(outlet_kernel, lon, count, block_size, step_size, quantities),
-        [state_shape, packed, (3 * channels, cells), (channels, cells), (heads, block_size), powers],
-        slots, name="outlet", kinds=[F32] * 5 + [BF16], far_out=[5],
+        [state_shape, packed, plane, plane, plane],
+        [pltpu.VMEM((cells, HEADS * channels), BF16)], name="outlet",
     )
 
     def outlet_back(step):
@@ -979,8 +945,8 @@
             functools.partial(outlet_back_kernel, lon, count, block_size, step_size, quantities, segments, step),
             [state_shape, plane, small, (channels, 3 * channels), (channels, channels),
              (18 * GROUP, channels), (3 * GROUP, channels)],
-            [narrow, wide, pltpu.VMEM(state_shape, F32)] + slots,
-            {17: 3, 18: 4, 19: 5, 20: 6}, name="outlet_back", scalars=1, far_in=[12],
+            [narrow, wide, pltpu.VMEM(state_shape, F32), wide, narrow, narrow],
+            {17: 3, 18: 4, 19: 5, 20: 6}, name="outlet_back", scalars=1,
         )
 
     middle_back = call(
@@ -994,38 +960,33 @@
         {11: 2, 12: 3, 13: 4}, name="inlet_back",
     )
 
-    state = own_state
+    state = entry[: 3 * GROUP]
     path, saved = [], []
     cots = None
     for step in range(segments):
-        if plan.halved and not step:
-            state, inner, pre_one, sums_one = call(
-                functools.partial(entered_inlet_kernel, lon), [state_shape, plane, plane, small], [patches],
+        if not step:
+            if not plan.halved:
+                arrived = entry
+            state, own_cot, inner, pre_one, sums_one = call(
+                functools.partial(entered_inlet_kernel, lon), [state_shape, packed, plane, plane, small], [patches],
                 name="inlet", scalars=1,
-            )(ids, own_state, arrived_state, static_part, moving_cat, first_cat)
+            )(ids, entry, arrived, static_part, moving_cat, first_cat)
         else:
             inner, pre_one, sums_one = inlet(state, static_part, moving_cat, first_cat)
-        sums_one = micro_sum(plan, sums_one, True)
+        sums_one = micro_sum(plan, sums_one, first_core)
         pre_two, sums_two = middle(pre_one, sums_one, gain_one, shift_one, second_cat)
-        sums_two = micro_sum(plan, sums_two, True)
-        state_out, state_packed, qkv, mixed, weight, powers_kept = outlet(
-            state, inner, pre_two, sums_two, gain_two, shift_two, qkv_cat, mixer_cat, out_cat, b_out
+        sums_two = micro_sum(plan, sums_two, first_core)
+        state_out, state_packed, mixed, top, weight = outlet(
+            state, inner, pre_two, sums_two, gain_two, shift_two, heads_cat, mixer_cells, out_cat, b_out
         )
-        kept = (qkv, mixed, weight, powers_kept) if step >= segments - KEPT_STEPS else None
-        saved.append((state, inner, pre_one, pre_two, sums_one, sums_two, kept))
+        saved.append((state, inner, pre_one, pre_two, sums_one, sums_two, mixed, top, weight))
         path.append(state_packed)
         state = state_out
         if not step:
-            state, cot_local = lax.optimization_barrier((state, cotangent))
-            sent = call(
-                functools.partial(seeds_kernel, plan), [packed] * segments,
-                [pltpu.VMEM(state_rows.shape, F32), pltpu.SemaphoreType.DMA((1,))],
-                name="seeds", scalars=2, far_in=[2],
-            )(ids, grouping, jnp.swapaxes(cot_local[0], 0, 1))
-            cots = [moved(cot, plan.to_workers(steps)) for steps, cot in enumerate(sent)]
-            if plan.halved:
-                cots[0] = jnp.where(lax.axis_index("section") < 2, sent[0], cots[0])
-    cots = jnp.stack(cots)
+            state, sent_cots = lax.optimization_barrier((state, sent_cots))
+            cots = jnp.stack(
+                [own_cot] + [moved(cot, plan.to_workers(steps + 1)) for steps, cot in enumerate(sent_cots)]
+            )
 
     def put_home(start, parts):
         (out,) = call(
@@ -1054,29 +1015,23 @@
                 [pltpu.VMEM((segments, 4 * GROUP, cells), F32)], name="leave", scalars=1,
             )(ids, *path, *grads[1:])
             early = [sent[0]] + [moved(part, plan.to_homes(steps)) for steps, part in enumerate(sent)]
-        state, inner, pre_one, pre_two, sums_one, sums_two, kept = saved[step]
-        if kept is None:
-            state, d_state = lax.optimization_barrier((state, d_state))
-            kept = outlet(
-                state, inner, pre_two, sums_two, gain_two, shift_two, qkv_cat, mixer_cat, out_cat, b_out
-            )[2:]
-        qkv, mixed, weight, powers_kept = kept
+        state, inner, pre_one, pre_two, sums_one, sums_two, mixed, top, weight = saved[step]
         d_partial, d_two, grad_two, acc["qkv"], acc["mixer"], acc["velocity"], acc["small_two"] = outlet_back(step)(
             ids, state, d_state, cots, inner, pre_two, sums_two, gain_two, shift_two,
-            qkv, mixed, weight, powers_kept,
-            mixer_cat, qkv_back_cat, mixer_back_cat, out_back_cat,
+            mixed, top, weight,
+            qkv_cat, mixer_cat, qkv_back_cat, mixer_back_cat, out_back_cat,
             acc["qkv"], acc["mixer"], acc["velocity"], acc["small_two"],
         )
         if not step:
             d_two, grad_two, early = lax.optimization_barrier((d_two, grad_two, early))
             path_out = put_home(0, early)
-        grad_two = micro_sum(plan, grad_two)
+        grad_two = micro_sum(plan, grad_two, first_core)
         d_normed, grad_one, acc["second"], acc["small_one"] = middle_back(
             d_two, pre_two, sums_two, grad_two, gain_two,
             pre_one, sums_one, gain_one, shift_one, second_back_cat,
             acc["second"], acc["small_one"],
         )
-        grad_one = micro_sum(plan, grad_one)
+        grad_one = micro_sum(plan, grad_one, first_core)
         d_state, grads[step], acc["first"], acc["moving"], acc["inner"] = inlet_back(
             state, d_normed, pre_one, sums_one, grad_one, gain_one,
             inner, d_two, d_partial, first_back_cat, moving_back_cat,
@@ -1104,17 +1059,15 @@
         ids, static_maps, acc["inner"], acc["first"], acc["second"], acc["moving"], acc["qkv"], acc["mixer"],
         acc["velocity"], acc["small_one"], acc["small_two"],
     )
-    grads_out = None
     for bits, later in zip(rounds, rounds[1:] + [[]]):
         parts = swap(parts, bits)
-        if grads_out is None:
-            parts, late = lax.optimization_barrier((parts, late))
-            grads_out = put_home(2 * GROUP, early + late)
         rows >>= len(bits)
         parts = call(
             functools.partial(reduce_kernel, plan, later, len(parts)), shares(rows, later),
             [pltpu.VMEM((rows, channels), F32)], name="reduce_part", scalars=1,
         )(ids, *parts)
+    parts, late = lax.optimization_barrier((parts, late))
+    grads_out = put_home(2 * GROUP, early + late)
     for bits in rounds[::-1]:
         parts = swap([parts[0]] * (1 << len(bits)), bits)
         rows <<= len(bits)

time: 476 us -> 421 us (0.88)
  Pallas kernels: 174 us -> 141 us
  starting transfers between devices: 120 us -> 149 us
  waiting for transfers between devices: 132 us -> 104 us
  local copies, waits for them, and re-layouts: 35.7 us -> 16.8 us
    ppermute x0 -> x64, starting transfers between devices: none -> 79.6 us  [micro_sum(): total = total + lax.ppermute(value, ('section', 'dp'), pairs)]
    ppermute x94 -> x46, waiting for transfers between devices: 122 us -> 48.5 us  [exchanged(): lax.ppermute(value, ('section', 'dp'), [(own, own ^ mask) for own in rang...]
    ppermute x94 -> x46, starting transfers between devices: 100 us -> 49.6 us  [exchanged(): lax.ppermute(value, ('section', 'dp'), [(own, own ^ mask) for own in rang...]
    ppermute x0 -> x64, waiting for transfers between devices: none -> 42.2 us  [micro_sum(): total = total + lax.ppermute(value, ('section', 'dp'), pairs)]
    pallas_call x40 -> x36, Pallas kernels: 174 us -> 141 us  [run(): pl.pallas_call(kernel, out_shape=tuple((jax.ShapeDtypeStruct(shape, kind)...]
    unnamed x262 -> x96, local copies, waits for them, and re-layouts: 33.9 us -> 13.8 us
    ppermute x9 -> x8, waiting for transfers between devices: 2.01 us -> 7.69 us  [moved(): return lax.ppermute(value, ('section', 'dp'), going)]
    ppermute x9 -> x8, starting transfers between devices: 15.9 us -> 16 us  [moved(): return lax.ppermute(value, ('section', 'dp'), going)]
  transfers between devices with their start and end apart: 106 -> 121, of which waited for: 76 -> 74; matrix products, arithmetic and copies ran while one was open for 0% -> 1% of each run, Pallas kernels for 11% -> 5%
where the time goes in v6:
time: 421 us; the launch traced here: 415 us
  starting transfers between devices  149 us (35%)
  Pallas kernels  141 us (33%)
  waiting for transfers between devices  104 us (25%)
  local copies, waits for them, and re-layouts  16.8 us (4%)
    pallas_call x36, Pallas kernels, run(): pl.pallas_call(kernel, out_shape=tuple((jax.ShapeDtypeStruct(shape, kind)...  141 us
    ppermute x64, starting transfers between devices, micro_sum(): total = total + lax.ppermute(value, ('section', 'dp'), pairs)  79.6 us
    ppermute x46, starting transfers between devices, exchanged(): lax.ppermute(value, ('section', 'dp'), [(own, own ^ mask) for own in rang...  49.6 us
    ppermute x46, waiting for transfers between devices, exchanged(): lax.ppermute(value, ('section', 'dp'), [(own, own ^ mask) for own in rang...  48.5 us
    ppermute x64, waiting for transfers between devices, micro_sum(): total = total + lax.ppermute(value, ('section', 'dp'), pairs)  42.2 us
    ppermute x8, starting transfers between devices, moved(): return lax.ppermute(value, ('section', 'dp'), going)  16 us
    unnamed x96, local copies, waits for them, and re-layouts  13.8 us
  transfers between devices with their start and end apart: 121, of which 74 were waited for; matrix products, arithmetic and copies ran while one was open for 1% of the time, Pallas kernels for 5%

profile of v6, /device:TPU:0, one launch (start us, length us, event | category | flops | bytes accessed | tf_op | source)
XLA Modules:
  0.0 415.2 jit_solution(10919662384482065970)
XLA Ops:
  1.2 2.5 enter.1
  4.6 6.5 %weights.1 = (f32[1024,128]{1,0:T(8,128)}, bf16[768,256]{1,0:T(8,128)(2,1)}, bf16[768,256]{1,0:T(8,128)(2,1)}, bf16[2304,256]{1,0:T(8,128)(2,1)}, bf16[2304,256]...) custom-call(f32[9,100,128]{2,1,0:T(8,128)} %w_input_ref.1, ...), custom_call_target="tpu_custom_call" | custom-call | tf_op jit(solution)/shard_map/weights/pallas_call | solution.py:738
  14.5 3.7 inlet.4
  21.6 2.8 collective-permute-start.2
  24.4 6.7 %collective-permute-start.3 = (f32[8,128]{1,0:T(8,128)S(1)}, f32[8,128]{1,0:T(8,128)S(1)}, u32[]{:S(2)}, u32[]{:S(2)}) collective-permute-start(f32[8,128]{1,0:T(8,128)S(1)} %add.290), channel_id=1, source_target_pairs={{1,19},{3,17},{5,23},{7,21},{9,27},{11,25},{13,31},{15,29},{17,3},... | collective-permute-start | bytes 12296 | tf_op jit(solution)/shard_map/ppermute | solution.py:849
  32.7 2.9 collective-permute-done.4
  41.9 2.8 collective-permute-start.10
  46.4 2.8 collective-permute-done.8
  50.3 2.6 collective-permute-start.12
  61.9 5.7 %outlet.4 = (f32[24,1024]{1,0:T(8,128)S(1)}, f32[16,1024]{1,0:T(8,128)S(1)}, f32[1024,128]{1,0:T(8,128)S(1)}, f32[1024,128]{1,0:T(8,128)S(1)}, f32[1024,128]{1,0:T(8,128)S(1)}) custom-call(f32[24,1024]{1,0:T(8,128)S(1)} %copy-done.29, f32[1024,128]{1,0:T(8,128)S(1)} %copy-done.19, f32[1024,128]{1,0:T(8,128)S(1)} %copy-done.16, ...), custom_call_target="tpu_custom_call" | custom-call | tf_op jit(solution)/shard_map/outlet/pallas_call | solution.py:738
  67.6 3.1 inlet.5
  73.5 2.0 collective-permute-start.16
  78.0 2.3 collective-permute-start.18
  90.1 2.8 collective-permute-start.24
  93.7 5.8 %outlet.5 = (f32[24,1024]{1,0:T(8,128)S(1)}, f32[16,1024]{1,0:T(8,128)S(1)}, f32[1024,128]{1,0:T(8,128)S(1)}, f32[1024,128]{1,0:T(8,128)S(1)}, f32[1024,128]{1,0:T(8,128)S(1)}) custom-call(f32[24,1024]{1,0:T(8,128)S(1)} %get-tuple-element.201.state_ref, f32[1024,128]{1,0:T(8,128)S(1)} %get-tuple-element.202.inner_ref, ...), custom_call_target="tpu_custom_call" | custom-call | tf_op jit(solution)/shard_map/outlet/pallas_call | solution.py:738
  99.5 3.1 inlet.6
  105.3 2.0 collective-permute-start.28
  109.9 2.4 collective-permute-start.30
  122.1 2.8 collective-permute-start.36
  125.7 5.8 %outlet.6 = (f32[24,1024]{1,0:T(8,128)S(1)}, f32[16,1024]{1,0:T(8,128)S(1)}, f32[1024,128]{1,0:T(8,128)S(1)}, f32[1024,128]{1,0:T(8,128)S(1)}, f32[1024,128]{1,0:T(8,128)S(1)}) custom-call(f32[24,1024]{1,0:T(8,128)S(1)} %get-tuple-element.207.state_ref, f32[1024,128]{1,0:T(8,128)S(1)} %get-tuple-element.208.inner_ref, ...), custom_call_target="tpu_custom_call" | custom-call | tf_op jit(solution)/shard_map/outlet/pallas_call | solution.py:738
  131.5 3.1 inlet.7
  137.4 2.0 collective-permute-start.43
  141.9 2.4 collective-permute-start.45
  155.6 2.5 collective-permute-start.39
  158.1 2.3 collective-permute-start.51
  161.4 6.4 %outlet.7 = (f32[24,1024]{1,0:T(8,128)}, f32[16,1024]{1,0:T(8,128)S(1)}, f32[1024,128]{1,0:T(8,128)S(1)}, f32[1024,128]{1,0:T(8,128)S(1)}, f32[1024,128]{1,0:T(8,128)S(1)}) custom-call(f32[24,1024]{1,0:T(8,128)S(1)} %get-tuple-element.213.state_ref, f32[1024,128]{1,0:T(8,128)S(1)} %get-tuple-element.218.inner_ref, ...), custom_call_target="tpu_custom_call" | custom-call | tf_op jit(solution)/shard_map/outlet/pallas_call | solution.py:738
  167.9 12.1 %outlet_back.4 = (f32[24,1024]{1,0:T(8,128)S(1)}, f32[1024,128]{1,0:T(8,128)S(1)}, f32[8,128]{1,0:T(8,128)S(1)}, f32[128,384]{1,0:T(8,128)S(1)}, f32[128,128]{1,...) custom-call(s32[2]{0:T(128)S(1)} %copy-done.32, ...), custom_call_target="tpu_custom_call", output_to_operand_aliasing={{3}: (17, {}), {4}: (18, {}), {5}: (19, {}), {6}: (20, {})} | custom-call | tf_op jit(solution)/shard_map/outlet_back/pallas_call | solution.py:738
  182.6 2.0 collective-permute-start.53
  184.5 4.0 collective-permute-start.54
  190.1 2.9 collective-permute-done.55
  194.3 3.0 middle_back.4
  203.7 2.4 collective-permute-done.61
  207.6 4.3 %inlet_back.4 = (f32[24,1024]{1,0:T(8,128)S(1)}, f32[16,1024]{1,0:T(8,128)S(1)}, f32[9,128,128]{2,1,0:T(8,128)S(1)}, f32[3,128,128]{2,1,0:T(8,128)S(1)}, f32[1024,128]{1,0:T(8,128)S(1)}) custom-call(f32[24,1024]{1,0:T(8,128)S(1)} %get-tuple-element.213.state_ref, ...), custom_call_target="tpu_custom_call", output_to_operand_aliasing={{2}: (11, {}), {3}: (12, {}), {4}: (13, {})} | custom-call | tf_op jit(solution)/shard_map/inlet_back/pallas_call | solution.py:738
  211.9 12.0 %outlet_back.5 = (f32[24,1024]{1,0:T(8,128)S(1)}, f32[1024,128]{1,0:T(8,128)S(1)}, f32[8,128]{1,0:T(8,128)S(1)}, f32[128,384]{1,0:T(8,128)S(1)}, f32[128,128]{1,...) custom-call(s32[2]{0:T(128)S(1)} %copy-done.32, ...), custom_call_target="tpu_custom_call", output_to_operand_aliasing={{3}: (17, {}), {4}: (18, {}), {5}: (19, {}), {6}: (20, {})} | custom-call | tf_op jit(solution)/shard_map/outlet_back/pallas_call | solution.py:738
  226.6 2.9 collective-permute-start.66
  231.1 2.9 collective-permute-done.67
  235.4 3.0 middle_back.5
  244.7 2.4 collective-permute-done.73
  248.5 4.3 %inlet_back.5 = (f32[24,1024]{1,0:T(8,128)S(1)}, f32[16,1024]{1,0:T(8,128)S(1)}, f32[9,128,128]{2,1,0:T(8,128)S(1)}, f32[3,128,128]{2,1,0:T(8,128)S(1)}, f32[1024,128]{1,0:T(8,128)S(1)}) custom-call(f32[24,1024]{1,0:T(8,128)S(1)} %get-tuple-element.207.state_ref, ...), custom_call_target="tpu_custom_call", output_to_operand_aliasing={{2}: (11, {}), {3}: (12, {}), {4}: (13, {})} | custom-call | tf_op jit(solution)/shard_map/inlet_back/pallas_call | solution.py:738
  252.9 12.3 %outlet_back.6 = (f32[24,1024]{1,0:T(8,128)S(1)}, f32[1024,128]{1,0:T(8,128)S(1)}, f32[8,128]{1,0:T(8,128)S(1)}, f32[128,384]{1,0:T(8,128)S(1)}, f32[128,128]{1,...) custom-call(s32[2]{0:T(128)S(1)} %copy-done.32, ...), custom_call_target="tpu_custom_call", output_to_operand_aliasing={{3}: (17, {}), {4}: (18, {}), {5}: (19, {}), {6}: (20, {})} | custom-call | tf_op jit(solution)/shard_map/outlet_back/pallas_call | solution.py:738
  267.8 2.9 collective-permute-start.78
  272.3 2.9 collective-permute-done.79
  276.5 3.0 middle_back.6
  285.9 2.4 collective-permute-done.85
  289.7 4.3 %inlet_back.6 = (f32[24,1024]{1,0:T(8,128)S(1)}, f32[16,1024]{1,0:T(8,128)S(1)}, f32[9,128,128]{2,1,0:T(8,128)S(1)}, f32[3,128,128]{2,1,0:T(8,128)S(1)}, f32[1024,128]{1,0:T(8,128)S(1)}) custom-call(f32[24,1024]{1,0:T(8,128)S(1)} %get-tuple-element.201.state_ref, ...), custom_call_target="tpu_custom_call", output_to_operand_aliasing={{2}: (11, {}), {3}: (12, {}), {4}: (13, {})} | custom-call | tf_op jit(solution)/shard_map/inlet_back/pallas_call | solution.py:738
  296.8 6.5 %collective-permute-start.90 = (f32[32,1024]{1,0:T(8,128)S(1)}, f32[32,1024]{1,0:T(8,128)S(1)}, u32[]{:S(2)}, u32[]{:S(2)}) collective-permute-start(f32[32,1024]{1,0:T(8,128)S(1)} %get-tuple-element.294), channel_id=1, source_target_pairs={{0,16},{1,17},{2,18},{3,19},{4,20},{5,21},{6,22},{7,23},{8,24},{9,... | collective-permute-start | bytes 393224 | tf_op jit(solution)/shard_map/ppermute | solution.py:832
  303.9 11.8 %outlet_back.7 = (f32[24,1024]{1,0:T(8,128)S(1)}, f32[1024,128]{1,0:T(8,128)S(1)}, f32[8,128]{1,0:T(8,128)S(1)}, f32[128,384]{1,0:T(8,128)S(1)}, f32[128,128]{1,...) custom-call(s32[2]{0:T(128)S(1)} %copy-done.32, ...), custom_call_target="tpu_custom_call", output_to_operand_aliasing={{3}: (17, {}), {4}: (18, {}), {5}: (19, {}), {6}: (20, {})} | custom-call | tf_op jit(solution)/shard_map/outlet_back/pallas_call | solution.py:738
  315.8 6.1 %collective-permute-done.89.refs_1_ = f32[32,1024]{1,0:T(8,128)S(1)} collective-permute-done((f32[32,1024]{1,0:T(8,128)S(1)}, f32[32,1024]{1,0:T(8,128)S(1)}, u32[]{:S(2)}, u32[]{:S(2)}) %collective-permute-start.89) | collective-permute-done | bytes 131104 | tf_op jit(solution)/shard_map/ppermute | solution.py:832
  324.3 3.7 collective-permute-start.93
  335.1 3.0 middle_back.7
  346.7 3.1 collective-permute-start.103
  350.6 4.9 %inlet_back.7 = (f32[24,1024]{1,0:T(8,128)}, f32[16,1024]{1,0:T(8,128)S(1)}, f32[9,128,128]{2,1,0:T(8,128)S(1)}, f32[3,128,128]{2,1,0:T(8,128)S(1)}, f32[1024,128]{1,0:T(8,128)S(1)}) custom-call(f32[24,1024]{1,0:T(8,128)S(1)} %copy-done.30, ...), custom_call_target="tpu_custom_call", output_to_operand_aliasing={{2}: (11, {}), {3}: (12, {}), {4}: (13, {})} | custom-call | tf_op jit(solution)/shard_map/inlet_back/pallas_call | solution.py:738
  355.6 2.0 pack.1
  358.0 2.3 collective-permute-done.104.refs_1_
  364.6 5.6 %collective-permute-done.105.refs_1_ = f32[512,128]{1,0:T(8,128)S(1)} collective-permute-done((f32[512,128]{1,0:T(8,128)S(1)}, f32[512,128]{1,0:T(8,128)S(1)}, u32[]{:S(2)}, u32[]{:S(2)}) %collective-permute-start.105) | collective-permute-done | bytes 262176 | tf_op jit(solution)/shard_map/ppermute | solution.py:825
  370.2 5.1 %collective-permute-done.106.refs_2_ = f32[512,128]{1,0:T(8,128)S(1)} collective-permute-done((f32[512,128]{1,0:T(8,128)S(1)}, f32[512,128]{1,0:T(8,128)S(1)}, u32[]{:S(2)}, u32[]{:S(2)}) %collective-permute-start.106) | collective-permute-done | bytes 262176 | tf_op jit(solution)/shard_map/ppermute | solution.py:825
  377.6 2.8 collective-permute-start.110
  384.9 4.6 %collective-permute-done.111.refs_5_ = f32[16,1024]{1,0:T(8,128)S(1)} collective-permute-done((f32[16,1024]{1,0:T(8,128)S(1)}, f32[16,1024]{1,0:T(8,128)S(1)}, u32[]{:S(2)}, u32[]{:S(2)}) %collective-permute-start.111) | collective-permute-done | bytes 65568 | tf_op jit(solution)/shard_map/ppermute | solution.py:1041
  391.6 3.7 collective-permute-start.116
  396.0 2.2 collective-permute-done.116.refs_3_
  398.9 3.4 collective-permute-start.119
  402.3 3.6 collective-permute-done.117.refs_1_
  405.9 2.9 collective-permute-done.118.refs_2_
  412.2 2.0 unpack.1
  (376 shorter events, 157.6 us)
Async XLA Ops:
  3.8 7.4 %collective-permute-start = (f32[40,1024]{1,0:T(8,128)}, f32[40,1024]{1,0:T(8,128)S(1)}, u32[]{:S(2)}, u32[]{:S(2)}) collective-permute-start(f32[40,1024]{1,0:T(8,128)} %get-tuple-element.183.own_ref), channel_id=1, source_target_pairs={{16,20},{17,21},{18,22},{19,23},{20,16},{21,17},{22,18},{23,19},{2... | collective-permute-start | bytes 491528 | tf_op jit(solution)/shard_map/ppermute | solution.py:832
  21.6 10.2 %collective-permute-start.2 = (f32[8,128]{1,0:T(8,128)S(1)}, f32[8,128]{1,0:T(8,128)S(1)}, u32[]{:S(2)}, u32[]{:S(2)}) collective-permute-start(f32[8,128]{1,0:T(8,128)S(1)} %add.290), channel_id=1, source_target_pairs={{1,11},{3,9},{5,15},{7,13},{9,3},{11,1},{13,7},{15,5},{17,27},{19,... | collective-permute-start | bytes 12296 | tf_op jit(solution)/shard_map/ppermute | solution.py:849
  24.4 8.3 %collective-permute-start.3 = (f32[8,128]{1,0:T(8,128)S(1)}, f32[8,128]{1,0:T(8,128)S(1)}, u32[]{:S(2)}, u32[]{:S(2)}) collective-permute-start(f32[8,128]{1,0:T(8,128)S(1)} %add.290), channel_id=1, source_target_pairs={{1,19},{3,17},{5,23},{7,21},{9,27},{11,25},{13,31},{15,29},{17,3},... | collective-permute-start | bytes 12296 | tf_op jit(solution)/shard_map/ppermute | solution.py:849
  31.1 4.5 %collective-permute-start.4 = (f32[8,128]{1,0:T(8,128)S(1)}, f32[8,128]{1,0:T(8,128)S(1)}, u32[]{:S(2)}, u32[]{:S(2)}) collective-permute-start(f32[8,128]{1,0:T(8,128)S(1)} %add.290), channel_id=1, source_target_pairs={{1,27},{3,25},{5,31},{7,29},{9,19},{11,17},{13,23},{15,21},{17,11}... | collective-permute-start | bytes 12296 | tf_op jit(solution)/shard_map/ppermute | solution.py:849
  31.1 4.5 %collective-permute-start.5 = (f32[8,128]{1,0:T(8,128)S(1)}, f32[8,128]{1,0:T(8,128)S(1)}, u32[]{:S(2)}, u32[]{:S(2)}) collective-permute-start(f32[8,128]{1,0:T(8,128)S(1)} %add.290), channel_id=1, source_target_pairs={{1,3},{3,1},{5,7},{7,5},{9,11},{11,9},{13,15},{15,13},{17,19},{19,... | collective-permute-start | bytes 12296 | tf_op jit(solution)/shard_map/ppermute | solution.py:849
  41.9 4.5 %collective-permute-start.10 = (f32[8,128]{1,0:T(8,128)S(1)}, f32[8,128]{1,0:T(8,128)S(1)}, u32[]{:S(2)}, u32[]{:S(2)}) collective-permute-start(f32[8,128]{1,0:T(8,128)S(1)} %add.296), channel_id=1, source_target_pairs={{1,27},{3,25},{5,31},{7,29},{9,19},{11,17},{13,23},{15,21},{17,11}... | collective-permute-start | bytes 12296 | tf_op jit(solution)/shard_map/ppermute | solution.py:849
  50.3 4.7 %collective-permute-start.12 = (f32[8,128]{1,0:T(8,128)}, f32[8,128]{1,0:T(8,128)}, u32[]{:S(2)}, u32[]{:S(2)}) collective-permute-start(f32[8,128]{1,0:T(8,128)} %add_add_fusion.14), channel_id=1, source_target_pairs={{0,1},{1,0},{2,3},{3,2},{4,5},{5,4},{6,7},{7,6},{8,9},{9,8},{10,11... | collective-permute-start | bytes 12296 | tf_op jit(solution)/shard_map/ppermute | solution.py:825
  72.0 4.1 collective-permute-start.14
  73.5 4.5 %collective-permute-start.16 = (f32[8,128]{1,0:T(8,128)S(1)}, f32[8,128]{1,0:T(8,128)S(1)}, u32[]{:S(2)}, u32[]{:S(2)}) collective-permute-start(f32[8,128]{1,0:T(8,128)S(1)} %add.302), channel_id=1, source_target_pairs={{1,27},{3,25},{5,31},{7,29},{9,19},{11,17},{13,23},{15,21},{17,11}... | collective-permute-start | bytes 12296 | tf_op jit(solution)/shard_map/ppermute | solution.py:849
  84.0 4.4 %collective-permute-start.20 = (f32[8,128]{1,0:T(8,128)S(1)}, f32[8,128]{1,0:T(8,128)S(1)}, u32[]{:S(2)}, u32[]{:S(2)}) collective-permute-start(f32[8,128]{1,0:T(8,128)S(1)} %add.308), channel_id=1, source_target_pairs={{1,11},{3,9},{5,15},{7,13},{9,3},{11,1},{13,7},{15,5},{17,27},{19,... | collective-permute-start | bytes 12296 | tf_op jit(solution)/shard_map/ppermute | solution.py:849
  85.6 4.5 %collective-permute-start.22 = (f32[8,128]{1,0:T(8,128)S(1)}, f32[8,128]{1,0:T(8,128)S(1)}, u32[]{:S(2)}, u32[]{:S(2)}) collective-permute-start(f32[8,128]{1,0:T(8,128)S(1)} %add.308), channel_id=1, source_target_pairs={{1,27},{3,25},{5,31},{7,29},{9,19},{11,17},{13,23},{15,21},{17,11}... | collective-permute-start | bytes 12296 | tf_op jit(solution)/shard_map/ppermute | solution.py:849
  103.9 4.1 collective-permute-start.26
  105.3 4.5 %collective-permute-start.28 = (f32[8,128]{1,0:T(8,128)S(1)}, f32[8,128]{1,0:T(8,128)S(1)}, u32[]{:S(2)}, u32[]{:S(2)}) collective-permute-start(f32[8,128]{1,0:T(8,128)S(1)} %add.314), channel_id=1, source_target_pairs={{1,27},{3,25},{5,31},{7,29},{9,19},{11,17},{13,23},{15,21},{17,11}... | collective-permute-start | bytes 12296 | tf_op jit(solution)/shard_map/ppermute | solution.py:849
  116.0 4.6 %collective-permute-start.32 = (f32[8,128]{1,0:T(8,128)S(1)}, f32[8,128]{1,0:T(8,128)S(1)}, u32[]{:S(2)}, u32[]{:S(2)}) collective-permute-start(f32[8,128]{1,0:T(8,128)S(1)} %add.320), channel_id=1, source_target_pairs={{1,11},{3,9},{5,15},{7,13},{9,3},{11,1},{13,7},{15,5},{17,27},{19,... | collective-permute-start | bytes 12296 | tf_op jit(solution)/shard_map/ppermute | solution.py:849
  117.6 4.5 %collective-permute-start.34 = (f32[8,128]{1,0:T(8,128)S(1)}, f32[8,128]{1,0:T(8,128)S(1)}, u32[]{:S(2)}, u32[]{:S(2)}) collective-permute-start(f32[8,128]{1,0:T(8,128)S(1)} %add.320), channel_id=1, source_target_pairs={{1,27},{3,25},{5,31},{7,29},{9,19},{11,17},{13,23},{15,21},{17,11}... | collective-permute-start | bytes 12296 | tf_op jit(solution)/shard_map/ppermute | solution.py:849
  135.9 4.1 collective-permute-start.41
  137.4 4.5 %collective-permute-start.43 = (f32[8,128]{1,0:T(8,128)S(1)}, f32[8,128]{1,0:T(8,128)S(1)}, u32[]{:S(2)}, u32[]{:S(2)}) collective-permute-start(f32[8,128]{1,0:T(8,128)S(1)} %add.326), channel_id=1, source_target_pairs={{1,27},{3,25},{5,31},{7,29},{9,19},{11,17},{13,23},{15,21},{17,11}... | collective-permute-start | bytes 12296 | tf_op jit(solution)/shard_map/ppermute | solution.py:849
  148.0 5.7 %collective-permute-start.47 = (f32[8,128]{1,0:T(8,128)S(1)}, f32[8,128]{1,0:T(8,128)S(1)}, u32[]{:S(2)}, u32[]{:S(2)}) collective-permute-start(f32[8,128]{1,0:T(8,128)S(1)} %add.332), channel_id=1, source_target_pairs={{1,11},{3,9},{5,15},{7,13},{9,3},{11,1},{13,7},{15,5},{17,27},{19,... | collective-permute-start | bytes 12296 | tf_op jit(solution)/shard_map/ppermute | solution.py:849
  149.5 6.1 %collective-permute-start.48 = (f32[8,128]{1,0:T(8,128)S(1)}, f32[8,128]{1,0:T(8,128)S(1)}, u32[]{:S(2)}, u32[]{:S(2)}) collective-permute-start(f32[8,128]{1,0:T(8,128)S(1)} %add.332), channel_id=1, source_target_pairs={{1,19},{3,17},{5,23},{7,21},{9,27},{11,25},{13,31},{15,29},{17,3},... | collective-permute-start | bytes 12296 | tf_op jit(solution)/shard_map/ppermute | solution.py:849
  149.6 8.5 %collective-permute-start.49 = (f32[8,128]{1,0:T(8,128)S(1)}, f32[8,128]{1,0:T(8,128)S(1)}, u32[]{:S(2)}, u32[]{:S(2)}) collective-permute-start(f32[8,128]{1,0:T(8,128)S(1)} %add.332), channel_id=1, source_target_pairs={{1,27},{3,25},{5,31},{7,29},{9,19},{11,17},{13,23},{15,21},{17,11}... | collective-permute-start | bytes 12296 | tf_op jit(solution)/shard_map/ppermute | solution.py:849
  151.5 6.6 %collective-permute-start.50 = (f32[8,128]{1,0:T(8,128)S(1)}, f32[8,128]{1,0:T(8,128)S(1)}, u32[]{:S(2)}, u32[]{:S(2)}) collective-permute-start(f32[8,128]{1,0:T(8,128)S(1)} %add.332), channel_id=1, source_target_pairs={{1,3},{3,1},{5,7},{7,5},{9,11},{11,9},{13,15},{15,13},{17,19},{19,... | collective-permute-start | bytes 12296 | tf_op jit(solution)/shard_map/ppermute | solution.py:849
  152.2 8.3 %collective-permute-start.37 = (f32[16,1024]{1,0:T(8,128)S(1)}, f32[16,1024]{1,0:T(8,128)S(1)}, u32[]{:S(2)}, u32[]{:S(2)}) collective-permute-start(f32[16,1024]{1,0:T(8,128)S(1)} %copy-done.47), channel_id=1, source_target_pairs={{0,8},{1,9},{2,10},{3,11},{4,12},{5,13},{6,14},{7,15},{8,20},{9,21... | collective-permute-start | bytes 196616 | tf_op jit(solution)/shard_map/ppermute | solution.py:832
  153.7 6.8 %collective-permute-start.38 = (f32[16,1024]{1,0:T(8,128)S(1)}, f32[16,1024]{1,0:T(8,128)S(1)}, u32[]{:S(2)}, u32[]{:S(2)}) collective-permute-start(f32[16,1024]{1,0:T(8,128)S(1)} %copy-done.46), channel_id=1, source_target_pairs={{0,20},{1,21},{2,22},{3,23},{4,16},{5,17},{6,18},{7,19},{8,28},{9,... | collective-permute-start | bytes 196616 | tf_op jit(solution)/shard_map/ppermute | solution.py:832
  155.6 5.2 %collective-permute-start.39 = (f32[16,1024]{1,0:T(8,128)S(1)}, f32[16,1024]{1,0:T(8,128)S(1)}, u32[]{:S(2)}, u32[]{:S(2)}) collective-permute-start(f32[16,1024]{1,0:T(8,128)S(1)} %copy-done.45), channel_id=1, source_target_pairs={{0,28},{1,29},{2,30},{3,31},{4,24},{5,25},{6,26},{7,27},{8,0},{9,1... | collective-permute-start | bytes 196616 | tf_op jit(solution)/shard_map/ppermute | solution.py:832
  182.6 6.6 %collective-permute-start.53 = (f32[8,128]{1,0:T(8,128)S(1)}, f32[8,128]{1,0:T(8,128)S(1)}, u32[]{:S(2)}, u32[]{:S(2)}) collective-permute-start(f32[8,128]{1,0:T(8,128)S(1)} %add.338), channel_id=1, source_target_pairs={{1,11},{3,9},{5,15},{7,13},{9,3},{11,1},{13,7},{15,5},{17,27},{19,... | collective-permute-start | bytes 12296 | tf_op jit(solution)/shard_map/ppermute | solution.py:849
  184.5 5.5 %collective-permute-start.54 = (f32[8,128]{1,0:T(8,128)S(1)}, f32[8,128]{1,0:T(8,128)S(1)}, u32[]{:S(2)}, u32[]{:S(2)}) collective-permute-start(f32[8,128]{1,0:T(8,128)S(1)} %add.338), channel_id=1, source_target_pairs={{1,19},{3,17},{5,23},{7,21},{9,27},{11,25},{13,31},{15,29},{17,3},... | collective-permute-start | bytes 12296 | tf_op jit(solution)/shard_map/ppermute | solution.py:849
  188.5 4.5 %collective-permute-start.55 = (f32[8,128]{1,0:T(8,128)S(1)}, f32[8,128]{1,0:T(8,128)S(1)}, u32[]{:S(2)}, u32[]{:S(2)}) collective-permute-start(f32[8,128]{1,0:T(8,128)S(1)} %add.338), channel_id=1, source_target_pairs={{1,27},{3,25},{5,31},{7,29},{9,19},{11,17},{13,23},{15,21},{17,11}... | collective-permute-start | bytes 12296 | tf_op jit(solution)/shard_map/ppermute | solution.py:849
  188.5 4.5 %collective-permute-start.56 = (f32[8,128]{1,0:T(8,128)S(1)}, f32[8,128]{1,0:T(8,128)S(1)}, u32[]{:S(2)}, u32[]{:S(2)}) collective-permute-start(f32[8,128]{1,0:T(8,128)S(1)} %add.338), channel_id=1, source_target_pairs={{1,3},{3,1},{5,7},{7,5},{9,11},{11,9},{13,15},{15,13},{17,19},{19,... | collective-permute-start | bytes 12296 | tf_op jit(solution)/shard_map/ppermute | solution.py:849
  198.6 4.6 %collective-permute-start.59 = (f32[8,128]{1,0:T(8,128)S(1)}, f32[8,128]{1,0:T(8,128)S(1)}, u32[]{:S(2)}, u32[]{:S(2)}) collective-permute-start(f32[8,128]{1,0:T(8,128)S(1)} %add.344), channel_id=1, source_target_pairs={{1,11},{3,9},{5,15},{7,13},{9,3},{11,1},{13,7},{15,5},{17,27},{19,... | collective-permute-start | bytes 12296 | tf_op jit(solution)/shard_map/ppermute | solution.py:849
  201.5 4.5 %collective-permute-start.61 = (f32[8,128]{1,0:T(8,128)S(1)}, f32[8,128]{1,0:T(8,128)S(1)}, u32[]{:S(2)}, u32[]{:S(2)}) collective-permute-start(f32[8,128]{1,0:T(8,128)S(1)} %add.344), channel_id=1, source_target_pairs={{1,27},{3,25},{5,31},{7,29},{9,19},{11,17},{13,23},{15,21},{17,11}... | collective-permute-start | bytes 12296 | tf_op jit(solution)/shard_map/ppermute | solution.py:849
  225.2 5.0 %collective-permute-start.65 = (f32[8,128]{1,0:T(8,128)S(1)}, f32[8,128]{1,0:T(8,128)S(1)}, u32[]{:S(2)}, u32[]{:S(2)}) collective-permute-start(f32[8,128]{1,0:T(8,128)S(1)} %add.350), channel_id=1, source_target_pairs={{1,11},{3,9},{5,15},{7,13},{9,3},{11,1},{13,7},{15,5},{17,27},{19,... | collective-permute-start | bytes 12296 | tf_op jit(solution)/shard_map/ppermute | solution.py:849
  226.6 4.5 %collective-permute-start.66 = (f32[8,128]{1,0:T(8,128)S(1)}, f32[8,128]{1,0:T(8,128)S(1)}, u32[]{:S(2)}, u32[]{:S(2)}) collective-permute-start(f32[8,128]{1,0:T(8,128)S(1)} %add.350), channel_id=1, source_target_pairs={{1,19},{3,17},{5,23},{7,21},{9,27},{11,25},{13,31},{15,29},{17,3},... | collective-permute-start | bytes 12296 | tf_op jit(solution)/shard_map/ppermute | solution.py:849
  229.5 4.5 %collective-permute-start.67 = (f32[8,128]{1,0:T(8,128)S(1)}, f32[8,128]{1,0:T(8,128)S(1)}, u32[]{:S(2)}, u32[]{:S(2)}) collective-permute-start(f32[8,128]{1,0:T(8,128)S(1)} %add.350), channel_id=1, source_target_pairs={{1,27},{3,25},{5,31},{7,29},{9,19},{11,17},{13,23},{15,21},{17,11}... | collective-permute-start | bytes 12296 | tf_op jit(solution)/shard_map/ppermute | solution.py:849
  229.5 4.5 %collective-permute-start.68 = (f32[8,128]{1,0:T(8,128)S(1)}, f32[8,128]{1,0:T(8,128)S(1)}, u32[]{:S(2)}, u32[]{:S(2)}) collective-permute-start(f32[8,128]{1,0:T(8,128)S(1)} %add.350), channel_id=1, source_target_pairs={{1,3},{3,1},{5,7},{7,5},{9,11},{11,9},{13,15},{15,13},{17,19},{19,... | collective-permute-start | bytes 12296 | tf_op jit(solution)/shard_map/ppermute | solution.py:849
  242.6 4.5 %collective-permute-start.73 = (f32[8,128]{1,0:T(8,128)S(1)}, f32[8,128]{1,0:T(8,128)S(1)}, u32[]{:S(2)}, u32[]{:S(2)}) collective-permute-start(f32[8,128]{1,0:T(8,128)S(1)} %add.356), channel_id=1, source_target_pairs={{1,27},{3,25},{5,31},{7,29},{9,19},{11,17},{13,23},{15,21},{17,11}... | collective-permute-start | bytes 12296 | tf_op jit(solution)/shard_map/ppermute | solution.py:849
  266.4 5.0 %collective-permute-start.77 = (f32[8,128]{1,0:T(8,128)S(1)}, f32[8,128]{1,0:T(8,128)S(1)}, u32[]{:S(2)}, u32[]{:S(2)}) collective-permute-start(f32[8,128]{1,0:T(8,128)S(1)} %add.362), channel_id=1, source_target_pairs={{1,11},{3,9},{5,15},{7,13},{9,3},{11,1},{13,7},{15,5},{17,27},{19,... | collective-permute-start | bytes 12296 | tf_op jit(solution)/shard_map/ppermute | solution.py:849
  267.8 4.5 %collective-permute-start.78 = (f32[8,128]{1,0:T(8,128)S(1)}, f32[8,128]{1,0:T(8,128)S(1)}, u32[]{:S(2)}, u32[]{:S(2)}) collective-permute-start(f32[8,128]{1,0:T(8,128)S(1)} %add.362), channel_id=1, source_target_pairs={{1,19},{3,17},{5,23},{7,21},{9,27},{11,25},{13,31},{15,29},{17,3},... | collective-permute-start | bytes 12296 | tf_op jit(solution)/shard_map/ppermute | solution.py:849
  270.7 4.5 %collective-permute-start.79 = (f32[8,128]{1,0:T(8,128)S(1)}, f32[8,128]{1,0:T(8,128)S(1)}, u32[]{:S(2)}, u32[]{:S(2)}) collective-permute-start(f32[8,128]{1,0:T(8,128)S(1)} %add.362), channel_id=1, source_target_pairs={{1,27},{3,25},{5,31},{7,29},{9,19},{11,17},{13,23},{15,21},{17,11}... | collective-permute-start | bytes 12296 | tf_op jit(solution)/shard_map/ppermute | solution.py:849
  270.7 4.5 %collective-permute-start.80 = (f32[8,128]{1,0:T(8,128)S(1)}, f32[8,128]{1,0:T(8,128)S(1)}, u32[]{:S(2)}, u32[]{:S(2)}) collective-permute-start(f32[8,128]{1,0:T(8,128)S(1)} %add.362), channel_id=1, source_target_pairs={{1,3},{3,1},{5,7},{7,5},{9,11},{11,9},{13,15},{15,13},{17,19},{19,... | collective-permute-start | bytes 12296 | tf_op jit(solution)/shard_map/ppermute | solution.py:849
  280.8 4.1 collective-permute-start.83
  283.8 4.5 %collective-permute-start.85 = (f32[8,128]{1,0:T(8,128)S(1)}, f32[8,128]{1,0:T(8,128)S(1)}, u32[]{:S(2)}, u32[]{:S(2)}) collective-permute-start(f32[8,128]{1,0:T(8,128)S(1)} %add.368), channel_id=1, source_target_pairs={{1,27},{3,25},{5,31},{7,29},{9,19},{11,17},{13,23},{15,21},{17,11}... | collective-permute-start | bytes 12296 | tf_op jit(solution)/shard_map/ppermute | solution.py:849
  294.7 21.1 %collective-permute-start.88 = (f32[32,1024]{1,0:T(8,128)S(1)}, f32[32,1024]{1,0:T(8,128)S(1)}, u32[]{:S(2)}, u32[]{:S(2)}) collective-permute-start(f32[32,1024]{1,0:T(8,128)S(1)} %get-tuple-element.296.kept_ref), channel_id=1, source_target_pairs={{16,20},{17,21},{18,22},{19,23},{20,16},{21,17},{22,18},{23,19},{2... | collective-permute-start | bytes 393224 | tf_op jit(solution)/shard_map/ppermute | solution.py:832
  295.3 26.5 %collective-permute-start.89 = (f32[32,1024]{1,0:T(8,128)S(1)}, f32[32,1024]{1,0:T(8,128)S(1)}, u32[]{:S(2)}, u32[]{:S(2)}) collective-permute-start(f32[32,1024]{1,0:T(8,128)S(1)} %get-tuple-element.293), channel_id=1, source_target_pairs={{0,8},{1,9},{2,10},{3,11},{4,12},{5,13},{6,14},{7,15},{8,16},{9,17... | collective-permute-start | bytes 393224 | tf_op jit(solution)/shard_map/ppermute | solution.py:832
  296.8 26.3 %collective-permute-start.90 = (f32[32,1024]{1,0:T(8,128)S(1)}, f32[32,1024]{1,0:T(8,128)S(1)}, u32[]{:S(2)}, u32[]{:S(2)}) collective-permute-start(f32[32,1024]{1,0:T(8,128)S(1)} %get-tuple-element.294), channel_id=1, source_target_pairs={{0,16},{1,17},{2,18},{3,19},{4,20},{5,21},{6,22},{7,23},{8,24},{9,... | collective-permute-start | bytes 393224 | tf_op jit(solution)/shard_map/ppermute | solution.py:832
  303.3 19.8 %collective-permute-start.91 = (f32[32,1024]{1,0:T(8,128)S(1)}, f32[32,1024]{1,0:T(8,128)S(1)}, u32[]{:S(2)}, u32[]{:S(2)}) collective-permute-start(f32[32,1024]{1,0:T(8,128)S(1)} %get-tuple-element.295), channel_id=1, source_target_pairs={{0,24},{1,25},{2,26},{3,27},{4,28},{5,29},{6,30},{7,31},{8,0},{9,1... | collective-permute-start | bytes 393224 | tf_op jit(solution)/shard_map/ppermute | solution.py:832
  324.3 6.0 %collective-permute-start.93 = (f32[8,128]{1,0:T(8,128)S(1)}, f32[8,128]{1,0:T(8,128)S(1)}, u32[]{:S(2)}, u32[]{:S(2)}) collective-permute-start(f32[8,128]{1,0:T(8,128)S(1)} %add.374), channel_id=1, source_target_pairs={{1,11},{3,9},{5,15},{7,13},{9,3},{11,1},{13,7},{15,5},{17,27},{19,... | collective-permute-start | bytes 12296 | tf_op jit(solution)/shard_map/ppermute | solution.py:849
  328.0 4.5 %collective-permute-start.95 = (f32[8,128]{1,0:T(8,128)S(1)}, f32[8,128]{1,0:T(8,128)S(1)}, u32[]{:S(2)}, u32[]{:S(2)}) collective-permute-start(f32[8,128]{1,0:T(8,128)S(1)} %add.374), channel_id=1, source_target_pairs={{1,27},{3,25},{5,31},{7,29},{9,19},{11,17},{13,23},{15,21},{17,11}... | collective-permute-start | bytes 12296 | tf_op jit(solution)/shard_map/ppermute | solution.py:849
  339.4 4.2 %collective-permute-start.100 = (f32[8,128]{1,0:T(8,128)S(1)}, f32[8,128]{1,0:T(8,128)S(1)}, u32[]{:S(2)}, u32[]{:S(2)}) collective-permute-start(f32[8,128]{1,0:T(8,128)S(1)} %add.380), channel_id=1, source_target_pairs={{1,19},{3,17},{5,23},{7,21},{9,27},{11,25},{13,31},{15,29},{17,3},... | collective-permute-start | bytes 12296 | tf_op jit(solution)/shard_map/ppermute | solution.py:849
  340.4 4.5 %collective-permute-start.101 = (f32[8,128]{1,0:T(8,128)S(1)}, f32[8,128]{1,0:T(8,128)S(1)}, u32[]{:S(2)}, u32[]{:S(2)}) collective-permute-start(f32[8,128]{1,0:T(8,128)S(1)} %add.380), channel_id=1, source_target_pairs={{1,27},{3,25},{5,31},{7,29},{9,19},{11,17},{13,23},{15,21},{17,11}... | collective-permute-start | bytes 12296 | tf_op jit(solution)/shard_map/ppermute | solution.py:849
  361.1 9.2 %collective-permute-start.105 = (f32[512,128]{1,0:T(8,128)S(1)}, f32[512,128]{1,0:T(8,128)S(1)}, u32[]{:S(2)}, u32[]{:S(2)}) collective-permute-start(f32[512,128]{1,0:T(8,128)S(1)} %get-tuple-element.323), channel_id=1, source_target_pairs={{0,8},{1,9},{2,10},{3,11},{4,12},{5,13},{6,14},{7,15},{8,0},{9,1},... | collective-permute-start | bytes 786440 | tf_op jit(solution)/shard_map/ppermute | solution.py:825
  361.1 14.2 %collective-permute-start.106 = (f32[512,128]{1,0:T(8,128)S(1)}, f32[512,128]{1,0:T(8,128)S(1)}, u32[]{:S(2)}, u32[]{:S(2)}) collective-permute-start(f32[512,128]{1,0:T(8,128)S(1)} %get-tuple-element.324), channel_id=1, source_target_pairs={{0,16},{1,17},{2,18},{3,19},{4,20},{5,21},{6,22},{7,23},{8,24},{9,... | collective-permute-start | bytes 786440 | tf_op jit(solution)/shard_map/ppermute | solution.py:825
  362.7 12.7 %collective-permute-start.107 = (f32[512,128]{1,0:T(8,128)S(1)}, f32[512,128]{1,0:T(8,128)S(1)}, u32[]{:S(2)}, u32[]{:S(2)}) collective-permute-start(f32[512,128]{1,0:T(8,128)S(1)} %get-tuple-element.325), channel_id=1, source_target_pairs={{0,24},{1,25},{2,26},{3,27},{4,28},{5,29},{6,30},{7,31},{8,16},{9,... | collective-permute-start | bytes 786440 | tf_op jit(solution)/shard_map/ppermute | solution.py:825
  376.0 7.0 %collective-permute-start.108 = (f32[128,128]{1,0:T(8,128)S(1)}, f32[128,128]{1,0:T(8,128)S(1)}, u32[]{:S(2)}, u32[]{:S(2)}) collective-permute-start(f32[128,128]{1,0:T(8,128)S(1)} %get-tuple-element.327), channel_id=1, source_target_pairs={{0,2},{1,3},{2,0},{3,1},{4,6},{5,7},{6,4},{7,5},{8,10},{9,11},{10,... | collective-permute-start | bytes 196616 | tf_op jit(solution)/shard_map/ppermute | solution.py:825
  376.6 7.8 %collective-permute-start.109 = (f32[128,128]{1,0:T(8,128)S(1)}, f32[128,128]{1,0:T(8,128)S(1)}, u32[]{:S(2)}, u32[]{:S(2)}) collective-permute-start(f32[128,128]{1,0:T(8,128)S(1)} %get-tuple-element.328), channel_id=1, source_target_pairs={{0,4},{1,5},{2,6},{3,7},{4,0},{5,1},{6,2},{7,3},{8,12},{9,13},{10,... | collective-permute-start | bytes 196616 | tf_op jit(solution)/shard_map/ppermute | solution.py:825
  377.6 6.7 %collective-permute-start.110 = (f32[128,128]{1,0:T(8,128)S(1)}, f32[128,128]{1,0:T(8,128)S(1)}, u32[]{:S(2)}, u32[]{:S(2)}) collective-permute-start(f32[128,128]{1,0:T(8,128)S(1)} %get-tuple-element.329), channel_id=1, source_target_pairs={{0,6},{1,7},{2,4},{3,5},{4,2},{5,3},{6,0},{7,1},{8,14},{9,15},{10,... | collective-permute-start | bytes 196616 | tf_op jit(solution)/shard_map/ppermute | solution.py:825
  380.5 9.1 %collective-permute-start.111 = (f32[16,1024]{1,0:T(8,128)S(1)}, f32[16,1024]{1,0:T(8,128)S(1)}, u32[]{:S(2)}, u32[]{:S(2)}) collective-permute-start(f32[16,1024]{1,0:T(8,128)S(1)} %get-tuple-element.331.refs_4_), channel_id=1, source_target_pairs={{24,4},{25,5},{26,6},{27,7},{28,0},{29,1},{30,2},{31,3}} | collective-permute-start | bytes 196616 | tf_op jit(solution)/shard_map/ppermute | solution.py:1041
  381.8 9.1 %collective-permute-start.112 = (f32[16,1024]{1,0:T(8,128)S(1)}, f32[16,1024]{1,0:T(8,128)S(1)}, u32[]{:S(2)}, u32[]{:S(2)}) collective-permute-start(f32[16,1024]{1,0:T(8,128)S(1)} %get-tuple-element.331.refs_4_), channel_id=1, source_target_pairs={{16,4},{17,5},{18,6},{19,7},{20,0},{21,1},{22,2},{23,3}} | collective-permute-start | bytes 196616 | tf_op jit(solution)/shard_map/ppermute | solution.py:1041
  383.1 7.8 %collective-permute-start.113 = (f32[16,1024]{1,0:T(8,128)S(1)}, f32[16,1024]{1,0:T(8,128)S(1)}, u32[]{:S(2)}, u32[]{:S(2)}) collective-permute-start(f32[16,1024]{1,0:T(8,128)S(1)} %get-tuple-element.331.refs_4_), channel_id=1, source_target_pairs={{8,0},{9,1},{10,2},{11,3},{12,4},{13,5},{14,6},{15,7}} | collective-permute-start | bytes 196616 | tf_op jit(solution)/shard_map/ppermute | solution.py:1041
  390.9 4.4 %collective-permute-start.114 = (f32[128,128]{1,0:T(8,128)S(1)}, f32[128,128]{1,0:T(8,128)S(1)}, u32[]{:S(2)}, u32[]{:S(2)}) collective-permute-start(f32[128,128]{1,0:T(8,128)S(1)} %reduce_part.5.refs_0_), channel_id=1, source_target_pairs={{0,2},{1,3},{2,0},{3,1},{4,6},{5,7},{6,4},{7,5},{8,10},{9,11},{10,... | collective-permute-start | bytes 196616 | tf_op jit(solution)/shard_map/ppermute | solution.py:825
  390.9 5.2 %collective-permute-start.115 = (f32[128,128]{1,0:T(8,128)S(1)}, f32[128,128]{1,0:T(8,128)S(1)}, u32[]{:S(2)}, u32[]{:S(2)}) collective-permute-start(f32[128,128]{1,0:T(8,128)S(1)} %reduce_part.5.refs_0_), channel_id=1, source_target_pairs={{0,4},{1,5},{2,6},{3,7},{4,0},{5,1},{6,2},{7,3},{8,12},{9,13},{10,... | collective-permute-start | bytes 196616 | tf_op jit(solution)/shard_map/ppermute | solution.py:825
  391.6 6.6 %collective-permute-start.116 = (f32[128,128]{1,0:T(8,128)S(1)}, f32[128,128]{1,0:T(8,128)S(1)}, u32[]{:S(2)}, u32[]{:S(2)}) collective-permute-start(f32[128,128]{1,0:T(8,128)S(1)} %reduce_part.5.refs_0_), channel_id=1, source_target_pairs={{0,6},{1,7},{2,4},{3,5},{4,2},{5,3},{6,0},{7,1},{8,14},{9,15},{10,... | collective-permute-start | bytes 196616 | tf_op jit(solution)/shard_map/ppermute | solution.py:825
  398.8 7.1 %collective-permute-start.117 = (f32[512,128]{1,0:T(8,128)S(1)}, f32[512,128]{1,0:T(8,128)S(1)}, u32[]{:S(2)}, u32[]{:S(2)}) collective-permute-start(f32[512,128]{1,0:T(8,128)S(1)} %gather_part.2.refs_0_), channel_id=1, source_target_pairs={{0,8},{1,9},{2,10},{3,11},{4,12},{5,13},{6,14},{7,15},{8,0},{9,1},... | collective-permute-start | bytes 786440 | tf_op jit(solution)/shard_map/ppermute | solution.py:825
  398.9 9.9 %collective-permute-start.118 = (f32[512,128]{1,0:T(8,128)S(1)}, f32[512,128]{1,0:T(8,128)S(1)}, u32[]{:S(2)}, u32[]{:S(2)}) collective-permute-start(f32[512,128]{1,0:T(8,128)S(1)} %gather_part.2.refs_0_), channel_id=1, source_target_pairs={{0,16},{1,17},{2,18},{3,19},{4,20},{5,21},{6,22},{7,23},{8,24},{9,... | collective-permute-start | bytes 786440 | tf_op jit(solution)/shard_map/ppermute | solution.py:825
  398.9 9.9 %collective-permute-start.119 = (f32[512,128]{1,0:T(8,128)S(1)}, f32[512,128]{1,0:T(8,128)S(1)}, u32[]{:S(2)}, u32[]{:S(2)}) collective-permute-start(f32[512,128]{1,0:T(8,128)S(1)} %gather_part.2.refs_0_), channel_id=1, source_target_pairs={{0,24},{1,25},{2,26},{3,27},{4,28},{5,29},{6,30},{7,31},{8,16},{9,... | collective-permute-start | bytes 786440 | tf_op jit(solution)/shard_map/ppermute | solution.py:825
  (105 other events, 678.1 us)

commit v7 on v6

--- a/solution.py
+++ b/solution.py
@@ -154,11 +154,12 @@
     return slice(rows.start + offset, rows.stop + offset)
 
 
-def entered_inlet_kernel(lon, ids_ref, own_ref, arrived_ref, *refs):
+def entered_inlet_kernel(plan, lon, ids_ref, own_ref, arrived_ref, *refs):
     state_ref, cot_ref = refs[3], refs[4]
     size = state_ref.shape[0]
-    state_ref[...] = jnp.where(ids_ref[0] < 2, own_ref[:size], arrived_ref[:size])
-    cot_ref[...] = jnp.where(ids_ref[0] < 2, own_ref[size:], arrived_ref[size:])
+    stays = plan.stays(ids_ref[0], ids_ref[1])
+    state_ref[...] = jnp.where(stays, own_ref[:size], arrived_ref[:size])
+    cot_ref[...] = jnp.where(stays, own_ref[size:], arrived_ref[size:])
     inlet_kernel(lon, state_ref, *refs[:3], *refs[5:])
 
 
@@ -512,14 +513,19 @@
     out_ref = refs[-1]
     size = kept_ref.shape[0] // 2
     early, late = refs[: plan.sections], refs[plan.sections : -1]
+    if late:
+        kept_late_ref, *late = late
     for steps, ref in enumerate(early):
         source = lax.rem(section - steps + plan.sections, plan.sections)
         place = order_ref[0, plan.slot(source, dp)]
         value = ref[start : start + size]
-        if plan.halved and not steps:
-            value = jnp.where(section < 2, kept_ref[start : start + size], value)
         if late:
             value = jnp.where(section == 0, late[steps][...], value)
+        if plan.halved and not steps:
+            kept = kept_ref[start : start + size]
+            if late:
+                kept = jnp.where(section == 0, kept_late_ref[...], kept)
+            value = jnp.where(plan.stays(section, dp), kept, value)
         for row in range(out_ref.shape[0]):
             out_ref[row, pl.ds(place, 1)] = value[row : row + 1]
 
@@ -750,7 +756,7 @@
 
 
 VMEM_LIMIT = 24 * 1024 * 1024
-ALONE_LIMIT = 56 * 1024 * 1024
+ALONE_LIMIT = 46 * 1024 * 1024
 
 
 def in_groups(array, axis, groups):
@@ -786,10 +792,13 @@
     def slot(self, section, home):
         if not self.halved:
             return section
-        return lax.rem(home // self.half + section // 2, 2) * 2 + lax.rem(section, 2)
+        return lax.rem(home // self.half + section // 2 + home, 2) * 2 + lax.rem(section, 2)
+
+    def stays(self, section, dp):
+        return lax.rem(section // 2 + dp, 2) == 0
 
     def other(self, section, dp):
-        return dp ^ self.half if self.halved and section >= 2 else dp
+        return dp ^ self.half if self.halved and (section // 2 + dp) % 2 else dp
 
     def to_workers(self, steps):
         return [
@@ -968,7 +977,7 @@
             if not plan.halved:
                 arrived = entry
             state, own_cot, inner, pre_one, sums_one = call(
-                functools.partial(entered_inlet_kernel, lon), [state_shape, packed, plane, plane, small], [patches],
+                functools.partial(entered_inlet_kernel, plan, lon), [state_shape, packed, plane, plane, small], [patches],
                 name="inlet", scalars=1,
             )(ids, entry, arrived, static_part, moving_cat, first_cat)
         else:
@@ -1037,9 +1046,7 @@
             inner, d_two, d_partial, first_back_cat, moving_back_cat,
             acc["first"], acc["moving"], acc["inner"],
         )
-    late = [grads[0]] + [
-        lax.ppermute(grads[0], ("section", "dp"), plan.to_first_home(steps)) for steps in range(1, segments)
-    ]
+    late = [grads[0]] + [moved(grads[0], plan.to_first_home(steps)) for steps in range(segments)]
 
     rounds = plan.all_rounds
     rows = 2 * 9 * channels + 9 * (statics + -statics % GROUP) + 45 * GROUP + 4 * channels + 23 * GROUP
@@ -1059,15 +1066,17 @@
         ids, static_maps, acc["inner"], acc["first"], acc["second"], acc["moving"], acc["qkv"], acc["mixer"],
         acc["velocity"], acc["small_one"], acc["small_two"],
     )
-    for bits, later in zip(rounds, rounds[1:] + [[]]):
+    for place, (bits, later) in enumerate(zip(rounds, rounds[1:] + [[]])):
         parts = swap(parts, bits)
+        if place == 1:
+            parts, late = lax.optimization_barrier((parts, late))
+            grads_out = put_home(2 * GROUP, early + late)
+            parts, path_out, grads_out = lax.optimization_barrier((parts, path_out, grads_out))
         rows >>= len(bits)
         parts = call(
             functools.partial(reduce_kernel, plan, later, len(parts)), shares(rows, later),
             [pltpu.VMEM((rows, channels), F32)], name="reduce_part", scalars=1,
         )(ids, *parts)
-    parts, late = lax.optimization_barrier((parts, late))
-    grads_out = put_home(2 * GROUP, early + late)
     for bits in rounds[::-1]:
         parts = swap([parts[0]] * (1 << len(bits)), bits)
         rows <<= len(bits)

time: 421 us -> 426 us (1.012)
  local copies, waits for them, and re-layouts: 16.8 us -> 28.1 us
  waiting for transfers between devices: 104 us -> 96.4 us
    ppermute x46, starting transfers between devices: 49.6 us -> 64.9 us  [exchanged(): lax.ppermute(value, ('section', 'dp'), [(own, own ^ mask) for own in rang...]
    unnamed x96 -> x130, local copies, waits for them, and re-layouts: 13.8 us -> 25 us
    ppermute x64, starting transfers between devices: 79.6 us -> 68.6 us  [micro_sum(): total = total + lax.ppermute(value, ('section', 'dp'), pairs)]
    ppermute x64, waiting for transfers between devices: 42.2 us -> 33 us  [micro_sum(): total = total + lax.ppermute(value, ('section', 'dp'), pairs)]
    ppermute x3 -> x0, waiting for transfers between devices: 5.91 us -> none  [on_device(): lax.ppermute(grads[0], ('section', 'dp'), plan.to_first_home(steps))]
    ppermute x8 -> x12, waiting for transfers between devices: 7.69 us -> 13.4 us  [moved(): return lax.ppermute(value, ('section', 'dp'), going)]
    ppermute x8 -> x12, starting transfers between devices: 16 us -> 18.6 us  [moved(): return lax.ppermute(value, ('section', 'dp'), going)]
  transfers between devices with their start and end apart: 121 -> 122, of which waited for: 74 -> 72; matrix products, arithmetic and copies ran while one was open for 1% -> 0% of each run, Pallas kernels for 5% -> 4%
where the time goes in v7:
time: 426 us; the launch traced here: 420 us
  starting transfers between devices  152 us (36%)
  Pallas kernels  138 us (32%)
  waiting for transfers between devices  96.4 us (23%)
  local copies, waits for them, and re-layouts  28.1 us (7%)
    pallas_call x36, Pallas kernels, run(): pl.pallas_call(kernel, out_shape=tuple((jax.ShapeDtypeStruct(shape, kind)...  138 us
    ppermute x64, starting transfers between devices, micro_sum(): total = total + lax.ppermute(value, ('section', 'dp'), pairs)  68.6 us
    ppermute x46, starting transfers between devices, exchanged(): lax.ppermute(value, ('section', 'dp'), [(own, own ^ mask) for own in rang...  64.9 us
    ppermute x46, waiting for transfers between devices, exchanged(): lax.ppermute(value, ('section', 'dp'), [(own, own ^ mask) for own in rang...  50 us
    ppermute x64, waiting for transfers between devices, micro_sum(): total = total + lax.ppermute(value, ('section', 'dp'), pairs)  33 us
    unnamed x130, local copies, waits for them, and re-layouts  25 us
    ppermute x12, starting transfers between devices, moved(): return lax.ppermute(value, ('section', 'dp'), going)  18.6 us
    ppermute x12, waiting for transfers between devices, moved(): return lax.ppermute(value, ('section', 'dp'), going)  13.4 us
  transfers between devices with their start and end apart: 122, of which 72 were waited for; matrix products, arithmetic and copies ran while one was open for 0% of the time, Pallas kernels for 4%

profile of v7, /device:TPU:0, one launch (start us, length us, event | category | flops | bytes accessed | tf_op | source)
XLA Modules:
  0.0 419.6 jit_solution(7680536313471931658)
XLA Ops:
  16.2 4.4 %weights.1 = (f32[1024,128]{1,0:T(8,128)S(1)}, bf16[768,256]{1,0:T(8,128)(2,1)S(1)}, bf16[768,256]{1,0:T(8,128)(2,1)S(1)}, bf16[2304,256]{1,0:T(8,128)(2,1)S(1)}...) custom-call(f32[9,100,128]{2,1,0:T(8,128)S(1)} %copy-done.37, ...), custom_call_target="tpu_custom_call" | custom-call | tf_op jit(solution)/shard_map/weights/pallas_call | solution.py:744
  21.4 3.7 inlet.4
  28.0 4.8 %collective-permute-start.1 = (f32[8,128]{1,0:T(8,128)S(1)}, f32[8,128]{1,0:T(8,128)S(1)}, u32[]{:S(2)}, u32[]{:S(2)}) collective-permute-start(f32[8,128]{1,0:T(8,128)S(1)} %get-tuple-element.200), channel_id=1, source_target_pairs={{0,1},{1,0},{2,3},{3,2},{4,5},{5,4},{6,7},{7,6},{8,9},{9,8},{10,11... | collective-permute-start | bytes 12296 | tf_op jit(solution)/shard_map/ppermute | solution.py:834
  35.7 2.3 collective-permute-start.3
  40.0 2.9 collective-permute-done.4
  50.0 3.1 collective-permute-start.10
  54.6 3.0 collective-permute-done.8
  58.7 1.8 collective-permute-start.12
  69.5 5.7 %outlet.4 = (f32[24,1024]{1,0:T(8,128)S(1)}, f32[16,1024]{1,0:T(8,128)S(1)}, f32[1024,128]{1,0:T(8,128)S(1)}, f32[1024,128]{1,0:T(8,128)S(1)}, f32[1024,128]{1,0:T(8,128)S(1)}) custom-call(f32[24,1024]{1,0:T(8,128)S(1)} %copy-done.33, f32[1024,128]{1,0:T(8,128)S(1)} %copy-done.17, f32[1024,128]{1,0:T(8,128)S(1)} %copy-done.14, ...), custom_call_target="tpu_custom_call" | custom-call | tf_op jit(solution)/shard_map/outlet/pallas_call | solution.py:744
  75.3 3.1 inlet.5
  86.1 2.6 collective-permute-start.18
  93.9 2.0 collective-permute-start.22
  98.4 2.1 collective-permute-start.24
  101.4 5.8 %outlet.5 = (f32[24,1024]{1,0:T(8,128)S(1)}, f32[16,1024]{1,0:T(8,128)S(1)}, f32[1024,128]{1,0:T(8,128)S(1)}, f32[1024,128]{1,0:T(8,128)S(1)}, f32[1024,128]{1,0:T(8,128)S(1)}) custom-call(f32[24,1024]{1,0:T(8,128)S(1)} %get-tuple-element.211.state_ref, f32[1024,128]{1,0:T(8,128)S(1)} %get-tuple-element.212.inner_ref, ...), custom_call_target="tpu_custom_call" | custom-call | tf_op jit(solution)/shard_map/outlet/pallas_call | solution.py:744
  107.1 3.1 inlet.6
  117.9 2.8 collective-permute-start.30
  125.9 2.0 collective-permute-start.34
  130.4 2.1 collective-permute-start.36
  133.4 5.8 %outlet.6 = (f32[24,1024]{1,0:T(8,128)S(1)}, f32[16,1024]{1,0:T(8,128)S(1)}, f32[1024,128]{1,0:T(8,128)S(1)}, f32[1024,128]{1,0:T(8,128)S(1)}, f32[1024,128]{1,0:T(8,128)S(1)}) custom-call(f32[24,1024]{1,0:T(8,128)S(1)} %get-tuple-element.217.state_ref, f32[1024,128]{1,0:T(8,128)S(1)} %get-tuple-element.218.inner_ref, ...), custom_call_target="tpu_custom_call" | custom-call | tf_op jit(solution)/shard_map/outlet/pallas_call | solution.py:744
  139.1 3.1 inlet.7
  150.0 2.8 collective-permute-start.45
  157.9 2.0 collective-permute-start.49
  162.2 1.8 collective-permute-start.38
  166.5 1.9 collective-permute-done.39
  168.5 6.4 %outlet.7 = (f32[24,1024]{1,0:T(8,128)}, f32[16,1024]{1,0:T(8,128)S(1)}, f32[1024,128]{1,0:T(8,128)S(1)}, f32[1024,128]{1,0:T(8,128)S(1)}, f32[1024,128]{1,0:T(8,128)S(1)}) custom-call(f32[24,1024]{1,0:T(8,128)S(1)} %get-tuple-element.223.state_ref, f32[1024,128]{1,0:T(8,128)S(1)} %get-tuple-element.228.inner_ref, ...), custom_call_target="tpu_custom_call" | custom-call | tf_op jit(solution)/shard_map/outlet/pallas_call | solution.py:744
  175.1 12.3 %outlet_back.4 = (f32[24,1024]{1,0:T(8,128)S(1)}, f32[1024,128]{1,0:T(8,128)S(1)}, f32[8,128]{1,0:T(8,128)S(1)}, f32[128,384]{1,0:T(8,128)S(1)}, f32[128,128]{1,...) custom-call(s32[2]{0:T(128)S(1)} %pad_add_fusion.ids_ref, ...), custom_call_target="tpu_custom_call", output_to_operand_aliasing={{3}: (17, {}), {4}: (18, {}), {5}: (19, {}), {6}: (20, {})} | custom-call | tf_op jit(solution)/shard_map/outlet_back/pallas_call | solution.py:744
  187.4 3.7 collective-permute-start.52
  200.8 3.0 middle_back.4
  211.7 2.8 collective-permute-start.63
  215.5 4.3 %inlet_back.4 = (f32[24,1024]{1,0:T(8,128)S(1)}, f32[16,1024]{1,0:T(8,128)S(1)}, f32[9,128,128]{2,1,0:T(8,128)S(1)}, f32[3,128,128]{2,1,0:T(8,128)S(1)}, f32[1024,128]{1,0:T(8,128)S(1)}) custom-call(f32[24,1024]{1,0:T(8,128)S(1)} %get-tuple-element.223.state_ref, ...), custom_call_target="tpu_custom_call", output_to_operand_aliasing={{2}: (11, {}), {3}: (12, {}), {4}: (13, {})} | custom-call | tf_op jit(solution)/shard_map/inlet_back/pallas_call | solution.py:744
  219.8 12.3 %outlet_back.5 = (f32[24,1024]{1,0:T(8,128)S(1)}, f32[1024,128]{1,0:T(8,128)S(1)}, f32[8,128]{1,0:T(8,128)S(1)}, f32[128,384]{1,0:T(8,128)S(1)}, f32[128,128]{1,...) custom-call(s32[2]{0:T(128)S(1)} %pad_add_fusion.ids_ref, ...), custom_call_target="tpu_custom_call", output_to_operand_aliasing={{3}: (17, {}), {4}: (18, {}), {5}: (19, {}), {6}: (20, {})} | custom-call | tf_op jit(solution)/shard_map/outlet_back/pallas_call | solution.py:744
  234.9 1.9 collective-permute-start.67
  239.5 1.9 collective-permute-start.69
  242.1 3.0 middle_back.5
  253.0 2.8 collective-permute-start.75
  256.6 4.3 %inlet_back.5 = (f32[24,1024]{1,0:T(8,128)S(1)}, f32[16,1024]{1,0:T(8,128)S(1)}, f32[9,128,128]{2,1,0:T(8,128)S(1)}, f32[3,128,128]{2,1,0:T(8,128)S(1)}, f32[1024,128]{1,0:T(8,128)S(1)}) custom-call(f32[24,1024]{1,0:T(8,128)S(1)} %get-tuple-element.217.state_ref, ...), custom_call_target="tpu_custom_call", output_to_operand_aliasing={{2}: (11, {}), {3}: (12, {}), {4}: (13, {})} | custom-call | tf_op jit(solution)/shard_map/inlet_back/pallas_call | solution.py:744
  261.0 12.0 %outlet_back.6 = (f32[24,1024]{1,0:T(8,128)S(1)}, f32[1024,128]{1,0:T(8,128)S(1)}, f32[8,128]{1,0:T(8,128)S(1)}, f32[128,384]{1,0:T(8,128)S(1)}, f32[128,128]{1,...) custom-call(s32[2]{0:T(128)S(1)} %pad_add_fusion.ids_ref, ...), custom_call_target="tpu_custom_call", output_to_operand_aliasing={{3}: (17, {}), {4}: (18, {}), {5}: (19, {}), {6}: (20, {})} | custom-call | tf_op jit(solution)/shard_map/outlet_back/pallas_call | solution.py:744
  275.8 1.9 collective-permute-start.79
  280.4 1.9 collective-permute-start.81
  283.1 3.0 middle_back.6
  293.9 2.8 collective-permute-start.87
  297.6 4.3 %inlet_back.6 = (f32[24,1024]{1,0:T(8,128)S(1)}, f32[16,1024]{1,0:T(8,128)S(1)}, f32[9,128,128]{2,1,0:T(8,128)S(1)}, f32[3,128,128]{2,1,0:T(8,128)S(1)}, f32[1024,128]{1,0:T(8,128)S(1)}) custom-call(f32[24,1024]{1,0:T(8,128)S(1)} %get-tuple-element.211.state_ref, ...), custom_call_target="tpu_custom_call", output_to_operand_aliasing={{2}: (11, {}), {3}: (12, {}), {4}: (13, {})} | custom-call | tf_op jit(solution)/shard_map/inlet_back/pallas_call | solution.py:744
  304.7 3.7 collective-permute-start.90
  308.5 2.5 collective-permute-start.91
  310.9 11.8 %outlet_back.7 = (f32[24,1024]{1,0:T(8,128)S(1)}, f32[1024,128]{1,0:T(8,128)S(1)}, f32[8,128]{1,0:T(8,128)S(1)}, f32[128,384]{1,0:T(8,128)S(1)}, f32[128,128]{1,...) custom-call(s32[2]{0:T(128)S(1)} %pad_add_fusion.ids_ref, ...), custom_call_target="tpu_custom_call", output_to_operand_aliasing={{3}: (17, {}), {4}: (18, {}), {5}: (19, {}), {6}: (20, {})} | custom-call | tf_op jit(solution)/shard_map/outlet_back/pallas_call | solution.py:744
  324.7 2.9 collective-permute-start.95
  329.2 2.7 collective-permute-start.97
  332.7 3.0 middle_back.7
  343.3 2.4 collective-permute-start.103
  346.5 5.0 %inlet_back.7 = (f32[24,1024]{1,0:T(8,128)}, f32[16,1024]{1,0:T(8,128)S(1)}, f32[9,128,128]{2,1,0:T(8,128)S(1)}, f32[3,128,128]{2,1,0:T(8,128)S(1)}, f32[1024,128]{1,0:T(8,128)S(1)}) custom-call(f32[24,1024]{1,0:T(8,128)S(1)} %copy-done.34, ...), custom_call_target="tpu_custom_call", output_to_operand_aliasing={{2}: (11, {}), {3}: (12, {}), {4}: (13, {})} | custom-call | tf_op jit(solution)/shard_map/inlet_back/pallas_call | solution.py:744
  351.5 2.0 pack.1
  353.9 2.3 collective-permute-done.104.refs_1_
  357.0 2.3 collective-permute-start.105
  364.1 7.5 %collective-permute-done.109.refs_6_ = f32[16,1024]{1,0:T(8,128)S(1)} collective-permute-done((f32[16,1024]{1,0:T(8,128)S(1)}, f32[16,1024]{1,0:T(8,128)S(1)}, u32[]{:S(2)}, u32[]{:S(2)}) %collective-permute-start.109) | collective-permute-done | bytes 65568 | tf_op jit(solution)/shard_map/ppermute | solution.py:841
  374.2 3.5 collective-permute-done.111.refs_8_
  381.1 3.1 collective-permute-start.114
  385.0 2.8 collective-permute-done.114.refs_3_
  388.4 3.0 collective-permute-start.116
  393.8 4.3 %collective-permute-done.117.refs_3_ = f32[128,128]{1,0:T(8,128)S(1)} collective-permute-done((f32[128,128]{1,0:T(8,128)S(1)}, f32[128,128]{1,0:T(8,128)S(1)}, u32[]{:S(2)}, u32[]{:S(2)}) %collective-permute-start.117) | collective-permute-done | bytes 65568 | tf_op jit(solution)/shard_map/ppermute | solution.py:834
  398.9 3.4 collective-permute-start.120
  402.3 5.6 %collective-permute-done.118.refs_1_ = f32[512,128]{1,0:T(8,128)S(1)} collective-permute-done((f32[512,128]{1,0:T(8,128)S(1)}, f32[512,128]{1,0:T(8,128)S(1)}, u32[]{:S(2)}, u32[]{:S(2)}) %collective-permute-start.118) | collective-permute-done | bytes 262176 | tf_op jit(solution)/shard_map/ppermute | solution.py:834
  407.9 5.0 %collective-permute-done.119.refs_2_ = f32[512,128]{1,0:T(8,128)S(1)} collective-permute-done((f32[512,128]{1,0:T(8,128)S(1)}, f32[512,128]{1,0:T(8,128)S(1)}, u32[]{:S(2)}, u32[]{:S(2)}) %collective-permute-start.119) | collective-permute-done | bytes 262176 | tf_op jit(solution)/shard_map/ppermute | solution.py:834
  413.7 2.6 collective-permute-done.121.refs_1_
  416.3 2.0 unpack.1
  (412 shorter events, 174.1 us)
Async XLA Ops:
  6.5 14.9 %collective-permute-start = (f32[40,1024]{1,0:T(8,128)S(1)}, f32[40,1024]{1,0:T(8,128)S(1)}, u32[]{:S(2)}, u32[]{:S(2)}) collective-permute-start(f32[40,1024]{1,0:T(8,128)S(1)} %get-tuple-element.193.own_ref), channel_id=1, source_target_pairs={{1,5},{3,7},{5,1},{7,3},{9,13},{11,15},{13,9},{15,11},{16,20},{18,... | collective-permute-start | bytes 491528 | tf_op jit(solution)/shard_map/ppermute | solution.py:841
  28.0 5.7 %collective-permute-start.1 = (f32[8,128]{1,0:T(8,128)S(1)}, f32[8,128]{1,0:T(8,128)S(1)}, u32[]{:S(2)}, u32[]{:S(2)}) collective-permute-start(f32[8,128]{1,0:T(8,128)S(1)} %get-tuple-element.200), channel_id=1, source_target_pairs={{0,1},{1,0},{2,3},{3,2},{4,5},{5,4},{6,7},{7,6},{8,9},{9,8},{10,11... | collective-permute-start | bytes 12296 | tf_op jit(solution)/shard_map/ppermute | solution.py:834
  34.3 5.0 %collective-permute-start.2 = (f32[8,128]{1,0:T(8,128)}, f32[8,128]{1,0:T(8,128)S(1)}, u32[]{:S(2)}, u32[]{:S(2)}) collective-permute-start(f32[8,128]{1,0:T(8,128)} %add.290), channel_id=1, source_target_pairs={{1,11},{3,9},{5,15},{7,13},{9,3},{11,1},{13,7},{15,5},{17,27},{19,... | collective-permute-start | bytes 12296 | tf_op jit(solution)/shard_map/ppermute | solution.py:858
  35.7 4.2 %collective-permute-start.3 = (f32[8,128]{1,0:T(8,128)}, f32[8,128]{1,0:T(8,128)}, u32[]{:S(2)}, u32[]{:S(2)}) collective-permute-start(f32[8,128]{1,0:T(8,128)} %add.290), channel_id=1, source_target_pairs={{1,19},{3,17},{5,23},{7,21},{9,27},{11,25},{13,31},{15,29},{17,3},... | collective-permute-start | bytes 12296 | tf_op jit(solution)/shard_map/ppermute | solution.py:858
  38.1 4.8 %collective-permute-start.4 = (f32[8,128]{1,0:T(8,128)}, f32[8,128]{1,0:T(8,128)}, u32[]{:S(2)}, u32[]{:S(2)}) collective-permute-start(f32[8,128]{1,0:T(8,128)} %add.290), channel_id=1, source_target_pairs={{1,27},{3,25},{5,31},{7,29},{9,19},{11,17},{13,23},{15,21},{17,11}... | collective-permute-start | bytes 12296 | tf_op jit(solution)/shard_map/ppermute | solution.py:858
  38.1 4.8 %collective-permute-start.5 = (f32[8,128]{1,0:T(8,128)}, f32[8,128]{1,0:T(8,128)}, u32[]{:S(2)}, u32[]{:S(2)}) collective-permute-start(f32[8,128]{1,0:T(8,128)} %add.290), channel_id=1, source_target_pairs={{1,3},{3,1},{5,7},{7,5},{9,11},{11,9},{13,15},{15,13},{17,19},{19,... | collective-permute-start | bytes 12296 | tf_op jit(solution)/shard_map/ppermute | solution.py:858
  50.0 4.6 %collective-permute-start.10 = (f32[8,128]{1,0:T(8,128)S(1)}, f32[8,128]{1,0:T(8,128)S(1)}, u32[]{:S(2)}, u32[]{:S(2)}) collective-permute-start(f32[8,128]{1,0:T(8,128)S(1)} %add.296), channel_id=1, source_target_pairs={{1,27},{3,25},{5,31},{7,29},{9,19},{11,17},{13,23},{15,21},{17,11}... | collective-permute-start | bytes 12296 | tf_op jit(solution)/shard_map/ppermute | solution.py:858
  53.9 3.7 collective-permute-start.8
  58.7 3.9 collective-permute-start.12
  79.7 4.1 collective-permute-start.14
  81.6 4.5 %collective-permute-start.16 = (f32[8,128]{1,0:T(8,128)S(1)}, f32[8,128]{1,0:T(8,128)S(1)}, u32[]{:S(2)}, u32[]{:S(2)}) collective-permute-start(f32[8,128]{1,0:T(8,128)S(1)} %add.302), channel_id=1, source_target_pairs={{1,27},{3,25},{5,31},{7,29},{9,19},{11,17},{13,23},{15,21},{17,11}... | collective-permute-start | bytes 12296 | tf_op jit(solution)/shard_map/ppermute | solution.py:858
  92.4 4.6 %collective-permute-start.20 = (f32[8,128]{1,0:T(8,128)S(1)}, f32[8,128]{1,0:T(8,128)S(1)}, u32[]{:S(2)}, u32[]{:S(2)}) collective-permute-start(f32[8,128]{1,0:T(8,128)S(1)} %add.308), channel_id=1, source_target_pairs={{1,11},{3,9},{5,15},{7,13},{9,3},{11,1},{13,7},{15,5},{17,27},{19,... | collective-permute-start | bytes 12296 | tf_op jit(solution)/shard_map/ppermute | solution.py:858
  93.9 4.5 %collective-permute-start.22 = (f32[8,128]{1,0:T(8,128)S(1)}, f32[8,128]{1,0:T(8,128)S(1)}, u32[]{:S(2)}, u32[]{:S(2)}) collective-permute-start(f32[8,128]{1,0:T(8,128)S(1)} %add.308), channel_id=1, source_target_pairs={{1,27},{3,25},{5,31},{7,29},{9,19},{11,17},{13,23},{15,21},{17,11}... | collective-permute-start | bytes 12296 | tf_op jit(solution)/shard_map/ppermute | solution.py:858
  111.5 4.1 collective-permute-start.26
  113.4 4.5 %collective-permute-start.28 = (f32[8,128]{1,0:T(8,128)S(1)}, f32[8,128]{1,0:T(8,128)S(1)}, u32[]{:S(2)}, u32[]{:S(2)}) collective-permute-start(f32[8,128]{1,0:T(8,128)S(1)} %add.314), channel_id=1, source_target_pairs={{1,27},{3,25},{5,31},{7,29},{9,19},{11,17},{13,23},{15,21},{17,11}... | collective-permute-start | bytes 12296 | tf_op jit(solution)/shard_map/ppermute | solution.py:858
  124.4 4.3 %collective-permute-start.32 = (f32[8,128]{1,0:T(8,128)S(1)}, f32[8,128]{1,0:T(8,128)S(1)}, u32[]{:S(2)}, u32[]{:S(2)}) collective-permute-start(f32[8,128]{1,0:T(8,128)S(1)} %add.320), channel_id=1, source_target_pairs={{1,11},{3,9},{5,15},{7,13},{9,3},{11,1},{13,7},{15,5},{17,27},{19,... | collective-permute-start | bytes 12296 | tf_op jit(solution)/shard_map/ppermute | solution.py:858
  125.9 4.5 %collective-permute-start.34 = (f32[8,128]{1,0:T(8,128)S(1)}, f32[8,128]{1,0:T(8,128)S(1)}, u32[]{:S(2)}, u32[]{:S(2)}) collective-permute-start(f32[8,128]{1,0:T(8,128)S(1)} %add.320), channel_id=1, source_target_pairs={{1,27},{3,25},{5,31},{7,29},{9,19},{11,17},{13,23},{15,21},{17,11}... | collective-permute-start | bytes 12296 | tf_op jit(solution)/shard_map/ppermute | solution.py:858
  143.5 4.1 collective-permute-start.41
  145.5 4.5 %collective-permute-start.43 = (f32[8,128]{1,0:T(8,128)S(1)}, f32[8,128]{1,0:T(8,128)S(1)}, u32[]{:S(2)}, u32[]{:S(2)}) collective-permute-start(f32[8,128]{1,0:T(8,128)S(1)} %add.326), channel_id=1, source_target_pairs={{1,27},{3,25},{5,31},{7,29},{9,19},{11,17},{13,23},{15,21},{17,11}... | collective-permute-start | bytes 12296 | tf_op jit(solution)/shard_map/ppermute | solution.py:858
  156.5 5.7 %collective-permute-start.47 = (f32[8,128]{1,0:T(8,128)S(1)}, f32[8,128]{1,0:T(8,128)S(1)}, u32[]{:S(2)}, u32[]{:S(2)}) collective-permute-start(f32[8,128]{1,0:T(8,128)S(1)} %add.332), channel_id=1, source_target_pairs={{1,11},{3,9},{5,15},{7,13},{9,3},{11,1},{13,7},{15,5},{17,27},{19,... | collective-permute-start | bytes 12296 | tf_op jit(solution)/shard_map/ppermute | solution.py:858
  157.9 6.0 %collective-permute-start.48 = (f32[8,128]{1,0:T(8,128)S(1)}, f32[8,128]{1,0:T(8,128)S(1)}, u32[]{:S(2)}, u32[]{:S(2)}) collective-permute-start(f32[8,128]{1,0:T(8,128)S(1)} %add.332), channel_id=1, source_target_pairs={{1,19},{3,17},{5,23},{7,21},{9,27},{11,25},{13,31},{15,29},{17,3},... | collective-permute-start | bytes 12296 | tf_op jit(solution)/shard_map/ppermute | solution.py:858
  157.9 7.7 %collective-permute-start.49 = (f32[8,128]{1,0:T(8,128)S(1)}, f32[8,128]{1,0:T(8,128)S(1)}, u32[]{:S(2)}, u32[]{:S(2)}) collective-permute-start(f32[8,128]{1,0:T(8,128)S(1)} %add.332), channel_id=1, source_target_pairs={{1,27},{3,25},{5,31},{7,29},{9,19},{11,17},{13,23},{15,21},{17,11}... | collective-permute-start | bytes 12296 | tf_op jit(solution)/shard_map/ppermute | solution.py:858
  159.9 5.7 %collective-permute-start.50 = (f32[8,128]{1,0:T(8,128)S(1)}, f32[8,128]{1,0:T(8,128)S(1)}, u32[]{:S(2)}, u32[]{:S(2)}) collective-permute-start(f32[8,128]{1,0:T(8,128)S(1)} %add.332), channel_id=1, source_target_pairs={{1,3},{3,1},{5,7},{7,5},{9,11},{11,9},{13,15},{15,13},{17,19},{19,... | collective-permute-start | bytes 12296 | tf_op jit(solution)/shard_map/ppermute | solution.py:858
  160.6 5.4 %collective-permute-start.37 = (f32[16,1024]{1,0:T(8,128)S(1)}, f32[16,1024]{1,0:T(8,128)S(1)}, u32[]{:S(2)}, u32[]{:S(2)}) collective-permute-start(f32[16,1024]{1,0:T(8,128)S(1)} %copy-done.64), channel_id=1, source_target_pairs={{0,8},{1,13},{2,10},{3,15},{4,12},{5,9},{6,14},{7,11},{8,20},{9,17... | collective-permute-start | bytes 196616 | tf_op jit(solution)/shard_map/ppermute | solution.py:841
  162.2 4.4 %collective-permute-start.38 = (f32[16,1024]{1,0:T(8,128)S(1)}, f32[16,1024]{1,0:T(8,128)S(1)}, u32[]{:S(2)}, u32[]{:S(2)}) collective-permute-start(f32[16,1024]{1,0:T(8,128)S(1)} %copy-done.62), channel_id=1, source_target_pairs={{0,20},{1,17},{2,22},{3,19},{4,16},{5,21},{6,18},{7,23},{8,28},{9,... | collective-permute-start | bytes 196616 | tf_op jit(solution)/shard_map/ppermute | solution.py:841
  164.0 4.5 %collective-permute-start.39 = (f32[16,1024]{1,0:T(8,128)S(1)}, f32[16,1024]{1,0:T(8,128)S(1)}, u32[]{:S(2)}, u32[]{:S(2)}) collective-permute-start(f32[16,1024]{1,0:T(8,128)S(1)} %copy-done.60), channel_id=1, source_target_pairs={{0,28},{1,25},{2,30},{3,27},{4,24},{5,29},{6,26},{7,31},{8,0},{9,5... | collective-permute-start | bytes 196616 | tf_op jit(solution)/shard_map/ppermute | solution.py:841
  187.4 4.5 %collective-permute-start.52 = (f32[8,128]{1,0:T(8,128)S(1)}, f32[8,128]{1,0:T(8,128)S(1)}, u32[]{:S(2)}, u32[]{:S(2)}) collective-permute-start(f32[8,128]{1,0:T(8,128)S(1)} %get-tuple-element.242), channel_id=1, source_target_pairs={{0,1},{1,0},{2,3},{3,2},{4,5},{5,4},{6,7},{7,6},{8,9},{9,8},{10,11... | collective-permute-start | bytes 12296 | tf_op jit(solution)/shard_map/ppermute | solution.py:834
  191.9 4.1 collective-permute-start.53
  193.7 4.5 %collective-permute-start.55 = (f32[8,128]{1,0:T(8,128)S(1)}, f32[8,128]{1,0:T(8,128)S(1)}, u32[]{:S(2)}, u32[]{:S(2)}) collective-permute-start(f32[8,128]{1,0:T(8,128)S(1)} %add.338), channel_id=1, source_target_pairs={{1,27},{3,25},{5,31},{7,29},{9,19},{11,17},{13,23},{15,21},{17,11}... | collective-permute-start | bytes 12296 | tf_op jit(solution)/shard_map/ppermute | solution.py:858
  205.1 4.3 %collective-permute-start.59 = (f32[8,128]{1,0:T(8,128)S(1)}, f32[8,128]{1,0:T(8,128)S(1)}, u32[]{:S(2)}, u32[]{:S(2)}) collective-permute-start(f32[8,128]{1,0:T(8,128)S(1)} %add.344), channel_id=1, source_target_pairs={{1,11},{3,9},{5,15},{7,13},{9,3},{11,1},{13,7},{15,5},{17,27},{19,... | collective-permute-start | bytes 12296 | tf_op jit(solution)/shard_map/ppermute | solution.py:858
  207.1 4.5 %collective-permute-start.61 = (f32[8,128]{1,0:T(8,128)S(1)}, f32[8,128]{1,0:T(8,128)S(1)}, u32[]{:S(2)}, u32[]{:S(2)}) collective-permute-start(f32[8,128]{1,0:T(8,128)S(1)} %add.344), channel_id=1, source_target_pairs={{1,27},{3,25},{5,31},{7,29},{9,19},{11,17},{13,23},{15,21},{17,11}... | collective-permute-start | bytes 12296 | tf_op jit(solution)/shard_map/ppermute | solution.py:858
  233.3 4.1 collective-permute-start.65
  234.9 4.5 %collective-permute-start.67 = (f32[8,128]{1,0:T(8,128)S(1)}, f32[8,128]{1,0:T(8,128)S(1)}, u32[]{:S(2)}, u32[]{:S(2)}) collective-permute-start(f32[8,128]{1,0:T(8,128)S(1)} %add.350), channel_id=1, source_target_pairs={{1,27},{3,25},{5,31},{7,29},{9,19},{11,17},{13,23},{15,21},{17,11}... | collective-permute-start | bytes 12296 | tf_op jit(solution)/shard_map/ppermute | solution.py:858
  246.4 4.1 collective-permute-start.71
  248.4 4.5 %collective-permute-start.73 = (f32[8,128]{1,0:T(8,128)S(1)}, f32[8,128]{1,0:T(8,128)S(1)}, u32[]{:S(2)}, u32[]{:S(2)}) collective-permute-start(f32[8,128]{1,0:T(8,128)S(1)} %add.356), channel_id=1, source_target_pairs={{1,27},{3,25},{5,31},{7,29},{9,19},{11,17},{13,23},{15,21},{17,11}... | collective-permute-start | bytes 12296 | tf_op jit(solution)/shard_map/ppermute | solution.py:858
  274.2 4.1 collective-permute-start.77
  275.8 4.5 %collective-permute-start.79 = (f32[8,128]{1,0:T(8,128)S(1)}, f32[8,128]{1,0:T(8,128)S(1)}, u32[]{:S(2)}, u32[]{:S(2)}) collective-permute-start(f32[8,128]{1,0:T(8,128)S(1)} %add.362), channel_id=1, source_target_pairs={{1,27},{3,25},{5,31},{7,29},{9,19},{11,17},{13,23},{15,21},{17,11}... | collective-permute-start | bytes 12296 | tf_op jit(solution)/shard_map/ppermute | solution.py:858
  287.3 4.1 collective-permute-start.83
  289.4 4.5 %collective-permute-start.85 = (f32[8,128]{1,0:T(8,128)S(1)}, f32[8,128]{1,0:T(8,128)S(1)}, u32[]{:S(2)}, u32[]{:S(2)}) collective-permute-start(f32[8,128]{1,0:T(8,128)S(1)} %add.368), channel_id=1, source_target_pairs={{1,27},{3,25},{5,31},{7,29},{9,19},{11,17},{13,23},{15,21},{17,11}... | collective-permute-start | bytes 12296 | tf_op jit(solution)/shard_map/ppermute | solution.py:858
  302.5 20.3 %collective-permute-start.88 = (f32[32,1024]{1,0:T(8,128)S(1)}, f32[32,1024]{1,0:T(8,128)S(1)}, u32[]{:S(2)}, u32[]{:S(2)}) collective-permute-start(f32[32,1024]{1,0:T(8,128)S(1)} %get-tuple-element.336.kept_ref), channel_id=1, source_target_pairs={{1,5},{3,7},{5,1},{7,3},{9,13},{11,15},{13,9},{15,11},{16,20},{18,... | collective-permute-start | bytes 393224 | tf_op jit(solution)/shard_map/ppermute | solution.py:841
  303.2 19.6 %collective-permute-start.89 = (f32[32,1024]{1,0:T(8,128)S(1)}, f32[32,1024]{1,0:T(8,128)S(1)}, u32[]{:S(2)}, u32[]{:S(2)}) collective-permute-start(f32[32,1024]{1,0:T(8,128)S(1)} %get-tuple-element.303), channel_id=1, source_target_pairs={{0,8},{1,13},{2,10},{3,15},{4,12},{5,9},{6,14},{7,11},{8,16},{9,21... | collective-permute-start | bytes 393224 | tf_op jit(solution)/shard_map/ppermute | solution.py:841
  304.7 18.1 %collective-permute-start.90 = (f32[32,1024]{1,0:T(8,128)S(1)}, f32[32,1024]{1,0:T(8,128)S(1)}, u32[]{:S(2)}, u32[]{:S(2)}) collective-permute-start(f32[32,1024]{1,0:T(8,128)S(1)} %get-tuple-element.304), channel_id=1, source_target_pairs={{0,16},{1,21},{2,18},{3,23},{4,20},{5,17},{6,22},{7,19},{8,24},{9,... | collective-permute-start | bytes 393224 | tf_op jit(solution)/shard_map/ppermute | solution.py:841
  308.5 14.4 %collective-permute-start.91 = (f32[32,1024]{1,0:T(8,128)S(1)}, f32[32,1024]{1,0:T(8,128)S(1)}, u32[]{:S(2)}, u32[]{:S(2)}) collective-permute-start(f32[32,1024]{1,0:T(8,128)S(1)} %get-tuple-element.305), channel_id=1, source_target_pairs={{0,24},{1,29},{2,26},{3,31},{4,28},{5,25},{6,30},{7,27},{8,0},{9,5... | collective-permute-start | bytes 393224 | tf_op jit(solution)/shard_map/ppermute | solution.py:841
  324.1 4.4 %collective-permute-start.93 = (f32[8,128]{1,0:T(8,128)S(1)}, f32[8,128]{1,0:T(8,128)S(1)}, u32[]{:S(2)}, u32[]{:S(2)}) collective-permute-start(f32[8,128]{1,0:T(8,128)S(1)} %add.374), channel_id=1, source_target_pairs={{1,11},{3,9},{5,15},{7,13},{9,3},{11,1},{13,7},{15,5},{17,27},{19,... | collective-permute-start | bytes 12296 | tf_op jit(solution)/shard_map/ppermute | solution.py:858
  324.1 4.4 %collective-permute-start.94 = (f32[8,128]{1,0:T(8,128)S(1)}, f32[8,128]{1,0:T(8,128)S(1)}, u32[]{:S(2)}, u32[]{:S(2)}) collective-permute-start(f32[8,128]{1,0:T(8,128)S(1)} %add.374), channel_id=1, source_target_pairs={{1,19},{3,17},{5,23},{7,21},{9,27},{11,25},{13,31},{15,29},{17,3},... | collective-permute-start | bytes 12296 | tf_op jit(solution)/shard_map/ppermute | solution.py:858
  324.7 4.5 %collective-permute-start.95 = (f32[8,128]{1,0:T(8,128)S(1)}, f32[8,128]{1,0:T(8,128)S(1)}, u32[]{:S(2)}, u32[]{:S(2)}) collective-permute-start(f32[8,128]{1,0:T(8,128)S(1)} %add.374), channel_id=1, source_target_pairs={{1,27},{3,25},{5,31},{7,29},{9,19},{11,17},{13,23},{15,21},{17,11}... | collective-permute-start | bytes 12296 | tf_op jit(solution)/shard_map/ppermute | solution.py:858
  337.0 4.2 %collective-permute-start.100 = (f32[8,128]{1,0:T(8,128)S(1)}, f32[8,128]{1,0:T(8,128)S(1)}, u32[]{:S(2)}, u32[]{:S(2)}) collective-permute-start(f32[8,128]{1,0:T(8,128)S(1)} %add.380), channel_id=1, source_target_pairs={{1,19},{3,17},{5,23},{7,21},{9,27},{11,25},{13,31},{15,29},{17,3},... | collective-permute-start | bytes 12296 | tf_op jit(solution)/shard_map/ppermute | solution.py:858
  337.5 4.5 %collective-permute-start.101 = (f32[8,128]{1,0:T(8,128)S(1)}, f32[8,128]{1,0:T(8,128)S(1)}, u32[]{:S(2)}, u32[]{:S(2)}) collective-permute-start(f32[8,128]{1,0:T(8,128)S(1)} %add.380), channel_id=1, source_target_pairs={{1,27},{3,25},{5,31},{7,29},{9,19},{11,17},{13,23},{15,21},{17,11}... | collective-permute-start | bytes 12296 | tf_op jit(solution)/shard_map/ppermute | solution.py:858
  339.6 3.7 collective-permute-start.99
  357.0 20.8 %collective-permute-start.105 = (f32[512,128]{1,0:T(8,128)S(1)}, f32[512,128]{1,0:T(8,128)S(1)}, u32[]{:S(2)}, u32[]{:S(2)}) collective-permute-start(f32[512,128]{1,0:T(8,128)S(1)} %get-tuple-element.328), channel_id=1, source_target_pairs={{0,8},{1,9},{2,10},{3,11},{4,12},{5,13},{6,14},{7,15},{8,0},{9,1},... | collective-permute-start | bytes 786440 | tf_op jit(solution)/shard_map/ppermute | solution.py:834
  359.3 18.5 %collective-permute-start.106 = (f32[512,128]{1,0:T(8,128)S(1)}, f32[512,128]{1,0:T(8,128)S(1)}, u32[]{:S(2)}, u32[]{:S(2)}) collective-permute-start(f32[512,128]{1,0:T(8,128)S(1)} %get-tuple-element.329), channel_id=1, source_target_pairs={{0,16},{1,17},{2,18},{3,19},{4,20},{5,21},{6,22},{7,23},{8,24},{9,... | collective-permute-start | bytes 786440 | tf_op jit(solution)/shard_map/ppermute | solution.py:834
  359.4 18.3 %collective-permute-start.107 = (f32[512,128]{1,0:T(8,128)S(1)}, f32[512,128]{1,0:T(8,128)S(1)}, u32[]{:S(2)}, u32[]{:S(2)}) collective-permute-start(f32[512,128]{1,0:T(8,128)S(1)} %get-tuple-element.330), channel_id=1, source_target_pairs={{0,24},{1,25},{2,26},{3,27},{4,28},{5,29},{6,30},{7,31},{8,16},{9,... | collective-permute-start | bytes 786440 | tf_op jit(solution)/shard_map/ppermute | solution.py:834
  361.5 10.1 %collective-permute-start.109 = (f32[16,1024]{1,0:T(8,128)S(1)}, f32[16,1024]{1,0:T(8,128)S(1)}, u32[]{:S(2)}, u32[]{:S(2)}) collective-permute-start(f32[16,1024]{1,0:T(8,128)S(1)} %get-tuple-element.341.refs_4_), channel_id=1, source_target_pairs={{24,4},{25,1},{26,6},{27,3},{28,0},{29,5},{30,2},{31,7}} | collective-permute-start | bytes 196616 | tf_op jit(solution)/shard_map/ppermute | solution.py:841
  362.8 11.4 %collective-permute-start.110 = (f32[16,1024]{1,0:T(8,128)S(1)}, f32[16,1024]{1,0:T(8,128)S(1)}, u32[]{:S(2)}, u32[]{:S(2)}) collective-permute-start(f32[16,1024]{1,0:T(8,128)S(1)} %get-tuple-element.341.refs_4_), channel_id=1, source_target_pairs={{16,4},{17,1},{18,6},{19,3},{20,0},{21,5},{22,2},{23,7}} | collective-permute-start | bytes 196616 | tf_op jit(solution)/shard_map/ppermute | solution.py:841
  371.6 6.1 %collective-permute-start.111 = (f32[16,1024]{1,0:T(8,128)S(1)}, f32[16,1024]{1,0:T(8,128)S(1)}, u32[]{:S(2)}, u32[]{:S(2)}) collective-permute-start(f32[16,1024]{1,0:T(8,128)S(1)} %get-tuple-element.341.refs_4_), channel_id=1, source_target_pairs={{8,0},{9,5},{10,2},{11,7},{12,4},{13,1},{14,6},{15,3}} | collective-permute-start | bytes 196616 | tf_op jit(solution)/shard_map/ppermute | solution.py:841
  379.7 4.5 %collective-permute-start.112 = (f32[128,128]{1,0:T(8,128)S(1)}, f32[128,128]{1,0:T(8,128)S(1)}, u32[]{:S(2)}, u32[]{:S(2)}) collective-permute-start(f32[128,128]{1,0:T(8,128)S(1)} %get-tuple-element.353), channel_id=1, source_target_pairs={{0,2},{1,3},{2,0},{3,1},{4,6},{5,7},{6,4},{7,5},{8,10},{9,11},{10,... | collective-permute-start | bytes 196616 | tf_op jit(solution)/shard_map/ppermute | solution.py:834
  379.8 5.2 %collective-permute-start.113 = (f32[128,128]{1,0:T(8,128)S(1)}, f32[128,128]{1,0:T(8,128)S(1)}, u32[]{:S(2)}, u32[]{:S(2)}) collective-permute-start(f32[128,128]{1,0:T(8,128)S(1)} %get-tuple-element.354), channel_id=1, source_target_pairs={{0,4},{1,5},{2,6},{3,7},{4,0},{5,1},{6,2},{7,3},{8,12},{9,13},{10,... | collective-permute-start | bytes 196616 | tf_op jit(solution)/shard_map/ppermute | solution.py:834
  381.1 6.7 %collective-permute-start.114 = (f32[128,128]{1,0:T(8,128)S(1)}, f32[128,128]{1,0:T(8,128)S(1)}, u32[]{:S(2)}, u32[]{:S(2)}) collective-permute-start(f32[128,128]{1,0:T(8,128)S(1)} %get-tuple-element.355), channel_id=1, source_target_pairs={{0,6},{1,7},{2,4},{3,5},{4,2},{5,3},{6,0},{7,1},{8,14},{9,15},{10,... | collective-permute-start | bytes 196616 | tf_op jit(solution)/shard_map/ppermute | solution.py:834
  388.4 4.5 %collective-permute-start.115 = (f32[128,128]{1,0:T(8,128)S(1)}, f32[128,128]{1,0:T(8,128)S(1)}, u32[]{:S(2)}, u32[]{:S(2)}) collective-permute-start(f32[128,128]{1,0:T(8,128)S(1)} %reduce_part.5.refs_0_), channel_id=1, source_target_pairs={{0,2},{1,3},{2,0},{3,1},{4,6},{5,7},{6,4},{7,5},{8,10},{9,11},{10,... | collective-permute-start | bytes 196616 | tf_op jit(solution)/shard_map/ppermute | solution.py:834
  388.4 5.4 %collective-permute-start.116 = (f32[128,128]{1,0:T(8,128)S(1)}, f32[128,128]{1,0:T(8,128)S(1)}, u32[]{:S(2)}, u32[]{:S(2)}) collective-permute-start(f32[128,128]{1,0:T(8,128)S(1)} %reduce_part.5.refs_0_), channel_id=1, source_target_pairs={{0,4},{1,5},{2,6},{3,7},{4,0},{5,1},{6,2},{7,3},{8,12},{9,13},{10,... | collective-permute-start | bytes 196616 | tf_op jit(solution)/shard_map/ppermute | solution.py:834
  391.5 6.7 %collective-permute-start.117 = (f32[128,128]{1,0:T(8,128)S(1)}, f32[128,128]{1,0:T(8,128)S(1)}, u32[]{:S(2)}, u32[]{:S(2)}) collective-permute-start(f32[128,128]{1,0:T(8,128)S(1)} %reduce_part.5.refs_0_), channel_id=1, source_target_pairs={{0,6},{1,7},{2,4},{3,5},{4,2},{5,3},{6,0},{7,1},{8,14},{9,15},{10,... | collective-permute-start | bytes 196616 | tf_op jit(solution)/shard_map/ppermute | solution.py:834
  398.7 9.2 %collective-permute-start.118 = (f32[512,128]{1,0:T(8,128)S(1)}, f32[512,128]{1,0:T(8,128)S(1)}, u32[]{:S(2)}, u32[]{:S(2)}) collective-permute-start(f32[512,128]{1,0:T(8,128)S(1)} %gather_part.2.refs_0_), channel_id=1, source_target_pairs={{0,8},{1,9},{2,10},{3,11},{4,12},{5,13},{6,14},{7,15},{8,0},{9,1},... | collective-permute-start | bytes 786440 | tf_op jit(solution)/shard_map/ppermute | solution.py:834
  398.8 14.1 %collective-permute-start.119 = (f32[512,128]{1,0:T(8,128)S(1)}, f32[512,128]{1,0:T(8,128)S(1)}, u32[]{:S(2)}, u32[]{:S(2)}) collective-permute-start(f32[512,128]{1,0:T(8,128)S(1)} %gather_part.2.refs_0_), channel_id=1, source_target_pairs={{0,16},{1,17},{2,18},{3,19},{4,20},{5,21},{6,22},{7,23},{8,24},{9,... | collective-permute-start | bytes 786440 | tf_op jit(solution)/shard_map/ppermute | solution.py:834
  398.9 14.0 %collective-permute-start.120 = (f32[512,128]{1,0:T(8,128)S(1)}, f32[512,128]{1,0:T(8,128)S(1)}, u32[]{:S(2)}, u32[]{:S(2)}) collective-permute-start(f32[512,128]{1,0:T(8,128)S(1)} %gather_part.2.refs_0_), channel_id=1, source_target_pairs={{0,24},{1,25},{2,26},{3,27},{4,28},{5,29},{6,30},{7,31},{8,16},{9,... | collective-permute-start | bytes 786440 | tf_op jit(solution)/shard_map/ppermute | solution.py:834
  (123 other events, 613.1 us)

commit v8 on v7

--- a/solution.py
+++ b/solution.py
@@ -90,10 +90,17 @@
         patches_ref[lon : lon + cells, start + channels : start + 2 * channels] = low
 
 
+def doubled(weight_ref, channels):
+    taps = weight_ref.shape[0] // channels
+    rows = [weight_ref[tap * channels : (tap + 1) * channels] for tap in range(taps) for unused in range(2)]
+    return jnp.concatenate(rows, axis=0)
+
+
 def conv_patches(patches_ref, weight_ref, lon):
     cells = patches_ref.shape[0] - 2 * lon
     rows = [patches_ref[lon * place : lon * place + cells] for place in range(3)]
-    return folded(dot(jnp.concatenate(rows, axis=1), weight_ref[...]), 1)
+    channels = patches_ref.shape[1] // 6
+    return folded(dot(jnp.concatenate(rows, axis=1), doubled(weight_ref, channels)), 1)
 
 
 def sigmoid(value):
@@ -155,18 +162,20 @@
 
 
 def entered_inlet_kernel(plan, lon, ids_ref, own_ref, arrived_ref, *refs):
-    state_ref, cot_ref = refs[3], refs[4]
+    state_ref, cot_ref = refs[2], refs[3]
     size = state_ref.shape[0]
     stays = plan.stays(ids_ref[0], ids_ref[1])
     state_ref[...] = jnp.where(stays, own_ref[:size], arrived_ref[:size])
     cot_ref[...] = jnp.where(stays, own_ref[size:], arrived_ref[size:])
-    inlet_kernel(lon, state_ref, *refs[:3], *refs[5:])
+    inlet_kernel(lon, state_ref, *refs[:2], *refs[4:])
 
 
 def inlet_kernel(
-    lon, state_ref, static_ref, w_input_ref, w_first_ref,
+    lon, state_ref, static_ref, weights_ref,
     inner_ref, pre_ref, sums_ref, patches_ref,
 ):
+    w_input_ref = part_of(weights_ref, FORWARD_ROWS, "moving")
+    w_first_ref = part_of(weights_ref, FORWARD_ROWS, "first")
     cells = state_ref.shape[1]
     moving = inlet_channels(state_ref[...], lon).T
     width = patches_ref.shape[1]
@@ -175,7 +184,7 @@
     patches_ref[lon + cells :] = blank
     patches_ref[lon : lon + cells, :256] = beside(moving)
     rows = [patches_ref[lon * place : lon * place + cells, :256] for place in range(3)]
-    inner = folded(dot(jnp.concatenate(rows, axis=1), w_input_ref[...]), 1) + static_ref[...]
+    inner = folded(dot(jnp.concatenate(rows, axis=1), doubled(w_input_ref, width // 6)), 1) + static_ref[...]
     inner_ref[...] = inner
     fill_patches(patches_ref, inner * sigmoid(inner), lon)
     pre = conv_patches(patches_ref, w_first_ref, lon)
@@ -184,11 +193,12 @@
 
 
 def middle_kernel(
-    lon, count, pre_one_ref, sums_one_ref, gain_ref, shift_ref, w_second_ref,
+    lon, count, pre_one_ref, sums_one_ref, vectors_ref, weights_ref,
     pre_ref, sums_ref, patches_ref,
 ):
-    mean, unused_scale, factor = norm_of(sums_one_ref[...], gain_ref[...], count)
-    normed = (pre_one_ref[...] - mean) * factor + shift_ref[...]
+    w_second_ref = part_of(weights_ref, FORWARD_ROWS, "second")
+    mean, unused_scale, factor = norm_of(sums_one_ref[...], vectors_ref[0:1], count)
+    normed = (pre_one_ref[...] - mean) * factor + vectors_ref[1:2]
     fill_patches(patches_ref, normed * sigmoid(normed), lon)
     pre = conv_patches(patches_ref, w_second_ref, lon)
     pre_ref[...] = pre
@@ -209,16 +219,19 @@
 
 def outlet_kernel(
     lon, count, block_size, step_size, quantities,
-    state_ref, inner_ref, pre_two_ref, sums_two_ref, gain_ref, shift_ref,
-    w_heads_ref, w_mixer_ref, w_velocity_ref, b_velocity_ref,
+    state_ref, inner_ref, pre_two_ref, sums_two_ref, vectors_ref,
+    weights_ref,
     out_ref, packed_ref, mixed_ref, top_ref, weight_ref,
     query_ref,
 ):
     cells, channels = inner_ref.shape
+    w_mixer_ref = part_of(weights_ref, FORWARD_ROWS, "mixer")
+    w_velocity_ref = part_of(weights_ref, FORWARD_ROWS, "out")
+    w_heads = side_by_side(part_of(weights_ref, FORWARD_ROWS, "heads"), channels)
     act_two = act_two_of(
-        inner_ref[...], pre_two_ref[...], sums_two_ref[...], gain_ref[...], shift_ref[...], count
-    )
-    projected = folded(dot(beside(act_two), w_heads_ref[...]), 1)
+        inner_ref[...], pre_two_ref[...], sums_two_ref[...], vectors_ref[2:3], vectors_ref[3:4], count
+    )
+    projected = folded(dot(beside(act_two), jnp.concatenate([w_heads, w_heads], axis=0)), 1)
     query = projected[:, : HEADS * channels]
     query_high = query.astype(BF16).astype(F32)
     channel = lax.rem(lax.broadcasted_iota(jnp.int32, query.shape, 1), channels)
@@ -252,9 +265,9 @@
         mixed, tops, weights = own, all_top, all_weight
         if rows.stop == channels:
             mixed_ref[lanes], top_ref[lanes], weight_ref[lanes] = mixed, tops, weights
-    act_three = act_two + folded(dot(beside(mixed_ref[...]), w_mixer_ref[...]), 1)
+    act_three = act_two + folded(dot(beside(mixed_ref[...]), doubled(w_mixer_ref, channels)), 1)
     parts = folded(dot(w_velocity_ref[...], stacked(act_three.T)), 0)
-    forcing = jnp.zeros((2 * GROUP, cells), F32) + b_velocity_ref[...]
+    forcing = jnp.concatenate([vectors_ref[GROUP:]] * (cells // channels), axis=1)
     for column, lon_offset in enumerate((-1, 0, 1)):
         total = None
         for row, lat_offset in enumerate((-1, 0, 1)):
@@ -274,15 +287,19 @@
 def outlet_back_kernel(
     lon, count, block_size, step_size, quantities, sections, step,
     ids_ref,
-    state_ref, d_next_ref, cots_ref, inner_ref, pre_two_ref, sums_two_ref, gain_ref, shift_ref,
+    state_ref, d_next_ref, cots_ref, inner_ref, pre_two_ref, sums_two_ref, vectors_ref,
     mixed_ref, top_ref, weight_ref,
-    w_qkv_ref, w_mixer_ref, w_qkv_back_ref, w_mixer_back_ref, w_velocity_back_ref,
+    weights_ref,
     acc_qkv_ref, acc_mixer_ref, acc_velocity_ref, acc_small_ref,
     d_state_ref, d_two_ref, sums_ref,
     out_qkv_ref, out_mixer_ref, out_velocity_ref, out_small_ref,
     d_mixed_ref, d_qkv_ref, seed_ref, qkv_ref, mixed_rows_ref, top_rows_ref,
 ):
     channels = inner_ref.shape[1]
+    back = functools.partial(part_of, weights_ref, BACK_ROWS)
+    w_qkv_ref, w_mixer_ref, w_mixer_back_ref = back("qkv"), back("mixer"), back("mixer_back")
+    w_qkv_back = side_by_side(back("qkv_back"), 2 * channels)
+    w_velocity_back = side_by_side(back("out_back"), 2 * channels)[:, : 36 * GROUP]
     cells = inner_ref.shape[0]
     heads = heads_of(channels, cells, block_size)
 
@@ -304,13 +321,13 @@
         for lon_offset in (-1, 0, 1):
             pieces.append(lon_moved(moved_rows, -lon_offset, lon) if lon_offset else moved_rows)
     d_parts = stacked(jnp.concatenate(pieces, axis=0))
-    d_three = folded(dot(w_velocity_back_ref[...], d_parts), 0)
+    d_three = folded(dot(w_velocity_back, d_parts), 0)
     d_three_halves = stacked(d_three)
     d_mixed_ref[...] = folded(dot(w_mixer_back_ref[...], d_three_halves), 0) * weight_ref[...].T
     mixed_rows_ref[...] = mixed_ref[...].T
     top_rows_ref[...] = top_ref[...].T
     act_two = act_two_of(
-        inner_ref[...], pre_two_ref[...], sums_two_ref[...], gain_ref[...], shift_ref[...], count
+        inner_ref[...], pre_two_ref[...], sums_two_ref[...], vectors_ref[2:3], vectors_ref[3:4], count
     ).T
     act_two_halves = stacked(act_two)
     project(w_qkv_ref, act_two_halves, channels // HEADS, qkv_ref)
@@ -342,9 +359,9 @@
             d_qkv_ref[channels : 2 * channels, lanes] = folded(d_key, 1).T * (1.0 / LOG2_E)
             d_qkv_ref[2 * channels :, lanes] = folded(d_value, 1).T
     d_qkv_halves = stacked(d_qkv_ref[...])
-    d_two = (d_three + folded(dot(w_qkv_back_ref[...], d_qkv_halves), 0)).T
+    d_two = (d_three + folded(dot(w_qkv_back, d_qkv_halves), 0)).T
     d_two_ref[...] = d_two
-    mean, scale, unused_factor = norm_of(sums_two_ref[...], gain_ref[...], count)
+    mean, scale, unused_factor = norm_of(sums_two_ref[...], vectors_ref[2:3], count)
     sums = sums_of(d_two, pre_two_ref[...] - mean)
     sums_ref[...] = sums
 
@@ -380,22 +397,23 @@
 
 def middle_back_kernel(
     lon, count,
-    d_two_ref, pre_two_ref, sums_two_ref, all_two_ref, gain_two_ref,
-    pre_one_ref, sums_one_ref, gain_ref, shift_ref, w_second_back_ref,
+    d_two_ref, pre_two_ref, sums_two_ref, all_two_ref,
+    pre_one_ref, sums_one_ref, vectors_ref, weights_ref,
     acc_weight_ref, acc_small_ref,
     d_normed_ref, sums_ref, out_weight_ref, out_small_ref,
     patches_ref,
 ):
+    w_second_back_ref = part_of(weights_ref, BACK_ROWS, "second")
     sums_two = sums_two_ref[...]
     d_pre = d_pre_of(
         d_two_ref[...], pre_two_ref[...] - sums_two[0:1] / count, sums_two, all_two_ref[...],
-        gain_two_ref[...], count,
+        vectors_ref[2:3], count,
     )
     fill_patches(patches_ref, d_pre, lon)
     d_act = conv_patches(patches_ref, w_second_back_ref, lon)
-    mean, scale, factor = norm_of(sums_one_ref[...], gain_ref[...], count)
+    mean, scale, factor = norm_of(sums_one_ref[...], vectors_ref[0:1], count)
     centred = pre_one_ref[...] - mean
-    normed = centred * factor + shift_ref[...]
+    normed = centred * factor + vectors_ref[1:2]
     gate = sigmoid(normed)
     d_normed = d_act * gate * (1.0 + normed * (1.0 - gate))
     d_normed_ref[...] = d_normed
@@ -409,17 +427,19 @@
 
 def inlet_back_kernel(
     lon, count, quantities,
-    state_ref, d_normed_ref, pre_one_ref, sums_one_ref, all_one_ref, gain_ref,
-    inner_ref, d_two_ref, d_state_in_ref, w_first_back_ref, w_input_back_ref,
+    state_ref, d_normed_ref, pre_one_ref, sums_one_ref, all_one_ref, vectors_ref,
+    inner_ref, d_two_ref, d_state_in_ref, weights_ref,
     acc_first_ref, acc_input_ref, acc_inner_ref,
     d_state_ref, packed_ref, out_first_ref, out_input_ref, out_inner_ref,
     patches_ref,
 ):
     cells = inner_ref.shape[0]
+    w_first_back_ref = part_of(weights_ref, BACK_ROWS, "first")
+    w_input_back_ref = part_of(weights_ref, BACK_ROWS, "moving")
     sums_one = sums_one_ref[...]
     d_pre = d_pre_of(
         d_normed_ref[...], pre_one_ref[...] - sums_one[0:1] / count, sums_one, all_one_ref[...],
-        gain_ref[...], count,
+        vectors_ref[0:1], count,
     )
     fill_patches(patches_ref, d_pre, lon)
     d_act = conv_patches(patches_ref, w_first_back_ref, lon) + d_two_ref[...]
@@ -430,7 +450,7 @@
     out_inner_ref[...] = acc_inner_ref[...] + d_inner
     patches_ref[lon : lon + cells, :256] = beside(d_inner)
     rows = [patches_ref[lon * place : lon * place + cells, :256] for place in range(3)]
-    d_moving = folded(dot(jnp.concatenate(rows, axis=1), w_input_back_ref[...]), 1).T
+    d_moving = folded(dot(jnp.concatenate(rows, axis=1), doubled(w_input_back_ref, inner_ref.shape[1])), 1).T
     state = state_ref[...]
     moving_halves = stacked(inlet_channels(state, lon))
     for place in range(3):
@@ -532,36 +552,31 @@
 
 def put_conv_weight(out_ref, taps):
     for tap, weight in enumerate(taps):
-        wide = beside(weight)
         rows = weight.shape[0]
-        out_ref[2 * tap * rows : (2 * tap + 1) * rows] = wide
-        out_ref[(2 * tap + 1) * rows : (2 * tap + 2) * rows] = wide
-
-
-def put_left_weight(out_ref, weight):
-    rows = weight.shape[0]
-    for place, half in enumerate(halves(weight)):
-        out_ref[place * rows : (place + 1) * rows] = jnp.concatenate([half, half], axis=1)
+        out_ref[tap * rows : (tap + 1) * rows] = beside(weight)
 
 
 def weights_kernel(
     lon, quantities,
     w_input_ref, maps_ref, b_input_ref, w_first_ref, w_second_ref,
     w_query_ref, w_key_ref, w_value_ref, w_mixer_ref, w_velocity_ref,
-    static_part_ref, moving_cat_ref, moving_back_ref, first_cat_ref, second_cat_ref,
-    heads_ref, mixer_cells_ref, qkv_ref, qkv_back_ref, mixer_ref, mixer_back_ref, velocity_ref, velocity_back_ref,
-    first_back_ref, second_back_ref,
+    gain_one_ref, shift_one_ref, gain_two_ref, shift_two_ref, b_velocity_ref,
+    static_part_ref, forward_ref, back_ref, vectors_ref,
     patches_ref, weight_ref, taps_ref, rows_ref, *near_refs,
 ):
+    forward = functools.partial(part_of, forward_ref, FORWARD_ROWS)
+    back = functools.partial(part_of, back_ref, BACK_ROWS)
     near_refs, done_ref = near_refs[:-1], near_refs[-1]
     copies = fetched(
         [w_input_ref, maps_ref, b_input_ref, w_first_ref, w_second_ref,
-         w_query_ref, w_key_ref, w_value_ref, w_mixer_ref, w_velocity_ref],
+         w_query_ref, w_key_ref, w_value_ref, w_mixer_ref, w_velocity_ref,
+         gain_one_ref, shift_one_ref, gain_two_ref, shift_two_ref, b_velocity_ref],
         near_refs, done_ref,
     )
     (
         w_input_ref, maps_ref, b_input_ref, w_first_ref, w_second_ref,
         w_query_ref, w_key_ref, w_value_ref, w_mixer_ref, w_velocity_ref,
+        gain_one_ref, shift_one_ref, gain_two_ref, shift_two_ref, b_velocity_ref,
     ) = near_refs
     channels = w_input_ref.shape[2]
     moving = 5 * quantities
@@ -577,8 +592,8 @@
                 tap, group * quantities : (group + 1) * quantities
             ]
         taps_ref[tap, :statics] = w_input_ref[tap, moving:]
-    put_conv_weight(moving_cat_ref, [taps_ref[9 + row] for row in range(3)])
-    put_conv_weight(moving_back_ref, [taps_ref[11 - row].T for row in range(3)])
+    put_conv_weight(forward("moving"), [taps_ref[9 + row] for row in range(3)])
+    put_conv_weight(back("moving"), [taps_ref[11 - row].T for row in range(3)])
     put_conv_weight(weight_ref, [taps_ref[tap] for tap in range(9)])
     copies[1].wait()
     copies[2].wait()
@@ -589,20 +604,21 @@
     static_part_ref[...] = conv_patches(patches_ref, weight_ref, lon) + b_input_ref[...]
     for copy in copies[3:]:
         copy.wait()
-    put_conv_weight(first_cat_ref, [w_first_ref[tap] for tap in range(9)])
-    put_conv_weight(second_cat_ref, [w_second_ref[tap] for tap in range(9)])
-    put_conv_weight(first_back_ref, [w_first_ref[8 - tap].T for tap in range(9)])
-    put_conv_weight(second_back_ref, [w_second_ref[8 - tap].T for tap in range(9)])
+    put_conv_weight(forward("first"), [w_first_ref[tap] for tap in range(9)])
+    put_conv_weight(forward("second"), [w_second_ref[tap] for tap in range(9)])
+    put_conv_weight(back("first"), [w_first_ref[8 - tap].T for tap in range(9)])
+    put_conv_weight(back("second"), [w_second_ref[8 - tap].T for tap in range(9)])
     parts = [ref[...] for ref in (w_query_ref, w_key_ref, w_value_ref)]
     turned = [part.T for part in parts]
     width = channels // HEADS
     repeated = [turned[0][head * width : (head + 1) * width] for head in range(HEADS) for unused in range(HEADS)]
-    put_conv_weight(heads_ref, [jnp.concatenate([jnp.concatenate(repeated, axis=0).T, parts[1], parts[2]], axis=1)])
-    put_conv_weight(mixer_cells_ref, [w_mixer_ref[...]])
-    put_left_weight(qkv_ref, jnp.concatenate(turned, axis=0))
-    put_left_weight(qkv_back_ref, jnp.concatenate(parts, axis=1))
-    put_left_weight(mixer_ref, w_mixer_ref[...].T)
-    put_left_weight(mixer_back_ref, w_mixer_ref[...])
+    heads = jnp.concatenate([jnp.concatenate(repeated, axis=0).T, parts[1], parts[2]], axis=1)
+    put_blocks(forward("heads"), beside(heads))
+    put_conv_weight(forward("mixer"), [w_mixer_ref[...]])
+    back("qkv")[...] = left_form(jnp.concatenate(turned, axis=0))
+    put_blocks(back("qkv_back"), left_form(jnp.concatenate(parts, axis=1)))
+    back("mixer")[...] = left_form(w_mixer_ref[...].T)
+    back("mixer_back")[...] = left_form(w_mixer_ref[...])
     for tap in range(9):
         for group in range(2):
             start = (tap * 2 + group) * GROUP
@@ -610,8 +626,16 @@
                 tap, group * quantities : (group + 1) * quantities
             ]
     size = 18 * GROUP
-    put_left_weight(velocity_ref, rows_ref[:size])
-    put_left_weight(velocity_back_ref, rows_ref[...].T[:, :size])
+    vectors_ref[...] = jnp.zeros(vectors_ref.shape, F32)
+    for place, ref in enumerate((gain_one_ref, shift_one_ref, gain_two_ref, shift_two_ref)):
+        vectors_ref[place : place + 1] = ref[...]
+    bias = jnp.concatenate([b_velocity_ref[...], jnp.zeros((1, channels - 2 * quantities), F32)], axis=1)
+    bias = jnp.broadcast_to(bias, (channels, channels)).T
+    for group in range(2):
+        start = (group + 1) * GROUP
+        vectors_ref[start : start + quantities] = bias[group * quantities : (group + 1) * quantities]
+    forward("out")[...] = left_form(rows_ref[:size])
+    put_blocks(back("out_back"), left_form(rows_ref[...].T[:, :size]))
 
 
 def index_of(ids_ref, plan, bits):
@@ -756,7 +780,36 @@
 
 
 VMEM_LIMIT = 24 * 1024 * 1024
-ALONE_LIMIT = 46 * 1024 * 1024
+ALONE_LIMIT = 56 * 1024 * 1024
+
+FORWARD_ROWS = dict(moving=384, first=1152, second=1152, heads=768, mixer=128, out=288)
+BACK_ROWS = dict(moving=384, first=1152, second=1152, qkv=768, mixer=256, mixer_back=256, qkv_back=768, out_back=512)
+
+
+def part_of(ref, rows, name):
+    start = 0
+    for other, size in rows.items():
+        if other == name:
+            return ref.at[start : start + size]
+        start += size
+    return None
+
+
+def side_by_side(ref, rows):
+    return jnp.concatenate([ref[start : start + rows] for start in range(0, ref.shape[0], rows)], axis=1)
+
+
+def put_blocks(ref, value):
+    rows, width = value.shape[0], ref.shape[1]
+    for place in range(ref.shape[0] // rows):
+        block = value[:, place * width : (place + 1) * width]
+        if block.shape[1] < width:
+            block = jnp.concatenate([block, jnp.zeros((rows, width - block.shape[1]), value.dtype)], axis=1)
+        ref[place * rows : (place + 1) * rows] = block
+
+
+def left_form(weight):
+    return jnp.concatenate([jnp.concatenate([half, half], axis=1) for half in halves(weight)], axis=0)
 
 
 def in_groups(array, axis, groups):
@@ -848,13 +901,13 @@
         return value
     value = value + exchanged(value, 1)
     plane = masks_of([plan.dp, 2 * plan.dp])
-    other = [mask ^ 2 for mask in plane + [0]]
+    other = [mask ^ 2 for mask in plane]
     own = range(plan.sections * plan.dp)
     total = value * first_core
-    for turn in range(4):
-        pairs = [(device, device ^ other[turn]) for device in own if device & 1]
+    for turn, mask in enumerate(plane + [2]):
+        pairs = [(device, device ^ mask) for device in own if not device & 1]
         if turn < 3:
-            pairs += [(device, device ^ plane[turn]) for device in own if not device & 1]
+            pairs += [(device, device ^ other[turn]) for device in own if device & 1]
         total = total + lax.ppermute(value, ("section", "dp"), pairs)
     return total + exchanged(total, 1)
 
@@ -895,7 +948,7 @@
 
     plane = (cells, channels)
     small = (GROUP, channels)
-    conv = (9 * 2 * channels, 2 * channels)
+    conv = (9 * channels, 2 * channels)
     patches = pltpu.VMEM((cells + 2 * lon, 6 * channels), BF16)
     wide = pltpu.VMEM((3 * channels, cells), F32)
     narrow = pltpu.VMEM((channels, cells), F32)
@@ -917,25 +970,17 @@
     first_core = (1.0 - lax.rem(ids[1], 2).astype(F32)) * jnp.ones(small, F32)
     w_velocity_rows = jnp.swapaxes(w_velocity, 1, 2)
     weights = (
-        w_input, static_maps, b_input[None], w_first, w_second, w_query, w_key, w_value, w_mixer, w_velocity_rows
-    )
-    moving_conv, square_conv = (6 * channels, 2 * channels), (2 * channels, 2 * channels)
-    (
-        static_part, moving_cat, moving_back_cat, first_cat, second_cat,
-        heads_cat, mixer_cells, qkv_cat, qkv_back_cat, mixer_cat, mixer_back_cat, out_cat, out_back_cat,
-        first_back_cat, second_back_cat,
-    ) = call(
+        w_input, static_maps, b_input[None], w_first, w_second, w_query, w_key, w_value, w_mixer, w_velocity_rows,
+        gain_first[None], shift_first[None], gain_second[None], shift_second[None], b_velocity[None],
+    )
+    columns = 2 * channels
+    static_part, forward_weights, back_weights, vectors = call(
         functools.partial(weights_kernel, lon, quantities),
-        [plane, moving_conv, moving_conv, conv, conv,
-         (2 * channels, 2 * (HEADS + 2) * channels), square_conv, moving_conv, moving_conv[::-1],
-         square_conv, square_conv, (36 * GROUP, 2 * channels), (2 * channels, 36 * GROUP), conv, conv],
+        [plane, (sum(FORWARD_ROWS.values()), columns), (sum(BACK_ROWS.values()), columns), (3 * GROUP, channels)],
         [patches, pltpu.VMEM(conv, BF16), pltpu.VMEM((12, channels, channels), F32),
-         pltpu.VMEM((2 * channels, channels), F32)] + near(*weights),
-        name="weights", kinds=[F32] + [BF16] * 14, far_in=range(10), limit=ALONE_LIMIT,
+         pltpu.VMEM((columns, channels), F32)] + near(*weights),
+        name="weights", kinds=[F32, BF16, BF16, F32], far_in=range(15), limit=ALONE_LIMIT,
     )(*weights)
-    b_out = in_groups(b_velocity[:, None], 0, 2)
-    gain_one, shift_one = gain_first[None], shift_first[None]
-    gain_two, shift_two = gain_second[None], shift_second[None]
 
     inlet = call(
         functools.partial(inlet_kernel, lon), [plane, plane, small], [patches], name="inlet"
@@ -955,18 +1000,18 @@
             [state_shape, plane, small, (channels, 3 * channels), (channels, channels),
              (18 * GROUP, channels), (3 * GROUP, channels)],
             [narrow, wide, pltpu.VMEM(state_shape, F32), wide, narrow, narrow],
-            {17: 3, 18: 4, 19: 5, 20: 6}, name="outlet_back", scalars=1,
+            {12: 3, 13: 4, 14: 5, 15: 6}, name="outlet_back", scalars=1,
         )
 
     middle_back = call(
         functools.partial(middle_back_kernel, lon, count),
         [plane, small, (9, channels, channels), small], [patches],
-        {10: 2, 11: 3}, name="middle_back",
+        {8: 2, 9: 3}, name="middle_back",
     )
     inlet_back = call(
         functools.partial(inlet_back_kernel, lon, count, quantities),
         [state_shape, packed, (9, channels, channels), (3, channels, channels), plane], [patches],
-        {11: 2, 12: 3, 13: 4}, name="inlet_back",
+        {10: 2, 11: 3, 12: 4}, name="inlet_back",
     )
 
     state = entry[: 3 * GROUP]
@@ -979,14 +1024,14 @@
             state, own_cot, inner, pre_one, sums_one = call(
                 functools.partial(entered_inlet_kernel, plan, lon), [state_shape, packed, plane, plane, small], [patches],
                 name="inlet", scalars=1,
-            )(ids, entry, arrived, static_part, moving_cat, first_cat)
+            )(ids, entry, arrived, static_part, forward_weights)
         else:
-            inner, pre_one, sums_one = inlet(state, static_part, moving_cat, first_cat)
+            inner, pre_one, sums_one = inlet(state, static_part, forward_weights)
         sums_one = micro_sum(plan, sums_one, first_core)
-        pre_two, sums_two = middle(pre_one, sums_one, gain_one, shift_one, second_cat)
+        pre_two, sums_two = middle(pre_one, sums_one, vectors, forward_weights)
         sums_two = micro_sum(plan, sums_two, first_core)
         state_out, state_packed, mixed, top, weight = outlet(
-            state, inner, pre_two, sums_two, gain_two, shift_two, heads_cat, mixer_cells, out_cat, b_out
+            state, inner, pre_two, sums_two, vectors, forward_weights
         )
         saved.append((state, inner, pre_one, pre_two, sums_one, sums_two, mixed, top, weight))
         path.append(state_packed)
@@ -1026,9 +1071,8 @@
             early = [sent[0]] + [moved(part, plan.to_homes(steps)) for steps, part in enumerate(sent)]
         state, inner, pre_one, pre_two, sums_one, sums_two, mixed, top, weight = saved[step]
         d_partial, d_two, grad_two, acc["qkv"], acc["mixer"], acc["velocity"], acc["small_two"] = outlet_back(step)(
-            ids, state, d_state, cots, inner, pre_two, sums_two, gain_two, shift_two,
-            mixed, top, weight,
-            qkv_cat, mixer_cat, qkv_back_cat, mixer_back_cat, out_back_cat,
+            ids, state, d_state, cots, inner, pre_two, sums_two, vectors,
+            mixed, top, weight, back_weights,
             acc["qkv"], acc["mixer"], acc["velocity"], acc["small_two"],
         )
         if not step:
@@ -1036,14 +1080,14 @@
             path_out = put_home(0, early)
         grad_two = micro_sum(plan, grad_two, first_core)
         d_normed, grad_one, acc["second"], acc["small_one"] = middle_back(
-            d_two, pre_two, sums_two, grad_two, gain_two,
-            pre_one, sums_one, gain_one, shift_one, second_back_cat,
+            d_two, pre_two, sums_two, grad_two,
+            pre_one, sums_one, vectors, back_weights,
             acc["second"], acc["small_one"],
         )
         grad_one = micro_sum(plan, grad_one, first_core)
         d_state, grads[step], acc["first"], acc["moving"], acc["inner"] = inlet_back(
-            state, d_normed, pre_one, sums_one, grad_one, gain_one,
-            inner, d_two, d_partial, first_back_cat, moving_back_cat,
+            state, d_normed, pre_one, sums_one, grad_one, vectors,
+            inner, d_two, d_partial, back_weights,
             acc["first"], acc["moving"], acc["inner"],
         )
     late = [grads[0]] + [moved(grads[0], plan.to_first_home(steps)) for steps in range(segments)]

time: 426 us -> 413 us (0.969)
  local copies, waits for them, and re-layouts: 28.1 us -> 4.52 us
  waiting for transfers between devices: 96.4 us -> 109 us
    ppermute x46, starting transfers between devices: 64.9 us -> 24.4 us  [exchanged(): lax.ppermute(value, ('section', 'dp'), [(own, own ^ mask) for own in rang...]
    ppermute x64, starting transfers between devices: 68.6 us -> 107 us  [micro_sum(): total = total + lax.ppermute(value, ('section', 'dp'), pairs)]
    unnamed x130 -> x26, local copies, waits for them, and re-layouts: 25 us -> 3.55 us
    ppermute x46, waiting for transfers between devices: 50 us -> 58.7 us  [exchanged(): lax.ppermute(value, ('section', 'dp'), [(own, own ^ mask) for own in rang...]
  transfers between devices with their start and end apart: 122 -> 122, of which waited for: 72 -> 72; matrix products, arithmetic and copies ran while one was open for 0% -> 0% of each run, Pallas kernels for 4% -> 5%
where the time goes in v8:
time: 413 us; the launch traced here: 407 us
  starting transfers between devices  150 us (36%)
  Pallas kernels  140 us (34%)
  waiting for transfers between devices  109 us (26%)
  local copies, waits for them, and re-layouts  4.52 us (1%)
    pallas_call x36, Pallas kernels, run(): pl.pallas_call(kernel, out_shape=tuple((jax.ShapeDtypeStruct(shape, kind)...  140 us
    ppermute x64, starting transfers between devices, micro_sum(): total = total + lax.ppermute(value, ('section', 'dp'), pairs)  107 us
    ppermute x46, waiting for transfers between devices, exchanged(): lax.ppermute(value, ('section', 'dp'), [(own, own ^ mask) for own in rang...  58.7 us
    ppermute x64, waiting for transfers between devices, micro_sum(): total = total + lax.ppermute(value, ('section', 'dp'), pairs)  37 us
    ppermute x46, starting transfers between devices, exchanged(): lax.ppermute(value, ('section', 'dp'), [(own, own ^ mask) for own in rang...  24.4 us
    ppermute x12, starting transfers between devices, moved(): return lax.ppermute(value, ('section', 'dp'), going)  19 us
    ppermute x12, waiting for transfers between devices, moved(): return lax.ppermute(value, ('section', 'dp'), going)  13.7 us
  transfers between devices with their start and end apart: 122, of which 72 were waited for; matrix products, arithmetic and copies ran while one was open for 0% of the time, Pallas kernels for 5%

profile of v8, /device:TPU:0, one launch (start us, length us, event | category | flops | bytes accessed | tf_op | source)
XLA Modules:
  0.0 407.4 jit_solution(7050053094800179525)
XLA Ops:
  1.2 2.7 enter.1
  4.6 5.9 %weights.1 = (f32[1024,128]{1,0:T(8,128)}, bf16[3872,256]{1,0:T(8,128)(2,1)}, bf16[5248,256]{1,0:T(8,128)(2,1)}, f32[24,128]{1,0:T(8,128)}) custom-call(f32[9,100,128]{2,1,0:T(8,128)} %w_input_ref.1, f32[75,1024]{1,0:T(8,128)} %maps_ref.3, f32[1,128]{1,0:T(1,128)} %bitcast.41, f32[9,128,128]{2,1,0:T(8,128)} %w_first_ref.1, f32[9,128,128]{2,1,0:T(8,128)} %w_second_ref.1, ...), custom_call_target="tpu_custom_call" | custom-call | tf_op jit(solution)/shard_map/weights/pallas_call | solution.py:768
  14.0 3.7 inlet.4
  17.7 4.9 %collective-permute-start.1 = (f32[8,128]{1,0:T(8,128)S(1)}, f32[8,128]{1,0:T(8,128)S(1)}, u32[]{:S(2)}, u32[]{:S(2)}) collective-permute-start(f32[8,128]{1,0:T(8,128)S(1)} %get-tuple-element.188), channel_id=1, source_target_pairs={{0,1},{1,0},{2,3},{3,2},{4,5},{5,4},{6,7},{7,6},{8,9},{9,8},{10,11... | collective-permute-start | bytes 12296 | tf_op jit(solution)/shard_map/ppermute | solution.py:887
  24.9 2.3 collective-permute-start.3
  27.2 3.5 collective-permute-start.5
  36.7 2.9 collective-permute-start.10
  39.6 3.6 collective-permute-start.11
  48.7 5.7 %outlet.4 = (f32[24,1024]{1,0:T(8,128)S(1)}, f32[16,1024]{1,0:T(8,128)S(1)}, f32[1024,128]{1,0:T(8,128)S(1)}, f32[1024,128]{1,0:T(8,128)S(1)}, f32[1024,128]{1,0:T(8,128)S(1)}) custom-call(f32[24,1024]{1,0:T(8,128)S(1)} %get-tuple-element.185.state_ref, f32[1024,128]{1,0:T(8,128)S(1)} %get-tuple-element.186.inner_ref, ...), custom_call_target="tpu_custom_call" | custom-call | tf_op jit(solution)/shard_map/outlet/pallas_call | solution.py:768
  54.5 3.1 inlet.5
  62.3 2.4 collective-permute-start.17
  64.8 3.0 collective-permute-done.17
  75.3 2.6 collective-permute-start.23
  77.9 2.9 collective-permute-done.23
  82.0 5.7 %outlet.5 = (f32[24,1024]{1,0:T(8,128)S(1)}, f32[16,1024]{1,0:T(8,128)S(1)}, f32[1024,128]{1,0:T(8,128)S(1)}, f32[1024,128]{1,0:T(8,128)S(1)}, f32[1024,128]{1,0:T(8,128)S(1)}) custom-call(f32[24,1024]{1,0:T(8,128)S(1)} %get-tuple-element.196.state_ref, f32[1024,128]{1,0:T(8,128)S(1)} %get-tuple-element.197.inner_ref, ...), custom_call_target="tpu_custom_call" | custom-call | tf_op jit(solution)/shard_map/outlet/pallas_call | solution.py:768
  87.7 3.1 inlet.6
  95.6 2.4 collective-permute-start.29
  98.1 3.0 collective-permute-done.29
  108.5 2.8 collective-permute-start.35
  111.3 2.7 collective-permute-done.35
  115.2 5.7 %outlet.6 = (f32[24,1024]{1,0:T(8,128)S(1)}, f32[16,1024]{1,0:T(8,128)S(1)}, f32[1024,128]{1,0:T(8,128)S(1)}, f32[1024,128]{1,0:T(8,128)S(1)}, f32[1024,128]{1,0:T(8,128)S(1)}) custom-call(f32[24,1024]{1,0:T(8,128)S(1)} %get-tuple-element.202.state_ref, f32[1024,128]{1,0:T(8,128)S(1)} %get-tuple-element.203.inner_ref, ...), custom_call_target="tpu_custom_call" | custom-call | tf_op jit(solution)/shard_map/outlet/pallas_call | solution.py:768
  121.0 3.1 inlet.7
  128.8 2.4 collective-permute-start.44
  131.4 3.0 collective-permute-done.44
  141.8 2.4 collective-permute-start.50
  152.1 6.4 %outlet.7 = (f32[24,1024]{1,0:T(8,128)}, f32[16,1024]{1,0:T(8,128)S(1)}, f32[1024,128]{1,0:T(8,128)S(1)}, f32[1024,128]{1,0:T(8,128)S(1)}, f32[1024,128]{1,0:T(8,128)S(1)}) custom-call(f32[24,1024]{1,0:T(8,128)S(1)} %get-tuple-element.208.state_ref, f32[1024,128]{1,0:T(8,128)S(1)} %get-tuple-element.213.inner_ref, ...), custom_call_target="tpu_custom_call" | custom-call | tf_op jit(solution)/shard_map/outlet/pallas_call | solution.py:768
  158.5 12.1 %outlet_back.4 = (f32[24,1024]{1,0:T(8,128)S(1)}, f32[1024,128]{1,0:T(8,128)S(1)}, f32[8,128]{1,0:T(8,128)S(1)}, f32[128,384]{1,0:T(8,128)S(1)}, f32[128,128]{1,...) custom-call(s32[2]{0:T(128)S(1)} %copy-done.8, ...), custom_call_target="tpu_custom_call", output_to_operand_aliasing={{3}: (12, {}), {4}: (13, {}), {5}: (14, {}), {6}: (15, {})} | custom-call | tf_op jit(solution)/shard_map/outlet_back/pallas_call | solution.py:768
  171.9 2.4 collective-permute-start.53
  174.3 2.1 collective-permute-start.54
  176.4 3.4 collective-permute-start.56
  183.1 3.1 middle_back.4
  190.9 3.9 collective-permute-start.62
  197.7 4.3 %inlet_back.4 = (f32[24,1024]{1,0:T(8,128)S(1)}, f32[16,1024]{1,0:T(8,128)S(1)}, f32[9,128,128]{2,1,0:T(8,128)S(1)}, f32[3,128,128]{2,1,0:T(8,128)S(1)}, f32[1024,128]{1,0:T(8,128)S(1)}) custom-call(f32[24,1024]{1,0:T(8,128)S(1)} %get-tuple-element.208.state_ref, ...), custom_call_target="tpu_custom_call", output_to_operand_aliasing={{2}: (10, {}), {3}: (11, {}), {4}: (12, {})} | custom-call | tf_op jit(solution)/shard_map/inlet_back/pallas_call | solution.py:768
  202.0 12.0 %outlet_back.5 = (f32[24,1024]{1,0:T(8,128)S(1)}, f32[1024,128]{1,0:T(8,128)S(1)}, f32[8,128]{1,0:T(8,128)S(1)}, f32[128,384]{1,0:T(8,128)S(1)}, f32[128,128]{1,...) custom-call(s32[2]{0:T(128)S(1)} %copy-done.8, ...), custom_call_target="tpu_custom_call", output_to_operand_aliasing={{3}: (12, {}), {4}: (13, {}), {5}: (14, {}), {6}: (15, {})} | custom-call | tf_op jit(solution)/shard_map/outlet_back/pallas_call | solution.py:768
  216.8 2.0 collective-permute-start.66
  218.8 3.4 collective-permute-start.68
  225.4 3.1 middle_back.5
  231.2 2.0 collective-permute-start.72
  233.3 3.4 collective-permute-start.74
  239.9 4.3 %inlet_back.5 = (f32[24,1024]{1,0:T(8,128)S(1)}, f32[16,1024]{1,0:T(8,128)S(1)}, f32[9,128,128]{2,1,0:T(8,128)S(1)}, f32[3,128,128]{2,1,0:T(8,128)S(1)}, f32[1024,128]{1,0:T(8,128)S(1)}) custom-call(f32[24,1024]{1,0:T(8,128)S(1)} %get-tuple-element.202.state_ref, ...), custom_call_target="tpu_custom_call", output_to_operand_aliasing={{2}: (10, {}), {3}: (11, {}), {4}: (12, {})} | custom-call | tf_op jit(solution)/shard_map/inlet_back/pallas_call | solution.py:768
  244.2 12.2 %outlet_back.6 = (f32[24,1024]{1,0:T(8,128)S(1)}, f32[1024,128]{1,0:T(8,128)S(1)}, f32[8,128]{1,0:T(8,128)S(1)}, f32[128,384]{1,0:T(8,128)S(1)}, f32[128,128]{1,...) custom-call(s32[2]{0:T(128)S(1)} %copy-done.8, ...), custom_call_target="tpu_custom_call", output_to_operand_aliasing={{3}: (12, {}), {4}: (13, {}), {5}: (14, {}), {6}: (15, {})} | custom-call | tf_op jit(solution)/shard_map/outlet_back/pallas_call | solution.py:768
  259.2 2.0 collective-permute-start.78
  261.2 3.4 collective-permute-start.80
  267.9 3.1 middle_back.6
  273.7 2.0 collective-permute-start.84
  275.7 3.4 collective-permute-start.86
  282.4 4.3 %inlet_back.6 = (f32[24,1024]{1,0:T(8,128)S(1)}, f32[16,1024]{1,0:T(8,128)S(1)}, f32[9,128,128]{2,1,0:T(8,128)S(1)}, f32[3,128,128]{2,1,0:T(8,128)S(1)}, f32[1024,128]{1,0:T(8,128)S(1)}) custom-call(f32[24,1024]{1,0:T(8,128)S(1)} %get-tuple-element.196.state_ref, ...), custom_call_target="tpu_custom_call", output_to_operand_aliasing={{2}: (10, {}), {3}: (11, {}), {4}: (12, {})} | custom-call | tf_op jit(solution)/shard_map/inlet_back/pallas_call | solution.py:768
  289.5 5.6 %collective-permute-start.90 = (f32[32,1024]{1,0:T(8,128)S(1)}, f32[32,1024]{1,0:T(8,128)S(1)}, u32[]{:S(2)}, u32[]{:S(2)}) collective-permute-start(f32[32,1024]{1,0:T(8,128)S(1)} %get-tuple-element.282), channel_id=1, source_target_pairs={{0,16},{1,21},{2,18},{3,23},{4,20},{5,17},{6,22},{7,19},{8,24},{9,... | collective-permute-start | bytes 393224 | tf_op jit(solution)/shard_map/ppermute | solution.py:894
  296.2 11.8 %outlet_back.7 = (f32[24,1024]{1,0:T(8,128)S(1)}, f32[1024,128]{1,0:T(8,128)S(1)}, f32[8,128]{1,0:T(8,128)S(1)}, f32[128,384]{1,0:T(8,128)S(1)}, f32[128,128]{1,...) custom-call(s32[2]{0:T(128)S(1)} %copy-done.8, ...), custom_call_target="tpu_custom_call", output_to_operand_aliasing={{3}: (12, {}), {4}: (13, {}), {5}: (14, {}), {6}: (15, {})} | custom-call | tf_op jit(solution)/shard_map/outlet_back/pallas_call | solution.py:768
  310.6 2.1 collective-permute-start.95
  312.7 3.6 collective-permute-start.96
  319.4 3.1 middle_back.7
  326.3 3.4 collective-permute-start.102
  334.6 4.9 %inlet_back.7 = (f32[24,1024]{1,0:T(8,128)}, f32[16,1024]{1,0:T(8,128)S(1)}, f32[9,128,128]{2,1,0:T(8,128)S(1)}, f32[3,128,128]{2,1,0:T(8,128)S(1)}, f32[1024,128]{1,0:T(8,128)S(1)}) custom-call(f32[24,1024]{1,0:T(8,128)S(1)} %get-tuple-element.185.state_ref, ...), custom_call_target="tpu_custom_call", output_to_operand_aliasing={{2}: (10, {}), {3}: (11, {}), {4}: (12, {})} | custom-call | tf_op jit(solution)/shard_map/inlet_back/pallas_call | solution.py:768
  341.7 2.5 collective-permute-done.104.refs_1_
  351.8 7.4 %collective-permute-done.109.refs_6_ = f32[16,1024]{1,0:T(8,128)S(1)} collective-permute-done((f32[16,1024]{1,0:T(8,128)S(1)}, f32[16,1024]{1,0:T(8,128)S(1)}, u32[]{:S(2)}, u32[]{:S(2)}) %collective-permute-start.109) | collective-permute-done | bytes 65568 | tf_op jit(solution)/shard_map/ppermute | solution.py:894
  361.8 3.5 collective-permute-done.111.refs_8_
  368.2 3.6 collective-permute-start.114
  372.6 3.0 collective-permute-done.114.refs_3_
  380.8 5.7 %collective-permute-done.116.refs_2_ = f32[128,128]{1,0:T(8,128)S(1)} collective-permute-done((f32[128,128]{1,0:T(8,128)S(1)}, f32[128,128]{1,0:T(8,128)S(1)}, u32[]{:S(2)}, u32[]{:S(2)}) %collective-permute-start.116) | collective-permute-done | bytes 65568 | tf_op jit(solution)/shard_map/ppermute | solution.py:887
  387.3 3.4 collective-permute-start.120
  390.7 5.7 %collective-permute-done.118.refs_1_ = f32[512,128]{1,0:T(8,128)S(1)} collective-permute-done((f32[512,128]{1,0:T(8,128)S(1)}, f32[512,128]{1,0:T(8,128)S(1)}, u32[]{:S(2)}, u32[]{:S(2)}) %collective-permute-start.118) | collective-permute-done | bytes 262176 | tf_op jit(solution)/shard_map/ppermute | solution.py:887
  396.3 4.6 %collective-permute-done.119.refs_2_ = f32[512,128]{1,0:T(8,128)S(1)} collective-permute-done((f32[512,128]{1,0:T(8,128)S(1)}, f32[512,128]{1,0:T(8,128)S(1)}, u32[]{:S(2)}, u32[]{:S(2)}) %collective-permute-start.119) | collective-permute-done | bytes 262176 | tf_op jit(solution)/shard_map/ppermute | solution.py:887
  401.7 2.6 collective-permute-done.121.refs_1_
  (305 shorter events, 145.1 us)
Async XLA Ops:
  3.9 6.6 %collective-permute-start = (f32[40,1024]{1,0:T(8,128)}, f32[40,1024]{1,0:T(8,128)S(1)}, u32[]{:S(2)}, u32[]{:S(2)}) collective-permute-start(f32[40,1024]{1,0:T(8,128)} %get-tuple-element.182.own_ref), channel_id=1, source_target_pairs={{1,5},{3,7},{5,1},{7,3},{9,13},{11,15},{13,9},{15,11},{16,20},{18,... | collective-permute-start | bytes 491528 | tf_op jit(solution)/shard_map/ppermute | solution.py:894
  17.7 5.7 %collective-permute-start.1 = (f32[8,128]{1,0:T(8,128)S(1)}, f32[8,128]{1,0:T(8,128)S(1)}, u32[]{:S(2)}, u32[]{:S(2)}) collective-permute-start(f32[8,128]{1,0:T(8,128)S(1)} %get-tuple-element.188), channel_id=1, source_target_pairs={{0,1},{1,0},{2,3},{3,2},{4,5},{5,4},{6,7},{7,6},{8,9},{9,8},{10,11... | collective-permute-start | bytes 12296 | tf_op jit(solution)/shard_map/ppermute | solution.py:887
  23.4 7.3 %collective-permute-start.2 = (f32[8,128]{1,0:T(8,128)S(1)}, f32[8,128]{1,0:T(8,128)S(1)}, u32[]{:S(2)}, u32[]{:S(2)}) collective-permute-start(f32[8,128]{1,0:T(8,128)S(1)} %add.288), channel_id=1, source_target_pairs={{0,8},{2,10},{4,12},{6,14},{8,0},{10,2},{12,4},{14,6},{16,24},{18,... | collective-permute-start | bytes 12296 | tf_op jit(solution)/shard_map/ppermute | solution.py:911
  24.9 5.8 %collective-permute-start.3 = (f32[8,128]{1,0:T(8,128)S(1)}, f32[8,128]{1,0:T(8,128)S(1)}, u32[]{:S(2)}, u32[]{:S(2)}) collective-permute-start(f32[8,128]{1,0:T(8,128)S(1)} %add.288), channel_id=1, source_target_pairs={{0,16},{2,18},{4,20},{6,22},{8,24},{10,26},{12,28},{14,30},{16,0},... | collective-permute-start | bytes 12296 | tf_op jit(solution)/shard_map/ppermute | solution.py:911
  27.2 5.5 %collective-permute-start.5 = (f32[8,128]{1,0:T(8,128)S(1)}, f32[8,128]{1,0:T(8,128)S(1)}, u32[]{:S(2)}, u32[]{:S(2)}) collective-permute-start(f32[8,128]{1,0:T(8,128)S(1)} %add.288), channel_id=1, source_target_pairs={{0,2},{2,0},{4,6},{6,4},{8,10},{10,8},{12,14},{14,12},{16,18},{18,... | collective-permute-start | bytes 12296 | tf_op jit(solution)/shard_map/ppermute | solution.py:911
  36.7 7.2 %collective-permute-start.10 = (f32[8,128]{1,0:T(8,128)S(1)}, f32[8,128]{1,0:T(8,128)S(1)}, u32[]{:S(2)}, u32[]{:S(2)}) collective-permute-start(f32[8,128]{1,0:T(8,128)S(1)} %add.294), channel_id=1, source_target_pairs={{0,24},{2,26},{4,28},{6,30},{8,16},{10,18},{12,20},{14,22},{16,8},... | collective-permute-start | bytes 12296 | tf_op jit(solution)/shard_map/ppermute | solution.py:911
  39.6 5.5 %collective-permute-start.11 = (f32[8,128]{1,0:T(8,128)S(1)}, f32[8,128]{1,0:T(8,128)S(1)}, u32[]{:S(2)}, u32[]{:S(2)}) collective-permute-start(f32[8,128]{1,0:T(8,128)S(1)} %add.294), channel_id=1, source_target_pairs={{0,2},{2,0},{4,6},{6,4},{8,10},{10,8},{12,14},{14,12},{16,18},{18,... | collective-permute-start | bytes 12296 | tf_op jit(solution)/shard_map/ppermute | solution.py:911
  58.8 5.9 %collective-permute-start.14 = (f32[8,128]{1,0:T(8,128)S(1)}, f32[8,128]{1,0:T(8,128)S(1)}, u32[]{:S(2)}, u32[]{:S(2)}) collective-permute-start(f32[8,128]{1,0:T(8,128)S(1)} %add.300), channel_id=1, source_target_pairs={{0,8},{2,10},{4,12},{6,14},{8,0},{10,2},{12,4},{14,6},{16,24},{18,... | collective-permute-start | bytes 12296 | tf_op jit(solution)/shard_map/ppermute | solution.py:911
  62.3 5.5 %collective-permute-start.17 = (f32[8,128]{1,0:T(8,128)S(1)}, f32[8,128]{1,0:T(8,128)S(1)}, u32[]{:S(2)}, u32[]{:S(2)}) collective-permute-start(f32[8,128]{1,0:T(8,128)S(1)} %add.300), channel_id=1, source_target_pairs={{0,2},{2,0},{4,6},{6,4},{8,10},{10,8},{12,14},{14,12},{16,18},{18,... | collective-permute-start | bytes 12296 | tf_op jit(solution)/shard_map/ppermute | solution.py:911
  71.8 6.1 %collective-permute-start.20 = (f32[8,128]{1,0:T(8,128)S(1)}, f32[8,128]{1,0:T(8,128)S(1)}, u32[]{:S(2)}, u32[]{:S(2)}) collective-permute-start(f32[8,128]{1,0:T(8,128)S(1)} %add.306), channel_id=1, source_target_pairs={{0,8},{2,10},{4,12},{6,14},{8,0},{10,2},{12,4},{14,6},{16,24},{18,... | collective-permute-start | bytes 12296 | tf_op jit(solution)/shard_map/ppermute | solution.py:911
  75.3 5.5 %collective-permute-start.23 = (f32[8,128]{1,0:T(8,128)S(1)}, f32[8,128]{1,0:T(8,128)S(1)}, u32[]{:S(2)}, u32[]{:S(2)}) collective-permute-start(f32[8,128]{1,0:T(8,128)S(1)} %add.306), channel_id=1, source_target_pairs={{0,2},{2,0},{4,6},{6,4},{8,10},{10,8},{12,14},{14,12},{16,18},{18,... | collective-permute-start | bytes 12296 | tf_op jit(solution)/shard_map/ppermute | solution.py:911
  92.1 5.9 %collective-permute-start.26 = (f32[8,128]{1,0:T(8,128)S(1)}, f32[8,128]{1,0:T(8,128)S(1)}, u32[]{:S(2)}, u32[]{:S(2)}) collective-permute-start(f32[8,128]{1,0:T(8,128)S(1)} %add.312), channel_id=1, source_target_pairs={{0,8},{2,10},{4,12},{6,14},{8,0},{10,2},{12,4},{14,6},{16,24},{18,... | collective-permute-start | bytes 12296 | tf_op jit(solution)/shard_map/ppermute | solution.py:911
  95.6 5.5 %collective-permute-start.29 = (f32[8,128]{1,0:T(8,128)S(1)}, f32[8,128]{1,0:T(8,128)S(1)}, u32[]{:S(2)}, u32[]{:S(2)}) collective-permute-start(f32[8,128]{1,0:T(8,128)S(1)} %add.312), channel_id=1, source_target_pairs={{0,2},{2,0},{4,6},{6,4},{8,10},{10,8},{12,14},{14,12},{16,18},{18,... | collective-permute-start | bytes 12296 | tf_op jit(solution)/shard_map/ppermute | solution.py:911
  105.1 6.3 %collective-permute-start.32 = (f32[8,128]{1,0:T(8,128)S(1)}, f32[8,128]{1,0:T(8,128)S(1)}, u32[]{:S(2)}, u32[]{:S(2)}) collective-permute-start(f32[8,128]{1,0:T(8,128)S(1)} %add.318), channel_id=1, source_target_pairs={{0,8},{2,10},{4,12},{6,14},{8,0},{10,2},{12,4},{14,6},{16,24},{18,... | collective-permute-start | bytes 12296 | tf_op jit(solution)/shard_map/ppermute | solution.py:911
  108.5 5.5 %collective-permute-start.35 = (f32[8,128]{1,0:T(8,128)S(1)}, f32[8,128]{1,0:T(8,128)S(1)}, u32[]{:S(2)}, u32[]{:S(2)}) collective-permute-start(f32[8,128]{1,0:T(8,128)S(1)} %add.318), channel_id=1, source_target_pairs={{0,2},{2,0},{4,6},{6,4},{8,10},{10,8},{12,14},{14,12},{16,18},{18,... | collective-permute-start | bytes 12296 | tf_op jit(solution)/shard_map/ppermute | solution.py:911
  125.4 5.9 %collective-permute-start.41 = (f32[8,128]{1,0:T(8,128)S(1)}, f32[8,128]{1,0:T(8,128)S(1)}, u32[]{:S(2)}, u32[]{:S(2)}) collective-permute-start(f32[8,128]{1,0:T(8,128)S(1)} %add.324), channel_id=1, source_target_pairs={{0,8},{2,10},{4,12},{6,14},{8,0},{10,2},{12,4},{14,6},{16,24},{18,... | collective-permute-start | bytes 12296 | tf_op jit(solution)/shard_map/ppermute | solution.py:911
  128.8 5.5 %collective-permute-start.44 = (f32[8,128]{1,0:T(8,128)S(1)}, f32[8,128]{1,0:T(8,128)S(1)}, u32[]{:S(2)}, u32[]{:S(2)}) collective-permute-start(f32[8,128]{1,0:T(8,128)S(1)} %add.324), channel_id=1, source_target_pairs={{0,2},{2,0},{4,6},{6,4},{8,10},{10,8},{12,14},{14,12},{16,18},{18,... | collective-permute-start | bytes 12296 | tf_op jit(solution)/shard_map/ppermute | solution.py:911
  138.4 7.4 %collective-permute-start.47 = (f32[8,128]{1,0:T(8,128)S(1)}, f32[8,128]{1,0:T(8,128)S(1)}, u32[]{:S(2)}, u32[]{:S(2)}) collective-permute-start(f32[8,128]{1,0:T(8,128)S(1)} %add.330), channel_id=1, source_target_pairs={{0,8},{2,10},{4,12},{6,14},{8,0},{10,2},{12,4},{14,6},{16,24},{18,... | collective-permute-start | bytes 12296 | tf_op jit(solution)/shard_map/ppermute | solution.py:911
  139.8 7.7 %collective-permute-start.48 = (f32[8,128]{1,0:T(8,128)S(1)}, f32[8,128]{1,0:T(8,128)S(1)}, u32[]{:S(2)}, u32[]{:S(2)}) collective-permute-start(f32[8,128]{1,0:T(8,128)S(1)} %add.330), channel_id=1, source_target_pairs={{0,16},{2,18},{4,20},{6,22},{8,24},{10,26},{12,28},{14,30},{16,0},... | collective-permute-start | bytes 12296 | tf_op jit(solution)/shard_map/ppermute | solution.py:911
  139.8 9.3 %collective-permute-start.49 = (f32[8,128]{1,0:T(8,128)S(1)}, f32[8,128]{1,0:T(8,128)S(1)}, u32[]{:S(2)}, u32[]{:S(2)}) collective-permute-start(f32[8,128]{1,0:T(8,128)S(1)} %add.330), channel_id=1, source_target_pairs={{0,24},{2,26},{4,28},{6,30},{8,16},{10,18},{12,20},{14,22},{16,8},... | collective-permute-start | bytes 12296 | tf_op jit(solution)/shard_map/ppermute | solution.py:911
  141.8 7.3 %collective-permute-start.50 = (f32[8,128]{1,0:T(8,128)S(1)}, f32[8,128]{1,0:T(8,128)S(1)}, u32[]{:S(2)}, u32[]{:S(2)}) collective-permute-start(f32[8,128]{1,0:T(8,128)S(1)} %add.330), channel_id=1, source_target_pairs={{0,2},{2,0},{4,6},{6,4},{8,10},{10,8},{12,14},{14,12},{16,18},{18,... | collective-permute-start | bytes 12296 | tf_op jit(solution)/shard_map/ppermute | solution.py:911
  144.2 5.2 %collective-permute-start.37 = (f32[16,1024]{1,0:T(8,128)S(1)}, f32[16,1024]{1,0:T(8,128)S(1)}, u32[]{:S(2)}, u32[]{:S(2)}) collective-permute-start(f32[16,1024]{1,0:T(8,128)S(1)} %copy-done.12), channel_id=1, source_target_pairs={{0,8},{1,13},{2,10},{3,15},{4,12},{5,9},{6,14},{7,11},{8,20},{9,17... | collective-permute-start | bytes 196616 | tf_op jit(solution)/shard_map/ppermute | solution.py:894
  171.9 7.9 %collective-permute-start.53 = (f32[8,128]{1,0:T(8,128)S(1)}, f32[8,128]{1,0:T(8,128)S(1)}, u32[]{:S(2)}, u32[]{:S(2)}) collective-permute-start(f32[8,128]{1,0:T(8,128)S(1)} %add.336), channel_id=1, source_target_pairs={{0,8},{2,10},{4,12},{6,14},{8,0},{10,2},{12,4},{14,6},{16,24},{18,... | collective-permute-start | bytes 12296 | tf_op jit(solution)/shard_map/ppermute | solution.py:911
  174.3 5.5 %collective-permute-start.54 = (f32[8,128]{1,0:T(8,128)S(1)}, f32[8,128]{1,0:T(8,128)S(1)}, u32[]{:S(2)}, u32[]{:S(2)}) collective-permute-start(f32[8,128]{1,0:T(8,128)S(1)} %add.336), channel_id=1, source_target_pairs={{0,16},{2,18},{4,20},{6,22},{8,24},{10,26},{12,28},{14,30},{16,0},... | collective-permute-start | bytes 12296 | tf_op jit(solution)/shard_map/ppermute | solution.py:911
  176.4 5.5 %collective-permute-start.56 = (f32[8,128]{1,0:T(8,128)S(1)}, f32[8,128]{1,0:T(8,128)S(1)}, u32[]{:S(2)}, u32[]{:S(2)}) collective-permute-start(f32[8,128]{1,0:T(8,128)S(1)} %add.336), channel_id=1, source_target_pairs={{0,2},{2,0},{4,6},{6,4},{8,10},{10,8},{12,14},{14,12},{16,18},{18,... | collective-permute-start | bytes 12296 | tf_op jit(solution)/shard_map/ppermute | solution.py:911
  187.5 7.4 %collective-permute-start.59 = (f32[8,128]{1,0:T(8,128)S(1)}, f32[8,128]{1,0:T(8,128)S(1)}, u32[]{:S(2)}, u32[]{:S(2)}) collective-permute-start(f32[8,128]{1,0:T(8,128)S(1)} %add.342), channel_id=1, source_target_pairs={{0,8},{2,10},{4,12},{6,14},{8,0},{10,2},{12,4},{14,6},{16,24},{18,... | collective-permute-start | bytes 12296 | tf_op jit(solution)/shard_map/ppermute | solution.py:911
  188.9 5.9 %collective-permute-start.60 = (f32[8,128]{1,0:T(8,128)S(1)}, f32[8,128]{1,0:T(8,128)S(1)}, u32[]{:S(2)}, u32[]{:S(2)}) collective-permute-start(f32[8,128]{1,0:T(8,128)S(1)} %add.342), channel_id=1, source_target_pairs={{0,16},{2,18},{4,20},{6,22},{8,24},{10,26},{12,28},{14,30},{16,0},... | collective-permute-start | bytes 12296 | tf_op jit(solution)/shard_map/ppermute | solution.py:911
  190.9 5.5 %collective-permute-start.62 = (f32[8,128]{1,0:T(8,128)S(1)}, f32[8,128]{1,0:T(8,128)S(1)}, u32[]{:S(2)}, u32[]{:S(2)}) collective-permute-start(f32[8,128]{1,0:T(8,128)S(1)} %add.342), channel_id=1, source_target_pairs={{0,2},{2,0},{4,6},{6,4},{8,10},{10,8},{12,14},{14,12},{16,18},{18,... | collective-permute-start | bytes 12296 | tf_op jit(solution)/shard_map/ppermute | solution.py:911
  215.3 6.9 %collective-permute-start.65 = (f32[8,128]{1,0:T(8,128)S(1)}, f32[8,128]{1,0:T(8,128)S(1)}, u32[]{:S(2)}, u32[]{:S(2)}) collective-permute-start(f32[8,128]{1,0:T(8,128)S(1)} %add.348), channel_id=1, source_target_pairs={{0,8},{2,10},{4,12},{6,14},{8,0},{10,2},{12,4},{14,6},{16,24},{18,... | collective-permute-start | bytes 12296 | tf_op jit(solution)/shard_map/ppermute | solution.py:911
  216.8 5.4 %collective-permute-start.66 = (f32[8,128]{1,0:T(8,128)S(1)}, f32[8,128]{1,0:T(8,128)S(1)}, u32[]{:S(2)}, u32[]{:S(2)}) collective-permute-start(f32[8,128]{1,0:T(8,128)S(1)} %add.348), channel_id=1, source_target_pairs={{0,16},{2,18},{4,20},{6,22},{8,24},{10,26},{12,28},{14,30},{16,0},... | collective-permute-start | bytes 12296 | tf_op jit(solution)/shard_map/ppermute | solution.py:911
  218.8 5.5 %collective-permute-start.68 = (f32[8,128]{1,0:T(8,128)S(1)}, f32[8,128]{1,0:T(8,128)S(1)}, u32[]{:S(2)}, u32[]{:S(2)}) collective-permute-start(f32[8,128]{1,0:T(8,128)S(1)} %add.348), channel_id=1, source_target_pairs={{0,2},{2,0},{4,6},{6,4},{8,10},{10,8},{12,14},{14,12},{16,18},{18,... | collective-permute-start | bytes 12296 | tf_op jit(solution)/shard_map/ppermute | solution.py:911
  229.8 6.9 %collective-permute-start.71 = (f32[8,128]{1,0:T(8,128)S(1)}, f32[8,128]{1,0:T(8,128)S(1)}, u32[]{:S(2)}, u32[]{:S(2)}) collective-permute-start(f32[8,128]{1,0:T(8,128)S(1)} %add.354), channel_id=1, source_target_pairs={{0,8},{2,10},{4,12},{6,14},{8,0},{10,2},{12,4},{14,6},{16,24},{18,... | collective-permute-start | bytes 12296 | tf_op jit(solution)/shard_map/ppermute | solution.py:911
  231.2 5.4 %collective-permute-start.72 = (f32[8,128]{1,0:T(8,128)S(1)}, f32[8,128]{1,0:T(8,128)S(1)}, u32[]{:S(2)}, u32[]{:S(2)}) collective-permute-start(f32[8,128]{1,0:T(8,128)S(1)} %add.354), channel_id=1, source_target_pairs={{0,16},{2,18},{4,20},{6,22},{8,24},{10,26},{12,28},{14,30},{16,0},... | collective-permute-start | bytes 12296 | tf_op jit(solution)/shard_map/ppermute | solution.py:911
  233.3 5.5 %collective-permute-start.74 = (f32[8,128]{1,0:T(8,128)S(1)}, f32[8,128]{1,0:T(8,128)S(1)}, u32[]{:S(2)}, u32[]{:S(2)}) collective-permute-start(f32[8,128]{1,0:T(8,128)S(1)} %add.354), channel_id=1, source_target_pairs={{0,2},{2,0},{4,6},{6,4},{8,10},{10,8},{12,14},{14,12},{16,18},{18,... | collective-permute-start | bytes 12296 | tf_op jit(solution)/shard_map/ppermute | solution.py:911
  257.7 6.9 %collective-permute-start.77 = (f32[8,128]{1,0:T(8,128)S(1)}, f32[8,128]{1,0:T(8,128)S(1)}, u32[]{:S(2)}, u32[]{:S(2)}) collective-permute-start(f32[8,128]{1,0:T(8,128)S(1)} %add.360), channel_id=1, source_target_pairs={{0,8},{2,10},{4,12},{6,14},{8,0},{10,2},{12,4},{14,6},{16,24},{18,... | collective-permute-start | bytes 12296 | tf_op jit(solution)/shard_map/ppermute | solution.py:911
  259.2 5.4 %collective-permute-start.78 = (f32[8,128]{1,0:T(8,128)S(1)}, f32[8,128]{1,0:T(8,128)S(1)}, u32[]{:S(2)}, u32[]{:S(2)}) collective-permute-start(f32[8,128]{1,0:T(8,128)S(1)} %add.360), channel_id=1, source_target_pairs={{0,16},{2,18},{4,20},{6,22},{8,24},{10,26},{12,28},{14,30},{16,0},... | collective-permute-start | bytes 12296 | tf_op jit(solution)/shard_map/ppermute | solution.py:911
  261.2 5.5 %collective-permute-start.80 = (f32[8,128]{1,0:T(8,128)S(1)}, f32[8,128]{1,0:T(8,128)S(1)}, u32[]{:S(2)}, u32[]{:S(2)}) collective-permute-start(f32[8,128]{1,0:T(8,128)S(1)} %add.360), channel_id=1, source_target_pairs={{0,2},{2,0},{4,6},{6,4},{8,10},{10,8},{12,14},{14,12},{16,18},{18,... | collective-permute-start | bytes 12296 | tf_op jit(solution)/shard_map/ppermute | solution.py:911
  272.2 6.9 %collective-permute-start.83 = (f32[8,128]{1,0:T(8,128)S(1)}, f32[8,128]{1,0:T(8,128)S(1)}, u32[]{:S(2)}, u32[]{:S(2)}) collective-permute-start(f32[8,128]{1,0:T(8,128)S(1)} %add.366), channel_id=1, source_target_pairs={{0,8},{2,10},{4,12},{6,14},{8,0},{10,2},{12,4},{14,6},{16,24},{18,... | collective-permute-start | bytes 12296 | tf_op jit(solution)/shard_map/ppermute | solution.py:911
  273.7 5.4 %collective-permute-start.84 = (f32[8,128]{1,0:T(8,128)S(1)}, f32[8,128]{1,0:T(8,128)S(1)}, u32[]{:S(2)}, u32[]{:S(2)}) collective-permute-start(f32[8,128]{1,0:T(8,128)S(1)} %add.366), channel_id=1, source_target_pairs={{0,16},{2,18},{4,20},{6,22},{8,24},{10,26},{12,28},{14,30},{16,0},... | collective-permute-start | bytes 12296 | tf_op jit(solution)/shard_map/ppermute | solution.py:911
  275.7 5.5 %collective-permute-start.86 = (f32[8,128]{1,0:T(8,128)S(1)}, f32[8,128]{1,0:T(8,128)S(1)}, u32[]{:S(2)}, u32[]{:S(2)}) collective-permute-start(f32[8,128]{1,0:T(8,128)S(1)} %add.366), channel_id=1, source_target_pairs={{0,2},{2,0},{4,6},{6,4},{8,10},{10,8},{12,14},{14,12},{16,18},{18,... | collective-permute-start | bytes 12296 | tf_op jit(solution)/shard_map/ppermute | solution.py:911
  287.3 20.7 %collective-permute-start.88 = (f32[32,1024]{1,0:T(8,128)S(1)}, f32[32,1024]{1,0:T(8,128)S(1)}, u32[]{:S(2)}, u32[]{:S(2)}) collective-permute-start(f32[32,1024]{1,0:T(8,128)S(1)} %get-tuple-element.314.kept_ref), channel_id=1, source_target_pairs={{1,5},{3,7},{5,1},{7,3},{9,13},{11,15},{13,9},{15,11},{16,20},{18,... | collective-permute-start | bytes 393224 | tf_op jit(solution)/shard_map/ppermute | solution.py:894
  288.0 20.0 %collective-permute-start.89 = (f32[32,1024]{1,0:T(8,128)S(1)}, f32[32,1024]{1,0:T(8,128)S(1)}, u32[]{:S(2)}, u32[]{:S(2)}) collective-permute-start(f32[32,1024]{1,0:T(8,128)S(1)} %get-tuple-element.281), channel_id=1, source_target_pairs={{0,8},{1,13},{2,10},{3,15},{4,12},{5,9},{6,14},{7,11},{8,16},{9,21... | collective-permute-start | bytes 393224 | tf_op jit(solution)/shard_map/ppermute | solution.py:894
  289.5 18.5 %collective-permute-start.90 = (f32[32,1024]{1,0:T(8,128)S(1)}, f32[32,1024]{1,0:T(8,128)S(1)}, u32[]{:S(2)}, u32[]{:S(2)}) collective-permute-start(f32[32,1024]{1,0:T(8,128)S(1)} %get-tuple-element.282), channel_id=1, source_target_pairs={{0,16},{1,21},{2,18},{3,23},{4,20},{5,17},{6,22},{7,19},{8,24},{9,... | collective-permute-start | bytes 393224 | tf_op jit(solution)/shard_map/ppermute | solution.py:894
  295.1 12.9 %collective-permute-start.91 = (f32[32,1024]{1,0:T(8,128)S(1)}, f32[32,1024]{1,0:T(8,128)S(1)}, u32[]{:S(2)}, u32[]{:S(2)}) collective-permute-start(f32[32,1024]{1,0:T(8,128)S(1)} %get-tuple-element.283), channel_id=1, source_target_pairs={{0,24},{1,29},{2,26},{3,31},{4,28},{5,25},{6,30},{7,27},{8,0},{9,5... | collective-permute-start | bytes 393224 | tf_op jit(solution)/shard_map/ppermute | solution.py:894
  309.2 7.1 %collective-permute-start.93 = (f32[8,128]{1,0:T(8,128)S(1)}, f32[8,128]{1,0:T(8,128)S(1)}, u32[]{:S(2)}, u32[]{:S(2)}) collective-permute-start(f32[8,128]{1,0:T(8,128)S(1)} %add.372), channel_id=1, source_target_pairs={{0,8},{2,10},{4,12},{6,14},{8,0},{10,2},{12,4},{14,6},{16,24},{18,... | collective-permute-start | bytes 12296 | tf_op jit(solution)/shard_map/ppermute | solution.py:911
  310.4 6.0 %collective-permute-start.94 = (f32[8,128]{1,0:T(8,128)S(1)}, f32[8,128]{1,0:T(8,128)S(1)}, u32[]{:S(2)}, u32[]{:S(2)}) collective-permute-start(f32[8,128]{1,0:T(8,128)S(1)} %add.372), channel_id=1, source_target_pairs={{0,16},{2,18},{4,20},{6,22},{8,24},{10,26},{12,28},{14,30},{16,0},... | collective-permute-start | bytes 12296 | tf_op jit(solution)/shard_map/ppermute | solution.py:911
  310.6 5.7 %collective-permute-start.95 = (f32[8,128]{1,0:T(8,128)S(1)}, f32[8,128]{1,0:T(8,128)S(1)}, u32[]{:S(2)}, u32[]{:S(2)}) collective-permute-start(f32[8,128]{1,0:T(8,128)S(1)} %add.372), channel_id=1, source_target_pairs={{0,24},{2,26},{4,28},{6,30},{8,16},{10,18},{12,20},{14,22},{16,8},... | collective-permute-start | bytes 12296 | tf_op jit(solution)/shard_map/ppermute | solution.py:911
  312.7 5.5 %collective-permute-start.96 = (f32[8,128]{1,0:T(8,128)S(1)}, f32[8,128]{1,0:T(8,128)S(1)}, u32[]{:S(2)}, u32[]{:S(2)}) collective-permute-start(f32[8,128]{1,0:T(8,128)S(1)} %add.372), channel_id=1, source_target_pairs={{0,2},{2,0},{4,6},{6,4},{8,10},{10,8},{12,14},{14,12},{16,18},{18,... | collective-permute-start | bytes 12296 | tf_op jit(solution)/shard_map/ppermute | solution.py:911
  323.7 7.0 %collective-permute-start.100 = (f32[8,128]{1,0:T(8,128)S(1)}, f32[8,128]{1,0:T(8,128)S(1)}, u32[]{:S(2)}, u32[]{:S(2)}) collective-permute-start(f32[8,128]{1,0:T(8,128)S(1)} %add.378), channel_id=1, source_target_pairs={{0,16},{2,18},{4,20},{6,22},{8,24},{10,26},{12,28},{14,30},{16,0},... | collective-permute-start | bytes 12296 | tf_op jit(solution)/shard_map/ppermute | solution.py:911
  324.4 6.3 %collective-permute-start.101 = (f32[8,128]{1,0:T(8,128)S(1)}, f32[8,128]{1,0:T(8,128)S(1)}, u32[]{:S(2)}, u32[]{:S(2)}) collective-permute-start(f32[8,128]{1,0:T(8,128)S(1)} %add.378), channel_id=1, source_target_pairs={{0,24},{2,26},{4,28},{6,30},{8,16},{10,18},{12,20},{14,22},{16,8},... | collective-permute-start | bytes 12296 | tf_op jit(solution)/shard_map/ppermute | solution.py:911
  326.3 5.5 %collective-permute-start.102 = (f32[8,128]{1,0:T(8,128)S(1)}, f32[8,128]{1,0:T(8,128)S(1)}, u32[]{:S(2)}, u32[]{:S(2)}) collective-permute-start(f32[8,128]{1,0:T(8,128)S(1)} %add.378), channel_id=1, source_target_pairs={{0,2},{2,0},{4,6},{6,4},{8,10},{10,8},{12,14},{14,12},{16,18},{18,... | collective-permute-start | bytes 12296 | tf_op jit(solution)/shard_map/ppermute | solution.py:911
  345.0 20.4 %collective-permute-start.105 = (f32[512,128]{1,0:T(8,128)S(1)}, f32[512,128]{1,0:T(8,128)S(1)}, u32[]{:S(2)}, u32[]{:S(2)}) collective-permute-start(f32[512,128]{1,0:T(8,128)S(1)} %get-tuple-element.306), channel_id=1, source_target_pairs={{0,8},{1,9},{2,10},{3,11},{4,12},{5,13},{6,14},{7,15},{8,0},{9,1},... | collective-permute-start | bytes 786440 | tf_op jit(solution)/shard_map/ppermute | solution.py:887
  345.9 19.4 %collective-permute-start.106 = (f32[512,128]{1,0:T(8,128)S(1)}, f32[512,128]{1,0:T(8,128)S(1)}, u32[]{:S(2)}, u32[]{:S(2)}) collective-permute-start(f32[512,128]{1,0:T(8,128)S(1)} %get-tuple-element.307), channel_id=1, source_target_pairs={{0,16},{1,17},{2,18},{3,19},{4,20},{5,21},{6,22},{7,23},{8,24},{9,... | collective-permute-start | bytes 786440 | tf_op jit(solution)/shard_map/ppermute | solution.py:887
  346.6 18.8 %collective-permute-start.107 = (f32[512,128]{1,0:T(8,128)S(1)}, f32[512,128]{1,0:T(8,128)S(1)}, u32[]{:S(2)}, u32[]{:S(2)}) collective-permute-start(f32[512,128]{1,0:T(8,128)S(1)} %get-tuple-element.308), channel_id=1, source_target_pairs={{0,24},{1,25},{2,26},{3,27},{4,28},{5,29},{6,30},{7,31},{8,16},{9,... | collective-permute-start | bytes 786440 | tf_op jit(solution)/shard_map/ppermute | solution.py:887
  349.2 10.0 %collective-permute-start.109 = (f32[16,1024]{1,0:T(8,128)S(1)}, f32[16,1024]{1,0:T(8,128)S(1)}, u32[]{:S(2)}, u32[]{:S(2)}) collective-permute-start(f32[16,1024]{1,0:T(8,128)S(1)} %get-tuple-element.319.refs_4_), channel_id=1, source_target_pairs={{24,4},{25,1},{26,6},{27,3},{28,0},{29,5},{30,2},{31,7}} | collective-permute-start | bytes 196616 | tf_op jit(solution)/shard_map/ppermute | solution.py:894
  350.5 11.3 %collective-permute-start.110 = (f32[16,1024]{1,0:T(8,128)S(1)}, f32[16,1024]{1,0:T(8,128)S(1)}, u32[]{:S(2)}, u32[]{:S(2)}) collective-permute-start(f32[16,1024]{1,0:T(8,128)S(1)} %get-tuple-element.319.refs_4_), channel_id=1, source_target_pairs={{16,4},{17,1},{18,6},{19,3},{20,0},{21,5},{22,2},{23,7}} | collective-permute-start | bytes 196616 | tf_op jit(solution)/shard_map/ppermute | solution.py:894
  359.2 6.1 %collective-permute-start.111 = (f32[16,1024]{1,0:T(8,128)S(1)}, f32[16,1024]{1,0:T(8,128)S(1)}, u32[]{:S(2)}, u32[]{:S(2)}) collective-permute-start(f32[16,1024]{1,0:T(8,128)S(1)} %get-tuple-element.319.refs_4_), channel_id=1, source_target_pairs={{8,0},{9,5},{10,2},{11,7},{12,4},{13,1},{14,6},{15,3}} | collective-permute-start | bytes 196616 | tf_op jit(solution)/shard_map/ppermute | solution.py:894
  367.4 5.2 %collective-permute-start.113 = (f32[128,128]{1,0:T(8,128)S(1)}, f32[128,128]{1,0:T(8,128)S(1)}, u32[]{:S(2)}, u32[]{:S(2)}) collective-permute-start(f32[128,128]{1,0:T(8,128)S(1)} %get-tuple-element.332), channel_id=1, source_target_pairs={{0,4},{1,5},{2,6},{3,7},{4,0},{5,1},{6,2},{7,3},{8,12},{9,13},{10,... | collective-permute-start | bytes 196616 | tf_op jit(solution)/shard_map/ppermute | solution.py:887
  368.2 7.5 %collective-permute-start.114 = (f32[128,128]{1,0:T(8,128)S(1)}, f32[128,128]{1,0:T(8,128)S(1)}, u32[]{:S(2)}, u32[]{:S(2)}) collective-permute-start(f32[128,128]{1,0:T(8,128)S(1)} %get-tuple-element.333), channel_id=1, source_target_pairs={{0,6},{1,7},{2,4},{3,5},{4,2},{5,3},{6,0},{7,1},{8,14},{9,15},{10,... | collective-permute-start | bytes 196616 | tf_op jit(solution)/shard_map/ppermute | solution.py:887
  378.2 8.3 %collective-permute-start.116 = (f32[128,128]{1,0:T(8,128)S(1)}, f32[128,128]{1,0:T(8,128)S(1)}, u32[]{:S(2)}, u32[]{:S(2)}) collective-permute-start(f32[128,128]{1,0:T(8,128)S(1)} %reduce_part.5.refs_0_), channel_id=1, source_target_pairs={{0,4},{1,5},{2,6},{3,7},{4,0},{5,1},{6,2},{7,3},{8,12},{9,13},{10,... | collective-permute-start | bytes 196616 | tf_op jit(solution)/shard_map/ppermute | solution.py:887
  379.2 7.3 %collective-permute-start.117 = (f32[128,128]{1,0:T(8,128)S(1)}, f32[128,128]{1,0:T(8,128)S(1)}, u32[]{:S(2)}, u32[]{:S(2)}) collective-permute-start(f32[128,128]{1,0:T(8,128)S(1)} %reduce_part.5.refs_0_), channel_id=1, source_target_pairs={{0,6},{1,7},{2,4},{3,5},{4,2},{5,3},{6,0},{7,1},{8,14},{9,15},{10,... | collective-permute-start | bytes 196616 | tf_op jit(solution)/shard_map/ppermute | solution.py:887
  387.1 9.2 %collective-permute-start.118 = (f32[512,128]{1,0:T(8,128)S(1)}, f32[512,128]{1,0:T(8,128)S(1)}, u32[]{:S(2)}, u32[]{:S(2)}) collective-permute-start(f32[512,128]{1,0:T(8,128)S(1)} %gather_part.2.refs_0_), channel_id=1, source_target_pairs={{0,8},{1,9},{2,10},{3,11},{4,12},{5,13},{6,14},{7,15},{8,0},{9,1},... | collective-permute-start | bytes 786440 | tf_op jit(solution)/shard_map/ppermute | solution.py:887
  387.2 13.8 %collective-permute-start.119 = (f32[512,128]{1,0:T(8,128)S(1)}, f32[512,128]{1,0:T(8,128)S(1)}, u32[]{:S(2)}, u32[]{:S(2)}) collective-permute-start(f32[512,128]{1,0:T(8,128)S(1)} %gather_part.2.refs_0_), channel_id=1, source_target_pairs={{0,16},{1,17},{2,18},{3,19},{4,20},{5,21},{6,22},{7,23},{8,24},{9,... | collective-permute-start | bytes 786440 | tf_op jit(solution)/shard_map/ppermute | solution.py:887
  387.3 13.7 %collective-permute-start.120 = (f32[512,128]{1,0:T(8,128)S(1)}, f32[512,128]{1,0:T(8,128)S(1)}, u32[]{:S(2)}, u32[]{:S(2)}) collective-permute-start(f32[512,128]{1,0:T(8,128)S(1)} %gather_part.2.refs_0_), channel_id=1, source_target_pairs={{0,24},{1,25},{2,26},{3,27},{4,28},{5,29},{6,30},{7,31},{8,16},{9,... | collective-permute-start | bytes 786440 | tf_op jit(solution)/shard_map/ppermute | solution.py:887
  (71 other events, 347.5 us)

commit v9 on v8

--- a/solution.py
+++ b/solution.py
@@ -399,9 +399,8 @@
     lon, count,
     d_two_ref, pre_two_ref, sums_two_ref, all_two_ref,
     pre_one_ref, sums_one_ref, vectors_ref, weights_ref,
-    acc_weight_ref, acc_small_ref,
-    d_normed_ref, sums_ref, out_weight_ref, out_small_ref,
-    patches_ref,
+    acc_small_ref,
+    d_normed_ref, sums_ref, act_ref, patches_ref, out_small_ref,
 ):
     w_second_back_ref = part_of(weights_ref, BACK_ROWS, "second")
     sums_two = sums_two_ref[...]
@@ -419,19 +418,42 @@
     d_normed_ref[...] = d_normed
     sums = sums_of(d_normed, centred)
     sums_ref[...] = sums
-    weight_pairs(acc_weight_ref, out_weight_ref, stacked((normed * gate).T), patches_ref, lon)
+    act_ref[...] = normed * gate
     row = lax.broadcasted_iota(jnp.int32, sums.shape, 0)
     small = jnp.where(row == 0, sums[1:2] * scale, jnp.where(row == 1, sums[0:1], 0.0))
     out_small_ref[...] = acc_small_ref[...] + small
 
 
+def middle_grads_kernel(lon, act_ref, patches_ref, acc_ref, out_ref):
+    weight_pairs(acc_ref, out_ref, stacked(act_ref[...].T), patches_ref, lon)
+
+
+def inlet_grads_kernel(
+    lon, act_ref, patches_ref, d_inner_ref, state_ref, acc_first_ref, acc_input_ref, acc_inner_ref,
+    out_first_ref, out_input_ref, out_inner_ref, rows_ref,
+):
+    weight_pairs(acc_first_ref, out_first_ref, stacked(act_ref[...].T), patches_ref, lon)
+    d_inner = d_inner_ref[...]
+    out_inner_ref[...] = acc_inner_ref[...] + d_inner
+    cells = d_inner.shape[0]
+    blank = jnp.zeros((lon, rows_ref.shape[1]), BF16)
+    rows_ref[:lon] = blank
+    rows_ref[lon + cells :] = blank
+    rows_ref[lon : lon + cells] = beside(d_inner)
+    moving_halves = stacked(inlet_channels(state_ref[...], lon))
+    for place in range(3):
+        start = lon * (2 - place)
+        out_input_ref[place] = acc_input_ref[place] + folded(
+            folded(dot(moving_halves, rows_ref[start : start + cells]), 0), 1
+        )
+
+
 def inlet_back_kernel(
     lon, count, quantities,
-    state_ref, d_normed_ref, pre_one_ref, sums_one_ref, all_one_ref, vectors_ref,
+    d_normed_ref, pre_one_ref, sums_one_ref, all_one_ref, vectors_ref,
     inner_ref, d_two_ref, d_state_in_ref, weights_ref,
-    acc_first_ref, acc_input_ref, acc_inner_ref,
-    d_state_ref, packed_ref, out_first_ref, out_input_ref, out_inner_ref,
-    patches_ref,
+    d_state_ref, packed_ref, act_ref, patches_ref, d_inner_ref,
+    rows_ref,
 ):
     cells = inner_ref.shape[0]
     w_first_back_ref = part_of(weights_ref, BACK_ROWS, "first")
@@ -446,17 +468,14 @@
     inner = inner_ref[...]
     gate = sigmoid(inner)
     d_inner = d_act * gate * (1.0 + inner * (1.0 - gate))
-    weight_pairs(acc_first_ref, out_first_ref, stacked((inner * gate).T), patches_ref, lon)
-    out_inner_ref[...] = acc_inner_ref[...] + d_inner
-    patches_ref[lon : lon + cells, :256] = beside(d_inner)
-    rows = [patches_ref[lon * place : lon * place + cells, :256] for place in range(3)]
+    act_ref[...] = inner * gate
+    d_inner_ref[...] = d_inner
+    blank = jnp.zeros((lon, rows_ref.shape[1]), BF16)
+    rows_ref[:lon] = blank
+    rows_ref[lon + cells :] = blank
+    rows_ref[lon : lon + cells] = beside(d_inner)
+    rows = [rows_ref[lon * place : lon * place + cells] for place in range(3)]
     d_moving = folded(dot(jnp.concatenate(rows, axis=1), doubled(w_input_back_ref, inner_ref.shape[1])), 1).T
-    state = state_ref[...]
-    moving_halves = stacked(inlet_channels(state, lon))
-    for place in range(3):
-        out_input_ref[place] = acc_input_ref[place] + folded(
-            folded(dot(moving_halves, rows[2 - place]), 0), 1
-        )
     size = 5 * GROUP
     d_groups = (
         lon_moved(d_moving[:size], 1, lon)
@@ -894,22 +913,27 @@
     return lax.ppermute(value, ("section", "dp"), going)
 
 
-def micro_sum(plan, value, first_core):
+def micro_sum(plan, value, first_core, work=None):
     if not plan.halved or plan.half != 4:
         for bits in plan.sum_rounds:
             value = value + sum(exchanged(value, mask) for mask in masks_of(bits))
-        return value
+        return value, work and work[0](*work[1])
     value = value + exchanged(value, 1)
+    if work:
+        value, operands = lax.optimization_barrier((value, work[1]))
     plane = masks_of([plan.dp, 2 * plan.dp])
-    other = [mask ^ 2 for mask in plane]
+    other = [mask ^ 2 for mask in plane + [0]]
     own = range(plan.sections * plan.dp)
     total = value * first_core
-    for turn, mask in enumerate(plane + [2]):
-        pairs = [(device, device ^ mask) for device in own if not device & 1]
+    for turn in range(4):
+        pairs = [(device, device ^ other[turn]) for device in own if device & 1]
         if turn < 3:
-            pairs += [(device, device ^ other[turn]) for device in own if device & 1]
+            pairs += [(device, device ^ plane[turn]) for device in own if not device & 1]
         total = total + lax.ppermute(value, ("section", "dp"), pairs)
-    return total + exchanged(total, 1)
+    done = None
+    if work:
+        total, done = lax.optimization_barrier((total, work[0](*operands)))
+    return total + exchanged(total, 1), done
 
 
 def on_device(
@@ -1003,15 +1027,25 @@
             {12: 3, 13: 4, 14: 5, 15: 6}, name="outlet_back", scalars=1,
         )
 
+    patch_shape = (cells + 2 * lon, 6 * channels)
     middle_back = call(
         functools.partial(middle_back_kernel, lon, count),
-        [plane, small, (9, channels, channels), small], [patches],
-        {8: 2, 9: 3}, name="middle_back",
+        [plane, small, plane, patch_shape, small],
+        aliases={8: 4}, name="middle_back", kinds=[F32, F32, F32, BF16, F32],
+    )
+    middle_grads = call(
+        functools.partial(middle_grads_kernel, lon), [(9, channels, channels)], aliases={2: 0}, name="middle_grads",
     )
     inlet_back = call(
         functools.partial(inlet_back_kernel, lon, count, quantities),
-        [state_shape, packed, (9, channels, channels), (3, channels, channels), plane], [patches],
-        {10: 2, 11: 3, 12: 4}, name="inlet_back",
+        [state_shape, packed, plane, patch_shape, plane],
+        [pltpu.VMEM((cells + 2 * lon, 2 * channels), BF16)], name="inlet_back", kinds=[F32, F32, F32, BF16, F32],
+    )
+    inlet_grads = call(
+        functools.partial(inlet_grads_kernel, lon),
+        [(9, channels, channels), (3, channels, channels), plane],
+        [pltpu.VMEM((cells + 2 * lon, 2 * channels), BF16)],
+        {4: 0, 5: 1, 6: 2}, name="inlet_grads",
     )
 
     state = entry[: 3 * GROUP]
@@ -1027,9 +1061,9 @@
             )(ids, entry, arrived, static_part, forward_weights)
         else:
             inner, pre_one, sums_one = inlet(state, static_part, forward_weights)
-        sums_one = micro_sum(plan, sums_one, first_core)
+        sums_one, unused = micro_sum(plan, sums_one, first_core)
         pre_two, sums_two = middle(pre_one, sums_one, vectors, forward_weights)
-        sums_two = micro_sum(plan, sums_two, first_core)
+        sums_two, unused = micro_sum(plan, sums_two, first_core)
         state_out, state_packed, mixed, top, weight = outlet(
             state, inner, pre_two, sums_two, vectors, forward_weights
         )
@@ -1061,6 +1095,7 @@
     )
     d_state = jnp.zeros(state_shape, F32)
     grads = [None] * segments
+    inlet_work = None
     path_out = None
     for step in reversed(range(segments)):
         if not step:
@@ -1078,18 +1113,24 @@
         if not step:
             d_two, grad_two, early = lax.optimization_barrier((d_two, grad_two, early))
             path_out = put_home(0, early)
-        grad_two = micro_sum(plan, grad_two, first_core)
-        d_normed, grad_one, acc["second"], acc["small_one"] = middle_back(
+        work = inlet_work and (inlet_grads, inlet_work + (acc["first"], acc["moving"], acc["inner"]))
+        grad_two, done = micro_sum(plan, grad_two, first_core, work)
+        if done:
+            acc["first"], acc["moving"], acc["inner"] = done
+        d_normed, grad_one, act, act_patches, acc["small_one"] = middle_back(
             d_two, pre_two, sums_two, grad_two,
             pre_one, sums_one, vectors, back_weights,
-            acc["second"], acc["small_one"],
+            acc["small_one"],
         )
-        grad_one = micro_sum(plan, grad_one, first_core)
-        d_state, grads[step], acc["first"], acc["moving"], acc["inner"] = inlet_back(
-            state, d_normed, pre_one, sums_one, grad_one, vectors,
+        grad_one, (acc["second"],) = micro_sum(
+            plan, grad_one, first_core, (middle_grads, (act, act_patches, acc["second"]))
+        )
+        d_state, grads[step], act, act_patches, d_inner = inlet_back(
+            d_normed, pre_one, sums_one, grad_one, vectors,
             inner, d_two, d_partial, back_weights,
-            acc["first"], acc["moving"], acc["inner"],
         )
+        inlet_work = (act, act_patches, d_inner, state)
+    acc["first"], acc["moving"], acc["inner"] = inlet_grads(*inlet_work, acc["first"], acc["moving"], acc["inner"])
     late = [grads[0]] + [moved(grads[0], plan.to_first_home(steps)) for steps in range(segments)]
 
     rounds = plan.all_rounds
@@ -1112,8 +1153,9 @@
     )
     for place, (bits, later) in enumerate(zip(rounds, rounds[1:] + [[]])):
         parts = swap(parts, bits)
-        if place == 1:
+        if not place:
             parts, late = lax.optimization_barrier((parts, late))
+        elif place == 1:
             grads_out = put_home(2 * GROUP, early + late)
             parts, path_out, grads_out = lax.optimization_barrier((parts, path_out, grads_out))
         rows >>= len(bits)

time: 413 us -> 395 us (0.956)
  waiting for transfers between devices: 109 us -> 88.2 us
    ppermute x46, starting transfers between devices: 24.4 us -> 64.7 us  [exchanged(): lax.ppermute(value, ('section', 'dp'), [(own, own ^ mask) for own in rang...]
    ppermute x64, starting transfers between devices: 107 us -> 69 us  [micro_sum(): total = total + lax.ppermute(value, ('section', 'dp'), pairs)]
    ppermute x64, waiting for transfers between devices: 37 us -> 25.3 us  [micro_sum(): total = total + lax.ppermute(value, ('section', 'dp'), pairs)]
    ppermute x12, waiting for transfers between devices: 13.7 us -> 6.9 us  [moved(): return lax.ppermute(value, ('section', 'dp'), going)]
    pallas_call x36 -> x44, Pallas kernels: 140 us -> 142 us  [run(): pl.pallas_call(kernel, out_shape=tuple((jax.ShapeDtypeStruct(shape, kind)...]
  transfers between devices with their start and end apart: 122 -> 122, of which waited for: 72 -> 66; matrix products, arithmetic and copies ran while one was open for 0% -> 0% of each run, Pallas kernels for 5% -> 8%
where the time goes in v9:
time: 395 us; the launch traced here: 389 us
  starting transfers between devices  152 us (38%)
  Pallas kernels  142 us (36%)
  waiting for transfers between devices  88.2 us (22%)
    pallas_call x44, Pallas kernels, run(): pl.pallas_call(kernel, out_shape=tuple((jax.ShapeDtypeStruct(shape, kind)...  142 us
    ppermute x64, starting transfers between devices, micro_sum(): total = total + lax.ppermute(value, ('section', 'dp'), pairs)  69 us
    ppermute x46, starting transfers between devices, exchanged(): lax.ppermute(value, ('section', 'dp'), [(own, own ^ mask) for own in rang...  64.7 us
    ppermute x46, waiting for transfers between devices, exchanged(): lax.ppermute(value, ('section', 'dp'), [(own, own ^ mask) for own in rang...  56.1 us
    ppermute x64, waiting for transfers between devices, micro_sum(): total = total + lax.ppermute(value, ('section', 'dp'), pairs)  25.3 us
    ppermute x12, starting transfers between devices, moved(): return lax.ppermute(value, ('section', 'dp'), going)  18.5 us
  transfers between devices with their start and end apart: 122, of which 66 were waited for; matrix products, arithmetic and copies ran while one was open for 0% of the time, Pallas kernels for 8%

profile of v9, /device:TPU:0, one launch (start us, length us, event | category | flops | bytes accessed | tf_op | source)
XLA Modules:
  0.0 388.9 jit_solution(1211082251475182584)
XLA Ops:
  1.2 2.7 enter.1
  4.7 5.9 %weights.1 = (f32[1024,128]{1,0:T(8,128)}, bf16[3872,256]{1,0:T(8,128)(2,1)}, bf16[5248,256]{1,0:T(8,128)(2,1)}, f32[24,128]{1,0:T(8,128)}) custom-call(f32[9,100,128]{2,1,0:T(8,128)} %w_input_ref.1, f32[75,1024]{1,0:T(8,128)} %maps_ref.3, f32[1,128]{1,0:T(1,128)} %bitcast.41, f32[9,128,128]{2,1,0:T(8,128)} %w_first_ref.1, f32[9,128,128]{2,1,0:T(8,128)} %w_second_ref.1, ...), custom_call_target="tpu_custom_call" | custom-call | tf_op jit(solution)/shard_map/weights/pallas_call | solution.py:787
  13.2 3.7 inlet.4
  16.9 4.9 %collective-permute-start.1 = (f32[8,128]{1,0:T(8,128)S(1)}, f32[8,128]{1,0:T(8,128)S(1)}, u32[]{:S(2)}, u32[]{:S(2)}) collective-permute-start(f32[8,128]{1,0:T(8,128)S(1)} %get-tuple-element.262), channel_id=1, source_target_pairs={{0,1},{1,0},{2,3},{3,2},{4,5},{5,4},{6,7},{7,6},{8,9},{9,8},{10,11... | collective-permute-start | bytes 12296 | tf_op jit(solution)/shard_map/ppermute | solution.py:906
  24.1 2.3 collective-permute-start.3
  28.0 2.9 collective-permute-done.4
  35.6 3.1 collective-permute-start.10
  40.2 3.0 collective-permute-done.8
  43.7 1.8 collective-permute-start.12
  46.4 5.7 %outlet.4 = (f32[24,1024]{1,0:T(8,128)S(1)}, f32[16,1024]{1,0:T(8,128)S(1)}, f32[1024,128]{1,0:T(8,128)S(1)}, f32[1024,128]{1,0:T(8,128)S(1)}, f32[1024,128]{1,0:T(8,128)S(1)}) custom-call(f32[24,1024]{1,0:T(8,128)S(1)} %get-tuple-element.259.state_ref, f32[1024,128]{1,0:T(8,128)S(1)} %get-tuple-element.260.inner_ref, ...), custom_call_target="tpu_custom_call" | custom-call | tf_op jit(solution)/shard_map/outlet/pallas_call | solution.py:787
  52.1 3.1 inlet.5
  63.0 2.8 collective-permute-start.18
  70.9 2.0 collective-permute-start.22
  75.4 2.1 collective-permute-start.24
  78.4 5.7 %outlet.5 = (f32[24,1024]{1,0:T(8,128)S(1)}, f32[16,1024]{1,0:T(8,128)S(1)}, f32[1024,128]{1,0:T(8,128)S(1)}, f32[1024,128]{1,0:T(8,128)S(1)}, f32[1024,128]{1,0:T(8,128)S(1)}) custom-call(f32[24,1024]{1,0:T(8,128)S(1)} %get-tuple-element.418.state_ref, f32[1024,128]{1,0:T(8,128)S(1)} %get-tuple-element.271.inner_ref, ...), custom_call_target="tpu_custom_call" | custom-call | tf_op jit(solution)/shard_map/outlet/pallas_call | solution.py:787
  84.1 3.1 inlet.6
  94.9 2.8 collective-permute-start.30
  102.9 2.0 collective-permute-start.34
  107.4 2.1 collective-permute-start.36
  110.3 5.7 %outlet.6 = (f32[24,1024]{1,0:T(8,128)S(1)}, f32[16,1024]{1,0:T(8,128)S(1)}, f32[1024,128]{1,0:T(8,128)S(1)}, f32[1024,128]{1,0:T(8,128)S(1)}, f32[1024,128]{1,0:T(8,128)S(1)}) custom-call(f32[24,1024]{1,0:T(8,128)S(1)} %get-tuple-element.365.state_ref, f32[1024,128]{1,0:T(8,128)S(1)} %get-tuple-element.277.inner_ref, ...), custom_call_target="tpu_custom_call" | custom-call | tf_op jit(solution)/shard_map/outlet/pallas_call | solution.py:787
  116.1 3.1 inlet.7
  127.0 2.8 collective-permute-start.45
  134.9 2.0 collective-permute-start.49
  140.9 1.8 collective-permute-start.39
  142.8 2.2 collective-permute-start.51
  145.8 6.4 %outlet.7 = (f32[24,1024]{1,0:T(8,128)}, f32[16,1024]{1,0:T(8,128)S(1)}, f32[1024,128]{1,0:T(8,128)S(1)}, f32[1024,128]{1,0:T(8,128)S(1)}, f32[1024,128]{1,0:T(8,128)S(1)}) custom-call(f32[24,1024]{1,0:T(8,128)S(1)} %get-tuple-element.325.state_ref, f32[1024,128]{1,0:T(8,128)S(1)} %get-tuple-element.287.inner_ref, ...), custom_call_target="tpu_custom_call" | custom-call | tf_op jit(solution)/shard_map/outlet/pallas_call | solution.py:787
  152.3 12.0 %outlet_back.4 = (f32[24,1024]{1,0:T(8,128)S(1)}, f32[1024,128]{1,0:T(8,128)S(1)}, f32[8,128]{1,0:T(8,128)S(1)}, f32[128,384]{1,0:T(8,128)S(1)}, f32[128,128]{1,...) custom-call(s32[2]{0:T(128)S(1)} %copy-done.8, ...), custom_call_target="tpu_custom_call", output_to_operand_aliasing={{3}: (12, {}), {4}: (13, {}), {5}: (14, {}), {6}: (15, {})} | custom-call | tf_op jit(solution)/shard_map/outlet_back/pallas_call | solution.py:787
  164.3 3.4 collective-permute-start.52
  168.6 2.6 collective-permute-start.53
  187.8 2.1 collective-permute-start.63
  190.7 2.9 inlet_back.4
  193.6 12.2 %outlet_back.5 = (f32[24,1024]{1,0:T(8,128)S(1)}, f32[1024,128]{1,0:T(8,128)S(1)}, f32[8,128]{1,0:T(8,128)S(1)}, f32[128,384]{1,0:T(8,128)S(1)}, f32[128,128]{1,...) custom-call(s32[2]{0:T(128)S(1)} %copy-done.8, ...), custom_call_target="tpu_custom_call", output_to_operand_aliasing={{3}: (12, {}), {4}: (13, {}), {5}: (14, {}), {6}: (15, {})} | custom-call | tf_op jit(solution)/shard_map/outlet_back/pallas_call | solution.py:787
  207.1 2.2 collective-permute-start.65
  211.5 1.9 inlet_grads.4
  214.0 2.2 collective-permute-start.69
  219.8 2.2 collective-permute-start.71
  229.3 2.9 inlet_back.5
  232.3 12.0 %outlet_back.6 = (f32[24,1024]{1,0:T(8,128)S(1)}, f32[1024,128]{1,0:T(8,128)S(1)}, f32[8,128]{1,0:T(8,128)S(1)}, f32[128,384]{1,0:T(8,128)S(1)}, f32[128,128]{1,...) custom-call(s32[2]{0:T(128)S(1)} %copy-done.8, ...), custom_call_target="tpu_custom_call", output_to_operand_aliasing={{3}: (12, {}), {4}: (13, {}), {5}: (14, {}), {6}: (15, {})} | custom-call | tf_op jit(solution)/shard_map/outlet_back/pallas_call | solution.py:787
  245.5 2.2 collective-permute-start.77
  249.8 2.0 inlet_grads.5
  252.4 2.2 collective-permute-start.81
  258.1 2.2 collective-permute-start.83
  267.6 2.9 inlet_back.6
  271.9 2.2 collective-permute-start.89
  274.1 3.8 collective-permute-start.90
  279.2 11.8 %outlet_back.7 = (f32[24,1024]{1,0:T(8,128)S(1)}, f32[1024,128]{1,0:T(8,128)S(1)}, f32[8,128]{1,0:T(8,128)S(1)}, f32[128,384]{1,0:T(8,128)S(1)}, f32[128,128]{1,...) custom-call(s32[2]{0:T(128)S(1)} %copy-done.8, ...), custom_call_target="tpu_custom_call", output_to_operand_aliasing={{3}: (12, {}), {4}: (13, {}), {5}: (14, {}), {6}: (15, {})} | custom-call | tf_op jit(solution)/shard_map/outlet_back/pallas_call | solution.py:787
  293.9 1.9 collective-permute-start.95
  296.7 2.0 inlet_grads.6
  298.7 2.7 collective-permute-start.97
  305.6 1.8 collective-permute-start.101
  311.7 2.4 collective-permute-start.103
  315.0 3.5 inlet_back.7
  318.5 1.9 inlet_grads.7
  320.5 2.0 pack.1
  327.5 6.2 %collective-permute-done.106.refs_6_ = f32[16,1024]{1,0:T(8,128)S(1)} collective-permute-done((f32[16,1024]{1,0:T(8,128)S(1)}, f32[16,1024]{1,0:T(8,128)S(1)}, u32[]{:S(2)}, u32[]{:S(2)}) %collective-permute-start.106) | collective-permute-done | bytes 65568 | tf_op jit(solution)/shard_map/ppermute | solution.py:913
  334.7 3.4 collective-permute-start.111
  342.1 5.7 %collective-permute-done.110.refs_2_ = f32[512,128]{1,0:T(8,128)S(1)} collective-permute-done((f32[512,128]{1,0:T(8,128)S(1)}, f32[512,128]{1,0:T(8,128)S(1)}, u32[]{:S(2)}, u32[]{:S(2)}) %collective-permute-start.110) | collective-permute-done | bytes 262176 | tf_op jit(solution)/shard_map/ppermute | solution.py:906
  351.0 2.0 collective-permute-start.114
  353.2 5.3 %collective-permute-done.113.refs_2_ = f32[128,128]{1,0:T(8,128)S(1)} collective-permute-done((f32[128,128]{1,0:T(8,128)S(1)}, f32[128,128]{1,0:T(8,128)S(1)}, u32[]{:S(2)}, u32[]{:S(2)}) %collective-permute-start.113) | collective-permute-done | bytes 65568 | tf_op jit(solution)/shard_map/ppermute | solution.py:906
  363.6 5.2 %collective-permute-done.116.refs_2_ = f32[128,128]{1,0:T(8,128)S(1)} collective-permute-done((f32[128,128]{1,0:T(8,128)S(1)}, f32[128,128]{1,0:T(8,128)S(1)}, u32[]{:S(2)}, u32[]{:S(2)}) %collective-permute-start.116) | collective-permute-done | bytes 65568 | tf_op jit(solution)/shard_map/ppermute | solution.py:906
  372.9 5.3 %collective-permute-done.118.refs_1_ = f32[512,128]{1,0:T(8,128)S(1)} collective-permute-done((f32[512,128]{1,0:T(8,128)S(1)}, f32[512,128]{1,0:T(8,128)S(1)}, u32[]{:S(2)}, u32[]{:S(2)}) %collective-permute-start.118) | collective-permute-done | bytes 262176 | tf_op jit(solution)/shard_map/ppermute | solution.py:906
  378.3 4.0 %collective-permute-done.119.refs_2_ = f32[512,128]{1,0:T(8,128)S(1)} collective-permute-done((f32[512,128]{1,0:T(8,128)S(1)}, f32[512,128]{1,0:T(8,128)S(1)}, u32[]{:S(2)}, u32[]{:S(2)}) %collective-permute-start.119) | collective-permute-done | bytes 262176 | tf_op jit(solution)/shard_map/ppermute | solution.py:906
  383.0 2.6 collective-permute-done.121.refs_1_
  385.7 2.0 unpack.1
  (313 shorter events, 152.8 us)
Async XLA Ops:
  3.9 6.7 %collective-permute-start = (f32[40,1024]{1,0:T(8,128)}, f32[40,1024]{1,0:T(8,128)S(1)}, u32[]{:S(2)}, u32[]{:S(2)}) collective-permute-start(f32[40,1024]{1,0:T(8,128)} %get-tuple-element.256.own_ref), channel_id=1, source_target_pairs={{1,5},{3,7},{5,1},{7,3},{9,13},{11,15},{13,9},{15,11},{16,20},{18,... | collective-permute-start | bytes 491528 | tf_op jit(solution)/shard_map/ppermute | solution.py:913
  16.9 5.7 %collective-permute-start.1 = (f32[8,128]{1,0:T(8,128)S(1)}, f32[8,128]{1,0:T(8,128)S(1)}, u32[]{:S(2)}, u32[]{:S(2)}) collective-permute-start(f32[8,128]{1,0:T(8,128)S(1)} %get-tuple-element.262), channel_id=1, source_target_pairs={{0,1},{1,0},{2,3},{3,2},{4,5},{5,4},{6,7},{7,6},{8,9},{9,8},{10,11... | collective-permute-start | bytes 12296 | tf_op jit(solution)/shard_map/ppermute | solution.py:906
  22.7 4.4 %collective-permute-start.2 = (f32[8,128]{1,0:T(8,128)S(1)}, f32[8,128]{1,0:T(8,128)S(1)}, u32[]{:S(2)}, u32[]{:S(2)}) collective-permute-start(f32[8,128]{1,0:T(8,128)S(1)} %add.288), channel_id=1, source_target_pairs={{1,11},{3,9},{5,15},{7,13},{9,3},{11,1},{13,7},{15,5},{17,27},{19,... | collective-permute-start | bytes 12296 | tf_op jit(solution)/shard_map/ppermute | solution.py:932
  26.4 4.5 %collective-permute-start.4 = (f32[8,128]{1,0:T(8,128)S(1)}, f32[8,128]{1,0:T(8,128)S(1)}, u32[]{:S(2)}, u32[]{:S(2)}) collective-permute-start(f32[8,128]{1,0:T(8,128)S(1)} %add.288), channel_id=1, source_target_pairs={{1,27},{3,25},{5,31},{7,29},{9,19},{11,17},{13,23},{15,21},{17,11}... | collective-permute-start | bytes 12296 | tf_op jit(solution)/shard_map/ppermute | solution.py:932
  26.4 4.5 %collective-permute-start.5 = (f32[8,128]{1,0:T(8,128)S(1)}, f32[8,128]{1,0:T(8,128)S(1)}, u32[]{:S(2)}, u32[]{:S(2)}) collective-permute-start(f32[8,128]{1,0:T(8,128)S(1)} %add.288), channel_id=1, source_target_pairs={{1,3},{3,1},{5,7},{7,5},{9,11},{11,9},{13,15},{15,13},{17,19},{19,... | collective-permute-start | bytes 12296 | tf_op jit(solution)/shard_map/ppermute | solution.py:932
  35.6 4.6 %collective-permute-start.10 = (f32[8,128]{1,0:T(8,128)S(1)}, f32[8,128]{1,0:T(8,128)S(1)}, u32[]{:S(2)}, u32[]{:S(2)}) collective-permute-start(f32[8,128]{1,0:T(8,128)S(1)} %add.294), channel_id=1, source_target_pairs={{1,27},{3,25},{5,31},{7,29},{9,19},{11,17},{13,23},{15,21},{17,11}... | collective-permute-start | bytes 12296 | tf_op jit(solution)/shard_map/ppermute | solution.py:932
  56.5 4.1 %collective-permute-start.14 = (f32[8,128]{1,0:T(8,128)S(1)}, f32[8,128]{1,0:T(8,128)S(1)}, u32[]{:S(2)}, u32[]{:S(2)}) collective-permute-start(f32[8,128]{1,0:T(8,128)S(1)} %add.300), channel_id=1, source_target_pairs={{1,11},{3,9},{5,15},{7,13},{9,3},{11,1},{13,7},{15,5},{17,27},{19,... | collective-permute-start | bytes 12296 | tf_op jit(solution)/shard_map/ppermute | solution.py:932
  58.4 4.5 %collective-permute-start.16 = (f32[8,128]{1,0:T(8,128)S(1)}, f32[8,128]{1,0:T(8,128)S(1)}, u32[]{:S(2)}, u32[]{:S(2)}) collective-permute-start(f32[8,128]{1,0:T(8,128)S(1)} %add.300), channel_id=1, source_target_pairs={{1,27},{3,25},{5,31},{7,29},{9,19},{11,17},{13,23},{15,21},{17,11}... | collective-permute-start | bytes 12296 | tf_op jit(solution)/shard_map/ppermute | solution.py:932
  69.4 4.6 %collective-permute-start.20 = (f32[8,128]{1,0:T(8,128)S(1)}, f32[8,128]{1,0:T(8,128)S(1)}, u32[]{:S(2)}, u32[]{:S(2)}) collective-permute-start(f32[8,128]{1,0:T(8,128)S(1)} %add.306), channel_id=1, source_target_pairs={{1,11},{3,9},{5,15},{7,13},{9,3},{11,1},{13,7},{15,5},{17,27},{19,... | collective-permute-start | bytes 12296 | tf_op jit(solution)/shard_map/ppermute | solution.py:932
  70.9 4.5 %collective-permute-start.22 = (f32[8,128]{1,0:T(8,128)S(1)}, f32[8,128]{1,0:T(8,128)S(1)}, u32[]{:S(2)}, u32[]{:S(2)}) collective-permute-start(f32[8,128]{1,0:T(8,128)S(1)} %add.306), channel_id=1, source_target_pairs={{1,27},{3,25},{5,31},{7,29},{9,19},{11,17},{13,23},{15,21},{17,11}... | collective-permute-start | bytes 12296 | tf_op jit(solution)/shard_map/ppermute | solution.py:932
  88.5 4.1 %collective-permute-start.26 = (f32[8,128]{1,0:T(8,128)S(1)}, f32[8,128]{1,0:T(8,128)S(1)}, u32[]{:S(2)}, u32[]{:S(2)}) collective-permute-start(f32[8,128]{1,0:T(8,128)S(1)} %add.312), channel_id=1, source_target_pairs={{1,11},{3,9},{5,15},{7,13},{9,3},{11,1},{13,7},{15,5},{17,27},{19,... | collective-permute-start | bytes 12296 | tf_op jit(solution)/shard_map/ppermute | solution.py:932
  90.4 4.5 %collective-permute-start.28 = (f32[8,128]{1,0:T(8,128)S(1)}, f32[8,128]{1,0:T(8,128)S(1)}, u32[]{:S(2)}, u32[]{:S(2)}) collective-permute-start(f32[8,128]{1,0:T(8,128)S(1)} %add.312), channel_id=1, source_target_pairs={{1,27},{3,25},{5,31},{7,29},{9,19},{11,17},{13,23},{15,21},{17,11}... | collective-permute-start | bytes 12296 | tf_op jit(solution)/shard_map/ppermute | solution.py:932
  101.4 4.3 %collective-permute-start.32 = (f32[8,128]{1,0:T(8,128)S(1)}, f32[8,128]{1,0:T(8,128)S(1)}, u32[]{:S(2)}, u32[]{:S(2)}) collective-permute-start(f32[8,128]{1,0:T(8,128)S(1)} %add.318), channel_id=1, source_target_pairs={{1,11},{3,9},{5,15},{7,13},{9,3},{11,1},{13,7},{15,5},{17,27},{19,... | collective-permute-start | bytes 12296 | tf_op jit(solution)/shard_map/ppermute | solution.py:932
  102.9 4.5 %collective-permute-start.34 = (f32[8,128]{1,0:T(8,128)S(1)}, f32[8,128]{1,0:T(8,128)S(1)}, u32[]{:S(2)}, u32[]{:S(2)}) collective-permute-start(f32[8,128]{1,0:T(8,128)S(1)} %add.318), channel_id=1, source_target_pairs={{1,27},{3,25},{5,31},{7,29},{9,19},{11,17},{13,23},{15,21},{17,11}... | collective-permute-start | bytes 12296 | tf_op jit(solution)/shard_map/ppermute | solution.py:932
  120.5 4.1 %collective-permute-start.41 = (f32[8,128]{1,0:T(8,128)S(1)}, f32[8,128]{1,0:T(8,128)S(1)}, u32[]{:S(2)}, u32[]{:S(2)}) collective-permute-start(f32[8,128]{1,0:T(8,128)S(1)} %add.324), channel_id=1, source_target_pairs={{1,11},{3,9},{5,15},{7,13},{9,3},{11,1},{13,7},{15,5},{17,27},{19,... | collective-permute-start | bytes 12296 | tf_op jit(solution)/shard_map/ppermute | solution.py:932
  122.4 4.5 %collective-permute-start.43 = (f32[8,128]{1,0:T(8,128)S(1)}, f32[8,128]{1,0:T(8,128)S(1)}, u32[]{:S(2)}, u32[]{:S(2)}) collective-permute-start(f32[8,128]{1,0:T(8,128)S(1)} %add.324), channel_id=1, source_target_pairs={{1,27},{3,25},{5,31},{7,29},{9,19},{11,17},{13,23},{15,21},{17,11}... | collective-permute-start | bytes 12296 | tf_op jit(solution)/shard_map/ppermute | solution.py:932
  133.4 5.7 %collective-permute-start.47 = (f32[8,128]{1,0:T(8,128)S(1)}, f32[8,128]{1,0:T(8,128)S(1)}, u32[]{:S(2)}, u32[]{:S(2)}) collective-permute-start(f32[8,128]{1,0:T(8,128)S(1)} %add.330), channel_id=1, source_target_pairs={{1,11},{3,9},{5,15},{7,13},{9,3},{11,1},{13,7},{15,5},{17,27},{19,... | collective-permute-start | bytes 12296 | tf_op jit(solution)/shard_map/ppermute | solution.py:932
  134.9 6.0 %collective-permute-start.48 = (f32[8,128]{1,0:T(8,128)S(1)}, f32[8,128]{1,0:T(8,128)S(1)}, u32[]{:S(2)}, u32[]{:S(2)}) collective-permute-start(f32[8,128]{1,0:T(8,128)S(1)} %add.330), channel_id=1, source_target_pairs={{1,19},{3,17},{5,23},{7,21},{9,27},{11,25},{13,31},{15,29},{17,3},... | collective-permute-start | bytes 12296 | tf_op jit(solution)/shard_map/ppermute | solution.py:932
  134.9 7.9 %collective-permute-start.49 = (f32[8,128]{1,0:T(8,128)S(1)}, f32[8,128]{1,0:T(8,128)S(1)}, u32[]{:S(2)}, u32[]{:S(2)}) collective-permute-start(f32[8,128]{1,0:T(8,128)S(1)} %add.330), channel_id=1, source_target_pairs={{1,27},{3,25},{5,31},{7,29},{9,19},{11,17},{13,23},{15,21},{17,11}... | collective-permute-start | bytes 12296 | tf_op jit(solution)/shard_map/ppermute | solution.py:932
  136.9 5.9 %collective-permute-start.50 = (f32[8,128]{1,0:T(8,128)S(1)}, f32[8,128]{1,0:T(8,128)S(1)}, u32[]{:S(2)}, u32[]{:S(2)}) collective-permute-start(f32[8,128]{1,0:T(8,128)S(1)} %add.330), channel_id=1, source_target_pairs={{1,3},{3,1},{5,7},{7,5},{9,11},{11,9},{13,15},{15,13},{17,19},{19,... | collective-permute-start | bytes 12296 | tf_op jit(solution)/shard_map/ppermute | solution.py:932
  137.6 7.4 %collective-permute-start.37 = (f32[16,1024]{1,0:T(8,128)S(1)}, f32[16,1024]{1,0:T(8,128)S(1)}, u32[]{:S(2)}, u32[]{:S(2)}) collective-permute-start(f32[16,1024]{1,0:T(8,128)S(1)} %copy-done.12), channel_id=1, source_target_pairs={{0,8},{1,13},{2,10},{3,15},{4,12},{5,9},{6,14},{7,11},{8,20},{9,17... | collective-permute-start | bytes 196616 | tf_op jit(solution)/shard_map/ppermute | solution.py:913
  139.1 5.9 %collective-permute-start.38 = (f32[16,1024]{1,0:T(8,128)S(1)}, f32[16,1024]{1,0:T(8,128)S(1)}, u32[]{:S(2)}, u32[]{:S(2)}) collective-permute-start(f32[16,1024]{1,0:T(8,128)S(1)} %copy-done.11), channel_id=1, source_target_pairs={{0,20},{1,17},{2,22},{3,19},{4,16},{5,21},{6,18},{7,23},{8,28},{9,... | collective-permute-start | bytes 196616 | tf_op jit(solution)/shard_map/ppermute | solution.py:913
  140.9 4.7 %collective-permute-start.39 = (f32[16,1024]{1,0:T(8,128)S(1)}, f32[16,1024]{1,0:T(8,128)S(1)}, u32[]{:S(2)}, u32[]{:S(2)}) collective-permute-start(f32[16,1024]{1,0:T(8,128)S(1)} %copy-done.10), channel_id=1, source_target_pairs={{0,28},{1,25},{2,30},{3,27},{4,24},{5,29},{6,26},{7,31},{8,0},{9,5... | collective-permute-start | bytes 196616 | tf_op jit(solution)/shard_map/ppermute | solution.py:913
  164.3 4.3 %collective-permute-start.52 = (f32[8,128]{1,0:T(8,128)S(1)}, f32[8,128]{1,0:T(8,128)S(1)}, u32[]{:S(2)}, u32[]{:S(2)}) collective-permute-start(f32[8,128]{1,0:T(8,128)S(1)} %get-tuple-element.297), channel_id=1, source_target_pairs={{0,1},{1,0},{2,3},{3,2},{4,5},{5,4},{6,7},{7,6},{8,9},{9,8},{10,11... | collective-permute-start | bytes 12296 | tf_op jit(solution)/shard_map/ppermute | solution.py:906
  168.6 4.7 %collective-permute-start.53 = (f32[8,128]{1,0:T(8,128)S(1)}, f32[8,128]{1,0:T(8,128)S(1)}, u32[]{:S(2)}, u32[]{:S(2)}) collective-permute-start(f32[8,128]{1,0:T(8,128)S(1)} %add.336), channel_id=1, source_target_pairs={{1,11},{3,9},{5,15},{7,13},{9,3},{11,1},{13,7},{15,5},{17,27},{19,... | collective-permute-start | bytes 12296 | tf_op jit(solution)/shard_map/ppermute | solution.py:932
  171.5 4.5 %collective-permute-start.55 = (f32[8,128]{1,0:T(8,128)S(1)}, f32[8,128]{1,0:T(8,128)S(1)}, u32[]{:S(2)}, u32[]{:S(2)}) collective-permute-start(f32[8,128]{1,0:T(8,128)S(1)} %add.336), channel_id=1, source_target_pairs={{1,27},{3,25},{5,31},{7,29},{9,19},{11,17},{13,23},{15,21},{17,11}... | collective-permute-start | bytes 12296 | tf_op jit(solution)/shard_map/ppermute | solution.py:932
  181.2 5.7 %collective-permute-start.59 = (f32[8,128]{1,0:T(8,128)S(1)}, f32[8,128]{1,0:T(8,128)S(1)}, u32[]{:S(2)}, u32[]{:S(2)}) collective-permute-start(f32[8,128]{1,0:T(8,128)S(1)} %add.342), channel_id=1, source_target_pairs={{1,11},{3,9},{5,15},{7,13},{9,3},{11,1},{13,7},{15,5},{17,27},{19,... | collective-permute-start | bytes 12296 | tf_op jit(solution)/shard_map/ppermute | solution.py:932
  182.7 4.3 %collective-permute-start.60 = (f32[8,128]{1,0:T(8,128)S(1)}, f32[8,128]{1,0:T(8,128)S(1)}, u32[]{:S(2)}, u32[]{:S(2)}) collective-permute-start(f32[8,128]{1,0:T(8,128)S(1)} %add.342), channel_id=1, source_target_pairs={{1,19},{3,17},{5,23},{7,21},{9,27},{11,25},{13,31},{15,29},{17,3},... | collective-permute-start | bytes 12296 | tf_op jit(solution)/shard_map/ppermute | solution.py:932
  183.2 4.5 %collective-permute-start.61 = (f32[8,128]{1,0:T(8,128)S(1)}, f32[8,128]{1,0:T(8,128)S(1)}, u32[]{:S(2)}, u32[]{:S(2)}) collective-permute-start(f32[8,128]{1,0:T(8,128)S(1)} %add.342), channel_id=1, source_target_pairs={{1,27},{3,25},{5,31},{7,29},{9,19},{11,17},{13,23},{15,21},{17,11}... | collective-permute-start | bytes 12296 | tf_op jit(solution)/shard_map/ppermute | solution.py:932
  207.1 6.3 %collective-permute-start.65 = (f32[8,128]{1,0:T(8,128)S(1)}, f32[8,128]{1,0:T(8,128)S(1)}, u32[]{:S(2)}, u32[]{:S(2)}) collective-permute-start(f32[8,128]{1,0:T(8,128)S(1)} %add.348), channel_id=1, source_target_pairs={{1,11},{3,9},{5,15},{7,13},{9,3},{11,1},{13,7},{15,5},{17,27},{19,... | collective-permute-start | bytes 12296 | tf_op jit(solution)/shard_map/ppermute | solution.py:932
  209.3 4.2 %collective-permute-start.66 = (f32[8,128]{1,0:T(8,128)S(1)}, f32[8,128]{1,0:T(8,128)S(1)}, u32[]{:S(2)}, u32[]{:S(2)}) collective-permute-start(f32[8,128]{1,0:T(8,128)S(1)} %add.348), channel_id=1, source_target_pairs={{1,19},{3,17},{5,23},{7,21},{9,27},{11,25},{13,31},{15,29},{17,3},... | collective-permute-start | bytes 12296 | tf_op jit(solution)/shard_map/ppermute | solution.py:932
  209.5 4.5 %collective-permute-start.67 = (f32[8,128]{1,0:T(8,128)S(1)}, f32[8,128]{1,0:T(8,128)S(1)}, u32[]{:S(2)}, u32[]{:S(2)}) collective-permute-start(f32[8,128]{1,0:T(8,128)S(1)} %add.348), channel_id=1, source_target_pairs={{1,27},{3,25},{5,31},{7,29},{9,19},{11,17},{13,23},{15,21},{17,11}... | collective-permute-start | bytes 12296 | tf_op jit(solution)/shard_map/ppermute | solution.py:932
  219.8 5.8 %collective-permute-start.71 = (f32[8,128]{1,0:T(8,128)S(1)}, f32[8,128]{1,0:T(8,128)S(1)}, u32[]{:S(2)}, u32[]{:S(2)}) collective-permute-start(f32[8,128]{1,0:T(8,128)S(1)} %add.354), channel_id=1, source_target_pairs={{1,11},{3,9},{5,15},{7,13},{9,3},{11,1},{13,7},{15,5},{17,27},{19,... | collective-permute-start | bytes 12296 | tf_op jit(solution)/shard_map/ppermute | solution.py:932
  222.2 4.5 %collective-permute-start.73 = (f32[8,128]{1,0:T(8,128)S(1)}, f32[8,128]{1,0:T(8,128)S(1)}, u32[]{:S(2)}, u32[]{:S(2)}) collective-permute-start(f32[8,128]{1,0:T(8,128)S(1)} %add.354), channel_id=1, source_target_pairs={{1,27},{3,25},{5,31},{7,29},{9,19},{11,17},{13,23},{15,21},{17,11}... | collective-permute-start | bytes 12296 | tf_op jit(solution)/shard_map/ppermute | solution.py:932
  245.5 6.3 %collective-permute-start.77 = (f32[8,128]{1,0:T(8,128)S(1)}, f32[8,128]{1,0:T(8,128)S(1)}, u32[]{:S(2)}, u32[]{:S(2)}) collective-permute-start(f32[8,128]{1,0:T(8,128)S(1)} %add.360), channel_id=1, source_target_pairs={{1,11},{3,9},{5,15},{7,13},{9,3},{11,1},{13,7},{15,5},{17,27},{19,... | collective-permute-start | bytes 12296 | tf_op jit(solution)/shard_map/ppermute | solution.py:932
  247.9 4.5 %collective-permute-start.79 = (f32[8,128]{1,0:T(8,128)S(1)}, f32[8,128]{1,0:T(8,128)S(1)}, u32[]{:S(2)}, u32[]{:S(2)}) collective-permute-start(f32[8,128]{1,0:T(8,128)S(1)} %add.360), channel_id=1, source_target_pairs={{1,27},{3,25},{5,31},{7,29},{9,19},{11,17},{13,23},{15,21},{17,11}... | collective-permute-start | bytes 12296 | tf_op jit(solution)/shard_map/ppermute | solution.py:932
  258.1 5.8 %collective-permute-start.83 = (f32[8,128]{1,0:T(8,128)S(1)}, f32[8,128]{1,0:T(8,128)S(1)}, u32[]{:S(2)}, u32[]{:S(2)}) collective-permute-start(f32[8,128]{1,0:T(8,128)S(1)} %add.366), channel_id=1, source_target_pairs={{1,11},{3,9},{5,15},{7,13},{9,3},{11,1},{13,7},{15,5},{17,27},{19,... | collective-permute-start | bytes 12296 | tf_op jit(solution)/shard_map/ppermute | solution.py:932
  260.5 4.5 %collective-permute-start.85 = (f32[8,128]{1,0:T(8,128)S(1)}, f32[8,128]{1,0:T(8,128)S(1)}, u32[]{:S(2)}, u32[]{:S(2)}) collective-permute-start(f32[8,128]{1,0:T(8,128)S(1)} %add.366), channel_id=1, source_target_pairs={{1,27},{3,25},{5,31},{7,29},{9,19},{11,17},{13,23},{15,21},{17,11}... | collective-permute-start | bytes 12296 | tf_op jit(solution)/shard_map/ppermute | solution.py:932
  271.2 19.8 %collective-permute-start.88 = (f32[32,1024]{1,0:T(8,128)S(1)}, f32[32,1024]{1,0:T(8,128)S(1)}, u32[]{:S(2)}, u32[]{:S(2)}) collective-permute-start(f32[32,1024]{1,0:T(8,128)S(1)} %get-tuple-element.462.kept_ref), channel_id=1, source_target_pairs={{1,5},{3,7},{5,1},{7,3},{9,13},{11,15},{13,9},{15,11},{16,20},{18,... | collective-permute-start | bytes 393224 | tf_op jit(solution)/shard_map/ppermute | solution.py:913
  271.9 19.2 %collective-permute-start.89 = (f32[32,1024]{1,0:T(8,128)S(1)}, f32[32,1024]{1,0:T(8,128)S(1)}, u32[]{:S(2)}, u32[]{:S(2)}) collective-permute-start(f32[32,1024]{1,0:T(8,128)S(1)} %get-tuple-element.403), channel_id=1, source_target_pairs={{0,8},{1,13},{2,10},{3,15},{4,12},{5,9},{6,14},{7,11},{8,16},{9,21... | collective-permute-start | bytes 393224 | tf_op jit(solution)/shard_map/ppermute | solution.py:913
  274.1 16.9 %collective-permute-start.90 = (f32[32,1024]{1,0:T(8,128)S(1)}, f32[32,1024]{1,0:T(8,128)S(1)}, u32[]{:S(2)}, u32[]{:S(2)}) collective-permute-start(f32[32,1024]{1,0:T(8,128)S(1)} %get-tuple-element.404), channel_id=1, source_target_pairs={{0,16},{1,21},{2,18},{3,23},{4,20},{5,17},{6,22},{7,19},{8,24},{9,... | collective-permute-start | bytes 393224 | tf_op jit(solution)/shard_map/ppermute | solution.py:913
  277.9 13.1 %collective-permute-start.91 = (f32[32,1024]{1,0:T(8,128)S(1)}, f32[32,1024]{1,0:T(8,128)S(1)}, u32[]{:S(2)}, u32[]{:S(2)}) collective-permute-start(f32[32,1024]{1,0:T(8,128)S(1)} %get-tuple-element.405), channel_id=1, source_target_pairs={{0,24},{1,29},{2,26},{3,31},{4,28},{5,25},{6,30},{7,27},{8,0},{9,5... | collective-permute-start | bytes 393224 | tf_op jit(solution)/shard_map/ppermute | solution.py:913
  292.3 6.4 %collective-permute-start.93 = (f32[8,128]{1,0:T(8,128)S(1)}, f32[8,128]{1,0:T(8,128)S(1)}, u32[]{:S(2)}, u32[]{:S(2)}) collective-permute-start(f32[8,128]{1,0:T(8,128)S(1)} %add.372), channel_id=1, source_target_pairs={{1,11},{3,9},{5,15},{7,13},{9,3},{11,1},{13,7},{15,5},{17,27},{19,... | collective-permute-start | bytes 12296 | tf_op jit(solution)/shard_map/ppermute | solution.py:932
  293.2 5.5 %collective-permute-start.94 = (f32[8,128]{1,0:T(8,128)S(1)}, f32[8,128]{1,0:T(8,128)S(1)}, u32[]{:S(2)}, u32[]{:S(2)}) collective-permute-start(f32[8,128]{1,0:T(8,128)S(1)} %add.372), channel_id=1, source_target_pairs={{1,19},{3,17},{5,23},{7,21},{9,27},{11,25},{13,31},{15,29},{17,3},... | collective-permute-start | bytes 12296 | tf_op jit(solution)/shard_map/ppermute | solution.py:932
  293.9 4.8 %collective-permute-start.95 = (f32[8,128]{1,0:T(8,128)S(1)}, f32[8,128]{1,0:T(8,128)S(1)}, u32[]{:S(2)}, u32[]{:S(2)}) collective-permute-start(f32[8,128]{1,0:T(8,128)S(1)} %add.372), channel_id=1, source_target_pairs={{1,27},{3,25},{5,31},{7,29},{9,19},{11,17},{13,23},{15,21},{17,11}... | collective-permute-start | bytes 12296 | tf_op jit(solution)/shard_map/ppermute | solution.py:932
  305.0 5.7 %collective-permute-start.100 = (f32[8,128]{1,0:T(8,128)S(1)}, f32[8,128]{1,0:T(8,128)S(1)}, u32[]{:S(2)}, u32[]{:S(2)}) collective-permute-start(f32[8,128]{1,0:T(8,128)S(1)} %add.378), channel_id=1, source_target_pairs={{1,19},{3,17},{5,23},{7,21},{9,27},{11,25},{13,31},{15,29},{17,3},... | collective-permute-start | bytes 12296 | tf_op jit(solution)/shard_map/ppermute | solution.py:932
  305.6 5.2 %collective-permute-start.101 = (f32[8,128]{1,0:T(8,128)S(1)}, f32[8,128]{1,0:T(8,128)S(1)}, u32[]{:S(2)}, u32[]{:S(2)}) collective-permute-start(f32[8,128]{1,0:T(8,128)S(1)} %add.378), channel_id=1, source_target_pairs={{1,27},{3,25},{5,31},{7,29},{9,19},{11,17},{13,23},{15,21},{17,11}... | collective-permute-start | bytes 12296 | tf_op jit(solution)/shard_map/ppermute | solution.py:932
  322.5 11.3 %collective-permute-start.104 = (f32[2048,128]{1,0:T(8,128)S(1)}, f32[2048,128]{1,0:T(8,128)S(1)}, u32[]{:S(2)}, u32[]{:S(2)}) collective-permute-start(f32[2048,128]{1,0:T(8,128)S(1)} %get-tuple-element.454), channel_id=1, source_target_pairs={{0,1},{1,0},{2,3},{3,2},{4,5},{5,4},{6,7},{7,6},{8,9},{9,8},{10,11... | collective-permute-start | bytes 3145736 | tf_op jit(solution)/shard_map/ppermute | solution.py:906
  322.9 4.6 %collective-permute-start.105 = (f32[16,1024]{1,0:T(8,128)S(1)}, f32[16,1024]{1,0:T(8,128)S(1)}, u32[]{:S(2)}, u32[]{:S(2)}) collective-permute-start(f32[16,1024]{1,0:T(8,128)S(1)} %get-tuple-element.467.refs_4_), channel_id=1, source_target_pairs={{1,5},{3,7},{5,1},{7,3}} | collective-permute-start | bytes 196616 | tf_op jit(solution)/shard_map/ppermute | solution.py:913
  323.6 10.1 %collective-permute-start.106 = (f32[16,1024]{1,0:T(8,128)S(1)}, f32[16,1024]{1,0:T(8,128)S(1)}, u32[]{:S(2)}, u32[]{:S(2)}) collective-permute-start(f32[16,1024]{1,0:T(8,128)S(1)} %get-tuple-element.467.refs_4_), channel_id=1, source_target_pairs={{24,4},{25,1},{26,6},{27,3},{28,0},{29,5},{30,2},{31,7}} | collective-permute-start | bytes 196616 | tf_op jit(solution)/shard_map/ppermute | solution.py:913
  324.9 8.9 %collective-permute-start.107 = (f32[16,1024]{1,0:T(8,128)S(1)}, f32[16,1024]{1,0:T(8,128)S(1)}, u32[]{:S(2)}, u32[]{:S(2)}) collective-permute-start(f32[16,1024]{1,0:T(8,128)S(1)} %get-tuple-element.467.refs_4_), channel_id=1, source_target_pairs={{16,4},{17,1},{18,6},{19,3},{20,0},{21,5},{22,2},{23,7}} | collective-permute-start | bytes 196616 | tf_op jit(solution)/shard_map/ppermute | solution.py:913
  326.2 7.6 %collective-permute-start.108 = (f32[16,1024]{1,0:T(8,128)S(1)}, f32[16,1024]{1,0:T(8,128)S(1)}, u32[]{:S(2)}, u32[]{:S(2)}) collective-permute-start(f32[16,1024]{1,0:T(8,128)S(1)} %get-tuple-element.467.refs_4_), channel_id=1, source_target_pairs={{8,0},{9,5},{10,2},{11,7},{12,4},{13,1},{14,6},{15,3}} | collective-permute-start | bytes 196616 | tf_op jit(solution)/shard_map/ppermute | solution.py:913
  334.5 7.6 %collective-permute-start.109 = (f32[512,128]{1,0:T(8,128)S(1)}, f32[512,128]{1,0:T(8,128)S(1)}, u32[]{:S(2)}, u32[]{:S(2)}) collective-permute-start(f32[512,128]{1,0:T(8,128)S(1)} %get-tuple-element.459), channel_id=1, source_target_pairs={{0,8},{1,9},{2,10},{3,11},{4,12},{5,13},{6,14},{7,15},{8,0},{9,1},... | collective-permute-start | bytes 786440 | tf_op jit(solution)/shard_map/ppermute | solution.py:906
  334.6 13.3 %collective-permute-start.110 = (f32[512,128]{1,0:T(8,128)S(1)}, f32[512,128]{1,0:T(8,128)S(1)}, u32[]{:S(2)}, u32[]{:S(2)}) collective-permute-start(f32[512,128]{1,0:T(8,128)S(1)} %get-tuple-element.460), channel_id=1, source_target_pairs={{0,16},{1,17},{2,18},{3,19},{4,20},{5,21},{6,22},{7,23},{8,24},{9,... | collective-permute-start | bytes 786440 | tf_op jit(solution)/shard_map/ppermute | solution.py:906
  334.7 13.2 %collective-permute-start.111 = (f32[512,128]{1,0:T(8,128)S(1)}, f32[512,128]{1,0:T(8,128)S(1)}, u32[]{:S(2)}, u32[]{:S(2)}) collective-permute-start(f32[512,128]{1,0:T(8,128)S(1)} %get-tuple-element.461), channel_id=1, source_target_pairs={{0,24},{1,25},{2,26},{3,27},{4,28},{5,29},{6,30},{7,31},{8,16},{9,... | collective-permute-start | bytes 786440 | tf_op jit(solution)/shard_map/ppermute | solution.py:906
  348.5 4.7 %collective-permute-start.112 = (f32[128,128]{1,0:T(8,128)S(1)}, f32[128,128]{1,0:T(8,128)S(1)}, u32[]{:S(2)}, u32[]{:S(2)}) collective-permute-start(f32[128,128]{1,0:T(8,128)S(1)} %get-tuple-element.479), channel_id=1, source_target_pairs={{0,2},{1,3},{2,0},{3,1},{4,6},{5,7},{6,4},{7,5},{8,10},{9,11},{10,... | collective-permute-start | bytes 196616 | tf_op jit(solution)/shard_map/ppermute | solution.py:906
  350.0 8.6 %collective-permute-start.113 = (f32[128,128]{1,0:T(8,128)S(1)}, f32[128,128]{1,0:T(8,128)S(1)}, u32[]{:S(2)}, u32[]{:S(2)}) collective-permute-start(f32[128,128]{1,0:T(8,128)S(1)} %get-tuple-element.480), channel_id=1, source_target_pairs={{0,4},{1,5},{2,6},{3,7},{4,0},{5,1},{6,2},{7,3},{8,12},{9,13},{10,... | collective-permute-start | bytes 196616 | tf_op jit(solution)/shard_map/ppermute | solution.py:906
  351.0 7.5 %collective-permute-start.114 = (f32[128,128]{1,0:T(8,128)S(1)}, f32[128,128]{1,0:T(8,128)S(1)}, u32[]{:S(2)}, u32[]{:S(2)}) collective-permute-start(f32[128,128]{1,0:T(8,128)S(1)} %get-tuple-element.481), channel_id=1, source_target_pairs={{0,6},{1,7},{2,4},{3,5},{4,2},{5,3},{6,0},{7,1},{8,14},{9,15},{10,... | collective-permute-start | bytes 196616 | tf_op jit(solution)/shard_map/ppermute | solution.py:906
  359.1 4.5 %collective-permute-start.115 = (f32[128,128]{1,0:T(8,128)S(1)}, f32[128,128]{1,0:T(8,128)S(1)}, u32[]{:S(2)}, u32[]{:S(2)}) collective-permute-start(f32[128,128]{1,0:T(8,128)S(1)} %reduce_part.5.refs_0_), channel_id=1, source_target_pairs={{0,2},{1,3},{2,0},{3,1},{4,6},{5,7},{6,4},{7,5},{8,10},{9,11},{10,... | collective-permute-start | bytes 196616 | tf_op jit(solution)/shard_map/ppermute | solution.py:906
  360.9 7.9 %collective-permute-start.116 = (f32[128,128]{1,0:T(8,128)S(1)}, f32[128,128]{1,0:T(8,128)S(1)}, u32[]{:S(2)}, u32[]{:S(2)}) collective-permute-start(f32[128,128]{1,0:T(8,128)S(1)} %reduce_part.5.refs_0_), channel_id=1, source_target_pairs={{0,4},{1,5},{2,6},{3,7},{4,0},{5,1},{6,2},{7,3},{8,12},{9,13},{10,... | collective-permute-start | bytes 196616 | tf_op jit(solution)/shard_map/ppermute | solution.py:906
  361.8 7.0 %collective-permute-start.117 = (f32[128,128]{1,0:T(8,128)S(1)}, f32[128,128]{1,0:T(8,128)S(1)}, u32[]{:S(2)}, u32[]{:S(2)}) collective-permute-start(f32[128,128]{1,0:T(8,128)S(1)} %reduce_part.5.refs_0_), channel_id=1, source_target_pairs={{0,6},{1,7},{2,4},{3,5},{4,2},{5,3},{6,0},{7,1},{8,14},{9,15},{10,... | collective-permute-start | bytes 196616 | tf_op jit(solution)/shard_map/ppermute | solution.py:906
  369.4 8.9 %collective-permute-start.118 = (f32[512,128]{1,0:T(8,128)S(1)}, f32[512,128]{1,0:T(8,128)S(1)}, u32[]{:S(2)}, u32[]{:S(2)}) collective-permute-start(f32[512,128]{1,0:T(8,128)S(1)} %gather_part.2.refs_0_), channel_id=1, source_target_pairs={{0,8},{1,9},{2,10},{3,11},{4,12},{5,13},{6,14},{7,15},{8,0},{9,1},... | collective-permute-start | bytes 786440 | tf_op jit(solution)/shard_map/ppermute | solution.py:906
  371.2 11.1 %collective-permute-start.119 = (f32[512,128]{1,0:T(8,128)S(1)}, f32[512,128]{1,0:T(8,128)S(1)}, u32[]{:S(2)}, u32[]{:S(2)}) collective-permute-start(f32[512,128]{1,0:T(8,128)S(1)} %gather_part.2.refs_0_), channel_id=1, source_target_pairs={{0,16},{1,17},{2,18},{3,19},{4,20},{5,21},{6,22},{7,23},{8,24},{9,... | collective-permute-start | bytes 786440 | tf_op jit(solution)/shard_map/ppermute | solution.py:906
  371.4 10.9 %collective-permute-start.120 = (f32[512,128]{1,0:T(8,128)S(1)}, f32[512,128]{1,0:T(8,128)S(1)}, u32[]{:S(2)}, u32[]{:S(2)}) collective-permute-start(f32[512,128]{1,0:T(8,128)S(1)} %gather_part.2.refs_0_), channel_id=1, source_target_pairs={{0,24},{1,25},{2,26},{3,27},{4,28},{5,29},{6,30},{7,31},{8,16},{9,... | collective-permute-start | bytes 786440 | tf_op jit(solution)/shard_map/ppermute | solution.py:906
  (71 other events, 318.0 us)

commit v10 on v9

--- a/solution.py
+++ b/solution.py
@@ -859,7 +859,7 @@
             self.sum_rounds = in_pairs(dp_bits[:-1]) + in_pairs(section_bits)
         else:
             self.sum_rounds = in_pairs(dp_bits) + [section_bits[:1]]
-        self.all_rounds = [dp_bits[:1]] + in_pairs(section_bits) + in_pairs(dp_bits[1:])
+        self.all_rounds = [dp_bits[:1]] + in_pairs(section_bits) + [[bit] for bit in dp_bits[1:]]
 
     def slot(self, section, home):
         if not self.halved:

time: 395 us -> 402 us (1.018)
  waiting for transfers between devices: 88.2 us -> 98 us
    ppermute x46 -> x44, waiting for transfers between devices: 56.1 us -> 65.7 us  [exchanged(): lax.ppermute(value, ('section', 'dp'), [(own, own ^ mask) for own in rang...]
    ppermute x46 -> x44, starting transfers between devices: 64.7 us -> 60.8 us  [exchanged(): lax.ppermute(value, ('section', 'dp'), [(own, own ^ mask) for own in rang...]
    pallas_call x44 -> x46, Pallas kernels: 142 us -> 143 us  [run(): pl.pallas_call(kernel, out_shape=tuple((jax.ShapeDtypeStruct(shape, kind)...]
  transfers between devices with their start and end apart: 122 -> 120, of which waited for: 66 -> 67; matrix products, arithmetic and copies ran while one was open for 0% -> 0% of each run, Pallas kernels for 8% -> 8%
where the time goes in v10:
time: 402 us; the launch traced here: 396 us
  starting transfers between devices  148 us (37%)
  Pallas kernels  143 us (36%)
  waiting for transfers between devices  98 us (24%)
    pallas_call x46, Pallas kernels, run(): pl.pallas_call(kernel, out_shape=tuple((jax.ShapeDtypeStruct(shape, kind)...  143 us
    ppermute x64, starting transfers between devices, micro_sum(): total = total + lax.ppermute(value, ('section', 'dp'), pairs)  69 us
    ppermute x44, waiting for transfers between devices, exchanged(): lax.ppermute(value, ('section', 'dp'), [(own, own ^ mask) for own in rang...  65.7 us
    ppermute x44, starting transfers between devices, exchanged(): lax.ppermute(value, ('section', 'dp'), [(own, own ^ mask) for own in rang...  60.8 us
    ppermute x64, waiting for transfers between devices, micro_sum(): total = total + lax.ppermute(value, ('section', 'dp'), pairs)  25.3 us
    ppermute x12, starting transfers between devices, moved(): return lax.ppermute(value, ('section', 'dp'), going)  18.5 us
  transfers between devices with their start and end apart: 120, of which 67 were waited for; matrix products, arithmetic and copies ran while one was open for 0% of the time, Pallas kernels for 8%

profile of v10, /device:TPU:0, one launch (start us, length us, event | category | flops | bytes accessed | tf_op | source)
XLA Modules:
  0.0 396.0 jit_solution(5239350507062512213)
XLA Ops:
  1.2 2.7 enter.1
  4.7 5.9 %weights.1 = (f32[1024,128]{1,0:T(8,128)}, bf16[3872,256]{1,0:T(8,128)(2,1)}, bf16[5248,256]{1,0:T(8,128)(2,1)}, f32[24,128]{1,0:T(8,128)}) custom-call(f32[9,100,128]{2,1,0:T(8,128)} %w_input_ref.1, f32[75,1024]{1,0:T(8,128)} %maps_ref.3, f32[1,128]{1,0:T(1,128)} %bitcast.41, f32[9,128,128]{2,1,0:T(8,128)} %w_first_ref.1, f32[9,128,128]{2,1,0:T(8,128)} %w_second_ref.1, ...), custom_call_target="tpu_custom_call" | custom-call | tf_op jit(solution)/shard_map/weights/pallas_call | solution.py:787
  13.2 3.7 inlet.4
  16.9 4.9 %collective-permute-start.1 = (f32[8,128]{1,0:T(8,128)S(1)}, f32[8,128]{1,0:T(8,128)S(1)}, u32[]{:S(2)}, u32[]{:S(2)}) collective-permute-start(f32[8,128]{1,0:T(8,128)S(1)} %get-tuple-element.262), channel_id=1, source_target_pairs={{0,1},{1,0},{2,3},{3,2},{4,5},{5,4},{6,7},{7,6},{8,9},{9,8},{10,11... | collective-permute-start | bytes 12296 | tf_op jit(solution)/shard_map/ppermute | solution.py:906
  24.1 2.3 collective-permute-start.3
  28.0 2.9 collective-permute-done.4
  35.6 3.1 collective-permute-start.10
  40.2 3.0 collective-permute-done.8
  46.4 5.7 %outlet.4 = (f32[24,1024]{1,0:T(8,128)S(1)}, f32[16,1024]{1,0:T(8,128)S(1)}, f32[1024,128]{1,0:T(8,128)S(1)}, f32[1024,128]{1,0:T(8,128)S(1)}, f32[1024,128]{1,0:T(8,128)S(1)}) custom-call(f32[24,1024]{1,0:T(8,128)S(1)} %get-tuple-element.259.state_ref, f32[1024,128]{1,0:T(8,128)S(1)} %get-tuple-element.260.inner_ref, ...), custom_call_target="tpu_custom_call" | custom-call | tf_op jit(solution)/shard_map/outlet/pallas_call | solution.py:787
  52.2 3.1 inlet.5
  63.0 2.8 collective-permute-start.18
  70.9 2.0 collective-permute-start.22
  75.5 2.1 collective-permute-start.24
  78.4 5.7 %outlet.5 = (f32[24,1024]{1,0:T(8,128)S(1)}, f32[16,1024]{1,0:T(8,128)S(1)}, f32[1024,128]{1,0:T(8,128)S(1)}, f32[1024,128]{1,0:T(8,128)S(1)}, f32[1024,128]{1,0:T(8,128)S(1)}) custom-call(f32[24,1024]{1,0:T(8,128)S(1)} %get-tuple-element.418.state_ref, f32[1024,128]{1,0:T(8,128)S(1)} %get-tuple-element.271.inner_ref, ...), custom_call_target="tpu_custom_call" | custom-call | tf_op jit(solution)/shard_map/outlet/pallas_call | solution.py:787
  84.1 3.1 inlet.6
  95.0 2.8 collective-permute-start.30
  102.9 2.0 collective-permute-start.34
  107.4 2.1 collective-permute-start.36
  110.4 5.7 %outlet.6 = (f32[24,1024]{1,0:T(8,128)S(1)}, f32[16,1024]{1,0:T(8,128)S(1)}, f32[1024,128]{1,0:T(8,128)S(1)}, f32[1024,128]{1,0:T(8,128)S(1)}, f32[1024,128]{1,0:T(8,128)S(1)}) custom-call(f32[24,1024]{1,0:T(8,128)S(1)} %get-tuple-element.365.state_ref, f32[1024,128]{1,0:T(8,128)S(1)} %get-tuple-element.277.inner_ref, ...), custom_call_target="tpu_custom_call" | custom-call | tf_op jit(solution)/shard_map/outlet/pallas_call | solution.py:787
  116.1 3.1 inlet.7
  127.0 2.8 collective-permute-start.45
  134.9 2.0 collective-permute-start.49
  142.8 2.2 collective-permute-start.51
  145.8 6.4 %outlet.7 = (f32[24,1024]{1,0:T(8,128)}, f32[16,1024]{1,0:T(8,128)S(1)}, f32[1024,128]{1,0:T(8,128)S(1)}, f32[1024,128]{1,0:T(8,128)S(1)}, f32[1024,128]{1,0:T(8,128)S(1)}) custom-call(f32[24,1024]{1,0:T(8,128)S(1)} %get-tuple-element.325.state_ref, f32[1024,128]{1,0:T(8,128)S(1)} %get-tuple-element.287.inner_ref, ...), custom_call_target="tpu_custom_call" | custom-call | tf_op jit(solution)/shard_map/outlet/pallas_call | solution.py:787
  152.3 12.0 %outlet_back.4 = (f32[24,1024]{1,0:T(8,128)S(1)}, f32[1024,128]{1,0:T(8,128)S(1)}, f32[8,128]{1,0:T(8,128)S(1)}, f32[128,384]{1,0:T(8,128)S(1)}, f32[128,128]{1,...) custom-call(s32[2]{0:T(128)S(1)} %copy-done.7, ...), custom_call_target="tpu_custom_call", output_to_operand_aliasing={{3}: (12, {}), {4}: (13, {}), {5}: (14, {}), {6}: (15, {})} | custom-call | tf_op jit(solution)/shard_map/outlet_back/pallas_call | solution.py:787
  164.3 3.4 collective-permute-start.52
  168.6 2.6 collective-permute-start.53
  187.8 2.1 collective-permute-start.63
  190.7 2.9 inlet_back.4
  193.6 12.2 %outlet_back.5 = (f32[24,1024]{1,0:T(8,128)S(1)}, f32[1024,128]{1,0:T(8,128)S(1)}, f32[8,128]{1,0:T(8,128)S(1)}, f32[128,384]{1,0:T(8,128)S(1)}, f32[128,128]{1,...) custom-call(s32[2]{0:T(128)S(1)} %copy-done.7, ...), custom_call_target="tpu_custom_call", output_to_operand_aliasing={{3}: (12, {}), {4}: (13, {}), {5}: (14, {}), {6}: (15, {})} | custom-call | tf_op jit(solution)/shard_map/outlet_back/pallas_call | solution.py:787
  207.1 2.2 collective-permute-start.65
  211.5 1.9 inlet_grads.4
  214.0 2.2 collective-permute-start.69
  219.8 2.2 collective-permute-start.71
  229.3 2.9 inlet_back.5
  232.3 12.0 %outlet_back.6 = (f32[24,1024]{1,0:T(8,128)S(1)}, f32[1024,128]{1,0:T(8,128)S(1)}, f32[8,128]{1,0:T(8,128)S(1)}, f32[128,384]{1,0:T(8,128)S(1)}, f32[128,128]{1,...) custom-call(s32[2]{0:T(128)S(1)} %copy-done.7, ...), custom_call_target="tpu_custom_call", output_to_operand_aliasing={{3}: (12, {}), {4}: (13, {}), {5}: (14, {}), {6}: (15, {})} | custom-call | tf_op jit(solution)/shard_map/outlet_back/pallas_call | solution.py:787
  245.5 2.2 collective-permute-start.77
  249.8 2.0 inlet_grads.5
  252.4 2.2 collective-permute-start.81
  258.1 2.2 collective-permute-start.83
  267.6 2.9 inlet_back.6
  271.9 2.2 collective-permute-start.89
  274.1 3.8 collective-permute-start.90
  279.2 11.8 %outlet_back.7 = (f32[24,1024]{1,0:T(8,128)S(1)}, f32[1024,128]{1,0:T(8,128)S(1)}, f32[8,128]{1,0:T(8,128)S(1)}, f32[128,384]{1,0:T(8,128)S(1)}, f32[128,128]{1,...) custom-call(s32[2]{0:T(128)S(1)} %copy-done.7, ...), custom_call_target="tpu_custom_call", output_to_operand_aliasing={{3}: (12, {}), {4}: (13, {}), {5}: (14, {}), {6}: (15, {})} | custom-call | tf_op jit(solution)/shard_map/outlet_back/pallas_call | solution.py:787
  293.9 1.9 collective-permute-start.95
  296.7 2.0 inlet_grads.6
  298.7 2.7 collective-permute-start.97
  311.7 2.4 collective-permute-start.103
  315.0 3.5 inlet_back.7
  318.5 1.9 inlet_grads.7
  320.5 2.0 pack.1
  327.5 6.2 %collective-permute-done.106.refs_6_ = f32[16,1024]{1,0:T(8,128)S(1)} collective-permute-done((f32[16,1024]{1,0:T(8,128)S(1)}, f32[16,1024]{1,0:T(8,128)S(1)}, u32[]{:S(2)}, u32[]{:S(2)}) %collective-permute-start.106) | collective-permute-done | bytes 65568 | tf_op jit(solution)/shard_map/ppermute | solution.py:913
  334.7 3.4 collective-permute-start.111
  342.1 5.7 %collective-permute-done.110.refs_2_ = f32[512,128]{1,0:T(8,128)S(1)} collective-permute-done((f32[512,128]{1,0:T(8,128)S(1)}, f32[512,128]{1,0:T(8,128)S(1)}, u32[]{:S(2)}, u32[]{:S(2)}) %collective-permute-start.110) | collective-permute-done | bytes 262176 | tf_op jit(solution)/shard_map/ppermute | solution.py:906
  350.0 4.6 %collective-permute-done.112.refs_1_ = f32[256,128]{1,0:T(8,128)S(1)} collective-permute-done((f32[256,128]{1,0:T(8,128)S(1)}, f32[256,128]{1,0:T(8,128)S(1)}, u32[]{:S(2)}, u32[]{:S(2)}) %collective-permute-start.112) | collective-permute-done | bytes 131104 | tf_op jit(solution)/shard_map/ppermute | solution.py:906
  355.2 2.2 collective-permute-start.113
  357.4 4.4 %collective-permute-done.113.refs_1_ = f32[128,128]{1,0:T(8,128)S(1)} collective-permute-done((f32[128,128]{1,0:T(8,128)S(1)}, f32[128,128]{1,0:T(8,128)S(1)}, u32[]{:S(2)}, u32[]{:S(2)}) %collective-permute-start.113) | collective-permute-done | bytes 65568 | tf_op jit(solution)/shard_map/ppermute | solution.py:906
  363.2 4.9 %collective-permute-done.114.refs_1_ = f32[128,128]{1,0:T(8,128)S(1)} collective-permute-done((f32[128,128]{1,0:T(8,128)S(1)}, f32[128,128]{1,0:T(8,128)S(1)}, u32[]{:S(2)}, u32[]{:S(2)}) %collective-permute-start.114) | collective-permute-done | bytes 65568 | tf_op jit(solution)/shard_map/ppermute | solution.py:906
  368.8 5.0 %collective-permute-done.115.refs_1_ = f32[256,128]{1,0:T(8,128)S(1)} collective-permute-done((f32[256,128]{1,0:T(8,128)S(1)}, f32[256,128]{1,0:T(8,128)S(1)}, u32[]{:S(2)}, u32[]{:S(2)}) %collective-permute-start.115) | collective-permute-done | bytes 131104 | tf_op jit(solution)/shard_map/ppermute | solution.py:906
  374.3 2.6 collective-permute-start.116
  378.5 5.7 %collective-permute-done.116.refs_1_ = f32[512,128]{1,0:T(8,128)S(1)} collective-permute-done((f32[512,128]{1,0:T(8,128)S(1)}, f32[512,128]{1,0:T(8,128)S(1)}, u32[]{:S(2)}, u32[]{:S(2)}) %collective-permute-start.116) | collective-permute-done | bytes 262176 | tf_op jit(solution)/shard_map/ppermute | solution.py:906
  384.2 5.2 %collective-permute-done.117.refs_2_ = f32[512,128]{1,0:T(8,128)S(1)} collective-permute-done((f32[512,128]{1,0:T(8,128)S(1)}, f32[512,128]{1,0:T(8,128)S(1)}, u32[]{:S(2)}, u32[]{:S(2)}) %collective-permute-start.117) | collective-permute-done | bytes 262176 | tf_op jit(solution)/shard_map/ppermute | solution.py:906
  390.1 2.6 collective-permute-done.119.refs_1_
  392.7 2.0 unpack.1
  (311 shorter events, 152.7 us)
Async XLA Ops:
  3.9 6.7 %collective-permute-start = (f32[40,1024]{1,0:T(8,128)}, f32[40,1024]{1,0:T(8,128)S(1)}, u32[]{:S(2)}, u32[]{:S(2)}) collective-permute-start(f32[40,1024]{1,0:T(8,128)} %get-tuple-element.256.own_ref), channel_id=1, source_target_pairs={{1,5},{3,7},{5,1},{7,3},{9,13},{11,15},{13,9},{15,11},{16,20},{18,... | collective-permute-start | bytes 491528 | tf_op jit(solution)/shard_map/ppermute | solution.py:913
  16.9 5.7 %collective-permute-start.1 = (f32[8,128]{1,0:T(8,128)S(1)}, f32[8,128]{1,0:T(8,128)S(1)}, u32[]{:S(2)}, u32[]{:S(2)}) collective-permute-start(f32[8,128]{1,0:T(8,128)S(1)} %get-tuple-element.262), channel_id=1, source_target_pairs={{0,1},{1,0},{2,3},{3,2},{4,5},{5,4},{6,7},{7,6},{8,9},{9,8},{10,11... | collective-permute-start | bytes 12296 | tf_op jit(solution)/shard_map/ppermute | solution.py:906
  22.6 4.5 %collective-permute-start.2 = (f32[8,128]{1,0:T(8,128)S(1)}, f32[8,128]{1,0:T(8,128)S(1)}, u32[]{:S(2)}, u32[]{:S(2)}) collective-permute-start(f32[8,128]{1,0:T(8,128)S(1)} %add.288), channel_id=1, source_target_pairs={{1,11},{3,9},{5,15},{7,13},{9,3},{11,1},{13,7},{15,5},{17,27},{19,... | collective-permute-start | bytes 12296 | tf_op jit(solution)/shard_map/ppermute | solution.py:932
  24.1 3.9 collective-permute-start.3
  26.4 4.5 %collective-permute-start.4 = (f32[8,128]{1,0:T(8,128)S(1)}, f32[8,128]{1,0:T(8,128)S(1)}, u32[]{:S(2)}, u32[]{:S(2)}) collective-permute-start(f32[8,128]{1,0:T(8,128)S(1)} %add.288), channel_id=1, source_target_pairs={{1,27},{3,25},{5,31},{7,29},{9,19},{11,17},{13,23},{15,21},{17,11}... | collective-permute-start | bytes 12296 | tf_op jit(solution)/shard_map/ppermute | solution.py:932
  26.4 4.5 %collective-permute-start.5 = (f32[8,128]{1,0:T(8,128)S(1)}, f32[8,128]{1,0:T(8,128)S(1)}, u32[]{:S(2)}, u32[]{:S(2)}) collective-permute-start(f32[8,128]{1,0:T(8,128)S(1)} %add.288), channel_id=1, source_target_pairs={{1,3},{3,1},{5,7},{7,5},{9,11},{11,9},{13,15},{15,13},{17,19},{19,... | collective-permute-start | bytes 12296 | tf_op jit(solution)/shard_map/ppermute | solution.py:932
  35.6 4.7 %collective-permute-start.10 = (f32[8,128]{1,0:T(8,128)S(1)}, f32[8,128]{1,0:T(8,128)S(1)}, u32[]{:S(2)}, u32[]{:S(2)}) collective-permute-start(f32[8,128]{1,0:T(8,128)S(1)} %add.294), channel_id=1, source_target_pairs={{1,27},{3,25},{5,31},{7,29},{9,19},{11,17},{13,23},{15,21},{17,11}... | collective-permute-start | bytes 12296 | tf_op jit(solution)/shard_map/ppermute | solution.py:932
  56.5 4.1 %collective-permute-start.14 = (f32[8,128]{1,0:T(8,128)S(1)}, f32[8,128]{1,0:T(8,128)S(1)}, u32[]{:S(2)}, u32[]{:S(2)}) collective-permute-start(f32[8,128]{1,0:T(8,128)S(1)} %add.300), channel_id=1, source_target_pairs={{1,11},{3,9},{5,15},{7,13},{9,3},{11,1},{13,7},{15,5},{17,27},{19,... | collective-permute-start | bytes 12296 | tf_op jit(solution)/shard_map/ppermute | solution.py:932
  58.5 4.5 %collective-permute-start.16 = (f32[8,128]{1,0:T(8,128)S(1)}, f32[8,128]{1,0:T(8,128)S(1)}, u32[]{:S(2)}, u32[]{:S(2)}) collective-permute-start(f32[8,128]{1,0:T(8,128)S(1)} %add.300), channel_id=1, source_target_pairs={{1,27},{3,25},{5,31},{7,29},{9,19},{11,17},{13,23},{15,21},{17,11}... | collective-permute-start | bytes 12296 | tf_op jit(solution)/shard_map/ppermute | solution.py:932
  69.4 4.6 %collective-permute-start.20 = (f32[8,128]{1,0:T(8,128)S(1)}, f32[8,128]{1,0:T(8,128)S(1)}, u32[]{:S(2)}, u32[]{:S(2)}) collective-permute-start(f32[8,128]{1,0:T(8,128)S(1)} %add.306), channel_id=1, source_target_pairs={{1,11},{3,9},{5,15},{7,13},{9,3},{11,1},{13,7},{15,5},{17,27},{19,... | collective-permute-start | bytes 12296 | tf_op jit(solution)/shard_map/ppermute | solution.py:932
  70.9 4.5 %collective-permute-start.22 = (f32[8,128]{1,0:T(8,128)S(1)}, f32[8,128]{1,0:T(8,128)S(1)}, u32[]{:S(2)}, u32[]{:S(2)}) collective-permute-start(f32[8,128]{1,0:T(8,128)S(1)} %add.306), channel_id=1, source_target_pairs={{1,27},{3,25},{5,31},{7,29},{9,19},{11,17},{13,23},{15,21},{17,11}... | collective-permute-start | bytes 12296 | tf_op jit(solution)/shard_map/ppermute | solution.py:932
  88.5 4.1 %collective-permute-start.26 = (f32[8,128]{1,0:T(8,128)S(1)}, f32[8,128]{1,0:T(8,128)S(1)}, u32[]{:S(2)}, u32[]{:S(2)}) collective-permute-start(f32[8,128]{1,0:T(8,128)S(1)} %add.312), channel_id=1, source_target_pairs={{1,11},{3,9},{5,15},{7,13},{9,3},{11,1},{13,7},{15,5},{17,27},{19,... | collective-permute-start | bytes 12296 | tf_op jit(solution)/shard_map/ppermute | solution.py:932
  90.4 4.5 %collective-permute-start.28 = (f32[8,128]{1,0:T(8,128)S(1)}, f32[8,128]{1,0:T(8,128)S(1)}, u32[]{:S(2)}, u32[]{:S(2)}) collective-permute-start(f32[8,128]{1,0:T(8,128)S(1)} %add.312), channel_id=1, source_target_pairs={{1,27},{3,25},{5,31},{7,29},{9,19},{11,17},{13,23},{15,21},{17,11}... | collective-permute-start | bytes 12296 | tf_op jit(solution)/shard_map/ppermute | solution.py:932
  101.4 4.3 %collective-permute-start.32 = (f32[8,128]{1,0:T(8,128)S(1)}, f32[8,128]{1,0:T(8,128)S(1)}, u32[]{:S(2)}, u32[]{:S(2)}) collective-permute-start(f32[8,128]{1,0:T(8,128)S(1)} %add.318), channel_id=1, source_target_pairs={{1,11},{3,9},{5,15},{7,13},{9,3},{11,1},{13,7},{15,5},{17,27},{19,... | collective-permute-start | bytes 12296 | tf_op jit(solution)/shard_map/ppermute | solution.py:932
  102.9 4.5 %collective-permute-start.34 = (f32[8,128]{1,0:T(8,128)S(1)}, f32[8,128]{1,0:T(8,128)S(1)}, u32[]{:S(2)}, u32[]{:S(2)}) collective-permute-start(f32[8,128]{1,0:T(8,128)S(1)} %add.318), channel_id=1, source_target_pairs={{1,27},{3,25},{5,31},{7,29},{9,19},{11,17},{13,23},{15,21},{17,11}... | collective-permute-start | bytes 12296 | tf_op jit(solution)/shard_map/ppermute | solution.py:932
  120.5 4.1 %collective-permute-start.41 = (f32[8,128]{1,0:T(8,128)S(1)}, f32[8,128]{1,0:T(8,128)S(1)}, u32[]{:S(2)}, u32[]{:S(2)}) collective-permute-start(f32[8,128]{1,0:T(8,128)S(1)} %add.324), channel_id=1, source_target_pairs={{1,11},{3,9},{5,15},{7,13},{9,3},{11,1},{13,7},{15,5},{17,27},{19,... | collective-permute-start | bytes 12296 | tf_op jit(solution)/shard_map/ppermute | solution.py:932
  122.5 4.5 %collective-permute-start.43 = (f32[8,128]{1,0:T(8,128)S(1)}, f32[8,128]{1,0:T(8,128)S(1)}, u32[]{:S(2)}, u32[]{:S(2)}) collective-permute-start(f32[8,128]{1,0:T(8,128)S(1)} %add.324), channel_id=1, source_target_pairs={{1,27},{3,25},{5,31},{7,29},{9,19},{11,17},{13,23},{15,21},{17,11}... | collective-permute-start | bytes 12296 | tf_op jit(solution)/shard_map/ppermute | solution.py:932
  133.4 5.7 %collective-permute-start.47 = (f32[8,128]{1,0:T(8,128)S(1)}, f32[8,128]{1,0:T(8,128)S(1)}, u32[]{:S(2)}, u32[]{:S(2)}) collective-permute-start(f32[8,128]{1,0:T(8,128)S(1)} %add.330), channel_id=1, source_target_pairs={{1,11},{3,9},{5,15},{7,13},{9,3},{11,1},{13,7},{15,5},{17,27},{19,... | collective-permute-start | bytes 12296 | tf_op jit(solution)/shard_map/ppermute | solution.py:932
  134.9 6.0 %collective-permute-start.48 = (f32[8,128]{1,0:T(8,128)S(1)}, f32[8,128]{1,0:T(8,128)S(1)}, u32[]{:S(2)}, u32[]{:S(2)}) collective-permute-start(f32[8,128]{1,0:T(8,128)S(1)} %add.330), channel_id=1, source_target_pairs={{1,19},{3,17},{5,23},{7,21},{9,27},{11,25},{13,31},{15,29},{17,3},... | collective-permute-start | bytes 12296 | tf_op jit(solution)/shard_map/ppermute | solution.py:932
  134.9 7.9 %collective-permute-start.49 = (f32[8,128]{1,0:T(8,128)S(1)}, f32[8,128]{1,0:T(8,128)S(1)}, u32[]{:S(2)}, u32[]{:S(2)}) collective-permute-start(f32[8,128]{1,0:T(8,128)S(1)} %add.330), channel_id=1, source_target_pairs={{1,27},{3,25},{5,31},{7,29},{9,19},{11,17},{13,23},{15,21},{17,11}... | collective-permute-start | bytes 12296 | tf_op jit(solution)/shard_map/ppermute | solution.py:932
  136.9 5.9 %collective-permute-start.50 = (f32[8,128]{1,0:T(8,128)S(1)}, f32[8,128]{1,0:T(8,128)S(1)}, u32[]{:S(2)}, u32[]{:S(2)}) collective-permute-start(f32[8,128]{1,0:T(8,128)S(1)} %add.330), channel_id=1, source_target_pairs={{1,3},{3,1},{5,7},{7,5},{9,11},{11,9},{13,15},{15,13},{17,19},{19,... | collective-permute-start | bytes 12296 | tf_op jit(solution)/shard_map/ppermute | solution.py:932
  137.6 7.4 %collective-permute-start.37 = (f32[16,1024]{1,0:T(8,128)S(1)}, f32[16,1024]{1,0:T(8,128)S(1)}, u32[]{:S(2)}, u32[]{:S(2)}) collective-permute-start(f32[16,1024]{1,0:T(8,128)S(1)} %copy-done.12), channel_id=1, source_target_pairs={{0,8},{1,13},{2,10},{3,15},{4,12},{5,9},{6,14},{7,11},{8,20},{9,17... | collective-permute-start | bytes 196616 | tf_op jit(solution)/shard_map/ppermute | solution.py:913
  139.1 5.9 %collective-permute-start.38 = (f32[16,1024]{1,0:T(8,128)S(1)}, f32[16,1024]{1,0:T(8,128)S(1)}, u32[]{:S(2)}, u32[]{:S(2)}) collective-permute-start(f32[16,1024]{1,0:T(8,128)S(1)} %copy-done.11), channel_id=1, source_target_pairs={{0,20},{1,17},{2,22},{3,19},{4,16},{5,21},{6,18},{7,23},{8,28},{9,... | collective-permute-start | bytes 196616 | tf_op jit(solution)/shard_map/ppermute | solution.py:913
  140.9 4.7 %collective-permute-start.39 = (f32[16,1024]{1,0:T(8,128)S(1)}, f32[16,1024]{1,0:T(8,128)S(1)}, u32[]{:S(2)}, u32[]{:S(2)}) collective-permute-start(f32[16,1024]{1,0:T(8,128)S(1)} %copy-done.10), channel_id=1, source_target_pairs={{0,28},{1,25},{2,30},{3,27},{4,24},{5,29},{6,26},{7,31},{8,0},{9,5... | collective-permute-start | bytes 196616 | tf_op jit(solution)/shard_map/ppermute | solution.py:913
  164.3 4.3 %collective-permute-start.52 = (f32[8,128]{1,0:T(8,128)S(1)}, f32[8,128]{1,0:T(8,128)S(1)}, u32[]{:S(2)}, u32[]{:S(2)}) collective-permute-start(f32[8,128]{1,0:T(8,128)S(1)} %get-tuple-element.297), channel_id=1, source_target_pairs={{0,1},{1,0},{2,3},{3,2},{4,5},{5,4},{6,7},{7,6},{8,9},{9,8},{10,11... | collective-permute-start | bytes 12296 | tf_op jit(solution)/shard_map/ppermute | solution.py:906
  168.6 4.7 %collective-permute-start.53 = (f32[8,128]{1,0:T(8,128)S(1)}, f32[8,128]{1,0:T(8,128)S(1)}, u32[]{:S(2)}, u32[]{:S(2)}) collective-permute-start(f32[8,128]{1,0:T(8,128)S(1)} %add.336), channel_id=1, source_target_pairs={{1,11},{3,9},{5,15},{7,13},{9,3},{11,1},{13,7},{15,5},{17,27},{19,... | collective-permute-start | bytes 12296 | tf_op jit(solution)/shard_map/ppermute | solution.py:932
  171.5 4.5 %collective-permute-start.55 = (f32[8,128]{1,0:T(8,128)S(1)}, f32[8,128]{1,0:T(8,128)S(1)}, u32[]{:S(2)}, u32[]{:S(2)}) collective-permute-start(f32[8,128]{1,0:T(8,128)S(1)} %add.336), channel_id=1, source_target_pairs={{1,27},{3,25},{5,31},{7,29},{9,19},{11,17},{13,23},{15,21},{17,11}... | collective-permute-start | bytes 12296 | tf_op jit(solution)/shard_map/ppermute | solution.py:932
  181.2 5.7 %collective-permute-start.59 = (f32[8,128]{1,0:T(8,128)S(1)}, f32[8,128]{1,0:T(8,128)S(1)}, u32[]{:S(2)}, u32[]{:S(2)}) collective-permute-start(f32[8,128]{1,0:T(8,128)S(1)} %add.342), channel_id=1, source_target_pairs={{1,11},{3,9},{5,15},{7,13},{9,3},{11,1},{13,7},{15,5},{17,27},{19,... | collective-permute-start | bytes 12296 | tf_op jit(solution)/shard_map/ppermute | solution.py:932
  182.7 4.3 %collective-permute-start.60 = (f32[8,128]{1,0:T(8,128)S(1)}, f32[8,128]{1,0:T(8,128)S(1)}, u32[]{:S(2)}, u32[]{:S(2)}) collective-permute-start(f32[8,128]{1,0:T(8,128)S(1)} %add.342), channel_id=1, source_target_pairs={{1,19},{3,17},{5,23},{7,21},{9,27},{11,25},{13,31},{15,29},{17,3},... | collective-permute-start | bytes 12296 | tf_op jit(solution)/shard_map/ppermute | solution.py:932
  183.2 4.5 %collective-permute-start.61 = (f32[8,128]{1,0:T(8,128)S(1)}, f32[8,128]{1,0:T(8,128)S(1)}, u32[]{:S(2)}, u32[]{:S(2)}) collective-permute-start(f32[8,128]{1,0:T(8,128)S(1)} %add.342), channel_id=1, source_target_pairs={{1,27},{3,25},{5,31},{7,29},{9,19},{11,17},{13,23},{15,21},{17,11}... | collective-permute-start | bytes 12296 | tf_op jit(solution)/shard_map/ppermute | solution.py:932
  207.1 6.3 %collective-permute-start.65 = (f32[8,128]{1,0:T(8,128)S(1)}, f32[8,128]{1,0:T(8,128)S(1)}, u32[]{:S(2)}, u32[]{:S(2)}) collective-permute-start(f32[8,128]{1,0:T(8,128)S(1)} %add.348), channel_id=1, source_target_pairs={{1,11},{3,9},{5,15},{7,13},{9,3},{11,1},{13,7},{15,5},{17,27},{19,... | collective-permute-start | bytes 12296 | tf_op jit(solution)/shard_map/ppermute | solution.py:932
  209.3 4.2 %collective-permute-start.66 = (f32[8,128]{1,0:T(8,128)S(1)}, f32[8,128]{1,0:T(8,128)S(1)}, u32[]{:S(2)}, u32[]{:S(2)}) collective-permute-start(f32[8,128]{1,0:T(8,128)S(1)} %add.348), channel_id=1, source_target_pairs={{1,19},{3,17},{5,23},{7,21},{9,27},{11,25},{13,31},{15,29},{17,3},... | collective-permute-start | bytes 12296 | tf_op jit(solution)/shard_map/ppermute | solution.py:932
  209.5 4.5 %collective-permute-start.67 = (f32[8,128]{1,0:T(8,128)S(1)}, f32[8,128]{1,0:T(8,128)S(1)}, u32[]{:S(2)}, u32[]{:S(2)}) collective-permute-start(f32[8,128]{1,0:T(8,128)S(1)} %add.348), channel_id=1, source_target_pairs={{1,27},{3,25},{5,31},{7,29},{9,19},{11,17},{13,23},{15,21},{17,11}... | collective-permute-start | bytes 12296 | tf_op jit(solution)/shard_map/ppermute | solution.py:932
  219.8 5.8 %collective-permute-start.71 = (f32[8,128]{1,0:T(8,128)S(1)}, f32[8,128]{1,0:T(8,128)S(1)}, u32[]{:S(2)}, u32[]{:S(2)}) collective-permute-start(f32[8,128]{1,0:T(8,128)S(1)} %add.354), channel_id=1, source_target_pairs={{1,11},{3,9},{5,15},{7,13},{9,3},{11,1},{13,7},{15,5},{17,27},{19,... | collective-permute-start | bytes 12296 | tf_op jit(solution)/shard_map/ppermute | solution.py:932
  222.2 4.5 %collective-permute-start.73 = (f32[8,128]{1,0:T(8,128)S(1)}, f32[8,128]{1,0:T(8,128)S(1)}, u32[]{:S(2)}, u32[]{:S(2)}) collective-permute-start(f32[8,128]{1,0:T(8,128)S(1)} %add.354), channel_id=1, source_target_pairs={{1,27},{3,25},{5,31},{7,29},{9,19},{11,17},{13,23},{15,21},{17,11}... | collective-permute-start | bytes 12296 | tf_op jit(solution)/shard_map/ppermute | solution.py:932
  245.5 6.3 %collective-permute-start.77 = (f32[8,128]{1,0:T(8,128)S(1)}, f32[8,128]{1,0:T(8,128)S(1)}, u32[]{:S(2)}, u32[]{:S(2)}) collective-permute-start(f32[8,128]{1,0:T(8,128)S(1)} %add.360), channel_id=1, source_target_pairs={{1,11},{3,9},{5,15},{7,13},{9,3},{11,1},{13,7},{15,5},{17,27},{19,... | collective-permute-start | bytes 12296 | tf_op jit(solution)/shard_map/ppermute | solution.py:932
  247.7 4.1 %collective-permute-start.78 = (f32[8,128]{1,0:T(8,128)S(1)}, f32[8,128]{1,0:T(8,128)S(1)}, u32[]{:S(2)}, u32[]{:S(2)}) collective-permute-start(f32[8,128]{1,0:T(8,128)S(1)} %add.360), channel_id=1, source_target_pairs={{1,19},{3,17},{5,23},{7,21},{9,27},{11,25},{13,31},{15,29},{17,3},... | collective-permute-start | bytes 12296 | tf_op jit(solution)/shard_map/ppermute | solution.py:932
  247.9 4.5 %collective-permute-start.79 = (f32[8,128]{1,0:T(8,128)S(1)}, f32[8,128]{1,0:T(8,128)S(1)}, u32[]{:S(2)}, u32[]{:S(2)}) collective-permute-start(f32[8,128]{1,0:T(8,128)S(1)} %add.360), channel_id=1, source_target_pairs={{1,27},{3,25},{5,31},{7,29},{9,19},{11,17},{13,23},{15,21},{17,11}... | collective-permute-start | bytes 12296 | tf_op jit(solution)/shard_map/ppermute | solution.py:932
  258.1 5.8 %collective-permute-start.83 = (f32[8,128]{1,0:T(8,128)S(1)}, f32[8,128]{1,0:T(8,128)S(1)}, u32[]{:S(2)}, u32[]{:S(2)}) collective-permute-start(f32[8,128]{1,0:T(8,128)S(1)} %add.366), channel_id=1, source_target_pairs={{1,11},{3,9},{5,15},{7,13},{9,3},{11,1},{13,7},{15,5},{17,27},{19,... | collective-permute-start | bytes 12296 | tf_op jit(solution)/shard_map/ppermute | solution.py:932
  260.5 4.5 %collective-permute-start.85 = (f32[8,128]{1,0:T(8,128)S(1)}, f32[8,128]{1,0:T(8,128)S(1)}, u32[]{:S(2)}, u32[]{:S(2)}) collective-permute-start(f32[8,128]{1,0:T(8,128)S(1)} %add.366), channel_id=1, source_target_pairs={{1,27},{3,25},{5,31},{7,29},{9,19},{11,17},{13,23},{15,21},{17,11}... | collective-permute-start | bytes 12296 | tf_op jit(solution)/shard_map/ppermute | solution.py:932
  271.2 19.8 %collective-permute-start.88 = (f32[32,1024]{1,0:T(8,128)S(1)}, f32[32,1024]{1,0:T(8,128)S(1)}, u32[]{:S(2)}, u32[]{:S(2)}) collective-permute-start(f32[32,1024]{1,0:T(8,128)S(1)} %get-tuple-element.462.kept_ref), channel_id=1, source_target_pairs={{1,5},{3,7},{5,1},{7,3},{9,13},{11,15},{13,9},{15,11},{16,20},{18,... | collective-permute-start | bytes 393224 | tf_op jit(solution)/shard_map/ppermute | solution.py:913
  271.9 19.2 %collective-permute-start.89 = (f32[32,1024]{1,0:T(8,128)S(1)}, f32[32,1024]{1,0:T(8,128)S(1)}, u32[]{:S(2)}, u32[]{:S(2)}) collective-permute-start(f32[32,1024]{1,0:T(8,128)S(1)} %get-tuple-element.403), channel_id=1, source_target_pairs={{0,8},{1,13},{2,10},{3,15},{4,12},{5,9},{6,14},{7,11},{8,16},{9,21... | collective-permute-start | bytes 393224 | tf_op jit(solution)/shard_map/ppermute | solution.py:913
  274.1 16.9 %collective-permute-start.90 = (f32[32,1024]{1,0:T(8,128)S(1)}, f32[32,1024]{1,0:T(8,128)S(1)}, u32[]{:S(2)}, u32[]{:S(2)}) collective-permute-start(f32[32,1024]{1,0:T(8,128)S(1)} %get-tuple-element.404), channel_id=1, source_target_pairs={{0,16},{1,21},{2,18},{3,23},{4,20},{5,17},{6,22},{7,19},{8,24},{9,... | collective-permute-start | bytes 393224 | tf_op jit(solution)/shard_map/ppermute | solution.py:913
  277.9 13.2 %collective-permute-start.91 = (f32[32,1024]{1,0:T(8,128)S(1)}, f32[32,1024]{1,0:T(8,128)S(1)}, u32[]{:S(2)}, u32[]{:S(2)}) collective-permute-start(f32[32,1024]{1,0:T(8,128)S(1)} %get-tuple-element.405), channel_id=1, source_target_pairs={{0,24},{1,29},{2,26},{3,31},{4,28},{5,25},{6,30},{7,27},{8,0},{9,5... | collective-permute-start | bytes 393224 | tf_op jit(solution)/shard_map/ppermute | solution.py:913
  292.3 6.4 %collective-permute-start.93 = (f32[8,128]{1,0:T(8,128)S(1)}, f32[8,128]{1,0:T(8,128)S(1)}, u32[]{:S(2)}, u32[]{:S(2)}) collective-permute-start(f32[8,128]{1,0:T(8,128)S(1)} %add.372), channel_id=1, source_target_pairs={{1,11},{3,9},{5,15},{7,13},{9,3},{11,1},{13,7},{15,5},{17,27},{19,... | collective-permute-start | bytes 12296 | tf_op jit(solution)/shard_map/ppermute | solution.py:932
  293.2 5.5 %collective-permute-start.94 = (f32[8,128]{1,0:T(8,128)S(1)}, f32[8,128]{1,0:T(8,128)S(1)}, u32[]{:S(2)}, u32[]{:S(2)}) collective-permute-start(f32[8,128]{1,0:T(8,128)S(1)} %add.372), channel_id=1, source_target_pairs={{1,19},{3,17},{5,23},{7,21},{9,27},{11,25},{13,31},{15,29},{17,3},... | collective-permute-start | bytes 12296 | tf_op jit(solution)/shard_map/ppermute | solution.py:932
  293.9 4.8 %collective-permute-start.95 = (f32[8,128]{1,0:T(8,128)S(1)}, f32[8,128]{1,0:T(8,128)S(1)}, u32[]{:S(2)}, u32[]{:S(2)}) collective-permute-start(f32[8,128]{1,0:T(8,128)S(1)} %add.372), channel_id=1, source_target_pairs={{1,27},{3,25},{5,31},{7,29},{9,19},{11,17},{13,23},{15,21},{17,11}... | collective-permute-start | bytes 12296 | tf_op jit(solution)/shard_map/ppermute | solution.py:932
  305.0 5.7 %collective-permute-start.100 = (f32[8,128]{1,0:T(8,128)S(1)}, f32[8,128]{1,0:T(8,128)S(1)}, u32[]{:S(2)}, u32[]{:S(2)}) collective-permute-start(f32[8,128]{1,0:T(8,128)S(1)} %add.378), channel_id=1, source_target_pairs={{1,19},{3,17},{5,23},{7,21},{9,27},{11,25},{13,31},{15,29},{17,3},... | collective-permute-start | bytes 12296 | tf_op jit(solution)/shard_map/ppermute | solution.py:932
  305.6 5.2 %collective-permute-start.101 = (f32[8,128]{1,0:T(8,128)S(1)}, f32[8,128]{1,0:T(8,128)S(1)}, u32[]{:S(2)}, u32[]{:S(2)}) collective-permute-start(f32[8,128]{1,0:T(8,128)S(1)} %add.378), channel_id=1, source_target_pairs={{1,27},{3,25},{5,31},{7,29},{9,19},{11,17},{13,23},{15,21},{17,11}... | collective-permute-start | bytes 12296 | tf_op jit(solution)/shard_map/ppermute | solution.py:932
  322.5 11.3 %collective-permute-start.104 = (f32[2048,128]{1,0:T(8,128)S(1)}, f32[2048,128]{1,0:T(8,128)S(1)}, u32[]{:S(2)}, u32[]{:S(2)}) collective-permute-start(f32[2048,128]{1,0:T(8,128)S(1)} %get-tuple-element.454), channel_id=1, source_target_pairs={{0,1},{1,0},{2,3},{3,2},{4,5},{5,4},{6,7},{7,6},{8,9},{9,8},{10,11... | collective-permute-start | bytes 3145736 | tf_op jit(solution)/shard_map/ppermute | solution.py:906
  322.9 4.6 %collective-permute-start.105 = (f32[16,1024]{1,0:T(8,128)S(1)}, f32[16,1024]{1,0:T(8,128)S(1)}, u32[]{:S(2)}, u32[]{:S(2)}) collective-permute-start(f32[16,1024]{1,0:T(8,128)S(1)} %get-tuple-element.467.refs_4_), channel_id=1, source_target_pairs={{1,5},{3,7},{5,1},{7,3}} | collective-permute-start | bytes 196616 | tf_op jit(solution)/shard_map/ppermute | solution.py:913
  323.6 10.1 %collective-permute-start.106 = (f32[16,1024]{1,0:T(8,128)S(1)}, f32[16,1024]{1,0:T(8,128)S(1)}, u32[]{:S(2)}, u32[]{:S(2)}) collective-permute-start(f32[16,1024]{1,0:T(8,128)S(1)} %get-tuple-element.467.refs_4_), channel_id=1, source_target_pairs={{24,4},{25,1},{26,6},{27,3},{28,0},{29,5},{30,2},{31,7}} | collective-permute-start | bytes 196616 | tf_op jit(solution)/shard_map/ppermute | solution.py:913
  324.9 8.9 %collective-permute-start.107 = (f32[16,1024]{1,0:T(8,128)S(1)}, f32[16,1024]{1,0:T(8,128)S(1)}, u32[]{:S(2)}, u32[]{:S(2)}) collective-permute-start(f32[16,1024]{1,0:T(8,128)S(1)} %get-tuple-element.467.refs_4_), channel_id=1, source_target_pairs={{16,4},{17,1},{18,6},{19,3},{20,0},{21,5},{22,2},{23,7}} | collective-permute-start | bytes 196616 | tf_op jit(solution)/shard_map/ppermute | solution.py:913
  326.2 7.6 %collective-permute-start.108 = (f32[16,1024]{1,0:T(8,128)S(1)}, f32[16,1024]{1,0:T(8,128)S(1)}, u32[]{:S(2)}, u32[]{:S(2)}) collective-permute-start(f32[16,1024]{1,0:T(8,128)S(1)} %get-tuple-element.467.refs_4_), channel_id=1, source_target_pairs={{8,0},{9,5},{10,2},{11,7},{12,4},{13,1},{14,6},{15,3}} | collective-permute-start | bytes 196616 | tf_op jit(solution)/shard_map/ppermute | solution.py:913
  334.5 7.6 %collective-permute-start.109 = (f32[512,128]{1,0:T(8,128)S(1)}, f32[512,128]{1,0:T(8,128)S(1)}, u32[]{:S(2)}, u32[]{:S(2)}) collective-permute-start(f32[512,128]{1,0:T(8,128)S(1)} %get-tuple-element.459), channel_id=1, source_target_pairs={{0,8},{1,9},{2,10},{3,11},{4,12},{5,13},{6,14},{7,15},{8,0},{9,1},... | collective-permute-start | bytes 786440 | tf_op jit(solution)/shard_map/ppermute | solution.py:906
  334.6 13.3 %collective-permute-start.110 = (f32[512,128]{1,0:T(8,128)S(1)}, f32[512,128]{1,0:T(8,128)S(1)}, u32[]{:S(2)}, u32[]{:S(2)}) collective-permute-start(f32[512,128]{1,0:T(8,128)S(1)} %get-tuple-element.460), channel_id=1, source_target_pairs={{0,16},{1,17},{2,18},{3,19},{4,20},{5,21},{6,22},{7,23},{8,24},{9,... | collective-permute-start | bytes 786440 | tf_op jit(solution)/shard_map/ppermute | solution.py:906
  334.7 13.2 %collective-permute-start.111 = (f32[512,128]{1,0:T(8,128)S(1)}, f32[512,128]{1,0:T(8,128)S(1)}, u32[]{:S(2)}, u32[]{:S(2)}) collective-permute-start(f32[512,128]{1,0:T(8,128)S(1)} %get-tuple-element.461), channel_id=1, source_target_pairs={{0,24},{1,25},{2,26},{3,27},{4,28},{5,29},{6,30},{7,31},{8,16},{9,... | collective-permute-start | bytes 786440 | tf_op jit(solution)/shard_map/ppermute | solution.py:906
  348.5 6.1 %collective-permute-start.112 = (f32[256,128]{1,0:T(8,128)S(1)}, f32[256,128]{1,0:T(8,128)S(1)}, u32[]{:S(2)}, u32[]{:S(2)}) collective-permute-start(f32[256,128]{1,0:T(8,128)S(1)} %get-tuple-element.479), channel_id=1, source_target_pairs={{0,2},{1,3},{2,0},{3,1},{4,6},{5,7},{6,4},{7,5},{8,10},{9,11},{10,... | collective-permute-start | bytes 393224 | tf_op jit(solution)/shard_map/ppermute | solution.py:906
  355.2 6.6 %collective-permute-start.113 = (f32[128,128]{1,0:T(8,128)S(1)}, f32[128,128]{1,0:T(8,128)S(1)}, u32[]{:S(2)}, u32[]{:S(2)}) collective-permute-start(f32[128,128]{1,0:T(8,128)S(1)} %get-tuple-element.481), channel_id=1, source_target_pairs={{0,4},{1,5},{2,6},{3,7},{4,0},{5,1},{6,2},{7,3},{8,12},{9,13},{10,... | collective-permute-start | bytes 196616 | tf_op jit(solution)/shard_map/ppermute | solution.py:906
  362.4 5.7 %collective-permute-start.114 = (f32[128,128]{1,0:T(8,128)S(1)}, f32[128,128]{1,0:T(8,128)S(1)}, u32[]{:S(2)}, u32[]{:S(2)}) collective-permute-start(f32[128,128]{1,0:T(8,128)S(1)} %reduce_part.7.refs_0_), channel_id=1, source_target_pairs={{0,4},{1,5},{2,6},{3,7},{4,0},{5,1},{6,2},{7,3},{8,12},{9,13},{10,... | collective-permute-start | bytes 196616 | tf_op jit(solution)/shard_map/ppermute | solution.py:906
  368.7 5.0 %collective-permute-start.115 = (f32[256,128]{1,0:T(8,128)S(1)}, f32[256,128]{1,0:T(8,128)S(1)}, u32[]{:S(2)}, u32[]{:S(2)}) collective-permute-start(f32[256,128]{1,0:T(8,128)S(1)} %gather_part.3.refs_0_), channel_id=1, source_target_pairs={{0,2},{1,3},{2,0},{3,1},{4,6},{5,7},{6,4},{7,5},{8,10},{9,11},{10,... | collective-permute-start | bytes 393224 | tf_op jit(solution)/shard_map/ppermute | solution.py:906
  374.3 9.8 %collective-permute-start.116 = (f32[512,128]{1,0:T(8,128)S(1)}, f32[512,128]{1,0:T(8,128)S(1)}, u32[]{:S(2)}, u32[]{:S(2)}) collective-permute-start(f32[512,128]{1,0:T(8,128)S(1)} %gather_part.4.refs_0_), channel_id=1, source_target_pairs={{0,8},{1,9},{2,10},{3,11},{4,12},{5,13},{6,14},{7,15},{8,0},{9,1},... | collective-permute-start | bytes 786440 | tf_op jit(solution)/shard_map/ppermute | solution.py:906
  376.9 12.4 %collective-permute-start.117 = (f32[512,128]{1,0:T(8,128)S(1)}, f32[512,128]{1,0:T(8,128)S(1)}, u32[]{:S(2)}, u32[]{:S(2)}) collective-permute-start(f32[512,128]{1,0:T(8,128)S(1)} %gather_part.4.refs_0_), channel_id=1, source_target_pairs={{0,16},{1,17},{2,18},{3,19},{4,20},{5,21},{6,22},{7,23},{8,24},{9,... | collective-permute-start | bytes 786440 | tf_op jit(solution)/shard_map/ppermute | solution.py:906
  376.9 12.4 %collective-permute-start.118 = (f32[512,128]{1,0:T(8,128)S(1)}, f32[512,128]{1,0:T(8,128)S(1)}, u32[]{:S(2)}, u32[]{:S(2)}) collective-permute-start(f32[512,128]{1,0:T(8,128)S(1)} %gather_part.4.refs_0_), channel_id=1, source_target_pairs={{0,24},{1,25},{2,26},{3,27},{4,28},{5,29},{6,30},{7,31},{8,16},{9,... | collective-permute-start | bytes 786440 | tf_op jit(solution)/shard_map/ppermute | solution.py:906
  (69 other events, 310.1 us)
